TPU v7x, 32 devices: a whole 2x2x4 slice. The times are simulated.
32 devices in a mesh: tile: 16 (over z, x, core), depth: 2 (over y).
Axes of the slice: x: 2, y: 2, z: 4, core: 2. Of those that a mesh axis runs over, the one named last changes fastest.
Arguments:
- mask_tiles: float32 [32, 128, 128], P('tile'), may hold values from 0 to 1
- target_tiles: int32 [32, 128, 128], P('tile'), may hold values 0 or 1
- kernels: float32 [2, 2, 6, 25, 25], P(None, 'depth'), may hold values from -0.25 to 0.25
- socs_weights: float32 [2, 6], P('depth'), may hold values from 0.1 to 1
- thresholds: float32 [2], P('depth'), may hold values from 0.8 to 2.4
- partner_table: int32 [32], P('tile'), may hold values from 0 to 31, as said below
- mirror_flags: int32 [32], P('tile'), may hold values from 0 to 1, as said below
Outputs:
- mask_final: float32 [32, 128, 128], P('tile')
- step_gradient: float32 [32, 128, 128], P('tile')
Inputs may be any that keep to these rules, and one draw needn't show every extreme that they name: partner_table[t] is t itself or t XOR 2^b for some bit b, and partner_table[partner_table[t]] = t. mirror_flags is equal for the two tiles of a matched pair.
All inputs are finite; a program needn't handle non-finite values. No bound on the sum of `target_tiles` on one device may be relied on, other than what follows from the above.
Results may differ from a plain program's by a relative error of at most 0.0003.
Values sent between devices are 32-bit elements; how exact they have to be, the bound alone decides.
No kernel may reach another device: no remote copies, remote signals or barrier semaphores. Data moves between devices by JAX's collectives and lax.ppermute only.
A program may use at most 128 MiB of HBM per device.

v0:
```python
import functools

import jax
import jax.numpy as jnp
import ml_dtypes
import numpy as np
from jax import lax
from jax.experimental import pallas as pl
from jax.experimental.pallas import tpu as pltpu
from jax.sharding import PartitionSpec as P

HALO = 12
KSIZE = 25
STEPS = 2
STEEPNESS = 3.0
STEP_RATE = 0.05

CORE = 128
NY = 152
NX = 176
WIDE = 2 * HALO
XB = 96
YB = 128
NU = NY // 2 + 1
NV = NX // 2 + 1
ROWS = 160
ROW0 = 8
EDGE = 48
SLICE = 4
VMEM_LIMIT = 48 * 1024 * 1024

f32 = jnp.float32
bf16 = jnp.bfloat16


def np_split(a):
    hi = np.asarray(a, np.float32).astype(ml_dtypes.bfloat16)
    lo = (np.asarray(a, np.float64) - hi.astype(np.float64)).astype(ml_dtypes.bfloat16)
    return hi, lo


def x_rows(cols):
    out = np.zeros((2 * XB, len(cols)))
    ang = 2 * np.pi * np.outer(np.arange(NV), cols) / NX
    out[:NV] = np.cos(ang)
    out[XB : XB + NV] = np.sin(ang)
    out[XB] = 0.0
    out[XB + NV - 1] = 0.0
    return out


def y_lanes(rows):
    out = np.zeros((len(rows), 2 * YB))
    ang = 2 * np.pi * np.outer(rows, np.arange(NU)) / NY
    out[:, :NU] = np.cos(ang)
    out[:, YB : YB + NU] = np.sin(ang)
    out[:, YB] = 0.0
    out[:, YB + NU - 1] = 0.0
    return out


def half_weights(bins):
    weights = np.full(bins, 2.0)
    weights[0] = weights[-1] = 1.0
    return weights


def x_back(cols):
    kappa = np.zeros(2 * XB)
    kappa[:NV] = half_weights(NV) / 2
    kappa[XB : XB + NV] = half_weights(NV) / 2
    return x_rows(cols).T * kappa


def y_back(rows):
    weight = np.zeros(2 * YB)
    weight[:NU] = half_weights(NU)
    weight[YB : YB + NU] = -half_weights(NU)
    return (y_lanes(rows) * weight).T / (NX * NY)


def strip_rows(sliced, rows_each):
    idx = np.arange(2 * CORE)
    if not sliced:
        return idx // CORE, idx % CORE
    part, rest = idx // (2 * rows_each), idx % (2 * rows_each)
    return rest // rows_each, part * rows_each + rest % rows_each


def window_rows(sliced, rows_each, tile):
    t, r = strip_rows(sliced, rows_each)
    pos = t * CORE + r - tile * CORE + HALO
    return pos, (pos >= 0) & (pos < NY)


@functools.lru_cache(None)
def tables():
    tb = {}
    core_rows = np.arange(HALO, HALO + CORE)
    field_cols = np.arange(ROW0, ROW0 + ROWS)
    own_cols = np.arange(WIDE, WIDE + CORE)

    def put(name, a):
        tb[name + "_hi"], tb[name + "_lo"] = np_split(a)

    put("cx_own", x_rows(own_cols))
    left = np.zeros((2 * XB, EDGE))
    left[:, :WIDE] = x_rows(np.arange(WIDE))
    right = np.zeros((2 * XB, EDGE))
    right[:, :WIDE] = x_rows(np.arange(WIDE + CORE, NX))
    put("cx_left", left)
    put("cx_right", right)
    both = np.zeros((2 * XB, 256))
    both[:, :CORE] = x_rows(own_cols)
    both[:, 256 - WIDE :] = x_rows(np.arange(WIDE))
    both[:, CORE : CORE + WIDE] = x_rows(np.arange(WIDE + CORE, NX))
    put("cx_both", both)
    for name, sliced in (("by_nat", False), ("by_sl", True)):
        mats = []
        for t in range(2):
            pos, inside = window_rows(sliced, SLICE, t)
            mats.append(y_lanes(pos) * inside[:, None])
        put(name, np.concatenate(mats, axis=1))
    put("x2", x_back(field_cols))
    put("y2", y_back(core_rows))
    tb["y2_cat"] = np.concatenate([tb["y2_hi"], tb["y2_lo"]], axis=1)
    y3 = y_lanes(core_rows)
    put("y3", y3)
    tb["y3_dup"] = np.concatenate([tb["y3_hi"], tb["y3_hi"]], axis=0)
    put("x3", x_rows(field_cols))
    put("x4", x_back(own_cols))
    mats = []
    for t in range(2):
        pos, inside = window_rows(True, SLICE, t)
        mats.append(y_back(pos).T * inside[:, None])
    put("yg", np.stack(mats))
    offs = np.arange(KSIZE) - HALO
    kx = np.zeros((2 * XB, 128))
    kx[:, :KSIZE] = x_rows(offs)
    put("kx", kx)
    ky = np.zeros((4, 128, 2 * YB))
    for m in range(4):
        ky[m, 32 * m : 32 * m + KSIZE] = y_lanes(offs)
    put("ky", ky)
    sel = np.zeros((4, EDGE, 128), np.float32)
    for r in range(WIDE):
        sel[0, r, CORE - WIDE + r] = 1
        sel[2, r, r] = 1
    for r in range(HALO):
        sel[1, WIDE + r, CORE - HALO + r] = 1
        sel[3, WIDE + r, r] = 1
    tb["edge_sel"] = sel.astype(ml_dtypes.bfloat16)
    own = np.zeros((ROWS, CORE), np.float32)
    for c in range(CORE):
        own[WIDE - ROW0 + c, c] = 1
    tb["sel_own"] = own.astype(ml_dtypes.bfloat16)
    halo = np.zeros((2, ROWS, EDGE), np.float32)
    for r in range(HALO):
        halo[0, HALO + r - ROW0, WIDE + r] = 1
        halo[1, WIDE + CORE + r - ROW0, WIDE + r] = 1
    tb["sel_halo"] = halo.astype(ml_dtypes.bfloat16)
    tb["flip"] = np.eye(CORE, dtype=np.float32)[::-1].astype(ml_dtypes.bfloat16)
    return tb


def split(x):
    hi = x.astype(bf16)
    return hi, (x - hi.astype(f32)).astype(bf16)


def dot(a, b):
    return lax.dot_general(a, b, (((1,), (0,)), ((), ())), preferred_element_type=f32)


def dot_nt(a, b):
    return lax.dot_general(a, b, (((1,), (1,)), ((), ())), preferred_element_type=f32)


def dot3(a_hi, a_lo, b_hi, b_lo, mul=dot):
    return mul(a_hi, b_hi) + (mul(a_lo, b_hi) + mul(a_hi, b_lo))


def signed(spec):
    cc, cs = spec[:XB, :YB], spec[:XB, YB:]
    sc, ss = spec[XB:, :YB], spec[XB:, YB:]
    return cc - ss, -(cs + sc), cc + ss, sc - cs


def even_odd(pr, pi, mr, mi):
    top = jnp.concatenate([pr + mr, pi + mi], axis=1)
    low = jnp.concatenate([mi - pi, pr - mr], axis=1)
    return jnp.concatenate([top, low], axis=0)


def call(body, names, args, out_shape, scratch=(), smem=(), flops=0, nbytes=0):
    tb = tables()
    consts = [jnp.asarray(tb[n]) for n in names]
    vm = pl.BlockSpec(memory_space=pltpu.VMEM)
    sm = pl.BlockSpec(memory_space=pltpu.SMEM)
    in_specs = [sm if i in smem else vm for i in range(len(args))] + [vm] * len(consts)
    multi = isinstance(out_shape, (list, tuple))

    def wrapped(*refs):
        n_in = len(args)
        ins = refs[:n_in]
        tabs = dict(zip(names, refs[n_in : n_in + len(names)]))
        body(*ins, tabs, *refs[n_in + len(names) :])

    return pl.pallas_call(
        wrapped,
        out_shape=out_shape,
        in_specs=in_specs,
        out_specs=[vm] * len(out_shape) if multi else vm,
        scratch_shapes=list(scratch),
        compiler_params=pltpu.CompilerParams(vmem_limit_bytes=VMEM_LIMIT),
        cost_estimate=pl.CostEstimate(flops=flops, bytes_accessed=nbytes, transcendentals=0),
    )(*args, *consts)


def edges_kernel(mask_ref, target_ref, tb, a_ref, b_ref):
    even = lax.rem(lax.axis_index("tile"), 2) == 0
    m_hi, m_lo = split(mask_ref[...])
    tgt = target_ref[...].astype(f32).astype(bf16)
    sel = tb["edge_sel"]
    right = dot_nt(sel[0], m_hi) + dot_nt(sel[0], m_lo) + dot_nt(sel[1], tgt)
    left = dot_nt(sel[2], m_hi) + dot_nt(sel[2], m_lo) + dot_nt(sel[3], tgt)
    a_ref[...] = jnp.where(even, right, left)
    b_ref[...] = jnp.where(even, left, right)


def spectra_kernel(kern, ker_ref, tb, h_ref, hs_ref):
    hs_ref[...] = jnp.zeros_like(hs_ref)
    for k in range(kern):
        for part in range(2):
            row = 32 * (2 * k + part)
            hs_ref[row : row + KSIZE, :KSIZE] = ker_ref[part, 0, k]
    s_hi, s_lo = split(hs_ref[...])
    z = dot3(tb["kx_hi"][...], tb["kx_lo"][...], s_hi, s_lo, dot_nt)
    z_hi, z_lo = split(z)
    for c in range(2 * kern):
        lanes = slice(128 * (c // 4), 128 * (c // 4) + 128)
        spec = dot3(
            z_hi[:, lanes], z_lo[:, lanes], tb["ky_hi"][c % 4], tb["ky_lo"][c % 4]
        )
        for j, comp in enumerate(signed(spec)):
            h_ref[c, j] = comp


def to_spectrum(v, by_hi, by_lo, f_ref, base):
    v_hi, v_lo = split(v)
    for t in range(2):
        lanes = slice(256 * t, 256 * t + 256)
        spec = dot3(v_hi, v_lo, by_hi[:, lanes], by_lo[:, lanes])
        for j, comp in enumerate(signed(spec)):
            f_ref[t, j] = comp if base is None else base[t, j] - STEP_RATE * comp


def gradient_body(kern, last, f_ref, tgt_ref, h_ref, w_ref, thr_ref, tb, g_ref, fld, inten, tot):
    inten[...] = jnp.zeros_like(inten)

    @pl.loop(0, kern)
    def _(k):
        for t in range(2):
            parts = []
            for part in range(2):
                hpr, hpi, hmr, hmi = (h_ref[2 * k + part, j] for j in range(4))
                fpr, fpi, fmr, fmi = (f_ref[t, j] for j in range(4))
                pr, pi = hpr * fpr - hpi * fpi, hpr * fpi + hpi * fpr
                mr, mi = hmr * fmr - hmi * fmi, hmr * fmi + hmi * fmr
                r_hi, r_lo = split(even_odd(pr, pi, mr, mi))
                parts.append(dot3(tb["x2_hi"][...], tb["x2_lo"][...], r_hi, r_lo))
            g_hi, g_lo = split(jnp.concatenate(parts, axis=0))
            r = dot(g_hi, tb["y2_cat"][...])
            field = r[:, :CORE] + (r[:, CORE:] + dot(g_lo, tb["y2_hi"][...]))
            fld[t, k] = field
            inten[t] += w_ref[0, k] * (field[:ROWS] * field[:ROWS] + field[ROWS:] * field[ROWS:])

    tile = lax.axis_index("tile")
    first = jnp.where(tile == 0, WIDE, HALO) - ROW0
    end = jnp.where(tile == last, WIDE + CORE, WIDE + CORE + HALO) - ROW0
    row = lax.broadcasted_iota(jnp.int32, (ROWS, CORE), 0)
    inside = (row >= first) & (row < end)
    for t in range(2):
        resist = jax.nn.sigmoid(STEEPNESS * (inten[t] - thr_ref[0]))
        target = tgt_ref[:, CORE * t : CORE * t + CORE]
        slope = 2.0 * (resist - target) * STEEPNESS * resist * (1.0 - resist)
        inten[t] = jnp.where(inside, 2.0 * slope, 0.0)
    tot[...] = jnp.zeros_like(tot)

    @pl.loop(0, kern)
    def _(k):
        for t in range(2):
            scaled = w_ref[0, k] * inten[t]
            field = fld[t, k]
            r_hi, r_lo = split(
                jnp.concatenate([scaled * field[:ROWS], scaled * field[ROWS:]], axis=0)
            )
            w = dot(jnp.concatenate([r_hi, r_lo], axis=1), tb["y3_dup"][...])
            w_hi, w_lo = split(w + dot(r_hi, tb["y3_lo"][...]))
            acc = [tot[t, j] for j in range(4)]
            for part in range(2):
                rows = slice(ROWS * part, ROWS * part + ROWS)
                spec = dot3(tb["x3_hi"][...], tb["x3_lo"][...], w_hi[rows], w_lo[rows])
                bpr, bpi, bmr, bmi = signed(spec)
                hpr, hpi, hmr, hmi = (h_ref[2 * k + part, j] for j in range(4))
                acc[0] = acc[0] + (hpr * bpr + hpi * bpi)
                acc[1] = acc[1] + (hpr * bpi - hpi * bpr)
                acc[2] = acc[2] + (hmr * bmr + hmi * bmi)
                acc[3] = acc[3] + (hmr * bmi - hmi * bmr)
            for j in range(4):
                tot[t, j] = acc[j]

    out = None
    for t in range(2):
        r_hi, r_lo = split(even_odd(*(tot[t, j] for j in range(4))))
        u_hi, u_lo = split(dot3(tb["x4_hi"][...], tb["x4_lo"][...], r_hi, r_lo))
        term = dot3(tb["yg_hi"][t], tb["yg_lo"][t], u_hi, u_lo, dot_nt)
        out = term if out is None else out + term
    g_ref[...] = out


def pairs_of(*names):
    return [n + tail for n in names for tail in ("_hi", "_lo")]


GRAD_TABLES = pairs_of("x2", "x3", "x4", "yg") + ["y2_cat", "y2_hi", "y3_dup", "y3_lo"]
FIRST_TABLES = pairs_of("cx_own", "cx_left", "cx_right", "by_nat") + ["sel_own", "sel_halo"]
LATER_TABLES = pairs_of("cx_both", "by_sl")


def first_kernel(
    kern, last, w_ref, thr_ref, mask_ref, target_ref, a_ref, b_ref, h_ref, tb,
    g_ref, f_ref, tgt_ref, fld, inten, tot,
):
    even = lax.rem(lax.axis_index("tile"), 2) == 0
    from_a, from_b = a_ref[...], b_ref[...]
    left = jnp.where(even, from_b, from_a)
    right = jnp.where(even, from_a, from_b)
    m_hi, m_lo = split(mask_ref[...])
    l_hi, l_lo = split(left)
    r_hi, r_lo = split(right)
    v = dot3(tb["cx_own_hi"][...], tb["cx_own_lo"][...], m_hi, m_lo, dot_nt)
    v = v + dot3(tb["cx_left_hi"][...], tb["cx_left_lo"][...], l_hi, l_lo)
    v = v + dot3(tb["cx_right_hi"][...], tb["cx_right_lo"][...], r_hi, r_lo)
    to_spectrum(v, tb["by_nat_hi"], tb["by_nat_lo"], f_ref, None)
    tgt_ref[...] = (
        dot_nt(tb["sel_own"][...], target_ref[...].astype(f32).astype(bf16))
        + dot(tb["sel_halo"][0], l_hi)
        + dot(tb["sel_halo"][1], r_hi)
    )
    gradient_body(kern, last, f_ref, tgt_ref, h_ref, w_ref, thr_ref, tb, g_ref, fld, inten, tot)


def later_kernel(
    kern, last, w_ref, thr_ref, own_ref, f_in_ref, tgt_ref, h_ref, tb,
    g_ref, f_ref, fld, inten, tot,
):
    step = own_ref[...]
    rows = step.shape[0] * 8
    own = step[:, :8].reshape(rows, CORE)
    edge = step[:, 8:].reshape(rows, CORE)
    s_hi, s_lo = split(jnp.concatenate([own, edge], axis=1))
    v = dot3(tb["cx_both_hi"][...], tb["cx_both_lo"][...], s_hi, s_lo, dot_nt)
    to_spectrum(v, tb["by_sl_hi"], tb["by_sl_lo"], f_ref, f_in_ref)
    gradient_body(kern, last, f_ref, tgt_ref, h_ref, w_ref, thr_ref, tb, g_ref, fld, inten, tot)


def match_kernel(n_tile, copies, edges, table_ref, got_ref, tb, out_ref, src_ref):
    total = []
    for d in range(n_tile):
        s = got_ref[d * copies]
        for c in range(1, copies):
            s = s + got_ref[d * copies + c]
        total.append(s)
        src_ref[d] = s
    flat = jnp.concatenate(total, axis=0)
    hi = flat.astype(bf16)
    rest = flat - hi.astype(f32)
    mid = rest.astype(bf16)
    low = (rest - mid.astype(f32)).astype(bf16)
    flip = tb["flip"][...]
    turned = dot(hi, flip) + (dot(mid, flip) + dot(low, flip))
    for d in range(n_tile):
        src_ref[n_tile + d] = turned[8 * d : 8 * d + 8]
    upper = lax.broadcasted_iota(jnp.int32, (8, CORE), 0) < SLICE
    matched = []
    for d in range(n_tile):
        pick = []
        for t in range(2):
            partner = table_ref[d, t]
            value = src_ref[lax.div(partner, 2) + n_tile * table_ref[d, 2 + t]]
            moved = pltpu.roll(value, SLICE, 0)
            pick.append(jnp.where(lax.rem(partner, 2) == t, value, moved))
        matched.append(0.5 * (total[d] + jnp.where(upper, pick[0], pick[1])))
    lane = lax.broadcasted_iota(jnp.int32, (8, CORE), 1)
    zero = jnp.zeros((8, CORE), f32)
    for d in range(n_tile):
        rim = None
        if edges:
            before = matched[d - 1] if d > 0 else zero
            after = matched[d + 1] if d + 1 < n_tile else zero
            rim = jnp.where(lane >= CORE - WIDE, before, jnp.where(lane < WIDE, after, 0.0))
        for c in range(copies):
            out_ref[d * copies + c, :8] = matched[d]
            if edges:
                out_ref[d * copies + c, 8:] = rim


def final_kernel(slices, mask_ref, one_ref, two_ref, tb, mask_out, grad_out):
    for s in range(slices):
        rows = slice(SLICE * s, SLICE * s + SLICE)
        for t in range(2):
            at = slice(SLICE * t, SLICE * t + SLICE)
            two = two_ref[s, at]
            grad_out[t, rows] = two
            stepped = mask_ref[t, rows] - STEP_RATE * one_ref[s, at]
            mask_out[t, rows] = stepped - STEP_RATE * two


def per_device(
    n_tile, n_depth, mask_tiles, target_tiles, kernels, socs_weights, thresholds,
    partner_table, mirror_flags,
):
    tiles_dev, core, _ = mask_tiles.shape
    kern = kernels.shape[2]
    spread = n_tile * n_depth * SLICE == core
    axes = ("tile", "depth") if spread else ("tile",)
    copies = n_depth if spread else 1
    slices = n_tile * copies
    assert slices * SLICE == core and tiles_dev == 2 and core == CORE

    pairs_a = [(i, i ^ 1) for i in range(n_tile)]
    pairs_b = [p for i in range(1, n_tile - 1, 2) for p in ((i, i + 1), (i + 1, i))]

    mask_rows = mask_tiles.reshape(tiles_dev * core, core)
    target_rows = target_tiles.reshape(tiles_dev * core, core)
    edge = jax.ShapeDtypeStruct((EDGE, tiles_dev * core), f32)
    send_a, send_b = call(edges_kernel, ["edge_sel"], [mask_rows, target_rows], [edge, edge])
    from_a = lax.ppermute(send_a, "tile", pairs_a)
    from_b = lax.ppermute(send_b, "tile", pairs_b)
    mine = jnp.concatenate([partner_table, mirror_flags])[None]
    table = lax.all_gather(mine, "tile", axis=0, tiled=True)

    spectra = call(
        functools.partial(spectra_kernel, kern),
        pairs_of("kx", "ky"),
        [kernels],
        jax.ShapeDtypeStruct((2 * kern, 4, XB, YB), f32),
        [pltpu.VMEM((32 * 2 * kern, 128), f32)],
        flops=3 * 10**9,
        nbytes=4 * 10**6,
    )

    scratch = [
        pltpu.VMEM((2, kern, 2 * ROWS, CORE), f32),
        pltpu.VMEM((2, ROWS, CORE), f32),
        pltpu.VMEM((2, 4, XB, YB), f32),
    ]
    strip = jax.ShapeDtypeStruct((tiles_dev * core, core), f32)
    freq = jax.ShapeDtypeStruct((2, 4, XB, YB), f32)
    goal = jax.ShapeDtypeStruct((ROWS, 2 * CORE), f32)

    def exchange(grad, edges):
        grad = grad.reshape(slices, 8, core)
        if not spread:
            grad = lax.psum(grad, "depth")
        got = lax.all_to_all(grad, axes, 0, 0, tiled=True)
        back = call(
            functools.partial(match_kernel, n_tile, copies, edges),
            ["flip"],
            [table, got],
            jax.ShapeDtypeStruct((slices, 16 if edges else 8, core), f32),
            [pltpu.VMEM((2 * n_tile, 8, core), f32)],
            smem=(0,),
        )
        return lax.all_to_all(back, axes, 0, 0, tiled=True)

    grad, freq_now, goals = call(
        functools.partial(first_kernel, kern, n_tile - 1),
        GRAD_TABLES + FIRST_TABLES,
        [socs_weights, thresholds, mask_rows, target_rows, from_a, from_b, spectra],
        [strip, freq, goal],
        scratch,
        smem=(0, 1),
    )
    moves = [exchange(grad, STEPS > 1)]
    for step in range(1, STEPS):
        grad, freq_now = call(
            functools.partial(later_kernel, kern, n_tile - 1),
            GRAD_TABLES + LATER_TABLES,
            [socs_weights, thresholds, moves[-1], freq_now, goals, spectra],
            [strip, freq],
            scratch,
            smem=(0, 1),
        )
        moves.append(exchange(grad, step + 1 < STEPS))
    tiles = jax.ShapeDtypeStruct((tiles_dev, core, core), f32)
    return tuple(
        call(
            functools.partial(final_kernel, slices),
            [],
            [mask_tiles, *moves],
            [tiles, tiles],
        )
    )


def solution(mesh):
    return jax.shard_map(
        functools.partial(per_device, mesh.shape["tile"], mesh.shape["depth"]),
        mesh=mesh,
        in_specs=(
            P("tile", None, None),
            P("tile", None, None),
            P(None, "depth", None, None, None),
            P("depth", None),
            P("depth"),
            P("tile"),
            P("tile"),
        ),
        out_specs=(P("tile", None, None), P("tile", None, None)),
        check_vma=False,
    )
```

profile of v0, /device:TPU:0, one launch (start us, length us, event | category | flops | bytes accessed | tf_op | source)
XLA Modules:
  0.0 112.0 jit_solution(2260689111982803509)
XLA Ops:
  0.6 0.9 copy-done
  1.5 0.9 copy-done.6
  2.4 0.8 copy-done.42
  3.2 0.2 shard_map.374
  3.5 0.5 collective-permute-start
  4.0 0.7 collective-permute-start.1
  4.7 0.9 copy.42.refs_0_
  5.6 0.0 copy-start.45
  5.6 0.9 copy-done.45
  6.5 0.9 copy-done.46
  7.5 0.8 copy-done.47
  8.3 0.8 copy-done.48
  9.1 0.0 copy-start.5
  9.1 0.0 copy-start.10
  9.1 0.0 copy-start.11
  9.2 0.0 copy-start.13
  9.2 0.0 copy-start.15
  9.4 1.4 %shard_map.375.refs_6_.refs_5_ = f32[12,4,96,128]{3,2,1,0:T(8,128)S(1)} custom-call(f32[2,1,6,25,25]{4,3,2,1,0:T(8,128)S(1)} %copy.42.refs_0_, bf16[192,128]{1,0:T(8,128)(2,1)S(1)} %copy-done.48, bf16[192,128]{1,0:T(8,128)(2,1)S(1)} %copy-done.47, bf16[4,128,256]{2,1,0:T(8,128)(2,1)S(1)} %copy-done.46, bf16[4,128,256]{2,1,0:T(8,128)(2,1)S(1)} %copy-done.45), custom_call_target="tpu_custom_call" | custom-call | flops 3000000000 | bytes 4000000 | tf_op jit(solution)/shard_map/pallas_call | solution.py:209
  11.7 13.1 %shard_map.376 = (f32[256,128]{1,0:T(8,128)S(1)}, f32[2,4,96,128]{3,2,1,0:T(8,128)S(1)}, f32[160,256]{1,0:T(8,128)S(1)}) custom-call(f32[1,6]{1,0:T(1,128)S(1)} %copy-done.44, f32[1]{0:T(128)S(6)} %copy.44.refs_1_, f32[256,128]{1,0:T(8,128)S(1)} %bitcast.6, s32[256,128]{1,0:T(8,128)S(1)} %bitcast.8, f32[48,256]{1,0:T(8,128)S(1)} %collective-permute-done.refs_4_, ...), custom_call_target="tpu_custom_call" | custom-call | tf_op jit(solution)/shard_map/pallas_call | solution.py:209
  24.9 0.8 copy-done.8
  25.6 0.7 copy-done.29
  26.3 0.7 copy-done.31
  27.0 8.7 %all-to-all-start = ((f32[32,8,128]{2,1,0:T(8,128)}), f32[32,8,128]{2,1,0:T(8,128)S(1)}, u32[]{:S(2)}, u32[]{:S(2)}) async-start(f32[32,8,128]{2,1,0:T(8,128)} %bitcast.9), calls=%async_computation | async-start | bytes 262144 | tf_op jit(solution)/shard_map/all_to_all | solution.py:467
  35.7 0.6 dynamic-slice
  37.0 0.5 broadcast
  37.5 1.3 %add_dynamic-update-slice_fusion = s32[64]{0:T(128)} fusion(s32[64]{0:T(128)} %broadcast, u32[]{:T(128)} %bitcast, s32[2]{0:T(128)S(1)} %copy-done.49, s32[2]{0:T(128)S(1)} %copy-done.50), kind=kLoop, calls=%fused_computation | loop fusion | flops 4 | bytes 784
  38.8 12.4 %all-reduce = s32[64]{0:T(128)S(1)} all-reduce(s32[64]{0:T(128)} %add_dynamic-update-slice_fusion), channel_id=2, replica_groups=mesh['tile'=16,'depth'=2] {'tile'}, use_global_device_ids=true, to_apply=%add | all-reduce | flops 64 | bytes 512
  51.2 0.1 reshape.20.refs_0_
  51.3 0.9 shard_map.377
  52.2 12.7 %all_to_all.20.refs_2_.refs_1_ = f32[32,16,128]{2,1,0:T(8,128)S(1)} all-to-all(f32[32,16,128]{2,1,0:T(8,128)S(1)} %shard_map.377), channel_id=1, replica_groups=mesh['tile'=16,'depth'=2] {'tile','depth'}, dimensions={0} | all-to-all | bytes 524288 | tf_op jit(solution)/shard_map/all_to_all | solution.py:476
  64.9 1.0 copy-done.9
  65.9 0.9 copy-done.12
  66.8 0.9 copy-done.14
  67.7 0.9 copy-done.16
  68.5 0.8 copy-done.18
  69.4 0.8 copy-done.20
  70.2 0.8 copy-done.22
  71.1 0.8 copy-done.24
  71.9 0.9 copy-done.25
  72.9 0.9 copy-done.26
  73.8 0.9 copy-done.30
  74.7 0.9 copy-done.33
  75.6 0.9 copy-done.34
  76.5 12.7 %shard_map.378 = (f32[256,128]{1,0:T(8,128)S(1)}, f32[2,4,96,128]{3,2,1,0:T(8,128)}) custom-call(f32[1,6]{1,0:T(1,128)S(1)} %copy-done.44, f32[1]{0:T(128)S(6)} %copy.44.refs_1_, f32[32,16,128]{2,1,0:T(8,128)S(1)} %all_to_all.20.refs_2_.refs_1_, f32[2,4,96,128]{3,2,1,0:T(8,128)S(1)} %copy-done.9, f32[160,256]{1,0:T(8,128)S(1)} %copy-done.30, ...), custom_call_target="tpu_custom_call" | custom-call | tf_op jit(solution)/shard_map/pallas_call | solution.py:209
  89.2 10.7 %all_to_all.21.refs_1_ = f32[32,8,128]{2,1,0:T(8,128)S(1)} all-to-all(f32[32,8,128]{2,1,0:T(8,128)S(1)} %bitcast.10), channel_id=1, replica_groups=mesh['tile'=16,'depth'=2] {'tile','depth'}, dimensions={0} | all-to-all | bytes 262144 | tf_op jit(solution)/shard_map/all_to_all | solution.py:467
  100.0 0.9 shard_map.379
  100.9 10.3 %all_to_all.22.refs_2_ = f32[32,8,128]{2,1,0:T(8,128)S(1)} all-to-all(f32[32,8,128]{2,1,0:T(8,128)S(1)} %shard_map.379), channel_id=1, replica_groups=mesh['tile'=16,'depth'=2] {'tile','depth'}, dimensions={0} | all-to-all | bytes 262144 | tf_op jit(solution)/shard_map/all_to_all | solution.py:476
  111.2 0.8 shard_map.380
  (78 shorter events, 0.2 us)
Async XLA Ops:
  0.6 0.9 copy-start
  1.5 0.9 copy-start.6
  3.5 8.0 %collective-permute-start = (f32[48,256]{1,0:T(8,128)S(1)}, f32[48,256]{1,0:T(8,128)S(1)}, u32[]{:S(2)}, u32[]{:S(2)}) collective-permute-start(f32[48,256]{1,0:T(8,128)S(1)} %get-tuple-element.8), channel_id=1, source_target_pairs={{0,2},{2,0},{4,6},{6,4},{8,10},{10,8},{12,14},{14,12},{16,18},{18,... | collective-permute-start | bytes 147464 | tf_op jit(solution)/shard_map/ppermute | solution.py:439
  4.0 7.5 %collective-permute-start.1 = (f32[48,256]{1,0:T(8,128)S(1)}, f32[48,256]{1,0:T(8,128)S(1)}, u32[]{:S(2)}, u32[]{:S(2)}) collective-permute-start(f32[48,256]{1,0:T(8,128)S(1)} %get-tuple-element.9), channel_id=1, source_target_pairs={{2,4},{4,2},{6,8},{8,6},{10,12},{12,10},{14,16},{16,14},{18,20},{2... | collective-permute-start | bytes 147464 | tf_op jit(solution)/shard_map/ppermute | solution.py:440
  5.6 1.0 copy-start.45
  6.5 0.9 copy-start.46
  9.1 2.4 %copy-start.1 = (f32[2,128,128]{2,1,0:T(8,128)S(1)}, f32[2,128,128]{2,1,0:T(8,128)}, u32[]{:S(2)}) copy-start(f32[2,128,128]{2,1,0:T(8,128)} %refs_0_.6) | copy-start | bytes 393220
  9.1 2.4 %copy-start.2 = (bf16[2,256,256]{2,1,0:T(8,128)(2,1)S(1)}, bf16[2,256,256]{2,1,0:T(8,128)(2,1)}, u32[]{:S(2)}) copy-start(bf16[2,256,256]{2,1,0:T(8,128)(2,1)} %constant.76.clone.refs_14_.refs_13_) | copy-start | bytes 786436
  9.1 2.4 %copy-start.3 = (bf16[2,256,256]{2,1,0:T(8,128)(2,1)S(1)}, bf16[2,256,256]{2,1,0:T(8,128)(2,1)}, u32[]{:S(2)}) copy-start(bf16[2,256,256]{2,1,0:T(8,128)(2,1)} %constant.75.clone.refs_13_.refs_12_) | copy-start | bytes 786436
  9.1 2.4 %copy-start.4 = (bf16[256,256]{1,0:T(8,128)(2,1)S(1)}, bf16[256,256]{1,0:T(8,128)(2,1)}, u32[]{:S(2)}) copy-start(bf16[256,256]{1,0:T(8,128)(2,1)} %constant.79.clone.refs_17_.refs_16_) | copy-start | bytes 393220
  9.1 2.4 %copy-start.5 = (bf16[256,256]{1,0:T(8,128)(2,1)S(1)}, bf16[256,256]{1,0:T(8,128)(2,1)}, u32[]{:S(2)}) copy-start(bf16[256,256]{1,0:T(8,128)(2,1)} %constant.77.clone.refs_15_.refs_14_) | copy-start | bytes 393220
  9.1 2.4 %copy-start.7 = (s32[2,128,128]{2,1,0:T(8,128)S(1)}, s32[2,128,128]{2,1,0:T(8,128)}, u32[]{:S(2)}) copy-start(s32[2,128,128]{2,1,0:T(8,128)} %param.40) | copy-start | bytes 393220
  9.1 2.4 %copy-start.10 = (bf16[192,160]{1,0:T(8,128)(2,1)S(1)}, bf16[192,160]{1,0:T(8,128)(2,1)}, u32[]{:S(2)}) copy-start(bf16[192,160]{1,0:T(8,128)(2,1)} %constant.72.clone.refs_10_.refs_9_) | copy-start | bytes 184324
  9.1 2.4 %copy-start.11 = (bf16[192,160]{1,0:T(8,128)(2,1)S(1)}, bf16[192,160]{1,0:T(8,128)(2,1)}, u32[]{:S(2)}) copy-start(bf16[192,160]{1,0:T(8,128)(2,1)} %constant.71.clone.refs_9_.refs_8_) | copy-start | bytes 184324
  9.2 2.4 %copy-start.13 = (bf16[160,192]{1,0:T(8,128)(2,1)S(1)}, bf16[160,192]{1,0:T(8,128)(2,1)}, u32[]{:S(2)}) copy-start(bf16[160,192]{1,0:T(8,128)(2,1)} %constant.70.clone.refs_8_.refs_7_) | copy-start | bytes 184324
  9.2 2.4 %copy-start.15 = (bf16[160,192]{1,0:T(8,128)(2,1)S(1)}, bf16[160,192]{1,0:T(8,128)(2,1)}, u32[]{:S(2)}) copy-start(bf16[160,192]{1,0:T(8,128)(2,1)} %constant.69.clone.refs_7_.refs_6_) | copy-start | bytes 184324
  9.2 2.4 %copy-start.17 = (bf16[128,256]{1,0:T(8,128)(2,1)S(1)}, bf16[128,256]{1,0:T(8,128)(2,1)}, u32[]{:S(2)}) copy-start(bf16[128,256]{1,0:T(8,128)(2,1)} %constant.80.clone.refs_18_.refs_17_) | copy-start | bytes 196612
  9.2 2.4 %copy-start.19 = (bf16[256,128]{1,0:T(8,128)(2,1)S(1)}, bf16[256,128]{1,0:T(8,128)(2,1)}, u32[]{:S(2)}) copy-start(bf16[256,128]{1,0:T(8,128)(2,1)} %constant.78.clone.refs_16_.refs_15_) | copy-start | bytes 196612
  9.2 2.4 %copy-start.21 = (bf16[128,192]{1,0:T(8,128)(2,1)S(1)}, bf16[128,192]{1,0:T(8,128)(2,1)}, u32[]{:S(2)}) copy-start(bf16[128,192]{1,0:T(8,128)(2,1)} %constant.74.clone.refs_12_.refs_11_) | copy-start | bytes 147460
  9.2 2.4 %copy-start.23 = (bf16[128,192]{1,0:T(8,128)(2,1)S(1)}, bf16[128,192]{1,0:T(8,128)(2,1)}, u32[]{:S(2)}) copy-start(bf16[128,192]{1,0:T(8,128)(2,1)} %constant.73.clone.refs_11_.refs_10_) | copy-start | bytes 147460
  9.2 2.4 %copy-start.27 = (bf16[256,512]{1,0:T(8,128)(2,1)S(1)}, bf16[256,512]{1,0:T(8,128)(2,1)}, u32[]{:S(2)}) copy-start(bf16[256,512]{1,0:T(8,128)(2,1)} %constant.88.clone.refs_26_) | copy-start | bytes 786436
  9.2 2.4 %copy-start.28 = (bf16[256,512]{1,0:T(8,128)(2,1)S(1)}, bf16[256,512]{1,0:T(8,128)(2,1)}, u32[]{:S(2)}) copy-start(bf16[256,512]{1,0:T(8,128)(2,1)} %constant.87.clone.refs_25_) | copy-start | bytes 786436
  9.3 2.4 %copy-start.35 = (bf16[2,160,48]{2,1,0:T(8,128)(2,1)S(1)}, bf16[2,160,48]{2,1,0:T(8,128)(2,1)}, u32[]{:S(2)}) copy-start(bf16[2,160,48]{2,1,0:T(8,128)(2,1)} %constant.90.clone.refs_28_) | copy-start | bytes 92164
  9.3 2.4 %copy-start.36 = (bf16[192,48]{1,0:T(8,128)(2,1)S(1)}, bf16[192,48]{1,0:T(8,128)(2,1)}, u32[]{:S(2)}) copy-start(bf16[192,48]{1,0:T(8,128)(2,1)} %constant.86.clone.refs_24_) | copy-start | bytes 55300
  9.3 2.4 %copy-start.37 = (bf16[192,48]{1,0:T(8,128)(2,1)S(1)}, bf16[192,48]{1,0:T(8,128)(2,1)}, u32[]{:S(2)}) copy-start(bf16[192,48]{1,0:T(8,128)(2,1)} %constant.85.clone.refs_23_) | copy-start | bytes 55300
  9.3 2.4 %copy-start.38 = (bf16[192,48]{1,0:T(8,128)(2,1)S(1)}, bf16[192,48]{1,0:T(8,128)(2,1)}, u32[]{:S(2)}) copy-start(bf16[192,48]{1,0:T(8,128)(2,1)} %constant.84.clone.refs_22_) | copy-start | bytes 55300
  9.3 2.4 %copy-start.39 = (bf16[192,48]{1,0:T(8,128)(2,1)S(1)}, bf16[192,48]{1,0:T(8,128)(2,1)}, u32[]{:S(2)}) copy-start(bf16[192,48]{1,0:T(8,128)(2,1)} %constant.83.clone.refs_21_) | copy-start | bytes 55300
  9.3 2.4 %copy-start.40 = (bf16[192,128]{1,0:T(8,128)(2,1)S(1)}, bf16[192,128]{1,0:T(8,128)(2,1)}, u32[]{:S(2)}) copy-start(bf16[192,128]{1,0:T(8,128)(2,1)} %constant.82.clone.refs_20_) | copy-start | bytes 147460
  9.3 2.4 %copy-start.41 = (bf16[192,128]{1,0:T(8,128)(2,1)S(1)}, bf16[192,128]{1,0:T(8,128)(2,1)}, u32[]{:S(2)}) copy-start(bf16[192,128]{1,0:T(8,128)(2,1)} %constant.81.clone.refs_19_) | copy-start | bytes 147460
  9.3 2.4 %copy-start.43 = (bf16[160,128]{1,0:T(8,128)(2,1)S(1)}, bf16[160,128]{1,0:T(8,128)(2,1)}, u32[]{:S(2)}) copy-start(bf16[160,128]{1,0:T(8,128)(2,1)} %constant.89.clone.refs_27_) | copy-start | bytes 122884
  9.4 2.4 %copy-start.44 = (f32[1,6]{1,0:T(1,128)S(1)}, f32[1,6]{1,0:T(1,128)}, u32[]{:S(2)}) copy-start(f32[1,6]{1,0:T(1,128)} %refs_0_.5) | copy-start | bytes 76
  11.4 24.3 %copy-start.51 = (u32[32]{0:T(128)S(1)}, u32[32]{0:T(128)}, u32[]{:S(2)}) copy-start(u32[32]{0:T(128)} %constant.105) | copy-start | bytes 388
  11.4 26.1 %copy-start.49 = (s32[2]{0:T(128)S(1)}, s32[2]{0:T(128)}, u32[]{:S(2)}) copy-start(s32[2]{0:T(128)} %param.45) | copy-start | bytes 28
  11.4 26.1 %copy-start.50 = (s32[2]{0:T(128)S(1)}, s32[2]{0:T(128)}, u32[]{:S(2)}) copy-start(s32[2]{0:T(128)} %param.44) | copy-start | bytes 28
  11.4 39.8 %copy-start.32 = (bf16[128,128]{1,0:T(8,128)(2,1)S(1)}, bf16[128,128]{1,0:T(8,128)(2,1)}, u32[]{:S(2)}) copy-start(bf16[128,128]{1,0:T(8,128)(2,1)} %constant.91.clone.refs_2_) | copy-start | bytes 98308
  27.0 24.3 %all-to-all-start = ((f32[32,8,128]{2,1,0:T(8,128)}), f32[32,8,128]{2,1,0:T(8,128)S(1)}, u32[]{:S(2)}, u32[]{:S(2)}) async-start(f32[32,8,128]{2,1,0:T(8,128)} %bitcast.9), calls=%async_computation | async-start | bytes 262144 | tf_op jit(solution)/shard_map/all_to_all | solution.py:467
  64.9 1.0 copy-start.9
  65.9 0.9 copy-start.12
  66.8 0.9 copy-start.14
  67.7 0.9 copy-start.16
  68.5 0.8 copy-start.18
  69.4 0.8 copy-start.20
  70.2 0.8 copy-start.22
  71.9 0.9 copy-start.25
  72.9 0.9 copy-start.26
  73.8 0.9 copy-start.30
  74.7 0.9 copy-start.33
  75.6 0.9 copy-start.34
  (7 other events, 5.3 us)
where the time goes:
time: 113 us; the launch traced here: 112 us
  blocking collectives  46.1 us (41%)
  Pallas kernels  30.1 us (27%)
  local copies, waits for them, and re-layouts  22.1 us (20%)
  starting transfers between devices  9.91 us (9%)
  between operations  2.51 us (2%)
  other arithmetic  1.31 us (1%)
    pallas_call x7, Pallas kernels, call(): pl.pallas_call(wrapped, out_shape=out_shape, in_specs=in_specs, out_specs...  30.1 us
    all_to_all x2, blocking collectives, exchange(): return lax.all_to_all(back, axes, 0, 0, tiled=True)  23 us
    unnamed x107, local copies, waits for them, and re-layouts  22 us
    unnamed x1, blocking collectives  12.4 us
    all_to_all x1, blocking collectives, exchange(): got = lax.all_to_all(grad, axes, 0, 0, tiled=True)  10.7 us
    all_to_all x1, starting transfers between devices, exchange(): got = lax.all_to_all(grad, axes, 0, 0, tiled=True)  8.74 us
  transfers between devices with their start and end apart: 3, of which 0 were waited for; matrix products, arithmetic and copies ran while one was open for 3% of the time, Pallas kernels for 1%

commit v1 on v0

v1 whole, which is shorter than its diff:
```python
import functools

import jax
import jax.numpy as jnp
import ml_dtypes
import numpy as np
from jax import lax
from jax.experimental import pallas as pl
from jax.experimental.pallas import tpu as pltpu
from jax.sharding import PartitionSpec as P

HALO = 12
KSIZE = 25
STEPS = 2
STEEPNESS = 3.0
STEP_RATE = 0.05

CORE = 128
NY = 152
NX = 176
WIDE = 2 * HALO
XB = 96
YB = 128
NU = NY // 2 + 1
NV = NX // 2 + 1
ROWS = 160
ROW0 = 8
EDGE = 48
WIDE_PAD = 32
VMEM_LIMIT = 24 * 1024 * 1024

f32 = jnp.float32
bf16 = jnp.bfloat16


def np_split(a):
    hi = np.asarray(a, np.float32).astype(ml_dtypes.bfloat16)
    lo = (np.asarray(a, np.float64) - hi.astype(np.float64)).astype(ml_dtypes.bfloat16)
    return hi, lo


def x_rows(cols):
    out = np.zeros((2 * XB, len(cols)))
    ang = 2 * np.pi * np.outer(np.arange(NV), cols) / NX
    out[:NV] = np.cos(ang)
    out[XB : XB + NV] = np.sin(ang)
    out[XB] = 0.0
    out[XB + NV - 1] = 0.0
    return out


def y_lanes(rows):
    out = np.zeros((len(rows), 2 * YB))
    ang = 2 * np.pi * np.outer(rows, np.arange(NU)) / NY
    out[:, :NU] = np.cos(ang)
    out[:, YB : YB + NU] = np.sin(ang)
    out[:, YB] = 0.0
    out[:, YB + NU - 1] = 0.0
    return out


def half_weights(bins):
    weights = np.full(bins, 2.0)
    weights[0] = weights[-1] = 1.0
    return weights


def x_back(cols):
    kappa = np.zeros(2 * XB)
    kappa[:NV] = half_weights(NV) / 2
    kappa[XB : XB + NV] = half_weights(NV) / 2
    return x_rows(cols).T * kappa


def y_back(rows):
    weight = np.zeros(2 * YB)
    weight[:NU] = half_weights(NU)
    weight[YB : YB + NU] = -half_weights(NU)
    return (y_lanes(rows) * weight).T / (NX * NY)


def pack(parts):
    rows, where, at = [], {}, 0
    for name, a in parts:
        height = -(-a.shape[0] // 16) * 16
        block = np.zeros((height, 256), np.float64)
        block[: a.shape[0], : a.shape[1]] = a
        rows.append(block)
        where[name] = (at, a.shape[0], a.shape[1])
        at += height
    return np.concatenate(rows), where


def pack_split(parts):
    both = []
    for name, a in parts:
        hi, lo = np_split(a)
        both += [(name + "_hi", hi.astype(np.float64)), (name + "_lo", lo.astype(np.float64))]
    return both


@functools.lru_cache(None)
def tables():
    core_rows = np.arange(HALO, HALO + CORE)
    field_cols = np.arange(ROW0, ROW0 + ROWS)
    own_cols = np.arange(WIDE, WIDE + CORE)
    sides = np.zeros((2 * XB, 256))
    sides[:, :WIDE] = x_rows(np.arange(WIDE))
    sides[:, CORE : CORE + WIDE] = x_rows(np.arange(WIDE + CORE, NX))
    parts = [("cx_own", x_rows(own_cols)), ("cx_side", sides)]
    for t in range(2):
        pos = np.arange(2 * CORE) - t * CORE + HALO
        inside = (pos >= 0) & (pos < NY)
        parts.append((f"by{t}", y_lanes(pos) * inside[:, None]))
    parts += [("x2", x_back(field_cols)), ("x3", x_rows(field_cols)), ("x4", x_back(own_cols))]
    y2_hi, y2_lo = (a.astype(np.float64) for a in np_split(y_back(core_rows)))
    y3_hi, y3_lo = (a.astype(np.float64) for a in np_split(y_lanes(core_rows)))
    grad = pack_split(parts)
    grad += [("y2", np.concatenate([y2_hi, y2_lo], axis=1))]
    grad += [("y3_dup", np.concatenate([y3_hi, y3_hi])), ("y3_lo", y3_lo)]
    own = np.zeros((ROWS, CORE))
    own[np.arange(CORE) + WIDE - ROW0, np.arange(CORE)] = 1
    halo = np.zeros((ROWS, 256))
    for r in range(HALO):
        halo[HALO + r - ROW0, WIDE + r] = 1
        halo[WIDE + CORE + r - ROW0, CORE + WIDE + r] = 1
    grad += [("sel_own", own), ("sel_halo", halo)]
    offs = np.arange(KSIZE) - HALO
    kx = np.zeros((2 * XB, 128))
    kx[:, :KSIZE] = x_rows(offs)
    spec = [("kx", kx)]
    for m in range(4):
        ky = np.zeros((128, 2 * YB))
        ky[32 * m : 32 * m + KSIZE] = y_lanes(offs)
        spec.append((f"ky{m}", ky))
    sel = np.zeros((4, EDGE, 128))
    for r in range(WIDE):
        sel[0, r, CORE - WIDE + r] = 1
        sel[2, r, r] = 1
    for r in range(HALO):
        sel[1, WIDE + r, CORE - HALO + r] = 1
        sel[3, WIDE + r, r] = 1
    edge = [(f"edge{i}", sel[i]) for i in range(4)]
    edge.append(("flip", np.eye(CORE)[::-1]))
    return {"grad": pack(grad), "spec": pack(pack_split(spec)), "edge": pack(edge)}


def split(x):
    hi = x.astype(bf16)
    return hi, (x - hi.astype(f32)).astype(bf16)


def dot(a, b):
    return lax.dot_general(a, b, (((1,), (0,)), ((), ())), preferred_element_type=f32)


def dot_nt(a, b):
    return lax.dot_general(a, b, (((1,), (1,)), ((), ())), preferred_element_type=f32)


def dot3(a_hi, a_lo, b_hi, b_lo, mul=dot):
    return mul(a_hi, b_hi) + (mul(a_lo, b_hi) + mul(a_hi, b_lo))


def signed(spec):
    cc, cs = spec[:XB, :YB], spec[:XB, YB:]
    sc, ss = spec[XB:, :YB], spec[XB:, YB:]
    return cc - ss, -(cs + sc), cc + ss, sc - cs


def even_odd(pr, pi, mr, mi):
    top = jnp.concatenate([pr + mr, pi + mi], axis=1)
    low = jnp.concatenate([mi - pi, pr - mr], axis=1)
    return jnp.concatenate([top, low], axis=0)


def call(body, group, args, out_shape, scratch=(), smem=(), flops=0, nbytes=0):
    packed, where = tables()[group]
    vm = pl.BlockSpec(memory_space=pltpu.VMEM)
    sm = pl.BlockSpec(memory_space=pltpu.SMEM)
    multi = isinstance(out_shape, (list, tuple))
    n_in = len(args)

    def wrapped(*refs):
        def table(name, half=None):
            at, height, width = where[name]
            lanes = slice(0, width) if half is None else slice(128 * half, 128 * half + 128)
            return refs[n_in][at : at + height, lanes]

        body(*refs[:n_in], table, *refs[n_in + 1 :])

    return pl.pallas_call(
        wrapped,
        out_shape=out_shape,
        in_specs=[sm if i in smem else vm for i in range(n_in)] + [vm],
        out_specs=[vm] * len(out_shape) if multi else vm,
        scratch_shapes=list(scratch),
        compiler_params=pltpu.CompilerParams(vmem_limit_bytes=VMEM_LIMIT),
        cost_estimate=pl.CostEstimate(flops=flops, bytes_accessed=nbytes, transcendentals=0),
    )(*args, jnp.asarray(packed.astype(ml_dtypes.bfloat16)))


def is_even():
    return lax.rem(lax.axis_index("tile"), 2) == 0


def send_edges(right, left, a_ref, b_ref):
    even = is_even()
    a_ref[...] = jnp.where(even, right, left)
    b_ref[...] = jnp.where(even, left, right)


def edges_kernel(mask_ref, target_ref, tb, a_ref, b_ref):
    m_hi, m_lo = split(mask_ref[...])
    tgt = target_ref[...].astype(f32).astype(bf16)
    right = dot_nt(tb("edge0"), m_hi) + dot_nt(tb("edge0"), m_lo) + dot_nt(tb("edge1"), tgt)
    left = dot_nt(tb("edge2"), m_hi) + dot_nt(tb("edge2"), m_lo) + dot_nt(tb("edge3"), tgt)
    send_edges(right, left, a_ref, b_ref)


def spectra_kernel(kern, ker_ref, tb, h_ref, hs_ref):
    hs_ref[...] = jnp.zeros_like(hs_ref)
    for k in range(kern):
        for part in range(2):
            row = 32 * (2 * k + part)
            hs_ref[row : row + KSIZE, :KSIZE] = ker_ref[part, 0, k]
    s_hi, s_lo = split(hs_ref[...])
    z = dot3(tb("kx_hi"), tb("kx_lo"), s_hi, s_lo, dot_nt)
    z_hi, z_lo = split(z)
    for c in range(2 * kern):
        lanes = slice(128 * (c // 4), 128 * (c // 4) + 128)
        spec = dot3(z_hi[:, lanes], z_lo[:, lanes], tb(f"ky{c % 4}_hi"), tb(f"ky{c % 4}_lo"))
        for j, comp in enumerate(signed(spec)):
            h_ref[c, j] = comp


def sides(a_ref, b_ref, tb):
    even = is_even()
    from_a, from_b = a_ref[...], b_ref[...]
    l_hi, l_lo = split(jnp.where(even, from_b, from_a))
    r_hi, r_lo = split(jnp.where(even, from_a, from_b))
    height = l_hi.shape[0]
    v = None
    for half, hi, lo in ((0, l_hi, l_lo), (1, r_hi, r_lo)):
        c_hi, c_lo = tb("cx_side_hi", half), tb("cx_side_lo", half)
        term = dot3(c_hi[:, :height], c_lo[:, :height], hi, lo)
        v = term if v is None else v + term
    return v, l_hi, r_hi


def to_spectrum(v, tb, f_ref, base):
    v_hi, v_lo = split(v)
    for t in range(2):
        spec = dot3(v_hi, v_lo, tb(f"by{t}_hi"), tb(f"by{t}_lo"))
        for j, comp in enumerate(signed(spec)):
            f_ref[t, j] = comp if base is None else base[t, j] - STEP_RATE * comp


def gradient_body(kern, last, f_ref, tgt_ref, h_ref, w_ref, thr_ref, tb, g_ref, fld, inten, tot):
    inten[...] = jnp.zeros_like(inten)

    @pl.loop(0, kern)
    def _(k):
        for t in range(2):
            parts = []
            for part in range(2):
                hpr, hpi, hmr, hmi = (h_ref[2 * k + part, j] for j in range(4))
                fpr, fpi, fmr, fmi = (f_ref[t, j] for j in range(4))
                pr, pi = hpr * fpr - hpi * fpi, hpr * fpi + hpi * fpr
                mr, mi = hmr * fmr - hmi * fmi, hmr * fmi + hmi * fmr
                r_hi, r_lo = split(even_odd(pr, pi, mr, mi))
                parts.append(dot3(tb("x2_hi"), tb("x2_lo"), r_hi, r_lo))
            g_hi, g_lo = split(jnp.concatenate(parts, axis=0))
            r = dot(g_hi, tb("y2"))
            field = r[:, :CORE] + (r[:, CORE:] + dot(g_lo, tb("y2", 0)))
            fld[t, k] = field
            inten[t] += w_ref[0, k] * (field[:ROWS] * field[:ROWS] + field[ROWS:] * field[ROWS:])

    tile = lax.axis_index("tile")
    first = jnp.where(tile == 0, WIDE, HALO) - ROW0
    end = jnp.where(tile == last, WIDE + CORE, WIDE + CORE + HALO) - ROW0
    row = lax.broadcasted_iota(jnp.int32, (ROWS, CORE), 0)
    inside = (row >= first) & (row < end)
    for t in range(2):
        resist = jax.nn.sigmoid(STEEPNESS * (inten[t] - thr_ref[0]))
        target = tgt_ref[:, CORE * t : CORE * t + CORE]
        slope = 2.0 * (resist - target) * STEEPNESS * resist * (1.0 - resist)
        inten[t] = jnp.where(inside, 2.0 * slope, 0.0)
    tot[...] = jnp.zeros_like(tot)

    @pl.loop(0, kern)
    def _(k):
        for t in range(2):
            scaled = w_ref[0, k] * inten[t]
            field = fld[t, k]
            r_hi, r_lo = split(
                jnp.concatenate([scaled * field[:ROWS], scaled * field[ROWS:]], axis=0)
            )
            w = dot(jnp.concatenate([r_hi, r_lo], axis=1), tb("y3_dup"))
            w_hi, w_lo = split(w + dot(r_hi, tb("y3_lo")))
            acc = [tot[t, j] for j in range(4)]
            for part in range(2):
                rows = slice(ROWS * part, ROWS * part + ROWS)
                spec = dot3(tb("x3_hi"), tb("x3_lo"), w_hi[rows], w_lo[rows])
                bpr, bpi, bmr, bmi = signed(spec)
                hpr, hpi, hmr, hmi = (h_ref[2 * k + part, j] for j in range(4))
                acc[0] = acc[0] + (hpr * bpr + hpi * bpi)
                acc[1] = acc[1] + (hpr * bpi - hpi * bpr)
                acc[2] = acc[2] + (hmr * bmr + hmi * bmi)
                acc[3] = acc[3] + (hmr * bmi - hmi * bmr)
            for j in range(4):
                tot[t, j] = acc[j]

    lane = lax.broadcasted_iota(jnp.int32, (1, 2 * YB), 1)
    bin_at = lax.rem(lane, YB)
    weight = jnp.where((bin_at == 0) | (bin_at == NU - 1), 1.0, 2.0) / (NX * NY)
    weight = jnp.where(lane < YB, weight, -weight)
    out = None
    for t in range(2):
        r_hi, r_lo = split(even_odd(*(tot[t, j] for j in range(4))))
        u_hi, u_lo = split(weight * dot3(tb("x4_hi"), tb("x4_lo"), r_hi, r_lo))
        term = dot3(tb(f"by{t}_hi"), tb(f"by{t}_lo"), u_hi, u_lo, dot_nt)
        out = term if out is None else out + term
    g_ref[...] = out


def first_kernel(
    kern, last, w_ref, thr_ref, mask_ref, target_ref, a_ref, b_ref, h_ref, tb,
    g_ref, f_ref, tgt_ref, fld, inten, tot,
):
    m_hi, m_lo = split(mask_ref[...])
    v, left, right = sides(a_ref, b_ref, tb)
    v = v + dot3(tb("cx_own_hi"), tb("cx_own_lo"), m_hi, m_lo, dot_nt)
    to_spectrum(v, tb, f_ref, None)
    tgt_ref[...] = (
        dot_nt(tb("sel_own"), target_ref[...].astype(f32).astype(bf16))
        + dot(tb("sel_halo", 0)[:, :EDGE], left)
        + dot(tb("sel_halo", 1)[:, :EDGE], right)
    )
    gradient_body(kern, last, f_ref, tgt_ref, h_ref, w_ref, thr_ref, tb, g_ref, fld, inten, tot)


def later_kernel(
    kern, last, w_ref, thr_ref, own_ref, a_ref, b_ref, f_in_ref, tgt_ref, h_ref, tb,
    g_ref, f_ref, fld, inten, tot,
):
    s_hi, s_lo = split(own_ref[...])
    v, _, _ = sides(a_ref, b_ref, tb)
    v = v + dot3(tb("cx_own_hi"), tb("cx_own_lo"), s_hi, s_lo, dot_nt)
    to_spectrum(v, tb, f_ref, f_in_ref)
    gradient_body(kern, last, f_ref, tgt_ref, h_ref, w_ref, thr_ref, tb, g_ref, fld, inten, tot)


def match(table_ref, own_ref, got_refs, tb):
    device = lax.axis_index("tile")
    own = own_ref[...]
    flip = tb("flip")
    tiles = []
    for t in range(2):
        rows = slice(CORE * t, CORE * t + CORE)
        mine = own[rows]
        bit = lax.bitwise_xor(table_ref[t], 2 * device + t)
        other = jnp.where(bit == 1, own[CORE * (1 - t) : CORE * (1 - t) + CORE], mine)
        for b, got in enumerate(got_refs):
            other = jnp.where(bit == 2 << b, got[rows], other)
        hi = other.astype(bf16)
        rest = other - hi.astype(f32)
        mid = rest.astype(bf16)
        low = (rest - mid.astype(f32)).astype(bf16)
        turned = dot(hi, flip) + (dot(mid, flip) + dot(low, flip))
        tiles.append(0.5 * (mine + jnp.where(table_ref[2 + t] == 1, turned, other)))
    return tiles


def match_kernel(n_got, table_ref, own_ref, *refs):
    got_refs, (tb, out_ref, a_ref, b_ref) = refs[:n_got], refs[n_got:]
    matched = jnp.concatenate(match(table_ref, own_ref, got_refs, tb), axis=0)
    out_ref[...] = matched
    hi, lo = split(matched)
    right, left = tb("edge0")[:WIDE_PAD], tb("edge2")[:WIDE_PAD]
    send_edges(
        dot_nt(right, hi) + dot_nt(right, lo), dot_nt(left, hi) + dot_nt(left, lo), a_ref, b_ref
    )


def final_kernel(n_got, n_moves, table_ref, own_ref, *refs):
    got_refs, refs = refs[:n_got], refs[n_got:]
    mask_ref, moves, (tb, mask_out, grad_out) = refs[0], refs[1 : 1 + n_moves], refs[1 + n_moves :]
    for t, tile in enumerate(match(table_ref, own_ref, got_refs, tb)):
        grad_out[t] = tile
        now = mask_ref[t]
        for move in moves:
            now = now - STEP_RATE * move[CORE * t : CORE * t + CORE]
        mask_out[t] = now - STEP_RATE * tile


def per_device(
    n_tile, n_depth, mask_tiles, target_tiles, kernels, socs_weights, thresholds,
    partner_table, mirror_flags,
):
    tiles_dev, core, _ = mask_tiles.shape
    kern = kernels.shape[2]
    assert tiles_dev == 2 and core == CORE
    pairs_a = [(i, i ^ 1) for i in range(n_tile)]
    pairs_b = [p for i in range(1, n_tile - 1, 2) for p in ((i, i + 1), (i + 1, i))]

    def swap_edges(send_a, send_b):
        return lax.ppermute(send_b, "tile", pairs_b), lax.ppermute(send_a, "tile", pairs_a)

    def gather_sum(grad):
        bit = 1
        while bit < n_depth:
            pairs = [(i, i ^ bit) for i in range(n_depth)]
            grad = grad + lax.ppermute(grad, "depth", pairs)
            bit *= 2
        bits = [1 << b for b in range(n_tile.bit_length() - 1)]
        got = [
            lax.ppermute(grad, "tile", [(i, i ^ bit) for i in range(n_tile)])
            for bit in reversed(bits)
        ]
        return grad, got[::-1]

    mask_rows = mask_tiles.reshape(tiles_dev * core, core)
    target_rows = target_tiles.reshape(tiles_dev * core, core)
    strip = jax.ShapeDtypeStruct((tiles_dev * core, core), f32)
    edge = jax.ShapeDtypeStruct((EDGE, tiles_dev * core), f32)
    side = jax.ShapeDtypeStruct((WIDE_PAD, tiles_dev * core), f32)
    freq = jax.ShapeDtypeStruct((2, 4, XB, YB), f32)
    goal = jax.ShapeDtypeStruct((ROWS, 2 * CORE), f32)
    tiles = jax.ShapeDtypeStruct((tiles_dev, core, core), f32)
    scratch = [
        pltpu.VMEM((2, kern, 2 * ROWS, CORE), f32),
        pltpu.VMEM((2, ROWS, CORE), f32),
        pltpu.VMEM((2, 4, XB, YB), f32),
    ]

    send_a, send_b = call(edges_kernel, "edge", [mask_rows, target_rows], [edge, edge])
    from_b, from_a = swap_edges(send_a, send_b)
    table = jnp.concatenate([partner_table, mirror_flags])
    spectra = call(
        functools.partial(spectra_kernel, kern),
        "spec",
        [kernels],
        jax.ShapeDtypeStruct((2 * kern, 4, XB, YB), f32),
        [pltpu.VMEM((32 * 2 * kern, 128), f32)],
        flops=3 * 10**9,
        nbytes=4 * 10**6,
    )
    grad, freq_now, goals = call(
        functools.partial(first_kernel, kern, n_tile - 1),
        "grad",
        [socs_weights, thresholds, mask_rows, target_rows, from_a, from_b, spectra],
        [strip, freq, goal],
        scratch,
        smem=(0, 1),
    )
    moves = []
    for step in range(1, STEPS):
        total, got = gather_sum(grad)
        move, send_a, send_b = call(
            functools.partial(match_kernel, len(got)),
            "edge",
            [table, total, *got],
            [strip, side, side],
            smem=(0,),
        )
        from_b, from_a = swap_edges(send_a, send_b)
        moves.append(move)
        grad, freq_now = call(
            functools.partial(later_kernel, kern, n_tile - 1),
            "grad",
            [socs_weights, thresholds, move, from_a, from_b, freq_now, goals, spectra],
            [strip, freq],
            scratch,
            smem=(0, 1),
        )
    total, got = gather_sum(grad)
    return tuple(
        call(
            functools.partial(final_kernel, len(got), len(moves)),
            "edge",
            [table, total, *got, mask_tiles, *moves],
            [tiles, tiles],
            smem=(0,),
        )
    )


def solution(mesh):
    return jax.shard_map(
        functools.partial(per_device, mesh.shape["tile"], mesh.shape["depth"]),
        mesh=mesh,
        in_specs=(
            P("tile", None, None),
            P("tile", None, None),
            P(None, "depth", None, None, None),
            P("depth", None),
            P("depth"),
            P("tile"),
            P("tile"),
        ),
        out_specs=(P("tile", None, None), P("tile", None, None)),
        check_vma=False,
    )
```

time: 113 us -> 76.8 us (0.68)
  blocking collectives: 46.1 us -> 0 us
  local copies, waits for them, and re-layouts: 22.1 us -> 4.79 us
  waiting for transfers between devices: 0.01 us -> 16.7 us
  starting transfers between devices: 9.91 us -> 23 us
  other arithmetic: 1.31 us -> 0.11 us
    all_to_all x3 -> x0, blocking collectives: 33.7 us -> none  [the longest x2 23 us: exchange(): return lax.all_to_all(back, axes, 0, 0, tiled=True)]
    ppermute x2 -> x14, starting transfers between devices: 1.17 us -> 23 us  [the longest x8 17 us: gather_sum(): lax.ppermute(grad, 'tile', [(i, i ^ bit) for i in range(n_tile)])]
    unnamed x107 -> x23, local copies, waits for them, and re-layouts: 22 us -> 4.79 us
    ppermute x2 -> x14, waiting for transfers between devices: 0.01 us -> 16.7 us  [the longest x8 9.77 us: gather_sum(): lax.ppermute(grad, 'tile', [(i, i ^ bit) for i in range(n_tile)])]
    unnamed x1 -> x0, blocking collectives: 12.4 us -> none
    all_to_all x1 -> x0, starting transfers between devices: 8.74 us -> none  [exchange(): got = lax.all_to_all(grad, axes, 0, 0, tiled=True)]
    unnamed x1 -> x0, other arithmetic: 1.31 us -> none
    pallas_call x7 -> x6, Pallas kernels: 30.1 us -> 30.4 us  [call(): pl.pallas_call(wrapped, out_shape=out_shape, in_specs=[sm if i in smem el...]
  transfers between devices with their start and end apart: 3 -> 14, of which waited for: 0 -> 9; matrix products, arithmetic and copies ran while one was open for 3% -> 1% of each run, Pallas kernels for 1% -> 2%
where the time goes in v1:
time: 76.8 us; the launch traced here: 76.5 us
  Pallas kernels  30.4 us (40%)
  starting transfers between devices  23 us (30%)
  waiting for transfers between devices  16.7 us (22%)
  local copies, waits for them, and re-layouts  4.79 us (6%)
  between operations  1.47 us (2%)
    pallas_call x6, Pallas kernels, call(): pl.pallas_call(wrapped, out_shape=out_shape, in_specs=[sm if i in smem el...  30.4 us
    ppermute x8, starting transfers between devices, gather_sum(): lax.ppermute(grad, 'tile', [(i, i ^ bit) for i in range(n_tile)])  17 us
    ppermute x8, waiting for transfers between devices, gather_sum(): lax.ppermute(grad, 'tile', [(i, i ^ bit) for i in range(n_tile)])  9.77 us
    ppermute x2, waiting for transfers between devices, gather_sum(): grad = grad + lax.ppermute(grad, 'depth', pairs)  6.4 us
    unnamed x23, local copies, waits for them, and re-layouts  4.79 us
    ppermute x2, starting transfers between devices, gather_sum(): grad = grad + lax.ppermute(grad, 'depth', pairs)  4.19 us
  transfers between devices with their start and end apart: 14, of which 9 were waited for; matrix products, arithmetic and copies ran while one was open for 1% of the time, Pallas kernels for 2%

profile of v1, /device:TPU:0, one launch (start us, length us, event | category | flops | bytes accessed | tf_op | source)
XLA Modules:
  0.0 76.5 jit_solution(505701610943492617)
XLA Ops:
  0.6 0.0 copy-start.1
  0.6 0.9 %copy-done.1 = bf16[320,256]{1,0:T(8,128)(2,1)S(1)} copy-done((bf16[320,256]{1,0:T(8,128)(2,1)S(1)}, bf16[320,256]{1,0:T(8,128)(2,1)}, u32[]{:S(2)}) %copy-start.1) | copy-done | bytes 163864
  1.6 0.9 %copy-done.3 = f32[2,128,128]{2,1,0:T(8,128)S(1)} copy-done((f32[2,128,128]{2,1,0:T(8,128)S(1)}, f32[2,128,128]{2,1,0:T(8,128)}, u32[]{:S(2)}) %copy-start.3) | copy-done | bytes 131096
  2.5 0.9 %copy-done.5 = s32[2,128,128]{2,1,0:T(8,128)S(1)} copy-done((s32[2,128,128]{2,1,0:T(8,128)S(1)}, s32[2,128,128]{2,1,0:T(8,128)}, u32[]{:S(2)}) %copy-start.5) | copy-done | bytes 131096
  3.4 0.2 shard_map.140
  3.6 0.5 collective-permute-start
  4.1 0.7 collective-permute-start.1
  4.8 0.9 %copy.15.refs_0_ = f32[2,1,6,25,25]{4,3,2,1,0:T(8,128)S(1)} copy(f32[2,1,6,25,25]{4,1,3,2,0:T(1,128)} %param.15) | data formatting | bytes 60000 | tf_op args[2]
  5.7 0.0 copy-start.8
  5.7 1.1 %copy-done.8 = bf16[1408,256]{1,0:T(8,128)(2,1)S(1)} copy-done((bf16[1408,256]{1,0:T(8,128)(2,1)S(1)}, bf16[1408,256]{1,0:T(8,128)(2,1)}, u32[]{:S(2)}) %copy-start.8) | copy-done | bytes 720920
  6.8 1.4 %shard_map.141.refs_6_.refs_7_ = f32[12,4,96,128]{3,2,1,0:T(8,128)S(1)} custom-call(f32[2,1,6,25,25]{4,3,2,1,0:T(8,128)S(1)} %copy.15.refs_0_, bf16[1408,256]{1,0:T(8,128)(2,1)S(1)} %copy-done.8), custom_call_target="tpu_custom_call" | custom-call | flops 3000000000 | bytes 4000000 | tf_op jit(solution)/shard_map/pallas_call | solution.py:192
  8.9 0.0 copy-start.9
  8.9 0.0 copy-start.10
  8.9 0.0 copy-start.2
  8.9 0.0 collective-permute-done.refs_4_
  8.9 0.0 collective-permute-done.1.refs_5_
  8.9 0.0 copy-done
  8.9 0.0 copy-done.4
  8.9 0.0 copy-done.6
  9.0 13.3 %shard_map.142 = (f32[256,128]{1,0:T(8,128)S(1)}, f32[2,4,96,128]{3,2,1,0:T(8,128)S(1)}, f32[160,256]{1,0:T(8,128)S(1)}) custom-call(f32[1,6]{1,0:T(1,128)S(1)} %copy-done.7, f32[1]{0:T(128)S(6)} %copy.16.refs_1_, f32[256,128]{1,0:T(8,128)S(1)} %bitcast.3, s32[256,128]{1,0:T(8,128)S(1)} %bitcast.5, f32[48,256]{1,0:T(8,128)S(1)} %collective-permute-done.refs_4_, ...), custom_call_target="tpu_custom_call" | custom-call | tf_op jit(solution)/shard_map/pallas_call | solution.py:192
  22.3 2.6 %collective-permute-start.2 = (f32[256,128]{1,0:T(8,128)S(1)}, f32[256,128]{1,0:T(8,128)S(1)}, u32[]{:S(2)}, u32[]{:S(2)}) collective-permute-start(f32[256,128]{1,0:T(8,128)S(1)} %get-tuple-element.13), channel_id=1, source_target_pairs={{0,1},{1,0},{2,3},{3,2},{4,5},{5,4},{6,7},{7,6},{8,9},{9,8},{10,11... | collective-permute-start | bytes 393224 | tf_op jit(solution)/shard_map/ppermute | solution.py:414
  24.9 2.9 %collective-permute-done.2 = f32[256,128]{1,0:T(8,128)S(1)} collective-permute-done((f32[256,128]{1,0:T(8,128)S(1)}, f32[256,128]{1,0:T(8,128)S(1)}, u32[]{:S(2)}, u32[]{:S(2)}) %collective-permute-start.2) | collective-permute-done | bytes 131104 | tf_op jit(solution)/shard_map/ppermute | solution.py:414
  27.8 6.4 %collective-permute-start.6 = (f32[256,128]{1,0:T(8,128)S(1)}, f32[256,128]{1,0:T(8,128)S(1)}, u32[]{:S(2)}, u32[]{:S(2)}) collective-permute-start(f32[256,128]{1,0:T(8,128)S(1)} %add.6.refs_1_), channel_id=1, source_target_pairs={{0,16},{2,18},{4,20},{6,22},{8,24},{10,26},{12,28},{14,30},{16,0},... | collective-permute-start | bytes 393224 | tf_op jit(solution)/shard_map/ppermute | solution.py:418
  34.3 1.6 %collective-permute-start.5 = (f32[256,128]{1,0:T(8,128)S(1)}, f32[256,128]{1,0:T(8,128)S(1)}, u32[]{:S(2)}, u32[]{:S(2)}) collective-permute-start(f32[256,128]{1,0:T(8,128)S(1)} %add.6.refs_1_), channel_id=1, source_target_pairs={{0,8},{2,10},{4,12},{6,14},{8,0},{10,2},{12,4},{14,6},{16,24},{18,... | collective-permute-start | bytes 393224 | tf_op jit(solution)/shard_map/ppermute | solution.py:418
  35.9 0.1 collective-permute-start.4
  35.9 0.0 collective-permute-start.3
  36.0 0.1 pad_add_fusion.refs_0_
  36.0 4.1 %collective-permute-done.6.refs_5_ = f32[256,128]{1,0:T(8,128)S(1)} collective-permute-done((f32[256,128]{1,0:T(8,128)S(1)}, f32[256,128]{1,0:T(8,128)S(1)}, u32[]{:S(2)}, u32[]{:S(2)}) %collective-permute-start.6) | collective-permute-done | bytes 131104 | tf_op jit(solution)/shard_map/ppermute | solution.py:418
  40.1 0.3 collective-permute-done.5.refs_4_
  40.4 0.5 collective-permute-done.4.refs_3_
  40.8 0.0 collective-permute-done.3.refs_2_
  40.8 0.9 %shard_map.143 = (f32[256,128]{1,0:T(8,128)S(1)}, f32[32,256]{1,0:T(8,128)S(1)}, f32[32,256]{1,0:T(8,128)S(1)}) custom-call(s32[4]{0:T(128)S(1)} %pad_add_fusion.refs_0_, f32[256,128]{1,0:T(8,128)S(1)} %add.6.refs_1_, f32[256,128]{1,0:T(8,128)S(1)} %collective-permute-done.3.refs_2_, f32[256,128]{1,0:T(8,128)S(1)} %collective-permute-done.4.refs_3_, ...), custom_call_target="tpu_custom_call" | custom-call | tf_op jit(solution)/shard_map/pallas_call | solution.py:192
  41.8 0.0 collective-permute-start.7
  41.8 0.7 collective-permute-start.8
  42.5 0.5 collective-permute-done.7.refs_3_
  43.0 0.0 collective-permute-done.8.refs_4_
  43.0 13.1 %shard_map.144 = (f32[256,128]{1,0:T(8,128)S(1)}, f32[2,4,96,128]{3,2,1,0:T(8,128)}) custom-call(f32[1,6]{1,0:T(1,128)S(1)} %copy-done.7, f32[1]{0:T(128)S(6)} %copy.16.refs_1_, f32[256,128]{1,0:T(8,128)S(1)} %get-tuple-element.14.refs_2_.refs_7_, f32[32,256]{1,0:T(8,128)S(1)} %collective-permute-done.7.refs_3_, ...), custom_call_target="tpu_custom_call" | custom-call | tf_op jit(solution)/shard_map/pallas_call | solution.py:192
  56.1 1.6 %collective-permute-start.9 = (f32[256,128]{1,0:T(8,128)S(1)}, f32[256,128]{1,0:T(8,128)S(1)}, u32[]{:S(2)}, u32[]{:S(2)}) collective-permute-start(f32[256,128]{1,0:T(8,128)S(1)} %get-tuple-element.19), channel_id=1, source_target_pairs={{0,1},{1,0},{2,3},{3,2},{4,5},{5,4},{6,7},{7,6},{8,9},{9,8},{10,11... | collective-permute-start | bytes 393224 | tf_op jit(solution)/shard_map/ppermute | solution.py:414
  57.7 3.5 %collective-permute-done.9 = f32[256,128]{1,0:T(8,128)S(1)} collective-permute-done((f32[256,128]{1,0:T(8,128)S(1)}, f32[256,128]{1,0:T(8,128)S(1)}, u32[]{:S(2)}, u32[]{:S(2)}) %collective-permute-start.9) | collective-permute-done | bytes 131104 | tf_op jit(solution)/shard_map/ppermute | solution.py:414
  61.2 6.6 %collective-permute-start.13 = (f32[256,128]{1,0:T(8,128)S(1)}, f32[256,128]{1,0:T(8,128)S(1)}, u32[]{:S(2)}, u32[]{:S(2)}) collective-permute-start(f32[256,128]{1,0:T(8,128)S(1)} %add.7.refs_1_), channel_id=1, source_target_pairs={{0,16},{2,18},{4,20},{6,22},{8,24},{10,26},{12,28},{14,30},{16,0},... | collective-permute-start | bytes 393224 | tf_op jit(solution)/shard_map/ppermute | solution.py:418
  67.8 2.3 %collective-permute-start.12 = (f32[256,128]{1,0:T(8,128)S(1)}, f32[256,128]{1,0:T(8,128)S(1)}, u32[]{:S(2)}, u32[]{:S(2)}) collective-permute-start(f32[256,128]{1,0:T(8,128)S(1)} %add.7.refs_1_), channel_id=1, source_target_pairs={{0,8},{2,10},{4,12},{6,14},{8,0},{10,2},{12,4},{14,6},{16,24},{18,... | collective-permute-start | bytes 393224 | tf_op jit(solution)/shard_map/ppermute | solution.py:418
  70.1 0.0 collective-permute-start.11
  70.1 0.0 collective-permute-start.10
  70.1 2.9 %collective-permute-done.13.refs_5_ = f32[256,128]{1,0:T(8,128)S(1)} collective-permute-done((f32[256,128]{1,0:T(8,128)S(1)}, f32[256,128]{1,0:T(8,128)S(1)}, u32[]{:S(2)}, u32[]{:S(2)}) %collective-permute-start.13) | collective-permute-done | bytes 131104 | tf_op jit(solution)/shard_map/ppermute | solution.py:418
  73.0 0.8 collective-permute-done.12.refs_4_
  73.7 1.3 %collective-permute-done.11.refs_3_ = f32[256,128]{1,0:T(8,128)S(1)} collective-permute-done((f32[256,128]{1,0:T(8,128)S(1)}, f32[256,128]{1,0:T(8,128)S(1)}, u32[]{:S(2)}, u32[]{:S(2)}) %collective-permute-start.11) | collective-permute-done | bytes 131104 | tf_op jit(solution)/shard_map/ppermute | solution.py:418
  75.0 0.0 collective-permute-done.10.refs_2_
  75.0 1.5 %shard_map.145 = (f32[2,128,128]{2,1,0:T(8,128)}, f32[2,128,128]{2,1,0:T(8,128)}) custom-call(s32[4]{0:T(128)S(1)} %pad_add_fusion.refs_0_, f32[256,128]{1,0:T(8,128)S(1)} %add.7.refs_1_, f32[256,128]{1,0:T(8,128)S(1)} %collective-permute-done.10.refs_2_, f32[256,128]{1,0:T(8,128)S(1)} %collective-permute-done.11.refs_3_, ...), custom_call_target="tpu_custom_call" | custom-call | tf_op jit(solution)/shard_map/pallas_call | solution.py:192
  (12 shorter events, 0.0 us)
Async XLA Ops:
  0.6 0.9 %copy-start.1 = (bf16[320,256]{1,0:T(8,128)(2,1)S(1)}, bf16[320,256]{1,0:T(8,128)(2,1)}, u32[]{:S(2)}) copy-start(bf16[320,256]{1,0:T(8,128)(2,1)} %constant.6.clone.refs_2_.refs_6_.refs_8_) | copy-start | bytes 491524
  1.5 0.9 %copy-start.3 = (f32[2,128,128]{2,1,0:T(8,128)S(1)}, f32[2,128,128]{2,1,0:T(8,128)}, u32[]{:S(2)}) copy-start(f32[2,128,128]{2,1,0:T(8,128)} %refs_6_.2) | copy-start | bytes 393220
  2.5 0.9 %copy-start.5 = (s32[2,128,128]{2,1,0:T(8,128)S(1)}, s32[2,128,128]{2,1,0:T(8,128)}, u32[]{:S(2)}) copy-start(s32[2,128,128]{2,1,0:T(8,128)} %param.14) | copy-start | bytes 393220
  3.6 5.3 %collective-permute-start = (f32[48,256]{1,0:T(8,128)S(1)}, f32[48,256]{1,0:T(8,128)S(1)}, u32[]{:S(2)}, u32[]{:S(2)}) collective-permute-start(f32[48,256]{1,0:T(8,128)S(1)} %get-tuple-element.11), channel_id=1, source_target_pairs={{0,2},{2,0},{4,6},{6,4},{8,10},{10,8},{12,14},{14,12},{16,18},{18,... | collective-permute-start | bytes 147464 | tf_op jit(solution)/shard_map/ppermute | solution.py:408
  4.1 4.8 %collective-permute-start.1 = (f32[48,256]{1,0:T(8,128)S(1)}, f32[48,256]{1,0:T(8,128)S(1)}, u32[]{:S(2)}, u32[]{:S(2)}) collective-permute-start(f32[48,256]{1,0:T(8,128)S(1)} %get-tuple-element.12), channel_id=1, source_target_pairs={{2,4},{4,2},{6,8},{8,6},{10,12},{12,10},{14,16},{16,14},{18,20},{2... | collective-permute-start | bytes 147464 | tf_op jit(solution)/shard_map/ppermute | solution.py:408
  5.7 1.1 %copy-start.8 = (bf16[1408,256]{1,0:T(8,128)(2,1)S(1)}, bf16[1408,256]{1,0:T(8,128)(2,1)}, u32[]{:S(2)}) copy-start(bf16[1408,256]{1,0:T(8,128)(2,1)} %constant.7.clone.refs_1_) | copy-start | bytes 2162692
  6.8 2.1 %copy-start = (bf16[3712,256]{1,0:T(8,128)(2,1)S(1)}, bf16[3712,256]{1,0:T(8,128)(2,1)}, u32[]{:S(2)}) copy-start(bf16[3712,256]{1,0:T(8,128)(2,1)} %constant.8.clone.refs_7_.refs_8_) | copy-start | bytes 5701636
  6.8 2.1 %copy-start.4 = (f32[2,128,128]{2,1,0:T(8,128)S(1)}, f32[2,128,128]{2,1,0:T(8,128)}, u32[]{:S(2)}) copy-start(f32[2,128,128]{2,1,0:T(8,128)} %refs_6_.2) | copy-start | bytes 393220
  6.8 2.1 %copy-start.6 = (s32[2,128,128]{2,1,0:T(8,128)S(1)}, s32[2,128,128]{2,1,0:T(8,128)}, u32[]{:S(2)}) copy-start(s32[2,128,128]{2,1,0:T(8,128)} %param.14) | copy-start | bytes 393220
  6.8 2.1 %copy-start.7 = (f32[1,6]{1,0:T(1,128)S(1)}, f32[1,6]{1,0:T(1,128)}, u32[]{:S(2)}) copy-start(f32[1,6]{1,0:T(1,128)} %refs_0_.4) | copy-start | bytes 76
  8.9 27.1 %copy-start.9 = (s32[2]{0:T(128)S(1)}, s32[2]{0:T(128)}, u32[]{:S(2)}) copy-start(s32[2]{0:T(128)} %param.19) | copy-start | bytes 28
  8.9 27.1 %copy-start.10 = (s32[2]{0:T(128)S(1)}, s32[2]{0:T(128)}, u32[]{:S(2)}) copy-start(s32[2]{0:T(128)} %param.18) | copy-start | bytes 28
  8.9 32.0 %copy-start.2 = (bf16[320,256]{1,0:T(8,128)(2,1)S(1)}, bf16[320,256]{1,0:T(8,128)(2,1)}, u32[]{:S(2)}) copy-start(bf16[320,256]{1,0:T(8,128)(2,1)} %constant.6.clone.refs_2_.refs_6_.refs_8_) | copy-start | bytes 491524
  22.3 5.6 %collective-permute-start.2 = (f32[256,128]{1,0:T(8,128)S(1)}, f32[256,128]{1,0:T(8,128)S(1)}, u32[]{:S(2)}, u32[]{:S(2)}) collective-permute-start(f32[256,128]{1,0:T(8,128)S(1)} %get-tuple-element.13), channel_id=1, source_target_pairs={{0,1},{1,0},{2,3},{3,2},{4,5},{5,4},{6,7},{7,6},{8,9},{9,8},{10,11... | collective-permute-start | bytes 393224 | tf_op jit(solution)/shard_map/ppermute | solution.py:414
  27.8 12.2 %collective-permute-start.6 = (f32[256,128]{1,0:T(8,128)S(1)}, f32[256,128]{1,0:T(8,128)S(1)}, u32[]{:S(2)}, u32[]{:S(2)}) collective-permute-start(f32[256,128]{1,0:T(8,128)S(1)} %add.6.refs_1_), channel_id=1, source_target_pairs={{0,16},{2,18},{4,20},{6,22},{8,24},{10,26},{12,28},{14,30},{16,0},... | collective-permute-start | bytes 393224 | tf_op jit(solution)/shard_map/ppermute | solution.py:418
  34.3 6.1 %collective-permute-start.5 = (f32[256,128]{1,0:T(8,128)S(1)}, f32[256,128]{1,0:T(8,128)S(1)}, u32[]{:S(2)}, u32[]{:S(2)}) collective-permute-start(f32[256,128]{1,0:T(8,128)S(1)} %add.6.refs_1_), channel_id=1, source_target_pairs={{0,8},{2,10},{4,12},{6,14},{8,0},{10,2},{12,4},{14,6},{16,24},{18,... | collective-permute-start | bytes 393224 | tf_op jit(solution)/shard_map/ppermute | solution.py:418
  35.9 5.0 %collective-permute-start.4 = (f32[256,128]{1,0:T(8,128)S(1)}, f32[256,128]{1,0:T(8,128)S(1)}, u32[]{:S(2)}, u32[]{:S(2)}) collective-permute-start(f32[256,128]{1,0:T(8,128)S(1)} %add.6.refs_1_), channel_id=1, source_target_pairs={{0,4},{2,6},{4,0},{6,2},{8,12},{10,14},{12,8},{14,10},{16,20},{18,... | collective-permute-start | bytes 393224 | tf_op jit(solution)/shard_map/ppermute | solution.py:418
  35.9 4.9 %collective-permute-start.3 = (f32[256,128]{1,0:T(8,128)S(1)}, f32[256,128]{1,0:T(8,128)S(1)}, u32[]{:S(2)}, u32[]{:S(2)}) collective-permute-start(f32[256,128]{1,0:T(8,128)S(1)} %add.6.refs_1_), channel_id=1, source_target_pairs={{0,2},{2,0},{4,6},{6,4},{8,10},{10,8},{12,14},{14,12},{16,18},{18,... | collective-permute-start | bytes 393224 | tf_op jit(solution)/shard_map/ppermute | solution.py:418
  41.8 1.2 %collective-permute-start.7 = (f32[32,256]{1,0:T(8,128)S(1)}, f32[32,256]{1,0:T(8,128)S(1)}, u32[]{:S(2)}, u32[]{:S(2)}) collective-permute-start(f32[32,256]{1,0:T(8,128)S(1)} %get-tuple-element.15), channel_id=1, source_target_pairs={{0,2},{2,0},{4,6},{6,4},{8,10},{10,8},{12,14},{14,12},{16,18},{18,... | collective-permute-start | bytes 98312 | tf_op jit(solution)/shard_map/ppermute | solution.py:408
  41.8 1.2 %collective-permute-start.8 = (f32[32,256]{1,0:T(8,128)S(1)}, f32[32,256]{1,0:T(8,128)S(1)}, u32[]{:S(2)}, u32[]{:S(2)}) collective-permute-start(f32[32,256]{1,0:T(8,128)S(1)} %get-tuple-element.16), channel_id=1, source_target_pairs={{2,4},{4,2},{6,8},{8,6},{10,12},{12,10},{14,16},{16,14},{18,20},{2... | collective-permute-start | bytes 98312 | tf_op jit(solution)/shard_map/ppermute | solution.py:408
  56.1 5.0 %collective-permute-start.9 = (f32[256,128]{1,0:T(8,128)S(1)}, f32[256,128]{1,0:T(8,128)S(1)}, u32[]{:S(2)}, u32[]{:S(2)}) collective-permute-start(f32[256,128]{1,0:T(8,128)S(1)} %get-tuple-element.19), channel_id=1, source_target_pairs={{0,1},{1,0},{2,3},{3,2},{4,5},{5,4},{6,7},{7,6},{8,9},{9,8},{10,11... | collective-permute-start | bytes 393224 | tf_op jit(solution)/shard_map/ppermute | solution.py:414
  61.2 11.8 %collective-permute-start.13 = (f32[256,128]{1,0:T(8,128)S(1)}, f32[256,128]{1,0:T(8,128)S(1)}, u32[]{:S(2)}, u32[]{:S(2)}) collective-permute-start(f32[256,128]{1,0:T(8,128)S(1)} %add.7.refs_1_), channel_id=1, source_target_pairs={{0,16},{2,18},{4,20},{6,22},{8,24},{10,26},{12,28},{14,30},{16,0},... | collective-permute-start | bytes 393224 | tf_op jit(solution)/shard_map/ppermute | solution.py:418
  67.8 6.0 %collective-permute-start.12 = (f32[256,128]{1,0:T(8,128)S(1)}, f32[256,128]{1,0:T(8,128)S(1)}, u32[]{:S(2)}, u32[]{:S(2)}) collective-permute-start(f32[256,128]{1,0:T(8,128)S(1)} %add.7.refs_1_), channel_id=1, source_target_pairs={{0,8},{2,10},{4,12},{6,14},{8,0},{10,2},{12,4},{14,6},{16,24},{18,... | collective-permute-start | bytes 393224 | tf_op jit(solution)/shard_map/ppermute | solution.py:418
  70.1 5.0 %collective-permute-start.11 = (f32[256,128]{1,0:T(8,128)S(1)}, f32[256,128]{1,0:T(8,128)S(1)}, u32[]{:S(2)}, u32[]{:S(2)}) collective-permute-start(f32[256,128]{1,0:T(8,128)S(1)} %add.7.refs_1_), channel_id=1, source_target_pairs={{0,4},{2,6},{4,0},{6,2},{8,12},{10,14},{12,8},{14,10},{16,20},{18,... | collective-permute-start | bytes 393224 | tf_op jit(solution)/shard_map/ppermute | solution.py:418
  70.1 5.0 %collective-permute-start.10 = (f32[256,128]{1,0:T(8,128)S(1)}, f32[256,128]{1,0:T(8,128)S(1)}, u32[]{:S(2)}, u32[]{:S(2)}) collective-permute-start(f32[256,128]{1,0:T(8,128)S(1)} %add.7.refs_1_), channel_id=1, source_target_pairs={{0,2},{2,0},{4,6},{6,4},{8,10},{10,8},{12,14},{14,12},{16,18},{18,... | collective-permute-start | bytes 393224 | tf_op jit(solution)/shard_map/ppermute | solution.py:418

commit v2 on v1

--- a/solution.py
+++ b/solution.py
@@ -95,6 +95,9 @@
     both = []
     for name, a in parts:
         hi, lo = np_split(a)
+        if name in ("x2", "x3", "x4"):
+            both.append((name, np.concatenate([hi.astype(np.float64), lo.astype(np.float64)])))
+            continue
         both += [(name + "_hi", hi.astype(np.float64)), (name + "_lo", lo.astype(np.float64))]
     return both
 
@@ -162,6 +165,12 @@
     return mul(a_hi, b_hi) + (mul(a_lo, b_hi) + mul(a_hi, b_lo))
 
 
+def dot_stacked(table, b_hi, b_lo):
+    rows = table.shape[0] // 2
+    both = dot(table, b_hi)
+    return both[:rows] + (both[rows:] + dot(table[:rows], b_lo))
+
+
 def signed(spec):
     cc, cs = spec[:XB, :YB], spec[:XB, YB:]
     sc, ss = spec[XB:, :YB], spec[XB:, YB:]
@@ -174,20 +183,29 @@
     return jnp.concatenate([top, low], axis=0)
 
 
-def call(body, group, args, out_shape, scratch=(), smem=(), flops=0, nbytes=0):
-    packed, where = tables()[group]
+def table_array(group):
+    return jnp.asarray(tables()[group][0].astype(ml_dtypes.bfloat16))
+
+
+def table_reader(group, ref):
+    where = tables()[group][1]
+
+    def table(name, half=None):
+        at, height, width = where[name]
+        lanes = slice(0, width) if half is None else slice(128 * half, 128 * half + 128)
+        return ref[at : at + height, lanes]
+
+    return table
+
+
+def call(body, group, args, out_shape, scratch=(), smem=(), flops=0, nbytes=0, given=None):
     vm = pl.BlockSpec(memory_space=pltpu.VMEM)
     sm = pl.BlockSpec(memory_space=pltpu.SMEM)
     multi = isinstance(out_shape, (list, tuple))
     n_in = len(args)
 
     def wrapped(*refs):
-        def table(name, half=None):
-            at, height, width = where[name]
-            lanes = slice(0, width) if half is None else slice(128 * half, 128 * half + 128)
-            return refs[n_in][at : at + height, lanes]
-
-        body(*refs[:n_in], table, *refs[n_in + 1 :])
+        body(*refs[:n_in], table_reader(group, refs[n_in]), *refs[n_in + 1 :])
 
     return pl.pallas_call(
         wrapped,
@@ -197,7 +215,7 @@
         scratch_shapes=list(scratch),
         compiler_params=pltpu.CompilerParams(vmem_limit_bytes=VMEM_LIMIT),
         cost_estimate=pl.CostEstimate(flops=flops, bytes_accessed=nbytes, transcendentals=0),
-    )(*args, jnp.asarray(packed.astype(ml_dtypes.bfloat16)))
+    )(*args, table_array(group) if given is None else given)
 
 
 def is_even():
@@ -210,12 +228,55 @@
     b_ref[...] = jnp.where(even, left, right)
 
 
-def edges_kernel(mask_ref, target_ref, tb, a_ref, b_ref):
+def edges_kernel(
+    mask_hbm, target_hbm, table_hbm, ker_hbm, spec_hbm,
+    a_ref, b_ref, ker_ref, spec_ref, mask_ref, target_ref, table_ref, sems,
+):
+    moves = [
+        pltpu.make_async_copy(src, dst, sems.at[i])
+        for i, (src, dst) in enumerate(
+            (
+                (mask_hbm, mask_ref),
+                (target_hbm, target_ref),
+                (table_hbm, table_ref),
+                (ker_hbm, ker_ref),
+                (spec_hbm, spec_ref),
+            )
+        )
+    ]
+    for move in moves:
+        move.start()
+    for move in moves[:3]:
+        move.wait()
+    tb = table_reader("edge", table_ref)
     m_hi, m_lo = split(mask_ref[...])
     tgt = target_ref[...].astype(f32).astype(bf16)
     right = dot_nt(tb("edge0"), m_hi) + dot_nt(tb("edge0"), m_lo) + dot_nt(tb("edge1"), tgt)
     left = dot_nt(tb("edge2"), m_hi) + dot_nt(tb("edge2"), m_lo) + dot_nt(tb("edge3"), tgt)
     send_edges(right, left, a_ref, b_ref)
+    for move in moves[3:]:
+        move.wait()
+
+
+def send_first_edges(mask_rows, target_rows, kernels):
+    height = mask_rows.shape[0]
+    args = [mask_rows, target_rows, table_array("edge"), kernels, table_array("spec")]
+    edge = jax.ShapeDtypeStruct((EDGE, height), f32)
+    like = lambda x: jax.ShapeDtypeStruct(x.shape, x.dtype)
+    vm = pl.BlockSpec(memory_space=pltpu.VMEM)
+    return pl.pallas_call(
+        edges_kernel,
+        out_shape=[edge, edge, like(kernels), like(args[4])],
+        in_specs=[pl.BlockSpec(memory_space=pl.ANY)] * 5,
+        out_specs=[vm] * 4,
+        scratch_shapes=[
+            pltpu.VMEM(mask_rows.shape, f32),
+            pltpu.VMEM(target_rows.shape, jnp.int32),
+            pltpu.VMEM(args[2].shape, bf16),
+            pltpu.SemaphoreType.DMA((5,)),
+        ],
+        compiler_params=pltpu.CompilerParams(vmem_limit_bytes=VMEM_LIMIT),
+    )(*args)
 
 
 def spectra_kernel(kern, ker_ref, tb, h_ref, hs_ref):
@@ -259,18 +320,18 @@
 def gradient_body(kern, last, f_ref, tgt_ref, h_ref, w_ref, thr_ref, tb, g_ref, fld, inten, tot):
     inten[...] = jnp.zeros_like(inten)
 
-    @pl.loop(0, kern)
+    @pl.loop(0, kern, unroll=True)
     def _(k):
-        for t in range(2):
-            parts = []
-            for part in range(2):
-                hpr, hpi, hmr, hmi = (h_ref[2 * k + part, j] for j in range(4))
+        parts = [[], []]
+        for part in range(2):
+            hpr, hpi, hmr, hmi = (h_ref[2 * k + part, j] for j in range(4))
+            for t in range(2):
                 fpr, fpi, fmr, fmi = (f_ref[t, j] for j in range(4))
                 pr, pi = hpr * fpr - hpi * fpi, hpr * fpi + hpi * fpr
                 mr, mi = hmr * fmr - hmi * fmi, hmr * fmi + hmi * fmr
-                r_hi, r_lo = split(even_odd(pr, pi, mr, mi))
-                parts.append(dot3(tb("x2_hi"), tb("x2_lo"), r_hi, r_lo))
-            g_hi, g_lo = split(jnp.concatenate(parts, axis=0))
+                parts[t].append(dot_stacked(tb("x2"), *split(even_odd(pr, pi, mr, mi))))
+        for t in range(2):
+            g_hi, g_lo = split(jnp.concatenate(parts[t], axis=0))
             r = dot(g_hi, tb("y2"))
             field = r[:, :CORE] + (r[:, CORE:] + dot(g_lo, tb("y2", 0)))
             fld[t, k] = field
@@ -288,8 +349,10 @@
         inten[t] = jnp.where(inside, 2.0 * slope, 0.0)
     tot[...] = jnp.zeros_like(tot)
 
-    @pl.loop(0, kern)
+    @pl.loop(0, kern, unroll=True)
     def _(k):
+        acc = [[tot[t, j] for j in range(4)] for t in range(2)]
+        back = []
         for t in range(2):
             scaled = w_ref[0, k] * inten[t]
             field = fld[t, k]
@@ -297,19 +360,21 @@
                 jnp.concatenate([scaled * field[:ROWS], scaled * field[ROWS:]], axis=0)
             )
             w = dot(jnp.concatenate([r_hi, r_lo], axis=1), tb("y3_dup"))
-            w_hi, w_lo = split(w + dot(r_hi, tb("y3_lo")))
-            acc = [tot[t, j] for j in range(4)]
-            for part in range(2):
-                rows = slice(ROWS * part, ROWS * part + ROWS)
-                spec = dot3(tb("x3_hi"), tb("x3_lo"), w_hi[rows], w_lo[rows])
+            back.append(split(w + dot(r_hi, tb("y3_lo"))))
+        for part in range(2):
+            rows = slice(ROWS * part, ROWS * part + ROWS)
+            hpr, hpi, hmr, hmi = (h_ref[2 * k + part, j] for j in range(4))
+            for t in range(2):
+                w_hi, w_lo = back[t]
+                spec = dot_stacked(tb("x3"), w_hi[rows], w_lo[rows])
                 bpr, bpi, bmr, bmi = signed(spec)
-                hpr, hpi, hmr, hmi = (h_ref[2 * k + part, j] for j in range(4))
-                acc[0] = acc[0] + (hpr * bpr + hpi * bpi)
-                acc[1] = acc[1] + (hpr * bpi - hpi * bpr)
-                acc[2] = acc[2] + (hmr * bmr + hmi * bmi)
-                acc[3] = acc[3] + (hmr * bmi - hmi * bmr)
+                acc[t][0] = acc[t][0] + (hpr * bpr + hpi * bpi)
+                acc[t][1] = acc[t][1] + (hpr * bpi - hpi * bpr)
+                acc[t][2] = acc[t][2] + (hmr * bmr + hmi * bmi)
+                acc[t][3] = acc[t][3] + (hmr * bmi - hmi * bmr)
+        for t in range(2):
             for j in range(4):
-                tot[t, j] = acc[j]
+                tot[t, j] = acc[t][j]
 
     lane = lax.broadcasted_iota(jnp.int32, (1, 2 * YB), 1)
     bin_at = lax.rem(lane, YB)
@@ -318,7 +383,7 @@
     out = None
     for t in range(2):
         r_hi, r_lo = split(even_odd(*(tot[t, j] for j in range(4))))
-        u_hi, u_lo = split(weight * dot3(tb("x4_hi"), tb("x4_lo"), r_hi, r_lo))
+        u_hi, u_lo = split(weight * dot_stacked(tb("x4"), r_hi, r_lo))
         term = dot3(tb(f"by{t}_hi"), tb(f"by{t}_lo"), u_hi, u_lo, dot_nt)
         out = term if out is None else out + term
     g_ref[...] = out
@@ -423,7 +488,6 @@
     mask_rows = mask_tiles.reshape(tiles_dev * core, core)
     target_rows = target_tiles.reshape(tiles_dev * core, core)
     strip = jax.ShapeDtypeStruct((tiles_dev * core, core), f32)
-    edge = jax.ShapeDtypeStruct((EDGE, tiles_dev * core), f32)
     side = jax.ShapeDtypeStruct((WIDE_PAD, tiles_dev * core), f32)
     freq = jax.ShapeDtypeStruct((2, 4, XB, YB), f32)
     goal = jax.ShapeDtypeStruct((ROWS, 2 * CORE), f32)
@@ -434,7 +498,7 @@
         pltpu.VMEM((2, 4, XB, YB), f32),
     ]
 
-    send_a, send_b = call(edges_kernel, "edge", [mask_rows, target_rows], [edge, edge])
+    send_a, send_b, kernels, spec_table = send_first_edges(mask_rows, target_rows, kernels)
     from_b, from_a = swap_edges(send_a, send_b)
     table = jnp.concatenate([partner_table, mirror_flags])
     spectra = call(
@@ -445,6 +509,7 @@
         [pltpu.VMEM((32 * 2 * kern, 128), f32)],
         flops=3 * 10**9,
         nbytes=4 * 10**6,
+        given=spec_table,
     )
     grad, freq_now, goals = call(
         functools.partial(first_kernel, kern, n_tile - 1),

time: 76.8 us -> 71.3 us (0.928)
  Pallas kernels: 30.4 us -> 24.4 us
    pallas_call x6 -> x5, Pallas kernels: 30.4 us -> 23.2 us  [call(): pl.pallas_call(wrapped, out_shape=out_shape, in_specs=[sm if i in smem el...]
    pallas_call x0 -> x1, Pallas kernels: none -> 1.12 us  [send_first_edges(): pl.pallas_call(edges_kernel, out_shape=[edge, edge, like(kernels), like(a...]
  transfers between devices with their start and end apart: 14 -> 14, of which waited for: 9 -> 9; matrix products, arithmetic and copies ran while one was open for 1% -> 0% of each run, Pallas kernels for 2% -> 2%
where the time goes in v2:
time: 71.3 us; the launch traced here: 71 us
  Pallas kernels  24.4 us (34%)
  starting transfers between devices  23.7 us (33%)
  waiting for transfers between devices  16.6 us (23%)
  local copies, waits for them, and re-layouts  4.8 us (7%)
  between operations  1.47 us (2%)
    pallas_call x5, Pallas kernels, call(): pl.pallas_call(wrapped, out_shape=out_shape, in_specs=[sm if i in smem el...  23.2 us
    ppermute x8, starting transfers between devices, gather_sum(): lax.ppermute(grad, 'tile', [(i, i ^ bit) for i in range(n_tile)])  17.6 us
    ppermute x8, waiting for transfers between devices, gather_sum(): lax.ppermute(grad, 'tile', [(i, i ^ bit) for i in range(n_tile)])  9.81 us
    ppermute x2, waiting for transfers between devices, gather_sum(): grad = grad + lax.ppermute(grad, 'depth', pairs)  6.4 us
    unnamed x23, local copies, waits for them, and re-layouts  4.8 us
    ppermute x2, starting transfers between devices, gather_sum(): grad = grad + lax.ppermute(grad, 'depth', pairs)  4.12 us
    ppermute x2, starting transfers between devices, swap_edges(): lax.ppermute(send_b, 'tile', pairs_b)  1.5 us
  transfers between devices with their start and end apart: 14, of which 9 were waited for; matrix products, arithmetic and copies ran while one was open for 0% of the time, Pallas kernels for 2%

profile of v2, /device:TPU:0, one launch (start us, length us, event | category | flops | bytes accessed | tf_op | source)
XLA Modules:
  0.0 71.0 jit_solution(9697894114450318464)
XLA Ops:
  0.6 0.9 %copy.15.ker_hbm = f32[2,1,6,25,25]{4,3,2,1,0:T(8,128)S(1)} copy(f32[2,1,6,25,25]{4,1,3,2,0:T(1,128)} %param.15) | data formatting | bytes 60000 | tf_op args[2]
  1.6 0.0 copy-start.1
  1.6 0.9 %copy-done.1 = bf16[320,256]{1,0:T(8,128)(2,1)S(1)} copy-done((bf16[320,256]{1,0:T(8,128)(2,1)S(1)}, bf16[320,256]{1,0:T(8,128)(2,1)}, u32[]{:S(2)}) %copy-start.1) | copy-done | bytes 163864
  2.5 0.9 %copy-done.3 = f32[2,128,128]{2,1,0:T(8,128)S(1)} copy-done((f32[2,128,128]{2,1,0:T(8,128)S(1)}, f32[2,128,128]{2,1,0:T(8,128)}, u32[]{:S(2)}) %copy-start.3) | copy-done | bytes 131096
  3.4 1.1 %copy-done.5 = bf16[1408,256]{1,0:T(8,128)(2,1)S(1)} copy-done((bf16[1408,256]{1,0:T(8,128)(2,1)S(1)}, bf16[1408,256]{1,0:T(8,128)(2,1)}, u32[]{:S(2)}) %copy-start.5) | copy-done | bytes 720920
  4.5 0.9 %copy-done.6 = s32[2,128,128]{2,1,0:T(8,128)S(1)} copy-done((s32[2,128,128]{2,1,0:T(8,128)S(1)}, s32[2,128,128]{2,1,0:T(8,128)}, u32[]{:S(2)}) %copy-start.6) | copy-done | bytes 131096
  5.4 1.1 %shard_map.140 = (f32[48,256]{1,0:T(8,128)S(1)}, f32[48,256]{1,0:T(8,128)S(1)}, f32[2,1,6,25,25]{4,3,2,1,0:T(8,128)S(1)}, bf16[1408,256]{1,0:T(8,128)(2,1)S(1)}) custom-call(f32[256,128]{1,0:T(8,128)S(1)} %bitcast.2, s32[256,128]{1,0:T(8,128)S(1)} %bitcast.4, bf16[320,256]{1,0:T(8,128)(2,1)S(1)} %copy-done.1, f32[2,1,6,25,25]{4,3,2,1,0:T(8,128)S(1)} %copy.15.ker_hbm, ...), custom_call_target="tpu_custom_call" | custom-call | tf_op jit(solution)/shard_map/pallas_call | solution.py:267
  6.5 0.5 collective-permute-start
  7.1 0.7 collective-permute-start.1
  7.7 0.0 copy-start
  7.7 0.0 copy-start.4
  7.7 0.0 copy-start.7
  7.7 0.0 copy-start.8
  7.8 1.4 %shard_map.141.refs_6_.refs_7_ = f32[12,4,96,128]{3,2,1,0:T(8,128)S(1)} custom-call(f32[2,1,6,25,25]{4,3,2,1,0:T(8,128)S(1)} %get-tuple-element.15.refs_0_, bf16[1408,256]{1,0:T(8,128)(2,1)S(1)} %get-tuple-element.16.refs_1_), custom_call_target="tpu_custom_call" | custom-call | flops 3000000000 | bytes 4000000 | tf_op jit(solution)/shard_map/pallas_call | solution.py:210
  9.8 0.0 copy-start.9
  9.8 0.0 copy-start.10
  9.8 0.0 copy-start.2
  9.8 0.0 collective-permute-done.refs_4_
  9.8 0.0 collective-permute-done.1.refs_5_
  9.9 9.4 %shard_map.142 = (f32[256,128]{1,0:T(8,128)S(1)}, f32[2,4,96,128]{3,2,1,0:T(8,128)S(1)}, f32[160,256]{1,0:T(8,128)S(1)}) custom-call(f32[1,6]{1,0:T(1,128)S(1)} %copy-done.8, f32[1]{0:T(128)S(6)} %copy.16.refs_1_, f32[256,128]{1,0:T(8,128)S(1)} %bitcast.3, s32[256,128]{1,0:T(8,128)S(1)} %bitcast.5, f32[48,256]{1,0:T(8,128)S(1)} %collective-permute-done.refs_4_, ...), custom_call_target="tpu_custom_call" | custom-call | tf_op jit(solution)/shard_map/pallas_call | solution.py:210
  19.3 2.6 %collective-permute-start.2 = (f32[256,128]{1,0:T(8,128)S(1)}, f32[256,128]{1,0:T(8,128)S(1)}, u32[]{:S(2)}, u32[]{:S(2)}) collective-permute-start(f32[256,128]{1,0:T(8,128)S(1)} %get-tuple-element.17), channel_id=1, source_target_pairs={{0,1},{1,0},{2,3},{3,2},{4,5},{5,4},{6,7},{7,6},{8,9},{9,8},{10,11... | collective-permute-start | bytes 393224 | tf_op jit(solution)/shard_map/ppermute | solution.py:479
  21.9 2.9 %collective-permute-done.2 = f32[256,128]{1,0:T(8,128)S(1)} collective-permute-done((f32[256,128]{1,0:T(8,128)S(1)}, f32[256,128]{1,0:T(8,128)S(1)}, u32[]{:S(2)}, u32[]{:S(2)}) %collective-permute-start.2) | collective-permute-done | bytes 131104 | tf_op jit(solution)/shard_map/ppermute | solution.py:479
  24.9 7.2 %collective-permute-start.6 = (f32[256,128]{1,0:T(8,128)S(1)}, f32[256,128]{1,0:T(8,128)S(1)}, u32[]{:S(2)}, u32[]{:S(2)}) collective-permute-start(f32[256,128]{1,0:T(8,128)S(1)} %add.6.refs_1_), channel_id=1, source_target_pairs={{0,16},{2,18},{4,20},{6,22},{8,24},{10,26},{12,28},{14,30},{16,0},... | collective-permute-start | bytes 393224 | tf_op jit(solution)/shard_map/ppermute | solution.py:483
  32.1 1.6 %collective-permute-start.5 = (f32[256,128]{1,0:T(8,128)S(1)}, f32[256,128]{1,0:T(8,128)S(1)}, u32[]{:S(2)}, u32[]{:S(2)}) collective-permute-start(f32[256,128]{1,0:T(8,128)S(1)} %add.6.refs_1_), channel_id=1, source_target_pairs={{0,8},{2,10},{4,12},{6,14},{8,0},{10,2},{12,4},{14,6},{16,24},{18,... | collective-permute-start | bytes 393224 | tf_op jit(solution)/shard_map/ppermute | solution.py:483
  33.7 0.0 collective-permute-start.4
  33.7 0.0 collective-permute-start.3
  33.7 0.1 pad_add_fusion.refs_0_
  33.8 4.0 %collective-permute-done.6.refs_5_ = f32[256,128]{1,0:T(8,128)S(1)} collective-permute-done((f32[256,128]{1,0:T(8,128)S(1)}, f32[256,128]{1,0:T(8,128)S(1)}, u32[]{:S(2)}, u32[]{:S(2)}) %collective-permute-start.6) | collective-permute-done | bytes 131104 | tf_op jit(solution)/shard_map/ppermute | solution.py:483
  37.7 0.3 collective-permute-done.5.refs_4_
  38.0 0.6 collective-permute-done.4.refs_3_
  38.6 0.0 collective-permute-done.3.refs_2_
  38.6 0.9 %shard_map.143 = (f32[256,128]{1,0:T(8,128)S(1)}, f32[32,256]{1,0:T(8,128)S(1)}, f32[32,256]{1,0:T(8,128)S(1)}) custom-call(s32[4]{0:T(128)S(1)} %pad_add_fusion.refs_0_, f32[256,128]{1,0:T(8,128)S(1)} %add.6.refs_1_, f32[256,128]{1,0:T(8,128)S(1)} %collective-permute-done.3.refs_2_, f32[256,128]{1,0:T(8,128)S(1)} %collective-permute-done.4.refs_3_, ...), custom_call_target="tpu_custom_call" | custom-call | tf_op jit(solution)/shard_map/pallas_call | solution.py:210
  39.6 0.0 collective-permute-start.7
  39.6 0.8 %collective-permute-start.8 = (f32[32,256]{1,0:T(8,128)S(1)}, f32[32,256]{1,0:T(8,128)S(1)}, u32[]{:S(2)}, u32[]{:S(2)}) collective-permute-start(f32[32,256]{1,0:T(8,128)S(1)} %get-tuple-element.20), channel_id=1, source_target_pairs={{2,4},{4,2},{6,8},{8,6},{10,12},{12,10},{14,16},{16,14},{18,20},{2... | collective-permute-start | bytes 98312 | tf_op jit(solution)/shard_map/ppermute | solution.py:473
  40.4 0.4 collective-permute-done.7.refs_3_
  40.8 0.0 collective-permute-done.8.refs_4_
  40.8 10.0 %shard_map.144 = (f32[256,128]{1,0:T(8,128)S(1)}, f32[2,4,96,128]{3,2,1,0:T(8,128)}) custom-call(f32[1,6]{1,0:T(1,128)S(1)} %copy-done.8, f32[1]{0:T(128)S(6)} %copy.16.refs_1_, f32[256,128]{1,0:T(8,128)S(1)} %get-tuple-element.18.refs_2_.refs_7_, f32[32,256]{1,0:T(8,128)S(1)} %collective-permute-done.7.refs_3_, ...), custom_call_target="tpu_custom_call" | custom-call | tf_op jit(solution)/shard_map/pallas_call | solution.py:210
  50.8 1.5 %collective-permute-start.9 = (f32[256,128]{1,0:T(8,128)S(1)}, f32[256,128]{1,0:T(8,128)S(1)}, u32[]{:S(2)}, u32[]{:S(2)}) collective-permute-start(f32[256,128]{1,0:T(8,128)S(1)} %get-tuple-element.23), channel_id=1, source_target_pairs={{0,1},{1,0},{2,3},{3,2},{4,5},{5,4},{6,7},{7,6},{8,9},{9,8},{10,11... | collective-permute-start | bytes 393224 | tf_op jit(solution)/shard_map/ppermute | solution.py:479
  52.3 3.4 %collective-permute-done.9 = f32[256,128]{1,0:T(8,128)S(1)} collective-permute-done((f32[256,128]{1,0:T(8,128)S(1)}, f32[256,128]{1,0:T(8,128)S(1)}, u32[]{:S(2)}, u32[]{:S(2)}) %collective-permute-start.9) | collective-permute-done | bytes 131104 | tf_op jit(solution)/shard_map/ppermute | solution.py:479
  55.8 6.3 %collective-permute-start.13 = (f32[256,128]{1,0:T(8,128)S(1)}, f32[256,128]{1,0:T(8,128)S(1)}, u32[]{:S(2)}, u32[]{:S(2)}) collective-permute-start(f32[256,128]{1,0:T(8,128)S(1)} %add.7.refs_1_), channel_id=1, source_target_pairs={{0,16},{2,18},{4,20},{6,22},{8,24},{10,26},{12,28},{14,30},{16,0},... | collective-permute-start | bytes 393224 | tf_op jit(solution)/shard_map/ppermute | solution.py:483
  62.2 2.4 %collective-permute-start.12 = (f32[256,128]{1,0:T(8,128)S(1)}, f32[256,128]{1,0:T(8,128)S(1)}, u32[]{:S(2)}, u32[]{:S(2)}) collective-permute-start(f32[256,128]{1,0:T(8,128)S(1)} %add.7.refs_1_), channel_id=1, source_target_pairs={{0,8},{2,10},{4,12},{6,14},{8,0},{10,2},{12,4},{14,6},{16,24},{18,... | collective-permute-start | bytes 393224 | tf_op jit(solution)/shard_map/ppermute | solution.py:483
  64.6 0.0 collective-permute-start.11
  64.6 0.0 collective-permute-start.10
  64.6 3.2 %collective-permute-done.13.refs_5_ = f32[256,128]{1,0:T(8,128)S(1)} collective-permute-done((f32[256,128]{1,0:T(8,128)S(1)}, f32[256,128]{1,0:T(8,128)S(1)}, u32[]{:S(2)}, u32[]{:S(2)}) %collective-permute-start.13) | collective-permute-done | bytes 131104 | tf_op jit(solution)/shard_map/ppermute | solution.py:483
  67.7 0.6 collective-permute-done.12.refs_4_
  68.4 1.2 %collective-permute-done.11.refs_3_ = f32[256,128]{1,0:T(8,128)S(1)} collective-permute-done((f32[256,128]{1,0:T(8,128)S(1)}, f32[256,128]{1,0:T(8,128)S(1)}, u32[]{:S(2)}, u32[]{:S(2)}) %collective-permute-start.11) | collective-permute-done | bytes 131104 | tf_op jit(solution)/shard_map/ppermute | solution.py:483
  69.5 0.0 collective-permute-done.10.refs_2_
  69.5 1.5 %shard_map.145 = (f32[2,128,128]{2,1,0:T(8,128)}, f32[2,128,128]{2,1,0:T(8,128)}) custom-call(s32[4]{0:T(128)S(1)} %pad_add_fusion.refs_0_, f32[256,128]{1,0:T(8,128)S(1)} %add.7.refs_1_, f32[256,128]{1,0:T(8,128)S(1)} %collective-permute-done.10.refs_2_, f32[256,128]{1,0:T(8,128)S(1)} %collective-permute-done.11.refs_3_, ...), custom_call_target="tpu_custom_call" | custom-call | tf_op jit(solution)/shard_map/pallas_call | solution.py:210
  (12 shorter events, 0.1 us)
Async XLA Ops:
  1.6 0.9 %copy-start.1 = (bf16[320,256]{1,0:T(8,128)(2,1)S(1)}, bf16[320,256]{1,0:T(8,128)(2,1)}, u32[]{:S(2)}) copy-start(bf16[320,256]{1,0:T(8,128)(2,1)} %constant.6.clone.table_hbm.refs_6_.refs_8_) | copy-start | bytes 491524
  2.5 0.9 %copy-start.3 = (f32[2,128,128]{2,1,0:T(8,128)S(1)}, f32[2,128,128]{2,1,0:T(8,128)}, u32[]{:S(2)}) copy-start(f32[2,128,128]{2,1,0:T(8,128)} %refs_6_.2) | copy-start | bytes 393220
  3.4 1.1 %copy-start.5 = (bf16[1408,256]{1,0:T(8,128)(2,1)S(1)}, bf16[1408,256]{1,0:T(8,128)(2,1)}, u32[]{:S(2)}) copy-start(bf16[1408,256]{1,0:T(8,128)(2,1)} %constant.7.clone.spec_hbm) | copy-start | bytes 2162692
  4.5 0.9 %copy-start.6 = (s32[2,128,128]{2,1,0:T(8,128)S(1)}, s32[2,128,128]{2,1,0:T(8,128)}, u32[]{:S(2)}) copy-start(s32[2,128,128]{2,1,0:T(8,128)} %param.14) | copy-start | bytes 393220
  6.5 3.3 %collective-permute-start = (f32[48,256]{1,0:T(8,128)S(1)}, f32[48,256]{1,0:T(8,128)S(1)}, u32[]{:S(2)}, u32[]{:S(2)}) collective-permute-start(f32[48,256]{1,0:T(8,128)S(1)} %get-tuple-element.13), channel_id=1, source_target_pairs={{0,2},{2,0},{4,6},{6,4},{8,10},{10,8},{12,14},{14,12},{16,18},{18,... | collective-permute-start | bytes 147464 | tf_op jit(solution)/shard_map/ppermute | solution.py:473
  7.1 2.8 %collective-permute-start.1 = (f32[48,256]{1,0:T(8,128)S(1)}, f32[48,256]{1,0:T(8,128)S(1)}, u32[]{:S(2)}, u32[]{:S(2)}) collective-permute-start(f32[48,256]{1,0:T(8,128)S(1)} %get-tuple-element.14), channel_id=1, source_target_pairs={{2,4},{4,2},{6,8},{8,6},{10,12},{12,10},{14,16},{16,14},{18,20},{2... | collective-permute-start | bytes 147464 | tf_op jit(solution)/shard_map/ppermute | solution.py:473
  7.7 2.1 %copy-start = (bf16[3712,256]{1,0:T(8,128)(2,1)S(1)}, bf16[3712,256]{1,0:T(8,128)(2,1)}, u32[]{:S(2)}) copy-start(bf16[3712,256]{1,0:T(8,128)(2,1)} %constant.8.clone.refs_7_.refs_8_) | copy-start | bytes 5701636
  7.7 2.1 %copy-start.4 = (f32[2,128,128]{2,1,0:T(8,128)S(1)}, f32[2,128,128]{2,1,0:T(8,128)}, u32[]{:S(2)}) copy-start(f32[2,128,128]{2,1,0:T(8,128)} %refs_6_.2) | copy-start | bytes 393220
  7.7 2.1 %copy-start.7 = (s32[2,128,128]{2,1,0:T(8,128)S(1)}, s32[2,128,128]{2,1,0:T(8,128)}, u32[]{:S(2)}) copy-start(s32[2,128,128]{2,1,0:T(8,128)} %param.14) | copy-start | bytes 393220
  7.7 2.1 %copy-start.8 = (f32[1,6]{1,0:T(1,128)S(1)}, f32[1,6]{1,0:T(1,128)}, u32[]{:S(2)}) copy-start(f32[1,6]{1,0:T(1,128)} %refs_0_.3) | copy-start | bytes 76
  9.8 23.9 %copy-start.9 = (s32[2]{0:T(128)S(1)}, s32[2]{0:T(128)}, u32[]{:S(2)}) copy-start(s32[2]{0:T(128)} %param.19) | copy-start | bytes 28
  9.8 23.9 %copy-start.10 = (s32[2]{0:T(128)S(1)}, s32[2]{0:T(128)}, u32[]{:S(2)}) copy-start(s32[2]{0:T(128)} %param.18) | copy-start | bytes 28
  9.8 28.8 %copy-start.2 = (bf16[320,256]{1,0:T(8,128)(2,1)S(1)}, bf16[320,256]{1,0:T(8,128)(2,1)}, u32[]{:S(2)}) copy-start(bf16[320,256]{1,0:T(8,128)(2,1)} %constant.6.clone.table_hbm.refs_6_.refs_8_) | copy-start | bytes 491524
  19.3 5.6 %collective-permute-start.2 = (f32[256,128]{1,0:T(8,128)S(1)}, f32[256,128]{1,0:T(8,128)S(1)}, u32[]{:S(2)}, u32[]{:S(2)}) collective-permute-start(f32[256,128]{1,0:T(8,128)S(1)} %get-tuple-element.17), channel_id=1, source_target_pairs={{0,1},{1,0},{2,3},{3,2},{4,5},{5,4},{6,7},{7,6},{8,9},{9,8},{10,11... | collective-permute-start | bytes 393224 | tf_op jit(solution)/shard_map/ppermute | solution.py:479
  24.9 12.8 %collective-permute-start.6 = (f32[256,128]{1,0:T(8,128)S(1)}, f32[256,128]{1,0:T(8,128)S(1)}, u32[]{:S(2)}, u32[]{:S(2)}) collective-permute-start(f32[256,128]{1,0:T(8,128)S(1)} %add.6.refs_1_), channel_id=1, source_target_pairs={{0,16},{2,18},{4,20},{6,22},{8,24},{10,26},{12,28},{14,30},{16,0},... | collective-permute-start | bytes 393224 | tf_op jit(solution)/shard_map/ppermute | solution.py:483
  32.1 5.9 %collective-permute-start.5 = (f32[256,128]{1,0:T(8,128)S(1)}, f32[256,128]{1,0:T(8,128)S(1)}, u32[]{:S(2)}, u32[]{:S(2)}) collective-permute-start(f32[256,128]{1,0:T(8,128)S(1)} %add.6.refs_1_), channel_id=1, source_target_pairs={{0,8},{2,10},{4,12},{6,14},{8,0},{10,2},{12,4},{14,6},{16,24},{18,... | collective-permute-start | bytes 393224 | tf_op jit(solution)/shard_map/ppermute | solution.py:483
  33.7 5.0 %collective-permute-start.4 = (f32[256,128]{1,0:T(8,128)S(1)}, f32[256,128]{1,0:T(8,128)S(1)}, u32[]{:S(2)}, u32[]{:S(2)}) collective-permute-start(f32[256,128]{1,0:T(8,128)S(1)} %add.6.refs_1_), channel_id=1, source_target_pairs={{0,4},{2,6},{4,0},{6,2},{8,12},{10,14},{12,8},{14,10},{16,20},{18,... | collective-permute-start | bytes 393224 | tf_op jit(solution)/shard_map/ppermute | solution.py:483
  33.7 4.9 %collective-permute-start.3 = (f32[256,128]{1,0:T(8,128)S(1)}, f32[256,128]{1,0:T(8,128)S(1)}, u32[]{:S(2)}, u32[]{:S(2)}) collective-permute-start(f32[256,128]{1,0:T(8,128)S(1)} %add.6.refs_1_), channel_id=1, source_target_pairs={{0,2},{2,0},{4,6},{6,4},{8,10},{10,8},{12,14},{14,12},{16,18},{18,... | collective-permute-start | bytes 393224 | tf_op jit(solution)/shard_map/ppermute | solution.py:483
  39.6 1.2 %collective-permute-start.7 = (f32[32,256]{1,0:T(8,128)S(1)}, f32[32,256]{1,0:T(8,128)S(1)}, u32[]{:S(2)}, u32[]{:S(2)}) collective-permute-start(f32[32,256]{1,0:T(8,128)S(1)} %get-tuple-element.19), channel_id=1, source_target_pairs={{0,2},{2,0},{4,6},{6,4},{8,10},{10,8},{12,14},{14,12},{16,18},{18,... | collective-permute-start | bytes 98312 | tf_op jit(solution)/shard_map/ppermute | solution.py:473
  39.6 1.2 %collective-permute-start.8 = (f32[32,256]{1,0:T(8,128)S(1)}, f32[32,256]{1,0:T(8,128)S(1)}, u32[]{:S(2)}, u32[]{:S(2)}) collective-permute-start(f32[32,256]{1,0:T(8,128)S(1)} %get-tuple-element.20), channel_id=1, source_target_pairs={{2,4},{4,2},{6,8},{8,6},{10,12},{12,10},{14,16},{16,14},{18,20},{2... | collective-permute-start | bytes 98312 | tf_op jit(solution)/shard_map/ppermute | solution.py:473
  50.8 5.0 %collective-permute-start.9 = (f32[256,128]{1,0:T(8,128)S(1)}, f32[256,128]{1,0:T(8,128)S(1)}, u32[]{:S(2)}, u32[]{:S(2)}) collective-permute-start(f32[256,128]{1,0:T(8,128)S(1)} %get-tuple-element.23), channel_id=1, source_target_pairs={{0,1},{1,0},{2,3},{3,2},{4,5},{5,4},{6,7},{7,6},{8,9},{9,8},{10,11... | collective-permute-start | bytes 393224 | tf_op jit(solution)/shard_map/ppermute | solution.py:479
  55.8 11.9 %collective-permute-start.13 = (f32[256,128]{1,0:T(8,128)S(1)}, f32[256,128]{1,0:T(8,128)S(1)}, u32[]{:S(2)}, u32[]{:S(2)}) collective-permute-start(f32[256,128]{1,0:T(8,128)S(1)} %add.7.refs_1_), channel_id=1, source_target_pairs={{0,16},{2,18},{4,20},{6,22},{8,24},{10,26},{12,28},{14,30},{16,0},... | collective-permute-start | bytes 393224 | tf_op jit(solution)/shard_map/ppermute | solution.py:483
  62.2 6.2 %collective-permute-start.12 = (f32[256,128]{1,0:T(8,128)S(1)}, f32[256,128]{1,0:T(8,128)S(1)}, u32[]{:S(2)}, u32[]{:S(2)}) collective-permute-start(f32[256,128]{1,0:T(8,128)S(1)} %add.7.refs_1_), channel_id=1, source_target_pairs={{0,8},{2,10},{4,12},{6,14},{8,0},{10,2},{12,4},{14,6},{16,24},{18,... | collective-permute-start | bytes 393224 | tf_op jit(solution)/shard_map/ppermute | solution.py:483
  64.6 5.0 %collective-permute-start.11 = (f32[256,128]{1,0:T(8,128)S(1)}, f32[256,128]{1,0:T(8,128)S(1)}, u32[]{:S(2)}, u32[]{:S(2)}) collective-permute-start(f32[256,128]{1,0:T(8,128)S(1)} %add.7.refs_1_), channel_id=1, source_target_pairs={{0,4},{2,6},{4,0},{6,2},{8,12},{10,14},{12,8},{14,10},{16,20},{18,... | collective-permute-start | bytes 393224 | tf_op jit(solution)/shard_map/ppermute | solution.py:483
  64.6 5.0 %collective-permute-start.10 = (f32[256,128]{1,0:T(8,128)S(1)}, f32[256,128]{1,0:T(8,128)S(1)}, u32[]{:S(2)}, u32[]{:S(2)}) collective-permute-start(f32[256,128]{1,0:T(8,128)S(1)} %add.7.refs_1_), channel_id=1, source_target_pairs={{0,2},{2,0},{4,6},{6,4},{8,10},{10,8},{12,14},{14,12},{16,18},{18,... | collective-permute-start | bytes 393224 | tf_op jit(solution)/shard_map/ppermute | solution.py:483

commit v3 on v2

--- a/solution.py
+++ b/solution.py
@@ -26,6 +26,7 @@
 ROWS = 160
 ROW0 = 8
 EDGE = 48
+HALF = CORE // 2
 WIDE_PAD = 32
 VMEM_LIMIT = 24 * 1024 * 1024
 
@@ -203,19 +204,27 @@
     sm = pl.BlockSpec(memory_space=pltpu.SMEM)
     multi = isinstance(out_shape, (list, tuple))
     n_in = len(args)
+    if group is not None:
+        args = [*args, table_array(group) if given is None else given]
 
     def wrapped(*refs):
-        body(*refs[:n_in], table_reader(group, refs[n_in]), *refs[n_in + 1 :])
+        if group is not None:
+            refs = [*refs[:n_in], table_reader(group, refs[n_in]), *refs[n_in + 1 :]]
+        body(*refs)
 
     return pl.pallas_call(
         wrapped,
         out_shape=out_shape,
-        in_specs=[sm if i in smem else vm for i in range(n_in)] + [vm],
+        in_specs=[sm if i in smem else vm for i in range(len(args))],
         out_specs=[vm] * len(out_shape) if multi else vm,
         scratch_shapes=list(scratch),
         compiler_params=pltpu.CompilerParams(vmem_limit_bytes=VMEM_LIMIT),
         cost_estimate=pl.CostEstimate(flops=flops, bytes_accessed=nbytes, transcendentals=0),
-    )(*args, table_array(group) if given is None else given)
+    )(*args)
+
+
+def is_upper():
+    return lax.rem(lax.axis_index("depth"), 2) == 1
 
 
 def is_even():
@@ -267,7 +276,7 @@
     return pl.pallas_call(
         edges_kernel,
         out_shape=[edge, edge, like(kernels), like(args[4])],
-        in_specs=[pl.BlockSpec(memory_space=pl.ANY)] * 5,
+        in_specs=[pl.BlockSpec(memory_space=pltpu.HBM)] * 5,
         out_specs=[vm] * 4,
         scratch_shapes=[
             pltpu.VMEM(mask_rows.shape, f32),
@@ -317,7 +326,7 @@
             f_ref[t, j] = comp if base is None else base[t, j] - STEP_RATE * comp
 
 
-def gradient_body(kern, last, f_ref, tgt_ref, h_ref, w_ref, thr_ref, tb, g_ref, fld, inten, tot):
+def gradient_body(kern, last, f_ref, tgt_ref, h_ref, w_ref, thr_ref, tb, keep_ref, send_ref, fld, inten, tot):
     inten[...] = jnp.zeros_like(inten)
 
     @pl.loop(0, kern, unroll=True)
@@ -386,12 +395,23 @@
         u_hi, u_lo = split(weight * dot_stacked(tb("x4"), r_hi, r_lo))
         term = dot3(tb(f"by{t}_hi"), tb(f"by{t}_lo"), u_hi, u_lo, dot_nt)
         out = term if out is None else out + term
-    g_ref[...] = out
+    half = is_upper()
+    for t in range(2):
+        at = slice(HALF * t, HALF * t + HALF)
+        top, low = out[CORE * t : CORE * t + HALF], out[CORE * t + HALF : CORE * t + CORE]
+        keep_ref[at] = jnp.where(half, low, top)
+        send_ref[at] = jnp.where(half, top, low)
+
+
+def join(mine_ref, peer_ref, t):
+    at = slice(HALF * t, HALF * t + HALF)
+    mine, peer, half = mine_ref[at], peer_ref[at], is_upper()
+    return jnp.concatenate([jnp.where(half, peer, mine), jnp.where(half, mine, peer)], axis=0)
 
 
 def first_kernel(
     kern, last, w_ref, thr_ref, mask_ref, target_ref, a_ref, b_ref, h_ref, tb,
-    g_ref, f_ref, tgt_ref, fld, inten, tot,
+    keep_ref, send_ref, f_ref, tgt_ref, fld, inten, tot,
 ):
     m_hi, m_lo = split(mask_ref[...])
     v, left, right = sides(a_ref, b_ref, tb)
@@ -402,61 +422,68 @@
         + dot(tb("sel_halo", 0)[:, :EDGE], left)
         + dot(tb("sel_halo", 1)[:, :EDGE], right)
     )
-    gradient_body(kern, last, f_ref, tgt_ref, h_ref, w_ref, thr_ref, tb, g_ref, fld, inten, tot)
+    refs = (w_ref, thr_ref, tb, keep_ref, send_ref, fld, inten, tot)
+    gradient_body(kern, last, f_ref, tgt_ref, h_ref, *refs)
 
 
 def later_kernel(
-    kern, last, w_ref, thr_ref, own_ref, a_ref, b_ref, f_in_ref, tgt_ref, h_ref, tb,
-    g_ref, f_ref, fld, inten, tot,
+    kern, last, w_ref, thr_ref, mine_ref, peer_ref, rim_ref, far_ref, f_in_ref, tgt_ref, h_ref,
+    tb, keep_ref, send_ref, f_ref, fld, inten, tot,
 ):
-    s_hi, s_lo = split(own_ref[...])
-    v, _, _ = sides(a_ref, b_ref, tb)
+    own = [join(mine_ref, peer_ref, t) for t in range(2)]
+    s_hi, s_lo = split(jnp.concatenate(own, axis=0))
+    half = is_upper()
+    rim, far = rim_ref[...], far_ref[...]
+    first, second = jnp.where(half, far, rim), jnp.where(half, rim, far)
+    low = lax.broadcasted_iota(jnp.int32, rim.shape, 1) < HALF
+    tile0 = jnp.where(low, first, pltpu.roll(second, HALF, 1))
+    tile1 = jnp.where(low, pltpu.roll(first, HALF, 1), second)
+    rims = jnp.concatenate([tile0, tile1], axis=1)
+    v, _, _ = sides(rims[:WIDE_PAD], rims[WIDE_PAD:], tb)
     v = v + dot3(tb("cx_own_hi"), tb("cx_own_lo"), s_hi, s_lo, dot_nt)
     to_spectrum(v, tb, f_ref, f_in_ref)
-    gradient_body(kern, last, f_ref, tgt_ref, h_ref, w_ref, thr_ref, tb, g_ref, fld, inten, tot)
-
-
-def match(table_ref, own_ref, got_refs, tb):
+    refs = (w_ref, thr_ref, tb, keep_ref, send_ref, fld, inten, tot)
+    gradient_body(kern, last, f_ref, tgt_ref, h_ref, *refs)
+
+
+def match_kernel(n_got, edges, table_ref, own_ref, *refs):
+    got_refs, (tb, out_ref, *edge_refs) = refs[:n_got], refs[n_got:]
     device = lax.axis_index("tile")
     own = own_ref[...]
-    flip = tb("flip")
+    mine, other = [], []
+    for t in range(2):
+        rows = slice(HALF * t, HALF * t + HALF)
+        mine.append(own[rows])
+        bit = lax.bitwise_xor(table_ref[t], 2 * device + t)
+        value = jnp.where(bit == 1, own[HALF * (1 - t) : HALF * (1 - t) + HALF], mine[t])
+        for b, got in enumerate(got_refs):
+            value = jnp.where(bit == 2 << b, got[rows], value)
+        other.append(value)
+    hi, lo = split(jnp.concatenate(other, axis=0))
+    turned = dot(hi, tb("flip")) + dot(lo, tb("flip"))
     tiles = []
     for t in range(2):
-        rows = slice(CORE * t, CORE * t + CORE)
-        mine = own[rows]
-        bit = lax.bitwise_xor(table_ref[t], 2 * device + t)
-        other = jnp.where(bit == 1, own[CORE * (1 - t) : CORE * (1 - t) + CORE], mine)
-        for b, got in enumerate(got_refs):
-            other = jnp.where(bit == 2 << b, got[rows], other)
-        hi = other.astype(bf16)
-        rest = other - hi.astype(f32)
-        mid = rest.astype(bf16)
-        low = (rest - mid.astype(f32)).astype(bf16)
-        turned = dot(hi, flip) + (dot(mid, flip) + dot(low, flip))
-        tiles.append(0.5 * (mine + jnp.where(table_ref[2 + t] == 1, turned, other)))
-    return tiles
-
-
-def match_kernel(n_got, table_ref, own_ref, *refs):
-    got_refs, (tb, out_ref, a_ref, b_ref) = refs[:n_got], refs[n_got:]
-    matched = jnp.concatenate(match(table_ref, own_ref, got_refs, tb), axis=0)
+        flipped = turned[HALF * t : HALF * t + HALF]
+        tiles.append(0.5 * (mine[t] + jnp.where(table_ref[2 + t] == 1, flipped, other[t])))
+    matched = jnp.concatenate(tiles, axis=0)
     out_ref[...] = matched
-    hi, lo = split(matched)
-    right, left = tb("edge0")[:WIDE_PAD], tb("edge2")[:WIDE_PAD]
-    send_edges(
-        dot_nt(right, hi) + dot_nt(right, lo), dot_nt(left, hi) + dot_nt(left, lo), a_ref, b_ref
-    )
-
-
-def final_kernel(n_got, n_moves, table_ref, own_ref, *refs):
-    got_refs, refs = refs[:n_got], refs[n_got:]
-    mask_ref, moves, (tb, mask_out, grad_out) = refs[0], refs[1 : 1 + n_moves], refs[1 + n_moves :]
-    for t, tile in enumerate(match(table_ref, own_ref, got_refs, tb)):
-        grad_out[t] = tile
+    if edges:
+        hi, lo = split(matched)
+        right, left = tb("edge0")[:WIDE_PAD], tb("edge2")[:WIDE_PAD]
+        right = dot_nt(right, hi) + dot_nt(right, lo)
+        left = dot_nt(left, hi) + dot_nt(left, lo)
+        send_edges(right, left, *edge_refs)
+
+
+def final_kernel(n_moves, mask_ref, *refs):
+    moves, (mask_out, grad_out) = refs[: 2 * n_moves], refs[2 * n_moves :]
+    for t in range(2):
         now = mask_ref[t]
-        for move in moves:
-            now = now - STEP_RATE * move[CORE * t : CORE * t + CORE]
-        mask_out[t] = now - STEP_RATE * tile
+        for mine, peer in zip(moves[::2], moves[1::2]):
+            step = join(mine, peer, t)
+            now = now - STEP_RATE * step
+        grad_out[t] = step
+        mask_out[t] = now
 
 
 def per_device(
@@ -472,23 +499,26 @@
     def swap_edges(send_a, send_b):
         return lax.ppermute(send_b, "tile", pairs_b), lax.ppermute(send_a, "tile", pairs_a)
 
-    def gather_sum(grad):
-        bit = 1
+    def peer_of(x, bit):
+        return lax.ppermute(x, "depth", [(i, i ^ bit) for i in range(n_depth)])
+
+    def gather_sum(keep, send):
+        total = keep + peer_of(send, 1)
+        bit = 2
         while bit < n_depth:
-            pairs = [(i, i ^ bit) for i in range(n_depth)]
-            grad = grad + lax.ppermute(grad, "depth", pairs)
+            total = total + peer_of(total, bit)
             bit *= 2
         bits = [1 << b for b in range(n_tile.bit_length() - 1)]
         got = [
-            lax.ppermute(grad, "tile", [(i, i ^ bit) for i in range(n_tile)])
+            lax.ppermute(total, "tile", [(i, i ^ bit) for i in range(n_tile)])
             for bit in reversed(bits)
         ]
-        return grad, got[::-1]
+        return total, got[::-1]
 
     mask_rows = mask_tiles.reshape(tiles_dev * core, core)
     target_rows = target_tiles.reshape(tiles_dev * core, core)
-    strip = jax.ShapeDtypeStruct((tiles_dev * core, core), f32)
-    side = jax.ShapeDtypeStruct((WIDE_PAD, tiles_dev * core), f32)
+    strip = jax.ShapeDtypeStruct((core, core), f32)
+    side = jax.ShapeDtypeStruct((WIDE_PAD, core), f32)
     freq = jax.ShapeDtypeStruct((2, 4, XB, YB), f32)
     goal = jax.ShapeDtypeStruct((ROWS, 2 * CORE), f32)
     tiles = jax.ShapeDtypeStruct((tiles_dev, core, core), f32)
@@ -511,44 +541,42 @@
         nbytes=4 * 10**6,
         given=spec_table,
     )
-    grad, freq_now, goals = call(
+    keep, send, freq_now, goals = call(
         functools.partial(first_kernel, kern, n_tile - 1),
         "grad",
         [socs_weights, thresholds, mask_rows, target_rows, from_a, from_b, spectra],
-        [strip, freq, goal],
+        [strip, strip, freq, goal],
         scratch,
         smem=(0, 1),
     )
     moves = []
-    for step in range(1, STEPS):
-        total, got = gather_sum(grad)
-        move, send_a, send_b = call(
-            functools.partial(match_kernel, len(got)),
+    for step in range(1, STEPS + 1):
+        more = step < STEPS
+        total, got = gather_sum(keep, send)
+        outs = call(
+            functools.partial(match_kernel, len(got), more),
             "edge",
             [table, total, *got],
-            [strip, side, side],
+            [strip, side, side] if more else [strip],
             smem=(0,),
         )
-        from_b, from_a = swap_edges(send_a, send_b)
-        moves.append(move)
-        grad, freq_now = call(
-            functools.partial(later_kernel, kern, n_tile - 1),
-            "grad",
-            [socs_weights, thresholds, move, from_a, from_b, freq_now, goals, spectra],
-            [strip, freq],
-            scratch,
-            smem=(0, 1),
-        )
-    total, got = gather_sum(grad)
-    return tuple(
-        call(
-            functools.partial(final_kernel, len(got), len(moves)),
-            "edge",
-            [table, total, *got, mask_tiles, *moves],
-            [tiles, tiles],
-            smem=(0,),
-        )
-    )
+        mine = outs[0]
+        peer = peer_of(mine, 1)
+        moves += [mine, peer]
+        if more:
+            from_b, from_a = swap_edges(*outs[1:])
+            rim = jnp.concatenate([from_a, from_b])
+            far = peer_of(rim, 1)
+            keep, send, freq_now = call(
+                functools.partial(later_kernel, kern, n_tile - 1),
+                "grad",
+                [socs_weights, thresholds, mine, peer, rim, far, freq_now, goals, spectra],
+                [strip, strip, freq],
+                scratch,
+                smem=(0, 1),
+            )
+    final = functools.partial(final_kernel, STEPS)
+    return tuple(call(final, None, [mask_tiles, *moves], [tiles, tiles]))
 
 
 def solution(mesh):

time: 71.3 us -> 73.8 us (1.035)
  waiting for transfers between devices: 16.6 us -> 19.8 us
    ppermute x10 -> x13, waiting for transfers between devices: 16.2 us -> 19.8 us  [the longest x5 11.9 us: peer_of(): return lax.ppermute(x, 'depth', [(i, i ^ bit) for i in range(n_depth)])]
    ppermute x10 -> x13, starting transfers between devices: 21.7 us -> 21 us  [the longest x8 13.8 us: gather_sum(): lax.ppermute(total, 'tile', [(i, i ^ bit) for i in range(n_tile)])]
    pallas_call x5 -> x6, Pallas kernels: 23.2 us -> 23.2 us  [call(): pl.pallas_call(wrapped, out_shape=out_shape, in_specs=[sm if i in smem el...]
    unnamed x23 -> x24, local copies, waits for them, and re-layouts: 4.8 us -> 4.81 us
  transfers between devices with their start and end apart: 14 -> 17, of which waited for: 9 -> 10; matrix products, arithmetic and copies ran while one was open for 0% -> 0% of each run, Pallas kernels for 2% -> 2%
where the time goes in v3:
time: 73.8 us; the launch traced here: 73.5 us
  Pallas kernels  24.3 us (33%)
  starting transfers between devices  23 us (31%)
  waiting for transfers between devices  19.8 us (27%)
  local copies, waits for them, and re-layouts  4.81 us (7%)
  between operations  1.48 us (2%)
    pallas_call x6, Pallas kernels, call(): pl.pallas_call(wrapped, out_shape=out_shape, in_specs=[sm if i in smem el...  23.2 us
    ppermute x8, starting transfers between devices, gather_sum(): lax.ppermute(total, 'tile', [(i, i ^ bit) for i in range(n_tile)])  13.8 us
    ppermute x5, waiting for transfers between devices, peer_of(): return lax.ppermute(x, 'depth', [(i, i ^ bit) for i in range(n_depth)])  11.9 us
    ppermute x8, waiting for transfers between devices, gather_sum(): lax.ppermute(total, 'tile', [(i, i ^ bit) for i in range(n_tile)])  7.95 us
    ppermute x5, starting transfers between devices, peer_of(): return lax.ppermute(x, 'depth', [(i, i ^ bit) for i in range(n_depth)])  7.15 us
    unnamed x24, local copies, waits for them, and re-layouts  4.81 us
    ppermute x2, starting transfers between devices, swap_edges(): lax.ppermute(send_b, 'tile', pairs_b)  1.51 us
  transfers between devices with their start and end apart: 17, of which 10 were waited for; matrix products, arithmetic and copies ran while one was open for 0% of the time, Pallas kernels for 2%

profile of v3, /device:TPU:0, one launch (start us, length us, event | category | flops | bytes accessed | tf_op | source)
XLA Modules:
  0.0 73.5 jit_solution(15558665166720422496)
XLA Ops:
  0.6 0.9 %copy.15.ker_hbm = f32[2,1,6,25,25]{4,3,2,1,0:T(8,128)S(1)} copy(f32[2,1,6,25,25]{4,1,3,2,0:T(1,128)} %param.15) | data formatting | bytes 60000 | tf_op args[2]
  1.6 0.0 copy-start.1
  1.6 0.9 %copy-done.1 = bf16[320,256]{1,0:T(8,128)(2,1)S(1)} copy-done((bf16[320,256]{1,0:T(8,128)(2,1)S(1)}, bf16[320,256]{1,0:T(8,128)(2,1)}, u32[]{:S(2)}) %copy-start.1) | copy-done | bytes 163864
  2.5 0.9 %copy-done.3 = f32[2,128,128]{2,1,0:T(8,128)S(1)} copy-done((f32[2,128,128]{2,1,0:T(8,128)S(1)}, f32[2,128,128]{2,1,0:T(8,128)}, u32[]{:S(2)}) %copy-start.3) | copy-done | bytes 131096
  3.4 1.1 %copy-done.5 = bf16[1408,256]{1,0:T(8,128)(2,1)S(1)} copy-done((bf16[1408,256]{1,0:T(8,128)(2,1)S(1)}, bf16[1408,256]{1,0:T(8,128)(2,1)}, u32[]{:S(2)}) %copy-start.5) | copy-done | bytes 720920
  4.5 0.9 %copy-done.6 = s32[2,128,128]{2,1,0:T(8,128)S(1)} copy-done((s32[2,128,128]{2,1,0:T(8,128)S(1)}, s32[2,128,128]{2,1,0:T(8,128)}, u32[]{:S(2)}) %copy-start.6) | copy-done | bytes 131096
  5.4 1.1 %shard_map.140 = (f32[48,256]{1,0:T(8,128)S(1)}, f32[48,256]{1,0:T(8,128)S(1)}, f32[2,1,6,25,25]{4,3,2,1,0:T(8,128)S(1)}, bf16[1408,256]{1,0:T(8,128)(2,1)S(1)}) custom-call(f32[256,128]{1,0:T(8,128)S(1)} %bitcast.2, s32[256,128]{1,0:T(8,128)S(1)} %bitcast.4, bf16[320,256]{1,0:T(8,128)(2,1)S(1)} %copy-done.1, f32[2,1,6,25,25]{4,3,2,1,0:T(8,128)S(1)} %copy.15.ker_hbm, ...), custom_call_target="tpu_custom_call" | custom-call | tf_op jit(solution)/shard_map/pallas_call | solution.py:276
  6.5 0.5 collective-permute-start
  7.1 0.7 collective-permute-start.1
  7.7 0.0 copy-start
  7.7 0.0 copy-start.4
  7.7 0.0 copy-start.7
  7.7 0.0 copy-start.8
  7.8 1.4 %shard_map.141.refs_6_.refs_8_ = f32[12,4,96,128]{3,2,1,0:T(8,128)S(1)} custom-call(f32[2,1,6,25,25]{4,3,2,1,0:T(8,128)S(1)} %get-tuple-element.17.refs_0_, bf16[1408,256]{1,0:T(8,128)(2,1)S(1)} %get-tuple-element.18.refs_1_), custom_call_target="tpu_custom_call" | custom-call | flops 3000000000 | bytes 4000000 | tf_op jit(solution)/shard_map/pallas_call | solution.py:215
  9.8 0.0 copy-start.9
  9.8 0.0 copy-start.10
  9.8 0.0 copy-start.2
  9.8 0.0 collective-permute-done.1.refs_5_
  9.9 9.4 %shard_map.142 = (f32[128,128]{1,0:T(8,128)S(1)}, f32[128,128]{1,0:T(8,128)S(1)}, f32[2,4,96,128]{3,2,1,0:T(8,128)S(1)}, f32[160,256]{1,0:T(8,128)S(1)}) custom-call(f32[1,6]{1,0:T(1,128)S(1)} %copy-done.8, f32[1]{0:T(128)S(6)} %copy.17.refs_1_, f32[256,128]{1,0:T(8,128)S(1)} %bitcast.3, s32[256,128]{1,0:T(8,128)S(1)} %bitcast.5, ...), custom_call_target="tpu_custom_call" | custom-call | tf_op jit(solution)/shard_map/pallas_call | solution.py:215
  19.3 2.6 %collective-permute-start.2 = (f32[128,128]{1,0:T(8,128)S(1)}, f32[128,128]{1,0:T(8,128)S(1)}, u32[]{:S(2)}, u32[]{:S(2)}) collective-permute-start(f32[128,128]{1,0:T(8,128)S(1)} %get-tuple-element.20), channel_id=1, source_target_pairs={{0,1},{1,0},{2,3},{3,2},{4,5},{5,4},{6,7},{7,6},{8,9},{9,8},{10,11... | collective-permute-start | bytes 196616 | tf_op jit(solution)/shard_map/ppermute | solution.py:503
  21.9 2.2 %collective-permute-done.2 = f32[128,128]{1,0:T(8,128)S(1)} collective-permute-done((f32[128,128]{1,0:T(8,128)S(1)}, f32[128,128]{1,0:T(8,128)S(1)}, u32[]{:S(2)}, u32[]{:S(2)}) %collective-permute-start.2) | collective-permute-done | bytes 65568 | tf_op jit(solution)/shard_map/ppermute | solution.py:503
  24.2 6.7 %collective-permute-start.6 = (f32[128,128]{1,0:T(8,128)S(1)}, f32[128,128]{1,0:T(8,128)S(1)}, u32[]{:S(2)}, u32[]{:S(2)}) collective-permute-start(f32[128,128]{1,0:T(8,128)S(1)} %add.6.refs_1_), channel_id=1, source_target_pairs={{0,16},{2,18},{4,20},{6,22},{8,24},{10,26},{12,28},{14,30},{16,0},... | collective-permute-start | bytes 196616 | tf_op jit(solution)/shard_map/ppermute | solution.py:513
  30.9 1.6 %collective-permute-start.5 = (f32[128,128]{1,0:T(8,128)S(1)}, f32[128,128]{1,0:T(8,128)S(1)}, u32[]{:S(2)}, u32[]{:S(2)}) collective-permute-start(f32[128,128]{1,0:T(8,128)S(1)} %add.6.refs_1_), channel_id=1, source_target_pairs={{0,8},{2,10},{4,12},{6,14},{8,0},{10,2},{12,4},{14,6},{16,24},{18,... | collective-permute-start | bytes 196616 | tf_op jit(solution)/shard_map/ppermute | solution.py:513
  32.5 0.5 collective-permute-start.4
  33.0 0.1 pad_add_fusion.refs_0_
  33.1 0.2 collective-permute-done.6.refs_5_
  33.3 1.9 %collective-permute-done.5.refs_4_ = f32[128,128]{1,0:T(8,128)S(1)} collective-permute-done((f32[128,128]{1,0:T(8,128)S(1)}, f32[128,128]{1,0:T(8,128)S(1)}, u32[]{:S(2)}, u32[]{:S(2)}) %collective-permute-start.5) | collective-permute-done | bytes 65568 | tf_op jit(solution)/shard_map/ppermute | solution.py:513
  35.2 1.6 %collective-permute-done.4.refs_3_ = f32[128,128]{1,0:T(8,128)S(1)} collective-permute-done((f32[128,128]{1,0:T(8,128)S(1)}, f32[128,128]{1,0:T(8,128)S(1)}, u32[]{:S(2)}, u32[]{:S(2)}) %collective-permute-start.4) | collective-permute-done | bytes 65568 | tf_op jit(solution)/shard_map/ppermute | solution.py:513
  36.8 0.0 collective-permute-done.3.refs_2_
  36.8 0.9 %shard_map.143 = (f32[128,128]{1,0:T(8,128)S(1)}, f32[32,128]{1,0:T(8,128)S(1)}, f32[32,128]{1,0:T(8,128)S(1)}) custom-call(s32[4]{0:T(128)S(1)} %pad_add_fusion.refs_0_, f32[128,128]{1,0:T(8,128)S(1)} %add.6.refs_1_, f32[128,128]{1,0:T(8,128)S(1)} %collective-permute-done.3.refs_2_, f32[128,128]{1,0:T(8,128)S(1)} %collective-permute-done.4.refs_3_, ...), custom_call_target="tpu_custom_call" | custom-call | tf_op jit(solution)/shard_map/pallas_call | solution.py:215
  37.6 0.9 %collective-permute-start.9 = (f32[32,128]{1,0:T(8,128)S(1)}, f32[32,128]{1,0:T(8,128)S(1)}, u32[]{:S(2)}, u32[]{:S(2)}) collective-permute-start(f32[32,128]{1,0:T(8,128)S(1)} %get-tuple-element.23), channel_id=1, source_target_pairs={{2,4},{4,2},{6,8},{8,6},{10,12},{12,10},{14,16},{16,14},{18,20},{2... | collective-permute-start | bytes 49160 | tf_op jit(solution)/shard_map/ppermute | solution.py:500
  38.5 1.6 %collective-permute-start.7 = (f32[128,128]{1,0:T(8,128)S(1)}, f32[128,128]{1,0:T(8,128)S(1)}, u32[]{:S(2)}, u32[]{:S(2)}) collective-permute-start(f32[128,128]{1,0:T(8,128)S(1)} %get-tuple-element.21.refs_2_.refs_1_), channel_id=1, source_target_pairs={{0,1},{1,0},{2,3},{3,2},{4,5},{5,4},{6,7},{7,6},{8,9},{9,8},{10,11... | collective-permute-start | bytes 196616 | tf_op jit(solution)/shard_map/ppermute | solution.py:503
  40.1 0.0 collective-permute-done.8
  40.1 0.0 collective-permute-done.9
  40.1 0.6 collective-permute-start.10
  40.7 3.4 %collective-permute-done.10.refs_5_ = f32[64,128]{1,0:T(8,128)S(1)} collective-permute-done((f32[64,128]{1,0:T(8,128)S(1)}, f32[64,128]{1,0:T(8,128)S(1)}, u32[]{:S(2)}, u32[]{:S(2)}) %collective-permute-start.10) | collective-permute-done | bytes 32800 | tf_op jit(solution)/shard_map/ppermute | solution.py:503
  44.1 10.1 %shard_map.144 = (f32[128,128]{1,0:T(8,128)S(1)}, f32[128,128]{1,0:T(8,128)S(1)}, f32[2,4,96,128]{3,2,1,0:T(8,128)}) custom-call(f32[1,6]{1,0:T(1,128)S(1)} %copy-done.8, f32[1]{0:T(128)S(6)} %copy.17.refs_1_, f32[128,128]{1,0:T(8,128)S(1)} %get-tuple-element.21.refs_2_.refs_1_, f32[128,128]{1,0:T(8,128)S(1)} %collective-permute-done.7.refs_3_.refs_2_, ...), custom_call_target="tpu_custom_call" | custom-call | tf_op jit(solution)/shard_map/pallas_call | solution.py:215
  54.2 0.8 %collective-permute-start.11 = (f32[128,128]{1,0:T(8,128)S(1)}, f32[128,128]{1,0:T(8,128)S(1)}, u32[]{:S(2)}, u32[]{:S(2)}) collective-permute-start(f32[128,128]{1,0:T(8,128)S(1)} %get-tuple-element.27), channel_id=1, source_target_pairs={{0,1},{1,0},{2,3},{3,2},{4,5},{5,4},{6,7},{7,6},{8,9},{9,8},{10,11... | collective-permute-start | bytes 196616 | tf_op jit(solution)/shard_map/ppermute | solution.py:503
  55.0 3.5 %collective-permute-done.11 = f32[128,128]{1,0:T(8,128)S(1)} collective-permute-done((f32[128,128]{1,0:T(8,128)S(1)}, f32[128,128]{1,0:T(8,128)S(1)}, u32[]{:S(2)}, u32[]{:S(2)}) %collective-permute-start.11) | collective-permute-done | bytes 65568 | tf_op jit(solution)/shard_map/ppermute | solution.py:503
  58.5 3.8 %collective-permute-start.15 = (f32[128,128]{1,0:T(8,128)S(1)}, f32[128,128]{1,0:T(8,128)S(1)}, u32[]{:S(2)}, u32[]{:S(2)}) collective-permute-start(f32[128,128]{1,0:T(8,128)S(1)} %add.7.refs_1_), channel_id=1, source_target_pairs={{0,16},{2,18},{4,20},{6,22},{8,24},{10,26},{12,28},{14,30},{16,0},... | collective-permute-start | bytes 196616 | tf_op jit(solution)/shard_map/ppermute | solution.py:513
  62.3 1.2 %collective-permute-start.14 = (f32[128,128]{1,0:T(8,128)S(1)}, f32[128,128]{1,0:T(8,128)S(1)}, u32[]{:S(2)}, u32[]{:S(2)}) collective-permute-start(f32[128,128]{1,0:T(8,128)S(1)} %add.7.refs_1_), channel_id=1, source_target_pairs={{0,8},{2,10},{4,12},{6,14},{8,0},{10,2},{12,4},{14,6},{16,24},{18,... | collective-permute-start | bytes 196616 | tf_op jit(solution)/shard_map/ppermute | solution.py:513
  63.5 1.5 %collective-permute-done.15.refs_5_ = f32[128,128]{1,0:T(8,128)S(1)} collective-permute-done((f32[128,128]{1,0:T(8,128)S(1)}, f32[128,128]{1,0:T(8,128)S(1)}, u32[]{:S(2)}, u32[]{:S(2)}) %collective-permute-start.15) | collective-permute-done | bytes 65568 | tf_op jit(solution)/shard_map/ppermute | solution.py:513
  64.9 1.6 %collective-permute-done.14.refs_4_ = f32[128,128]{1,0:T(8,128)S(1)} collective-permute-done((f32[128,128]{1,0:T(8,128)S(1)}, f32[128,128]{1,0:T(8,128)S(1)}, u32[]{:S(2)}, u32[]{:S(2)}) %collective-permute-start.14) | collective-permute-done | bytes 65568 | tf_op jit(solution)/shard_map/ppermute | solution.py:513
  66.6 1.2 %collective-permute-done.13.refs_3_ = f32[128,128]{1,0:T(8,128)S(1)} collective-permute-done((f32[128,128]{1,0:T(8,128)S(1)}, f32[128,128]{1,0:T(8,128)S(1)}, u32[]{:S(2)}, u32[]{:S(2)}) %collective-permute-start.13) | collective-permute-done | bytes 65568 | tf_op jit(solution)/shard_map/ppermute | solution.py:513
  67.7 0.7 shard_map.145.refs_3_
  68.5 1.6 %collective-permute-start.16 = (f32[128,128]{1,0:T(8,128)S(1)}, f32[128,128]{1,0:T(8,128)S(1)}, u32[]{:S(2)}, u32[]{:S(2)}) collective-permute-start(f32[128,128]{1,0:T(8,128)S(1)} %shard_map.145.refs_3_), channel_id=1, source_target_pairs={{0,1},{1,0},{2,3},{3,2},{4,5},{5,4},{6,7},{7,6},{8,9},{9,8},{10,11... | collective-permute-start | bytes 196616 | tf_op jit(solution)/shard_map/ppermute | solution.py:503
  70.0 2.7 %collective-permute-done.16.refs_4_ = f32[128,128]{1,0:T(8,128)S(1)} collective-permute-done((f32[128,128]{1,0:T(8,128)S(1)}, f32[128,128]{1,0:T(8,128)S(1)}, u32[]{:S(2)}, u32[]{:S(2)}) %collective-permute-start.16) | collective-permute-done | bytes 65568 | tf_op jit(solution)/shard_map/ppermute | solution.py:503
  72.8 0.7 shard_map.146
  (21 shorter events, 0.1 us)
Async XLA Ops:
  1.6 0.9 %copy-start.1 = (bf16[320,256]{1,0:T(8,128)(2,1)S(1)}, bf16[320,256]{1,0:T(8,128)(2,1)}, u32[]{:S(2)}) copy-start(bf16[320,256]{1,0:T(8,128)(2,1)} %constant.6.clone.table_hbm.refs_6_) | copy-start | bytes 491524
  2.5 0.9 %copy-start.3 = (f32[2,128,128]{2,1,0:T(8,128)S(1)}, f32[2,128,128]{2,1,0:T(8,128)}, u32[]{:S(2)}) copy-start(f32[2,128,128]{2,1,0:T(8,128)} %refs_0_.5) | copy-start | bytes 393220
  3.4 1.1 %copy-start.5 = (bf16[1408,256]{1,0:T(8,128)(2,1)S(1)}, bf16[1408,256]{1,0:T(8,128)(2,1)}, u32[]{:S(2)}) copy-start(bf16[1408,256]{1,0:T(8,128)(2,1)} %constant.7.clone.spec_hbm) | copy-start | bytes 2162692
  4.5 0.9 %copy-start.6 = (s32[2,128,128]{2,1,0:T(8,128)S(1)}, s32[2,128,128]{2,1,0:T(8,128)}, u32[]{:S(2)}) copy-start(s32[2,128,128]{2,1,0:T(8,128)} %param.14) | copy-start | bytes 393220
  6.5 3.3 %collective-permute-start = (f32[48,256]{1,0:T(8,128)S(1)}, f32[48,256]{1,0:T(8,128)S(1)}, u32[]{:S(2)}, u32[]{:S(2)}) collective-permute-start(f32[48,256]{1,0:T(8,128)S(1)} %get-tuple-element.15), channel_id=1, source_target_pairs={{0,2},{2,0},{4,6},{6,4},{8,10},{10,8},{12,14},{14,12},{16,18},{18,... | collective-permute-start | bytes 147464 | tf_op jit(solution)/shard_map/ppermute | solution.py:500
  7.1 2.8 %collective-permute-start.1 = (f32[48,256]{1,0:T(8,128)S(1)}, f32[48,256]{1,0:T(8,128)S(1)}, u32[]{:S(2)}, u32[]{:S(2)}) collective-permute-start(f32[48,256]{1,0:T(8,128)S(1)} %get-tuple-element.16), channel_id=1, source_target_pairs={{2,4},{4,2},{6,8},{8,6},{10,12},{12,10},{14,16},{16,14},{18,20},{2... | collective-permute-start | bytes 147464 | tf_op jit(solution)/shard_map/ppermute | solution.py:500
  7.7 2.1 %copy-start = (bf16[3712,256]{1,0:T(8,128)(2,1)S(1)}, bf16[3712,256]{1,0:T(8,128)(2,1)}, u32[]{:S(2)}) copy-start(bf16[3712,256]{1,0:T(8,128)(2,1)} %constant.8.clone.refs_7_.refs_9_) | copy-start | bytes 5701636
  7.7 2.1 %copy-start.4 = (f32[2,128,128]{2,1,0:T(8,128)S(1)}, f32[2,128,128]{2,1,0:T(8,128)}, u32[]{:S(2)}) copy-start(f32[2,128,128]{2,1,0:T(8,128)} %refs_0_.5) | copy-start | bytes 393220
  7.7 2.1 %copy-start.7 = (s32[2,128,128]{2,1,0:T(8,128)S(1)}, s32[2,128,128]{2,1,0:T(8,128)}, u32[]{:S(2)}) copy-start(s32[2,128,128]{2,1,0:T(8,128)} %param.14) | copy-start | bytes 393220
  7.7 2.1 %copy-start.8 = (f32[1,6]{1,0:T(1,128)S(1)}, f32[1,6]{1,0:T(1,128)}, u32[]{:S(2)}) copy-start(f32[1,6]{1,0:T(1,128)} %refs_0_.4) | copy-start | bytes 76
  9.8 23.2 %copy-start.9 = (s32[2]{0:T(128)S(1)}, s32[2]{0:T(128)}, u32[]{:S(2)}) copy-start(s32[2]{0:T(128)} %param.19) | copy-start | bytes 28
  9.8 23.2 %copy-start.10 = (s32[2]{0:T(128)S(1)}, s32[2]{0:T(128)}, u32[]{:S(2)}) copy-start(s32[2]{0:T(128)} %param.18) | copy-start | bytes 28
  9.8 27.0 %copy-start.2 = (bf16[320,256]{1,0:T(8,128)(2,1)S(1)}, bf16[320,256]{1,0:T(8,128)(2,1)}, u32[]{:S(2)}) copy-start(bf16[320,256]{1,0:T(8,128)(2,1)} %constant.6.clone.table_hbm.refs_6_) | copy-start | bytes 491524
  19.3 4.8 %collective-permute-start.2 = (f32[128,128]{1,0:T(8,128)S(1)}, f32[128,128]{1,0:T(8,128)S(1)}, u32[]{:S(2)}, u32[]{:S(2)}) collective-permute-start(f32[128,128]{1,0:T(8,128)S(1)} %get-tuple-element.20), channel_id=1, source_target_pairs={{0,1},{1,0},{2,3},{3,2},{4,5},{5,4},{6,7},{7,6},{8,9},{9,8},{10,11... | collective-permute-start | bytes 196616 | tf_op jit(solution)/shard_map/ppermute | solution.py:503
  24.2 9.1 %collective-permute-start.6 = (f32[128,128]{1,0:T(8,128)S(1)}, f32[128,128]{1,0:T(8,128)S(1)}, u32[]{:S(2)}, u32[]{:S(2)}) collective-permute-start(f32[128,128]{1,0:T(8,128)S(1)} %add.6.refs_1_), channel_id=1, source_target_pairs={{0,16},{2,18},{4,20},{6,22},{8,24},{10,26},{12,28},{14,30},{16,0},... | collective-permute-start | bytes 196616 | tf_op jit(solution)/shard_map/ppermute | solution.py:513
  30.9 4.3 %collective-permute-start.5 = (f32[128,128]{1,0:T(8,128)S(1)}, f32[128,128]{1,0:T(8,128)S(1)}, u32[]{:S(2)}, u32[]{:S(2)}) collective-permute-start(f32[128,128]{1,0:T(8,128)S(1)} %add.6.refs_1_), channel_id=1, source_target_pairs={{0,8},{2,10},{4,12},{6,14},{8,0},{10,2},{12,4},{14,6},{16,24},{18,... | collective-permute-start | bytes 196616 | tf_op jit(solution)/shard_map/ppermute | solution.py:513
  32.5 4.3 %collective-permute-start.4 = (f32[128,128]{1,0:T(8,128)S(1)}, f32[128,128]{1,0:T(8,128)S(1)}, u32[]{:S(2)}, u32[]{:S(2)}) collective-permute-start(f32[128,128]{1,0:T(8,128)S(1)} %add.6.refs_1_), channel_id=1, source_target_pairs={{0,4},{2,6},{4,0},{6,2},{8,12},{10,14},{12,8},{14,10},{16,20},{18,... | collective-permute-start | bytes 196616 | tf_op jit(solution)/shard_map/ppermute | solution.py:513
  33.0 3.8 %collective-permute-start.3 = (f32[128,128]{1,0:T(8,128)S(1)}, f32[128,128]{1,0:T(8,128)S(1)}, u32[]{:S(2)}, u32[]{:S(2)}) collective-permute-start(f32[128,128]{1,0:T(8,128)S(1)} %add.6.refs_1_), channel_id=1, source_target_pairs={{0,2},{2,0},{4,6},{6,4},{8,10},{10,8},{12,14},{14,12},{16,18},{18,... | collective-permute-start | bytes 196616 | tf_op jit(solution)/shard_map/ppermute | solution.py:513
  37.6 2.5 %collective-permute-start.8 = (f32[32,128]{1,0:T(8,128)S(1)}, f32[32,128]{1,0:T(8,128)S(1)}, u32[]{:S(2)}, u32[]{:S(2)}) collective-permute-start(f32[32,128]{1,0:T(8,128)S(1)} %get-tuple-element.22), channel_id=1, source_target_pairs={{0,2},{2,0},{4,6},{6,4},{8,10},{10,8},{12,14},{14,12},{16,18},{18,... | collective-permute-start | bytes 49160 | tf_op jit(solution)/shard_map/ppermute | solution.py:500
  37.6 2.5 %collective-permute-start.9 = (f32[32,128]{1,0:T(8,128)S(1)}, f32[32,128]{1,0:T(8,128)S(1)}, u32[]{:S(2)}, u32[]{:S(2)}) collective-permute-start(f32[32,128]{1,0:T(8,128)S(1)} %get-tuple-element.23), channel_id=1, source_target_pairs={{2,4},{4,2},{6,8},{8,6},{10,12},{12,10},{14,16},{16,14},{18,20},{2... | collective-permute-start | bytes 49160 | tf_op jit(solution)/shard_map/ppermute | solution.py:500
  38.5 5.6 %collective-permute-start.7 = (f32[128,128]{1,0:T(8,128)S(1)}, f32[128,128]{1,0:T(8,128)S(1)}, u32[]{:S(2)}, u32[]{:S(2)}) collective-permute-start(f32[128,128]{1,0:T(8,128)S(1)} %get-tuple-element.21.refs_2_.refs_1_), channel_id=1, source_target_pairs={{0,1},{1,0},{2,3},{3,2},{4,5},{5,4},{6,7},{7,6},{8,9},{9,8},{10,11... | collective-permute-start | bytes 196616 | tf_op jit(solution)/shard_map/ppermute | solution.py:503
  40.1 4.0 %collective-permute-start.10 = (f32[64,128]{1,0:T(8,128)S(1)}, f32[64,128]{1,0:T(8,128)S(1)}, u32[]{:S(2)}, u32[]{:S(2)}) collective-permute-start(f32[64,128]{1,0:T(8,128)S(1)} %constant_dynamic-update-slice_fusion.refs_4_), channel_id=1, source_target_pairs={{0,1},{1,0},{2,3},{3,2},{4,5},{5,4},{6,7},{7,6},{8,9},{9,8},{10,11... | collective-permute-start | bytes 98312 | tf_op jit(solution)/shard_map/ppermute | solution.py:503
  54.2 4.3 %collective-permute-start.11 = (f32[128,128]{1,0:T(8,128)S(1)}, f32[128,128]{1,0:T(8,128)S(1)}, u32[]{:S(2)}, u32[]{:S(2)}) collective-permute-start(f32[128,128]{1,0:T(8,128)S(1)} %get-tuple-element.27), channel_id=1, source_target_pairs={{0,1},{1,0},{2,3},{3,2},{4,5},{5,4},{6,7},{7,6},{8,9},{9,8},{10,11... | collective-permute-start | bytes 196616 | tf_op jit(solution)/shard_map/ppermute | solution.py:503
  58.5 6.5 %collective-permute-start.15 = (f32[128,128]{1,0:T(8,128)S(1)}, f32[128,128]{1,0:T(8,128)S(1)}, u32[]{:S(2)}, u32[]{:S(2)}) collective-permute-start(f32[128,128]{1,0:T(8,128)S(1)} %add.7.refs_1_), channel_id=1, source_target_pairs={{0,16},{2,18},{4,20},{6,22},{8,24},{10,26},{12,28},{14,30},{16,0},... | collective-permute-start | bytes 196616 | tf_op jit(solution)/shard_map/ppermute | solution.py:513
  62.3 4.3 %collective-permute-start.14 = (f32[128,128]{1,0:T(8,128)S(1)}, f32[128,128]{1,0:T(8,128)S(1)}, u32[]{:S(2)}, u32[]{:S(2)}) collective-permute-start(f32[128,128]{1,0:T(8,128)S(1)} %add.7.refs_1_), channel_id=1, source_target_pairs={{0,8},{2,10},{4,12},{6,14},{8,0},{10,2},{12,4},{14,6},{16,24},{18,... | collective-permute-start | bytes 196616 | tf_op jit(solution)/shard_map/ppermute | solution.py:513
  63.5 4.3 %collective-permute-start.13 = (f32[128,128]{1,0:T(8,128)S(1)}, f32[128,128]{1,0:T(8,128)S(1)}, u32[]{:S(2)}, u32[]{:S(2)}) collective-permute-start(f32[128,128]{1,0:T(8,128)S(1)} %add.7.refs_1_), channel_id=1, source_target_pairs={{0,4},{2,6},{4,0},{6,2},{8,12},{10,14},{12,8},{14,10},{16,20},{18,... | collective-permute-start | bytes 196616 | tf_op jit(solution)/shard_map/ppermute | solution.py:513
  63.5 4.3 %collective-permute-start.12 = (f32[128,128]{1,0:T(8,128)S(1)}, f32[128,128]{1,0:T(8,128)S(1)}, u32[]{:S(2)}, u32[]{:S(2)}) collective-permute-start(f32[128,128]{1,0:T(8,128)S(1)} %add.7.refs_1_), channel_id=1, source_target_pairs={{0,2},{2,0},{4,6},{6,4},{8,10},{10,8},{12,14},{14,12},{16,18},{18,... | collective-permute-start | bytes 196616 | tf_op jit(solution)/shard_map/ppermute | solution.py:513
  68.5 4.3 %collective-permute-start.16 = (f32[128,128]{1,0:T(8,128)S(1)}, f32[128,128]{1,0:T(8,128)S(1)}, u32[]{:S(2)}, u32[]{:S(2)}) collective-permute-start(f32[128,128]{1,0:T(8,128)S(1)} %shard_map.145.refs_3_), channel_id=1, source_target_pairs={{0,1},{1,0},{2,3},{3,2},{4,5},{5,4},{6,7},{7,6},{8,9},{9,8},{10,11... | collective-permute-start | bytes 196616 | tf_op jit(solution)/shard_map/ppermute | solution.py:503

commit v4 on v1

--- a/solution.py
+++ b/solution.py
@@ -95,6 +95,9 @@
     both = []
     for name, a in parts:
         hi, lo = np_split(a)
+        if name in ("x2", "x3", "x4"):
+            both.append((name, np.concatenate([hi.astype(np.float64), lo.astype(np.float64)])))
+            continue
         both += [(name + "_hi", hi.astype(np.float64)), (name + "_lo", lo.astype(np.float64))]
     return both
 
@@ -133,16 +136,7 @@
         ky = np.zeros((128, 2 * YB))
         ky[32 * m : 32 * m + KSIZE] = y_lanes(offs)
         spec.append((f"ky{m}", ky))
-    sel = np.zeros((4, EDGE, 128))
-    for r in range(WIDE):
-        sel[0, r, CORE - WIDE + r] = 1
-        sel[2, r, r] = 1
-    for r in range(HALO):
-        sel[1, WIDE + r, CORE - HALO + r] = 1
-        sel[3, WIDE + r, r] = 1
-    edge = [(f"edge{i}", sel[i]) for i in range(4)]
-    edge.append(("flip", np.eye(CORE)[::-1]))
-    return {"grad": pack(grad), "spec": pack(pack_split(spec)), "edge": pack(edge)}
+    return {"grad": pack(grad), "spec": pack(pack_split(spec))}
 
 
 def split(x):
@@ -160,6 +154,12 @@
 
 def dot3(a_hi, a_lo, b_hi, b_lo, mul=dot):
     return mul(a_hi, b_hi) + (mul(a_lo, b_hi) + mul(a_hi, b_lo))
+
+
+def dot_stacked(table, b_hi, b_lo):
+    rows = table.shape[0] // 2
+    both = dot(table, b_hi)
+    return both[:rows] + (both[rows:] + dot(table[:rows], b_lo))
 
 
 def signed(spec):
@@ -174,30 +174,42 @@
     return jnp.concatenate([top, low], axis=0)
 
 
+def table_array(group):
+    return jnp.asarray(tables()[group][0].astype(ml_dtypes.bfloat16))
+
+
+def table_reader(group, ref):
+    where = tables()[group][1]
+
+    def table(name, half=None):
+        at, height, width = where[name]
+        lanes = slice(0, width) if half is None else slice(128 * half, 128 * half + 128)
+        return ref[at : at + height, lanes]
+
+    return table
+
+
 def call(body, group, args, out_shape, scratch=(), smem=(), flops=0, nbytes=0):
-    packed, where = tables()[group]
     vm = pl.BlockSpec(memory_space=pltpu.VMEM)
     sm = pl.BlockSpec(memory_space=pltpu.SMEM)
-    multi = isinstance(out_shape, (list, tuple))
     n_in = len(args)
+    if group is not None:
+        args = [*args, table_array(group)]
 
     def wrapped(*refs):
-        def table(name, half=None):
-            at, height, width = where[name]
-            lanes = slice(0, width) if half is None else slice(128 * half, 128 * half + 128)
-            return refs[n_in][at : at + height, lanes]
-
-        body(*refs[:n_in], table, *refs[n_in + 1 :])
+        if group is not None:
+            refs = [*refs[:n_in], table_reader(group, refs[n_in]), *refs[n_in + 1 :]]
+        body(*refs)
 
     return pl.pallas_call(
         wrapped,
         out_shape=out_shape,
-        in_specs=[sm if i in smem else vm for i in range(n_in)] + [vm],
-        out_specs=[vm] * len(out_shape) if multi else vm,
+        in_specs=[sm if i in smem else vm for i in range(len(args))],
+        out_specs=[vm] * len(out_shape),
         scratch_shapes=list(scratch),
         compiler_params=pltpu.CompilerParams(vmem_limit_bytes=VMEM_LIMIT),
         cost_estimate=pl.CostEstimate(flops=flops, bytes_accessed=nbytes, transcendentals=0),
-    )(*args, jnp.asarray(packed.astype(ml_dtypes.bfloat16)))
+    )(*args)
 
 
 def is_even():
@@ -210,12 +222,28 @@
     b_ref[...] = jnp.where(even, left, right)
 
 
-def edges_kernel(mask_ref, target_ref, tb, a_ref, b_ref):
-    m_hi, m_lo = split(mask_ref[...])
-    tgt = target_ref[...].astype(f32).astype(bf16)
-    right = dot_nt(tb("edge0"), m_hi) + dot_nt(tb("edge0"), m_lo) + dot_nt(tb("edge1"), tgt)
-    left = dot_nt(tb("edge2"), m_hi) + dot_nt(tb("edge2"), m_lo) + dot_nt(tb("edge3"), tgt)
-    send_edges(right, left, a_ref, b_ref)
+def picker(rows, first, count, col):
+    row = lax.broadcasted_iota(jnp.int32, (rows, CORE), 0)
+    lane = lax.broadcasted_iota(jnp.int32, (rows, CORE), 1)
+    hit = (row - first == lane - col) & (row >= first) & (row < first + count)
+    return jnp.where(hit, 1.0, 0.0).astype(bf16)
+
+
+def edges_of(rows, strip, extra=None):
+    hi, lo = split(strip)
+    both = []
+    for col, more in ((CORE - WIDE, CORE - HALO), (0, 0)):
+        pick = picker(rows, 0, WIDE, col)
+        edge = dot_nt(pick, hi) + dot_nt(pick, lo)
+        if extra is not None:
+            edge = edge + dot_nt(picker(rows, WIDE, HALO, more), extra)
+        both.append(edge)
+    return both
+
+
+def edges_kernel(mask_ref, target_ref, a_ref, b_ref):
+    target = target_ref[...].astype(f32).astype(bf16)
+    send_edges(*edges_of(EDGE, mask_ref[...], target), a_ref, b_ref)
 
 
 def spectra_kernel(kern, ker_ref, tb, h_ref, hs_ref):
@@ -223,7 +251,7 @@
     for k in range(kern):
         for part in range(2):
             row = 32 * (2 * k + part)
-            hs_ref[row : row + KSIZE, :KSIZE] = ker_ref[part, 0, k]
+            hs_ref[row : row + KSIZE, :KSIZE] = ker_ref[part, k, :, 0, :]
     s_hi, s_lo = split(hs_ref[...])
     z = dot3(tb("kx_hi"), tb("kx_lo"), s_hi, s_lo, dot_nt)
     z_hi, z_lo = split(z)
@@ -259,7 +287,7 @@
 def gradient_body(kern, last, f_ref, tgt_ref, h_ref, w_ref, thr_ref, tb, g_ref, fld, inten, tot):
     inten[...] = jnp.zeros_like(inten)
 
-    @pl.loop(0, kern)
+    @pl.loop(0, kern, unroll=True)
     def _(k):
         for t in range(2):
             parts = []
@@ -268,13 +296,15 @@
                 fpr, fpi, fmr, fmi = (f_ref[t, j] for j in range(4))
                 pr, pi = hpr * fpr - hpi * fpi, hpr * fpi + hpi * fpr
                 mr, mi = hmr * fmr - hmi * fmi, hmr * fmi + hmi * fmr
-                r_hi, r_lo = split(even_odd(pr, pi, mr, mi))
-                parts.append(dot3(tb("x2_hi"), tb("x2_lo"), r_hi, r_lo))
-            g_hi, g_lo = split(jnp.concatenate(parts, axis=0))
-            r = dot(g_hi, tb("y2"))
-            field = r[:, :CORE] + (r[:, CORE:] + dot(g_lo, tb("y2", 0)))
+                parts.append(even_odd(pr, pi, mr, mi))
+            p_hi, p_lo = split(jnp.concatenate(parts, axis=0))
+            z = dot(p_hi, tb("y2"))
+            z = z[:, :CORE] + (z[:, CORE:] + dot(p_lo, tb("y2", 0)))
+            z_hi, z_lo = split(jnp.concatenate([z[: 2 * XB], z[2 * XB :]], axis=1))
+            field = dot_stacked(tb("x2"), z_hi, z_lo)
             fld[t, k] = field
-            inten[t] += w_ref[0, k] * (field[:ROWS] * field[:ROWS] + field[ROWS:] * field[ROWS:])
+            re, im = field[:, :CORE], field[:, CORE:]
+            inten[t] += w_ref[0, k] * (re * re + im * im)
 
     tile = lax.axis_index("tile")
     first = jnp.where(tile == 0, WIDE, HALO) - ROW0
@@ -288,24 +318,29 @@
         inten[t] = jnp.where(inside, 2.0 * slope, 0.0)
     tot[...] = jnp.zeros_like(tot)
 
-    @pl.loop(0, kern)
+    @pl.loop(0, kern, unroll=True)
     def _(k):
         for t in range(2):
             scaled = w_ref[0, k] * inten[t]
             field = fld[t, k]
             r_hi, r_lo = split(
-                jnp.concatenate([scaled * field[:ROWS], scaled * field[ROWS:]], axis=0)
+                jnp.concatenate([scaled * field[:, :CORE], scaled * field[:, CORE:]], axis=1)
             )
-            w = dot(jnp.concatenate([r_hi, r_lo], axis=1), tb("y3_dup"))
-            w_hi, w_lo = split(w + dot(r_hi, tb("y3_lo")))
+            w_hi, w_lo = split(dot_stacked(tb("x3"), r_hi, r_lo))
+            his = [w_hi[:, :CORE], w_hi[:, CORE:]]
+            los = [w_lo[:, :CORE], w_lo[:, CORE:]]
+            both = [jnp.concatenate([his[p], los[p]], axis=1) for p in range(2)]
+            specs = dot(jnp.concatenate(both, axis=0), tb("y3_dup"))
+            specs = specs + dot(jnp.concatenate(his, axis=0), tb("y3_lo"))
             acc = [tot[t, j] for j in range(4)]
             for part in range(2):
-                rows = slice(ROWS * part, ROWS * part + ROWS)
-                spec = dot3(tb("x3_hi"), tb("x3_lo"), w_hi[rows], w_lo[rows])
-                bpr, bpi, bmr, bmi = signed(spec)
+                spec = specs[2 * XB * part : 2 * XB * part + 2 * XB]
+                cc, cs = spec[:XB, :YB], spec[:XB, YB:]
+                sc, ss = spec[XB:, :YB], spec[XB:, YB:]
+                bpr, neg, bmr, bmi = cc - ss, cs + sc, cc + ss, sc - cs
                 hpr, hpi, hmr, hmi = (h_ref[2 * k + part, j] for j in range(4))
-                acc[0] = acc[0] + (hpr * bpr + hpi * bpi)
-                acc[1] = acc[1] + (hpr * bpi - hpi * bpr)
+                acc[0] = acc[0] + (hpr * bpr - hpi * neg)
+                acc[1] = acc[1] - (hpr * neg + hpi * bpr)
                 acc[2] = acc[2] + (hmr * bmr + hmi * bmi)
                 acc[3] = acc[3] + (hmr * bmi - hmi * bmr)
             for j in range(4):
@@ -318,7 +353,7 @@
     out = None
     for t in range(2):
         r_hi, r_lo = split(even_odd(*(tot[t, j] for j in range(4))))
-        u_hi, u_lo = split(weight * dot3(tb("x4_hi"), tb("x4_lo"), r_hi, r_lo))
+        u_hi, u_lo = split(weight * dot_stacked(tb("x4"), r_hi, r_lo))
         term = dot3(tb(f"by{t}_hi"), tb(f"by{t}_lo"), u_hi, u_lo, dot_nt)
         out = term if out is None else out + term
     g_ref[...] = out
@@ -341,57 +376,54 @@
 
 
 def later_kernel(
-    kern, last, w_ref, thr_ref, own_ref, a_ref, b_ref, f_in_ref, tgt_ref, h_ref, tb,
-    g_ref, f_ref, fld, inten, tot,
+    kern, last, w_ref, thr_ref, mine_ref, peer_ref, rim_ref, far_ref, f_in_ref, tgt_ref, h_ref,
+    tb, g_ref, f_ref, fld, inten, tot,
 ):
-    s_hi, s_lo = split(own_ref[...])
-    v, _, _ = sides(a_ref, b_ref, tb)
+    s_hi, s_lo = split(mine_ref[...] + peer_ref[...])
+    rims = rim_ref[...] + far_ref[...]
+    v, _, _ = sides(rims[:WIDE_PAD], rims[WIDE_PAD:], tb)
     v = v + dot3(tb("cx_own_hi"), tb("cx_own_lo"), s_hi, s_lo, dot_nt)
     to_spectrum(v, tb, f_ref, f_in_ref)
     gradient_body(kern, last, f_ref, tgt_ref, h_ref, w_ref, thr_ref, tb, g_ref, fld, inten, tot)
 
 
-def match(table_ref, own_ref, got_refs, tb):
+def match_kernel(n_got, table_ref, own_ref, *refs):
+    got_refs, (out_ref, *edge_refs) = refs[:n_got], refs[n_got:]
     device = lax.axis_index("tile")
-    own = own_ref[...]
-    flip = tb("flip")
+    other = []
+    for t in range(2):
+        rows = slice(CORE * t, CORE * t + CORE)
+        bit = lax.bitwise_xor(table_ref[t], 2 * device + t)
+        value = jnp.where(bit == 1, own_ref[CORE * (1 - t) : CORE * (2 - t)], own_ref[rows])
+        for b, got in enumerate(got_refs):
+            value = jnp.where(bit == 2 << b, got[rows], value)
+        other.append(value)
+    row = lax.broadcasted_iota(jnp.int32, (CORE, CORE), 0)
+    lane = lax.broadcasted_iota(jnp.int32, (CORE, CORE), 1)
+    flip = jnp.where(row + lane == CORE - 1, 1.0, 0.0).astype(bf16)
+    hi, lo = split(jnp.concatenate(other, axis=0))
+    turned = dot(hi, flip) + dot(lo, flip)
     tiles = []
     for t in range(2):
         rows = slice(CORE * t, CORE * t + CORE)
-        mine = own[rows]
-        bit = lax.bitwise_xor(table_ref[t], 2 * device + t)
-        other = jnp.where(bit == 1, own[CORE * (1 - t) : CORE * (1 - t) + CORE], mine)
-        for b, got in enumerate(got_refs):
-            other = jnp.where(bit == 2 << b, got[rows], other)
-        hi = other.astype(bf16)
-        rest = other - hi.astype(f32)
-        mid = rest.astype(bf16)
-        low = (rest - mid.astype(f32)).astype(bf16)
-        turned = dot(hi, flip) + (dot(mid, flip) + dot(low, flip))
-        tiles.append(0.5 * (mine + jnp.where(table_ref[2 + t] == 1, turned, other)))
-    return tiles
-
-
-def match_kernel(n_got, table_ref, own_ref, *refs):
-    got_refs, (tb, out_ref, a_ref, b_ref) = refs[:n_got], refs[n_got:]
-    matched = jnp.concatenate(match(table_ref, own_ref, got_refs, tb), axis=0)
+        value = jnp.where(table_ref[2 + t] == 1, turned[rows], other[t])
+        tiles.append(0.5 * (own_ref[rows] + value))
+    matched = jnp.concatenate(tiles, axis=0)
     out_ref[...] = matched
-    hi, lo = split(matched)
-    right, left = tb("edge0")[:WIDE_PAD], tb("edge2")[:WIDE_PAD]
-    send_edges(
-        dot_nt(right, hi) + dot_nt(right, lo), dot_nt(left, hi) + dot_nt(left, lo), a_ref, b_ref
-    )
-
-
-def final_kernel(n_got, n_moves, table_ref, own_ref, *refs):
-    got_refs, refs = refs[:n_got], refs[n_got:]
-    mask_ref, moves, (tb, mask_out, grad_out) = refs[0], refs[1 : 1 + n_moves], refs[1 + n_moves :]
-    for t, tile in enumerate(match(table_ref, own_ref, got_refs, tb)):
-        grad_out[t] = tile
+    if edge_refs:
+        send_edges(*edges_of(WIDE_PAD, matched), *edge_refs)
+
+
+def final_kernel(n_moves, mask_ref, *refs):
+    moves, (mask_out, grad_out) = refs[: 2 * n_moves], refs[2 * n_moves :]
+    for t in range(2):
+        rows = slice(CORE * t, CORE * t + CORE)
         now = mask_ref[t]
-        for move in moves:
-            now = now - STEP_RATE * move[CORE * t : CORE * t + CORE]
-        mask_out[t] = now - STEP_RATE * tile
+        for mine, peer in zip(moves[::2], moves[1::2]):
+            step = mine[rows] + peer[rows]
+            now = now - STEP_RATE * step
+        grad_out[t] = step
+        mask_out[t] = now
 
 
 def per_device(
@@ -407,41 +439,47 @@
     def swap_edges(send_a, send_b):
         return lax.ppermute(send_b, "tile", pairs_b), lax.ppermute(send_a, "tile", pairs_a)
 
-    def gather_sum(grad):
+    def depth_pair(x):
         bit = 1
-        while bit < n_depth:
-            pairs = [(i, i ^ bit) for i in range(n_depth)]
-            grad = grad + lax.ppermute(grad, "depth", pairs)
+        while True:
+            peer = lax.ppermute(x, "depth", [(i, i ^ bit) for i in range(n_depth)])
             bit *= 2
+            if bit >= n_depth:
+                return x, peer
+            x = x + peer
+
+    def from_partners(grad):
         bits = [1 << b for b in range(n_tile.bit_length() - 1)]
         got = [
             lax.ppermute(grad, "tile", [(i, i ^ bit) for i in range(n_tile)])
             for bit in reversed(bits)
         ]
-        return grad, got[::-1]
+        return got[::-1]
 
     mask_rows = mask_tiles.reshape(tiles_dev * core, core)
     target_rows = target_tiles.reshape(tiles_dev * core, core)
     strip = jax.ShapeDtypeStruct((tiles_dev * core, core), f32)
-    edge = jax.ShapeDtypeStruct((EDGE, tiles_dev * core), f32)
     side = jax.ShapeDtypeStruct((WIDE_PAD, tiles_dev * core), f32)
     freq = jax.ShapeDtypeStruct((2, 4, XB, YB), f32)
     goal = jax.ShapeDtypeStruct((ROWS, 2 * CORE), f32)
     tiles = jax.ShapeDtypeStruct((tiles_dev, core, core), f32)
     scratch = [
-        pltpu.VMEM((2, kern, 2 * ROWS, CORE), f32),
+        pltpu.VMEM((2, kern, ROWS, 2 * CORE), f32),
         pltpu.VMEM((2, ROWS, CORE), f32),
         pltpu.VMEM((2, 4, XB, YB), f32),
     ]
 
-    send_a, send_b = call(edges_kernel, "edge", [mask_rows, target_rows], [edge, edge])
+    edge = jax.ShapeDtypeStruct((EDGE, tiles_dev * core), f32)
+    send_a, send_b = call(
+        edges_kernel, None, [mask_rows, target_rows], [edge, edge], flops=3 * 10**9
+    )
     from_b, from_a = swap_edges(send_a, send_b)
     table = jnp.concatenate([partner_table, mirror_flags])
-    spectra = call(
+    (spectra,) = call(
         functools.partial(spectra_kernel, kern),
         "spec",
-        [kernels],
-        jax.ShapeDtypeStruct((2 * kern, 4, XB, YB), f32),
+        [kernels.transpose(0, 2, 3, 1, 4)],
+        [jax.ShapeDtypeStruct((2 * kern, 4, XB, YB), f32)],
         [pltpu.VMEM((32 * 2 * kern, 128), f32)],
         flops=3 * 10**9,
         nbytes=4 * 10**6,
@@ -453,37 +491,37 @@
         [strip, freq, goal],
         scratch,
         smem=(0, 1),
+        flops=10**10,
     )
     moves = []
-    for step in range(1, STEPS):
-        total, got = gather_sum(grad)
-        move, send_a, send_b = call(
+    for step in range(1, STEPS + 1):
+        got = from_partners(grad)
+        outs = call(
             functools.partial(match_kernel, len(got)),
-            "edge",
-            [table, total, *got],
-            [strip, side, side],
+            None,
+            [table, grad, *got],
+            [strip, side, side] if step < STEPS else [strip],
             smem=(0,),
         )
-        from_b, from_a = swap_edges(send_a, send_b)
-        moves.append(move)
-        grad, freq_now = call(
+        if step == STEPS:
+            moves += depth_pair(outs[0])
+            break
+        from_b, from_a = swap_edges(*outs[1:])
+        moves += depth_pair(outs[0])
+        rims = depth_pair(jnp.concatenate([from_a, from_b]))
+        kept = step + 1 < STEPS
+        grad, *rest = call(
             functools.partial(later_kernel, kern, n_tile - 1),
             "grad",
-            [socs_weights, thresholds, move, from_a, from_b, freq_now, goals, spectra],
-            [strip, freq],
-            scratch,
+            [socs_weights, thresholds, *moves[-2:], *rims, freq_now, goals, spectra],
+            [strip, freq] if kept else [strip],
+            scratch if kept else [pltpu.VMEM(freq.shape, f32)] + scratch,
             smem=(0, 1),
+            flops=10**10,
         )
-    total, got = gather_sum(grad)
-    return tuple(
-        call(
-            functools.partial(final_kernel, len(got), len(moves)),
-            "edge",
-            [table, total, *got, mask_tiles, *moves],
-            [tiles, tiles],
-            smem=(0,),
-        )
-    )
+        freq_now = rest[0] if kept else None
+    final = functools.partial(final_kernel, STEPS)
+    return tuple(call(final, None, [mask_tiles, *moves], [tiles, tiles]))
 
 
 def solution(mesh):

time: 76.8 us -> 66.4 us (0.86)
  Pallas kernels: 30.4 us -> 23.3 us
  local copies, waits for them, and re-layouts: 4.79 us -> 1.86 us
    pallas_call x6 -> x7, Pallas kernels: 30.4 us -> 23.3 us  [call(): pl.pallas_call(wrapped, out_shape=out_shape, in_specs=[sm if i in smem el...]
    unnamed x23 -> x21, local copies, waits for them, and re-layouts: 4.79 us -> 1.85 us
    ppermute x10 -> x11, waiting for transfers between devices: 16.2 us -> 17 us  [the longest x8 9.58 us: from_partners(): lax.ppermute(grad, 'tile', [(i, i ^ bit) for i in range(n_tile)])]
    ppermute x10 -> x11, starting transfers between devices: 21.2 us -> 20.4 us  [the longest x8 16.6 us: from_partners(): lax.ppermute(grad, 'tile', [(i, i ^ bit) for i in range(n_tile)])]
  transfers between devices with their start and end apart: 14 -> 15, of which waited for: 9 -> 7; matrix products, arithmetic and copies ran while one was open for 1% -> 0% of each run, Pallas kernels for 2% -> 2%
where the time goes in v4:
time: 66.4 us; the launch traced here: 66.2 us
  Pallas kernels  23.3 us (35%)
  starting transfers between devices  22.4 us (34%)
  waiting for transfers between devices  17.1 us (26%)
  local copies, waits for them, and re-layouts  1.86 us (3%)
  between operations  1.51 us (2%)
    pallas_call x7, Pallas kernels, call(): pl.pallas_call(wrapped, out_shape=out_shape, in_specs=[sm if i in smem el...  23.3 us
    ppermute x8, starting transfers between devices, from_partners(): lax.ppermute(grad, 'tile', [(i, i ^ bit) for i in range(n_tile)])  16.6 us
    ppermute x8, waiting for transfers between devices, from_partners(): lax.ppermute(grad, 'tile', [(i, i ^ bit) for i in range(n_tile)])  9.58 us
    ppermute x3, waiting for transfers between devices, depth_pair(): peer = lax.ppermute(x, 'depth', [(i, i ^ bit) for i in range(n_depth)])  7.46 us
    ppermute x3, starting transfers between devices, depth_pair(): peer = lax.ppermute(x, 'depth', [(i, i ^ bit) for i in range(n_depth)])  3.75 us
    unnamed x21, local copies, waits for them, and re-layouts  1.85 us
    ppermute x2, starting transfers between devices, swap_edges(): lax.ppermute(send_b, 'tile', pairs_b)  1.5 us
  transfers between devices with their start and end apart: 15, of which 7 were waited for; matrix products, arithmetic and copies ran while one was open for 0% of the time, Pallas kernels for 2%

profile of v4, /device:TPU:0, one launch (start us, length us, event | category | flops | bytes accessed | tf_op | source)
XLA Modules:
  0.0 66.2 jit_solution(14702754434611977554)
XLA Ops:
  0.6 0.0 copy-start
  0.6 0.9 %copy-done = f32[2,128,128]{2,1,0:T(8,128)S(1)} copy-done((f32[2,128,128]{2,1,0:T(8,128)S(1)}, f32[2,128,128]{2,1,0:T(8,128)}, u32[]{:S(2)}) %copy-start) | copy-done | bytes 131096
  1.5 0.9 %copy-done.3 = s32[2,128,128]{2,1,0:T(8,128)S(1)} copy-done((s32[2,128,128]{2,1,0:T(8,128)S(1)}, s32[2,128,128]{2,1,0:T(8,128)}, u32[]{:S(2)}) %copy-start.3) | copy-done | bytes 131096
  2.4 0.2 shard_map.113
  2.7 0.5 collective-permute-start
  3.2 0.7 collective-permute-start.1
  3.9 0.0 copy-done.2
  3.9 0.0 copy-start.1
  3.9 0.0 copy-start.4
  3.9 0.0 copy-start.5
  3.9 0.0 copy-start.6
  3.9 1.4 %shard_map.114.refs_6_.refs_8_ = f32[12,4,96,128]{3,2,1,0:T(8,128)S(1)} custom-call(f32[2,6,25,1,25]{4,3,2,1,0:T(1,128)S(1)} %bitcast.5, bf16[1408,256]{1,0:T(8,128)(2,1)S(1)} %copy-done.7), custom_call_target="tpu_custom_call" | custom-call | flops 3000000000 | bytes 4000000 | tf_op jit(solution)/shard_map/pallas_call | solution.py:204
  6.0 0.0 copy-start.8
  6.0 0.0 copy-start.9
  6.0 0.0 collective-permute-done.refs_4_
  6.0 0.0 collective-permute-done.1.refs_5_
  6.1 9.8 %shard_map.115 = (f32[256,128]{1,0:T(8,128)S(1)}, f32[2,4,96,128]{3,2,1,0:T(8,128)S(1)}, f32[160,256]{1,0:T(8,128)S(1)}) custom-call(f32[1,6]{1,0:T(1,128)S(1)} %copy-done.5, f32[1]{0:T(128)S(6)} %copy.13.refs_1_, f32[256,128]{1,0:T(8,128)S(1)} %bitcast.4, s32[256,128]{1,0:T(8,128)S(1)} %bitcast.7, f32[48,256]{1,0:T(8,128)S(1)} %collective-permute-done.refs_4_, ...), custom_call_target="tpu_custom_call" | custom-call | flops 10000000000 | tf_op jit(solution)/shard_map/pallas_call | solution.py:204
  15.9 7.2 %collective-permute-start.5 = (f32[256,128]{1,0:T(8,128)S(1)}, f32[256,128]{1,0:T(8,128)S(1)}, u32[]{:S(2)}, u32[]{:S(2)}) collective-permute-start(f32[256,128]{1,0:T(8,128)S(1)} %get-tuple-element.12.refs_1_), channel_id=1, source_target_pairs={{0,16},{2,18},{4,20},{6,22},{8,24},{10,26},{12,28},{14,30},{16,0},... | collective-permute-start | bytes 393224 | tf_op jit(solution)/shard_map/ppermute | solution.py:454
  23.1 1.6 %collective-permute-start.4 = (f32[256,128]{1,0:T(8,128)S(1)}, f32[256,128]{1,0:T(8,128)S(1)}, u32[]{:S(2)}, u32[]{:S(2)}) collective-permute-start(f32[256,128]{1,0:T(8,128)S(1)} %get-tuple-element.12.refs_1_), channel_id=1, source_target_pairs={{0,8},{2,10},{4,12},{6,14},{8,0},{10,2},{12,4},{14,6},{16,24},{18,... | collective-permute-start | bytes 393224 | tf_op jit(solution)/shard_map/ppermute | solution.py:454
  24.6 0.5 collective-permute-start.3
  25.1 0.0 collective-permute-start.2
  25.1 0.1 pad_add_fusion.refs_0_
  25.2 4.4 %collective-permute-done.5.refs_5_ = f32[256,128]{1,0:T(8,128)S(1)} collective-permute-done((f32[256,128]{1,0:T(8,128)S(1)}, f32[256,128]{1,0:T(8,128)S(1)}, u32[]{:S(2)}, u32[]{:S(2)}) %collective-permute-start.5) | collective-permute-done | bytes 131104 | tf_op jit(solution)/shard_map/ppermute | solution.py:454
  29.6 0.2 collective-permute-done.4.refs_4_
  29.8 0.0 collective-permute-done.3.refs_3_
  29.8 0.0 collective-permute-done.2.refs_2_
  29.8 0.9 %shard_map.116 = (f32[256,128]{1,0:T(8,128)S(1)}, f32[32,256]{1,0:T(8,128)S(1)}, f32[32,256]{1,0:T(8,128)S(1)}) custom-call(s32[4]{0:T(128)S(1)} %pad_add_fusion.refs_0_, f32[256,128]{1,0:T(8,128)S(1)} %get-tuple-element.12.refs_1_, f32[256,128]{1,0:T(8,128)S(1)} %collective-permute-done.2.refs_2_, f32[256,128]{1,0:T(8,128)S(1)} %collective-permute-done.3.refs_3_, ...), custom_call_target="tpu_custom_call" | custom-call | tf_op jit(solution)/shard_map/pallas_call | solution.py:204
  30.7 0.0 collective-permute-start.7
  30.8 0.8 %collective-permute-start.8 = (f32[32,256]{1,0:T(8,128)S(1)}, f32[32,256]{1,0:T(8,128)S(1)}, u32[]{:S(2)}, u32[]{:S(2)}) collective-permute-start(f32[32,256]{1,0:T(8,128)S(1)} %get-tuple-element.15), channel_id=1, source_target_pairs={{2,4},{4,2},{6,8},{8,6},{10,12},{12,10},{14,16},{16,14},{18,20},{2... | collective-permute-start | bytes 98312 | tf_op jit(solution)/shard_map/ppermute | solution.py:440
  31.6 1.6 %collective-permute-start.6 = (f32[256,128]{1,0:T(8,128)S(1)}, f32[256,128]{1,0:T(8,128)S(1)}, u32[]{:S(2)}, u32[]{:S(2)}) collective-permute-start(f32[256,128]{1,0:T(8,128)S(1)} %get-tuple-element.13.refs_2_.refs_1_), channel_id=1, source_target_pairs={{0,1},{1,0},{2,3},{3,2},{4,5},{5,4},{6,7},{7,6},{8,9},{9,8},{10,11... | collective-permute-start | bytes 393224 | tf_op jit(solution)/shard_map/ppermute | solution.py:445
  33.2 0.0 collective-permute-done.7
  33.2 0.0 collective-permute-done.8
  33.2 0.6 collective-permute-start.9
  33.8 4.0 %collective-permute-done.9.refs_5_ = f32[64,256]{1,0:T(8,128)S(1)} collective-permute-done((f32[64,256]{1,0:T(8,128)S(1)}, f32[64,256]{1,0:T(8,128)S(1)}, u32[]{:S(2)}, u32[]{:S(2)}) %collective-permute-start.9) | collective-permute-done | bytes 65568 | tf_op jit(solution)/shard_map/ppermute | solution.py:445
  37.8 0.0 collective-permute-done.6.refs_3_.refs_2_
  37.8 9.6 %shard_map.117.refs_1_ = f32[256,128]{1,0:T(8,128)S(1)} custom-call(f32[1,6]{1,0:T(1,128)S(1)} %copy-done.5, f32[1]{0:T(128)S(6)} %copy.13.refs_1_, f32[256,128]{1,0:T(8,128)S(1)} %get-tuple-element.13.refs_2_.refs_1_, f32[256,128]{1,0:T(8,128)S(1)} %collective-permute-done.6.refs_3_.refs_2_, f32[64,256]{1,0:T(8,128)S(1)} %constant_dynamic-update-slice_fusion.refs_4_, ...), custom_call_target="tpu_custom_call" | custom-call | flops 10000000000 | tf_op jit(solution)/shard_map/pallas_call | solution.py:204
  47.4 5.2 %collective-permute-start.13 = (f32[256,128]{1,0:T(8,128)S(1)}, f32[256,128]{1,0:T(8,128)S(1)}, u32[]{:S(2)}, u32[]{:S(2)}) collective-permute-start(f32[256,128]{1,0:T(8,128)S(1)} %shard_map.117.refs_1_), channel_id=1, source_target_pairs={{0,16},{2,18},{4,20},{6,22},{8,24},{10,26},{12,28},{14,30},{16,0},... | collective-permute-start | bytes 393224 | tf_op jit(solution)/shard_map/ppermute | solution.py:454
  52.5 2.2 %collective-permute-start.12 = (f32[256,128]{1,0:T(8,128)S(1)}, f32[256,128]{1,0:T(8,128)S(1)}, u32[]{:S(2)}, u32[]{:S(2)}) collective-permute-start(f32[256,128]{1,0:T(8,128)S(1)} %shard_map.117.refs_1_), channel_id=1, source_target_pairs={{0,8},{2,10},{4,12},{6,14},{8,0},{10,2},{12,4},{14,6},{16,24},{18,... | collective-permute-start | bytes 393224 | tf_op jit(solution)/shard_map/ppermute | solution.py:454
  54.7 0.0 collective-permute-start.11
  54.7 0.0 collective-permute-start.10
  54.7 3.3 %collective-permute-done.13.refs_5_ = f32[256,128]{1,0:T(8,128)S(1)} collective-permute-done((f32[256,128]{1,0:T(8,128)S(1)}, f32[256,128]{1,0:T(8,128)S(1)}, u32[]{:S(2)}, u32[]{:S(2)}) %collective-permute-start.13) | collective-permute-done | bytes 131104 | tf_op jit(solution)/shard_map/ppermute | solution.py:454
  58.0 0.7 %collective-permute-done.12.refs_4_ = f32[256,128]{1,0:T(8,128)S(1)} collective-permute-done((f32[256,128]{1,0:T(8,128)S(1)}, f32[256,128]{1,0:T(8,128)S(1)}, u32[]{:S(2)}, u32[]{:S(2)}) %collective-permute-start.12) | collective-permute-done | bytes 131104 | tf_op jit(solution)/shard_map/ppermute | solution.py:454
  58.7 1.0 %collective-permute-done.11.refs_3_ = f32[256,128]{1,0:T(8,128)S(1)} collective-permute-done((f32[256,128]{1,0:T(8,128)S(1)}, f32[256,128]{1,0:T(8,128)S(1)}, u32[]{:S(2)}, u32[]{:S(2)}) %collective-permute-start.11) | collective-permute-done | bytes 131104 | tf_op jit(solution)/shard_map/ppermute | solution.py:454
  59.7 0.0 collective-permute-done.10.refs_2_
  59.7 0.7 %shard_map.118.refs_3_ = f32[256,128]{1,0:T(8,128)S(1)} custom-call(s32[4]{0:T(128)S(1)} %pad_add_fusion.refs_0_, f32[256,128]{1,0:T(8,128)S(1)} %shard_map.117.refs_1_, f32[256,128]{1,0:T(8,128)S(1)} %collective-permute-done.10.refs_2_, f32[256,128]{1,0:T(8,128)S(1)} %collective-permute-done.11.refs_3_, f32[256,128]{1,0:T(8,128)S(1)} %collective-permute-done.12.refs_4_, ...), custom_call_target="tpu_custom_call" | custom-call | tf_op jit(solution)/shard_map/pallas_call | solution.py:204
  60.4 1.6 %collective-permute-start.14 = (f32[256,128]{1,0:T(8,128)S(1)}, f32[256,128]{1,0:T(8,128)S(1)}, u32[]{:S(2)}, u32[]{:S(2)}) collective-permute-start(f32[256,128]{1,0:T(8,128)S(1)} %shard_map.118.refs_3_), channel_id=1, source_target_pairs={{0,1},{1,0},{2,3},{3,2},{4,5},{5,4},{6,7},{7,6},{8,9},{9,8},{10,11... | collective-permute-start | bytes 393224 | tf_op jit(solution)/shard_map/ppermute | solution.py:445
  62.0 3.4 %collective-permute-done.14.refs_4_ = f32[256,128]{1,0:T(8,128)S(1)} collective-permute-done((f32[256,128]{1,0:T(8,128)S(1)}, f32[256,128]{1,0:T(8,128)S(1)}, u32[]{:S(2)}, u32[]{:S(2)}) %collective-permute-start.14) | collective-permute-done | bytes 131104 | tf_op jit(solution)/shard_map/ppermute | solution.py:445
  65.5 0.7 %shard_map.119 = (f32[2,128,128]{2,1,0:T(8,128)}, f32[2,128,128]{2,1,0:T(8,128)}) custom-call(f32[2,128,128]{2,1,0:T(8,128)S(1)} %copy-done.1, f32[256,128]{1,0:T(8,128)S(1)} %get-tuple-element.13.refs_2_.refs_1_, f32[256,128]{1,0:T(8,128)S(1)} %collective-permute-done.6.refs_3_.refs_2_, f32[256,128]{1,0:T(8,128)S(1)} %shard_map.118.refs_3_, ...), custom_call_target="tpu_custom_call" | custom-call | tf_op jit(solution)/shard_map/pallas_call | solution.py:204
  (12 shorter events, 0.0 us)
Async XLA Ops:
  0.6 0.9 %copy-start = (f32[2,128,128]{2,1,0:T(8,128)S(1)}, f32[2,128,128]{2,1,0:T(8,128)}, u32[]{:S(2)}) copy-start(f32[2,128,128]{2,1,0:T(8,128)} %refs_0_.5) | copy-start | bytes 393220
  1.5 0.9 %copy-start.3 = (s32[2,128,128]{2,1,0:T(8,128)S(1)}, s32[2,128,128]{2,1,0:T(8,128)}, u32[]{:S(2)}) copy-start(s32[2,128,128]{2,1,0:T(8,128)} %param.11) | copy-start | bytes 393220
  2.4 1.4 %copy-start.2 = (f32[2,1,6,25,25]{4,1,3,2,0:T(1,128)S(1)}, f32[2,1,6,25,25]{4,1,3,2,0:T(1,128)}, u32[]{:S(2)}) copy-start(f32[2,1,6,25,25]{4,1,3,2,0:T(1,128)} %param.12) | copy-start | bytes 90004
  2.4 1.4 %copy-start.7 = (bf16[1408,256]{1,0:T(8,128)(2,1)S(1)}, bf16[1408,256]{1,0:T(8,128)(2,1)}, u32[]{:S(2)}) copy-start(bf16[1408,256]{1,0:T(8,128)(2,1)} %constant.4.clone.refs_1_) | copy-start | bytes 2162692
  2.7 3.4 %collective-permute-start = (f32[48,256]{1,0:T(8,128)S(1)}, f32[48,256]{1,0:T(8,128)S(1)}, u32[]{:S(2)}, u32[]{:S(2)}) collective-permute-start(f32[48,256]{1,0:T(8,128)S(1)} %get-tuple-element.10), channel_id=1, source_target_pairs={{0,2},{2,0},{4,6},{6,4},{8,10},{10,8},{12,14},{14,12},{16,18},{18,... | collective-permute-start | bytes 147464 | tf_op jit(solution)/shard_map/ppermute | solution.py:440
  3.2 2.8 %collective-permute-start.1 = (f32[48,256]{1,0:T(8,128)S(1)}, f32[48,256]{1,0:T(8,128)S(1)}, u32[]{:S(2)}, u32[]{:S(2)}) collective-permute-start(f32[48,256]{1,0:T(8,128)S(1)} %get-tuple-element.11), channel_id=1, source_target_pairs={{2,4},{4,2},{6,8},{8,6},{10,12},{12,10},{14,16},{16,14},{18,20},{2... | collective-permute-start | bytes 147464 | tf_op jit(solution)/shard_map/ppermute | solution.py:440
  3.9 2.2 %copy-start.1 = (f32[2,128,128]{2,1,0:T(8,128)S(1)}, f32[2,128,128]{2,1,0:T(8,128)}, u32[]{:S(2)}) copy-start(f32[2,128,128]{2,1,0:T(8,128)} %refs_0_.5) | copy-start | bytes 393220
  3.9 2.2 %copy-start.4 = (s32[2,128,128]{2,1,0:T(8,128)S(1)}, s32[2,128,128]{2,1,0:T(8,128)}, u32[]{:S(2)}) copy-start(s32[2,128,128]{2,1,0:T(8,128)} %param.11) | copy-start | bytes 393220
  3.9 2.2 %copy-start.5 = (f32[1,6]{1,0:T(1,128)S(1)}, f32[1,6]{1,0:T(1,128)}, u32[]{:S(2)}) copy-start(f32[1,6]{1,0:T(1,128)} %refs_0_.4) | copy-start | bytes 76
  3.9 2.2 %copy-start.6 = (bf16[3712,256]{1,0:T(8,128)(2,1)S(1)}, bf16[3712,256]{1,0:T(8,128)(2,1)}, u32[]{:S(2)}) copy-start(bf16[3712,256]{1,0:T(8,128)(2,1)} %constant.5.clone.refs_7_.refs_9_) | copy-start | bytes 5701636
  6.0 19.1 %copy-start.8 = (s32[2]{0:T(128)S(1)}, s32[2]{0:T(128)}, u32[]{:S(2)}) copy-start(s32[2]{0:T(128)} %param.16) | copy-start | bytes 28
  6.0 19.1 %copy-start.9 = (s32[2]{0:T(128)S(1)}, s32[2]{0:T(128)}, u32[]{:S(2)}) copy-start(s32[2]{0:T(128)} %param.15) | copy-start | bytes 28
  15.9 13.8 %collective-permute-start.5 = (f32[256,128]{1,0:T(8,128)S(1)}, f32[256,128]{1,0:T(8,128)S(1)}, u32[]{:S(2)}, u32[]{:S(2)}) collective-permute-start(f32[256,128]{1,0:T(8,128)S(1)} %get-tuple-element.12.refs_1_), channel_id=1, source_target_pairs={{0,16},{2,18},{4,20},{6,22},{8,24},{10,26},{12,28},{14,30},{16,0},... | collective-permute-start | bytes 393224 | tf_op jit(solution)/shard_map/ppermute | solution.py:454
  23.1 6.8 %collective-permute-start.4 = (f32[256,128]{1,0:T(8,128)S(1)}, f32[256,128]{1,0:T(8,128)S(1)}, u32[]{:S(2)}, u32[]{:S(2)}) collective-permute-start(f32[256,128]{1,0:T(8,128)S(1)} %get-tuple-element.12.refs_1_), channel_id=1, source_target_pairs={{0,8},{2,10},{4,12},{6,14},{8,0},{10,2},{12,4},{14,6},{16,24},{18,... | collective-permute-start | bytes 393224 | tf_op jit(solution)/shard_map/ppermute | solution.py:454
  24.6 5.2 %collective-permute-start.3 = (f32[256,128]{1,0:T(8,128)S(1)}, f32[256,128]{1,0:T(8,128)S(1)}, u32[]{:S(2)}, u32[]{:S(2)}) collective-permute-start(f32[256,128]{1,0:T(8,128)S(1)} %get-tuple-element.12.refs_1_), channel_id=1, source_target_pairs={{0,4},{2,6},{4,0},{6,2},{8,12},{10,14},{12,8},{14,10},{16,20},{18,... | collective-permute-start | bytes 393224 | tf_op jit(solution)/shard_map/ppermute | solution.py:454
  25.1 4.7 %collective-permute-start.2 = (f32[256,128]{1,0:T(8,128)S(1)}, f32[256,128]{1,0:T(8,128)S(1)}, u32[]{:S(2)}, u32[]{:S(2)}) collective-permute-start(f32[256,128]{1,0:T(8,128)S(1)} %get-tuple-element.12.refs_1_), channel_id=1, source_target_pairs={{0,2},{2,0},{4,6},{6,4},{8,10},{10,8},{12,14},{14,12},{16,18},{18,... | collective-permute-start | bytes 393224 | tf_op jit(solution)/shard_map/ppermute | solution.py:454
  30.7 2.5 %collective-permute-start.7 = (f32[32,256]{1,0:T(8,128)S(1)}, f32[32,256]{1,0:T(8,128)S(1)}, u32[]{:S(2)}, u32[]{:S(2)}) collective-permute-start(f32[32,256]{1,0:T(8,128)S(1)} %get-tuple-element.14), channel_id=1, source_target_pairs={{0,2},{2,0},{4,6},{6,4},{8,10},{10,8},{12,14},{14,12},{16,18},{18,... | collective-permute-start | bytes 98312 | tf_op jit(solution)/shard_map/ppermute | solution.py:440
  30.8 2.5 %collective-permute-start.8 = (f32[32,256]{1,0:T(8,128)S(1)}, f32[32,256]{1,0:T(8,128)S(1)}, u32[]{:S(2)}, u32[]{:S(2)}) collective-permute-start(f32[32,256]{1,0:T(8,128)S(1)} %get-tuple-element.15), channel_id=1, source_target_pairs={{2,4},{4,2},{6,8},{8,6},{10,12},{12,10},{14,16},{16,14},{18,20},{2... | collective-permute-start | bytes 98312 | tf_op jit(solution)/shard_map/ppermute | solution.py:440
  31.6 6.2 %collective-permute-start.6 = (f32[256,128]{1,0:T(8,128)S(1)}, f32[256,128]{1,0:T(8,128)S(1)}, u32[]{:S(2)}, u32[]{:S(2)}) collective-permute-start(f32[256,128]{1,0:T(8,128)S(1)} %get-tuple-element.13.refs_2_.refs_1_), channel_id=1, source_target_pairs={{0,1},{1,0},{2,3},{3,2},{4,5},{5,4},{6,7},{7,6},{8,9},{9,8},{10,11... | collective-permute-start | bytes 393224 | tf_op jit(solution)/shard_map/ppermute | solution.py:445
  33.2 4.6 %collective-permute-start.9 = (f32[64,256]{1,0:T(8,128)S(1)}, f32[64,256]{1,0:T(8,128)S(1)}, u32[]{:S(2)}, u32[]{:S(2)}) collective-permute-start(f32[64,256]{1,0:T(8,128)S(1)} %constant_dynamic-update-slice_fusion.refs_4_), channel_id=1, source_target_pairs={{0,1},{1,0},{2,3},{3,2},{4,5},{5,4},{6,7},{7,6},{8,9},{9,8},{10,11... | collective-permute-start | bytes 196616 | tf_op jit(solution)/shard_map/ppermute | solution.py:445
  47.4 10.6 %collective-permute-start.13 = (f32[256,128]{1,0:T(8,128)S(1)}, f32[256,128]{1,0:T(8,128)S(1)}, u32[]{:S(2)}, u32[]{:S(2)}) collective-permute-start(f32[256,128]{1,0:T(8,128)S(1)} %shard_map.117.refs_1_), channel_id=1, source_target_pairs={{0,16},{2,18},{4,20},{6,22},{8,24},{10,26},{12,28},{14,30},{16,0},... | collective-permute-start | bytes 393224 | tf_op jit(solution)/shard_map/ppermute | solution.py:454
  52.5 6.2 %collective-permute-start.12 = (f32[256,128]{1,0:T(8,128)S(1)}, f32[256,128]{1,0:T(8,128)S(1)}, u32[]{:S(2)}, u32[]{:S(2)}) collective-permute-start(f32[256,128]{1,0:T(8,128)S(1)} %shard_map.117.refs_1_), channel_id=1, source_target_pairs={{0,8},{2,10},{4,12},{6,14},{8,0},{10,2},{12,4},{14,6},{16,24},{18,... | collective-permute-start | bytes 393224 | tf_op jit(solution)/shard_map/ppermute | solution.py:454
  54.7 5.0 %collective-permute-start.11 = (f32[256,128]{1,0:T(8,128)S(1)}, f32[256,128]{1,0:T(8,128)S(1)}, u32[]{:S(2)}, u32[]{:S(2)}) collective-permute-start(f32[256,128]{1,0:T(8,128)S(1)} %shard_map.117.refs_1_), channel_id=1, source_target_pairs={{0,4},{2,6},{4,0},{6,2},{8,12},{10,14},{12,8},{14,10},{16,20},{18,... | collective-permute-start | bytes 393224 | tf_op jit(solution)/shard_map/ppermute | solution.py:454
  54.7 5.0 %collective-permute-start.10 = (f32[256,128]{1,0:T(8,128)S(1)}, f32[256,128]{1,0:T(8,128)S(1)}, u32[]{:S(2)}, u32[]{:S(2)}) collective-permute-start(f32[256,128]{1,0:T(8,128)S(1)} %shard_map.117.refs_1_), channel_id=1, source_target_pairs={{0,2},{2,0},{4,6},{6,4},{8,10},{10,8},{12,14},{14,12},{16,18},{18,... | collective-permute-start | bytes 393224 | tf_op jit(solution)/shard_map/ppermute | solution.py:454
  60.4 5.0 %collective-permute-start.14 = (f32[256,128]{1,0:T(8,128)S(1)}, f32[256,128]{1,0:T(8,128)S(1)}, u32[]{:S(2)}, u32[]{:S(2)}) collective-permute-start(f32[256,128]{1,0:T(8,128)S(1)} %shard_map.118.refs_3_), channel_id=1, source_target_pairs={{0,1},{1,0},{2,3},{3,2},{4,5},{5,4},{6,7},{7,6},{8,9},{9,8},{10,11... | collective-permute-start | bytes 393224 | tf_op jit(solution)/shard_map/ppermute | solution.py:445

commit v5 on v4

--- a/solution.py
+++ b/solution.py
@@ -262,9 +262,8 @@
             h_ref[c, j] = comp
 
 
-def sides(a_ref, b_ref, tb):
+def sides(from_a, from_b, tb):
     even = is_even()
-    from_a, from_b = a_ref[...], b_ref[...]
     l_hi, l_lo = split(jnp.where(even, from_b, from_a))
     r_hi, r_lo = split(jnp.where(even, from_a, from_b))
     height = l_hi.shape[0]
@@ -284,27 +283,46 @@
             f_ref[t, j] = comp if base is None else base[t, j] - STEP_RATE * comp
 
 
-def gradient_body(kern, last, f_ref, tgt_ref, h_ref, w_ref, thr_ref, tb, g_ref, fld, inten, tot):
-    inten[...] = jnp.zeros_like(inten)
-
-    @pl.loop(0, kern, unroll=True)
-    def _(k):
-        for t in range(2):
-            parts = []
+def gradient_body(kern, last, f_ref, tgt_ref, h_ref, w_ref, thr_ref, tb, g_ref, work):
+    fld, inten, tot, a_hi, a_lo, b_hi, b_lo = work
+    chains = [(t, k) for t in range(2) for k in range(kern)]
+    rounds = range(len(chains) + 2)
+
+    def at(i):
+        return chains[i] if 0 <= i < len(chains) else None
+
+    for i in rounds:
+        new, mid, old = at(i), at(i - 1), at(i - 2)
+        if mid:
+            slot = (i - 1) % 2
+            z_one = dot(a_hi[slot], tb("y2"))
+            z_two = dot(a_lo[slot], tb("y2", 0))
+        if new:
+            t, k = new
+            slot = i % 2
             for part in range(2):
                 hpr, hpi, hmr, hmi = (h_ref[2 * k + part, j] for j in range(4))
                 fpr, fpi, fmr, fmi = (f_ref[t, j] for j in range(4))
                 pr, pi = hpr * fpr - hpi * fpi, hpr * fpi + hpi * fpr
                 mr, mi = hmr * fmr - hmi * fmi, hmr * fmi + hmi * fmr
-                parts.append(even_odd(pr, pi, mr, mi))
-            p_hi, p_lo = split(jnp.concatenate(parts, axis=0))
-            z = dot(p_hi, tb("y2"))
-            z = z[:, :CORE] + (z[:, CORE:] + dot(p_lo, tb("y2", 0)))
-            z_hi, z_lo = split(jnp.concatenate([z[: 2 * XB], z[2 * XB :]], axis=1))
-            field = dot_stacked(tb("x2"), z_hi, z_lo)
+                p_hi, p_lo = split(even_odd(pr, pi, mr, mi))
+                rows = slice(2 * XB * part, 2 * XB * part + 2 * XB)
+                a_hi[slot, rows] = p_hi
+                a_lo[slot, rows] = p_lo
+        if old:
+            slot = (i - 2) % 2
+            field = dot_stacked(tb("x2"), b_hi[slot], b_lo[slot])
+            t, k = old
             fld[t, k] = field
             re, im = field[:, :CORE], field[:, CORE:]
-            inten[t] += w_ref[0, k] * (re * re + im * im)
+            power = w_ref[0, k] * (re * re + im * im)
+            inten[t] = power if k == 0 else inten[t] + power
+        if mid:
+            slot = (i - 1) % 2
+            z = z_one[:, :CORE] + (z_one[:, CORE:] + z_two)
+            z_hi, z_lo = split(jnp.concatenate([z[: 2 * XB], z[2 * XB :]], axis=1))
+            b_hi[slot] = z_hi
+            b_lo[slot] = z_lo
 
     tile = lax.axis_index("tile")
     first = jnp.where(tile == 0, WIDE, HALO) - ROW0
@@ -316,23 +334,27 @@
         target = tgt_ref[:, CORE * t : CORE * t + CORE]
         slope = 2.0 * (resist - target) * STEEPNESS * resist * (1.0 - resist)
         inten[t] = jnp.where(inside, 2.0 * slope, 0.0)
-    tot[...] = jnp.zeros_like(tot)
-
-    @pl.loop(0, kern, unroll=True)
-    def _(k):
-        for t in range(2):
+    for i in rounds:
+        new, mid, old = at(i), at(i - 1), at(i - 2)
+        if mid:
+            slot = (i - 1) % 2
+            w_now = dot_stacked(tb("x3"), b_hi[slot, :ROWS], b_lo[slot, :ROWS])
+        if new:
+            t, k = new
+            slot = i % 2
             scaled = w_ref[0, k] * inten[t]
             field = fld[t, k]
             r_hi, r_lo = split(
                 jnp.concatenate([scaled * field[:, :CORE], scaled * field[:, CORE:]], axis=1)
             )
-            w_hi, w_lo = split(dot_stacked(tb("x3"), r_hi, r_lo))
-            his = [w_hi[:, :CORE], w_hi[:, CORE:]]
-            los = [w_lo[:, :CORE], w_lo[:, CORE:]]
-            both = [jnp.concatenate([his[p], los[p]], axis=1) for p in range(2)]
-            specs = dot(jnp.concatenate(both, axis=0), tb("y3_dup"))
-            specs = specs + dot(jnp.concatenate(his, axis=0), tb("y3_lo"))
-            acc = [tot[t, j] for j in range(4)]
+            b_hi[slot, :ROWS] = r_hi
+            b_lo[slot, :ROWS] = r_lo
+        if old:
+            slot = (i - 2) % 2
+            t, k = old
+            cat = a_hi[slot]
+            specs = dot(cat, tb("y3_dup")) + dot(cat[:, :CORE], tb("y3_lo"))
+            acc = [0.0] * 4 if k == 0 else [tot[t, j] for j in range(4)]
             for part in range(2):
                 spec = specs[2 * XB * part : 2 * XB * part + 2 * XB]
                 cc, cs = spec[:XB, :YB], spec[:XB, YB:]
@@ -345,6 +367,14 @@
                 acc[3] = acc[3] + (hmr * bmi - hmi * bmr)
             for j in range(4):
                 tot[t, j] = acc[j]
+        if mid:
+            slot = (i - 1) % 2
+            w_hi, w_lo = split(w_now)
+            for part in range(2):
+                rows = slice(2 * XB * part, 2 * XB * part + 2 * XB)
+                lanes = slice(CORE * part, CORE * part + CORE)
+                a_hi[slot, rows, :CORE] = w_hi[:, lanes]
+                a_hi[slot, rows, CORE:] = w_lo[:, lanes]
 
     lane = lax.broadcasted_iota(jnp.int32, (1, 2 * YB), 1)
     bin_at = lax.rem(lane, YB)
@@ -361,10 +391,10 @@
 
 def first_kernel(
     kern, last, w_ref, thr_ref, mask_ref, target_ref, a_ref, b_ref, h_ref, tb,
-    g_ref, f_ref, tgt_ref, fld, inten, tot,
+    g_ref, f_ref, tgt_ref, *work,
 ):
     m_hi, m_lo = split(mask_ref[...])
-    v, left, right = sides(a_ref, b_ref, tb)
+    v, left, right = sides(a_ref[...], b_ref[...], tb)
     v = v + dot3(tb("cx_own_hi"), tb("cx_own_lo"), m_hi, m_lo, dot_nt)
     to_spectrum(v, tb, f_ref, None)
     tgt_ref[...] = (
@@ -372,19 +402,20 @@
         + dot(tb("sel_halo", 0)[:, :EDGE], left)
         + dot(tb("sel_halo", 1)[:, :EDGE], right)
     )
-    gradient_body(kern, last, f_ref, tgt_ref, h_ref, w_ref, thr_ref, tb, g_ref, fld, inten, tot)
+    gradient_body(kern, last, f_ref, tgt_ref, h_ref, w_ref, thr_ref, tb, g_ref, work)
 
 
 def later_kernel(
-    kern, last, w_ref, thr_ref, mine_ref, peer_ref, rim_ref, far_ref, f_in_ref, tgt_ref, h_ref,
-    tb, g_ref, f_ref, fld, inten, tot,
+    kern, last, w_ref, thr_ref, mine_ref, peer_ref, a_ref, a2_ref, b_ref, b2_ref, f_in_ref, tgt_ref,
+    h_ref, tb, g_ref, f_ref, *work,
 ):
     s_hi, s_lo = split(mine_ref[...] + peer_ref[...])
-    rims = rim_ref[...] + far_ref[...]
-    v, _, _ = sides(rims[:WIDE_PAD], rims[WIDE_PAD:], tb)
+    from_a = a_ref[...] + a2_ref[...]
+    from_b = b_ref[...] + b2_ref[...]
+    v, _, _ = sides(from_a, from_b, tb)
     v = v + dot3(tb("cx_own_hi"), tb("cx_own_lo"), s_hi, s_lo, dot_nt)
     to_spectrum(v, tb, f_ref, f_in_ref)
-    gradient_body(kern, last, f_ref, tgt_ref, h_ref, w_ref, thr_ref, tb, g_ref, fld, inten, tot)
+    gradient_body(kern, last, f_ref, tgt_ref, h_ref, w_ref, thr_ref, tb, g_ref, work)
 
 
 def match_kernel(n_got, table_ref, own_ref, *refs):
@@ -436,8 +467,14 @@
     pairs_a = [(i, i ^ 1) for i in range(n_tile)]
     pairs_b = [p for i in range(1, n_tile - 1, 2) for p in ((i, i + 1), (i + 1, i))]
 
-    def swap_edges(send_a, send_b):
-        return lax.ppermute(send_b, "tile", pairs_b), lax.ppermute(send_a, "tile", pairs_a)
+    def swap_edges(send_a, send_b, cross=False):
+        def move(x, pairs):
+            if not cross:
+                return lax.ppermute(x, "tile", pairs)
+            both = [(2 * i + p, 2 * j + 1 - p) for i, j in pairs for p in range(2)]
+            return lax.ppermute(x, ("tile", "depth"), both)
+
+        return move(send_b, pairs_b), move(send_a, pairs_a)
 
     def depth_pair(x):
         bit = 1
@@ -467,6 +504,10 @@
         pltpu.VMEM((2, kern, ROWS, 2 * CORE), f32),
         pltpu.VMEM((2, ROWS, CORE), f32),
         pltpu.VMEM((2, 4, XB, YB), f32),
+        pltpu.VMEM((2, 4 * XB, 2 * YB), bf16),
+        pltpu.VMEM((2, 4 * XB, 2 * YB), bf16),
+        pltpu.VMEM((2, 2 * XB, 2 * CORE), bf16),
+        pltpu.VMEM((2, 2 * XB, 2 * CORE), bf16),
     ]
 
     edge = jax.ShapeDtypeStruct((EDGE, tiles_dev * core), f32)
@@ -506,9 +547,14 @@
         if step == STEPS:
             moves += depth_pair(outs[0])
             break
-        from_b, from_a = swap_edges(*outs[1:])
+        if n_depth == 2:
+            from_b, from_a = swap_edges(*outs[1:])
+            far_b, far_a = swap_edges(*outs[1:], cross=True)
+            rims = (from_a, far_a, from_b, far_b)
+        else:
+            from_b, from_a = swap_edges(*outs[1:])
+            rims = depth_pair(from_a) + depth_pair(from_b)
         moves += depth_pair(outs[0])
-        rims = depth_pair(jnp.concatenate([from_a, from_b]))
         kept = step + 1 < STEPS
         grad, *rest = call(
             functools.partial(later_kernel, kern, n_tile - 1),

time: 66.4 us -> 64.3 us (0.968)
  Pallas kernels: 23.3 us -> 19.1 us
  starting transfers between devices: 22.4 us -> 25.4 us
  waiting for transfers between devices: 17.1 us -> 16.1 us
    pallas_call x7, Pallas kernels: 23.3 us -> 19.1 us  [call(): pl.pallas_call(wrapped, out_shape=out_shape, in_specs=[sm if i in smem el...]
    ppermute x8, starting transfers between devices: 16.6 us -> 20 us  [from_partners(): lax.ppermute(grad, 'tile', [(i, i ^ bit) for i in range(n_tile)])]
    ppermute x3 -> x2, waiting for transfers between devices: 7.46 us -> 4.8 us  [depth_pair(): peer = lax.ppermute(x, 'depth', [(i, i ^ bit) for i in range(n_depth)])]
    ppermute x3 -> x2, starting transfers between devices: 3.75 us -> 2.12 us  [depth_pair(): peer = lax.ppermute(x, 'depth', [(i, i ^ bit) for i in range(n_depth)])]
    ppermute x4 -> x6, waiting for transfers between devices: 0.01 us -> 1.56 us  [the longest x2 1.55 us: move(): return lax.ppermute(x, ('tile', 'depth'), both)]
    ppermute x4 -> x6, starting transfers between devices: 2.05 us -> 3.29 us  [the longest x4 2.63 us: move(): return lax.ppermute(x, 'tile', pairs)]
    unnamed x21 -> x20, local copies, waits for them, and re-layouts: 1.85 us -> 1.85 us
  transfers between devices with their start and end apart: 15 -> 16, of which waited for: 7 -> 6; matrix products, arithmetic and copies ran while one was open for 0% -> 0% of each run, Pallas kernels for 2% -> 2%
where the time goes in v5:
time: 64.3 us; the launch traced here: 64.1 us
  starting transfers between devices  25.4 us (40%)
  Pallas kernels  19.1 us (30%)
  waiting for transfers between devices  16.1 us (25%)
  local copies, waits for them, and re-layouts  1.85 us (3%)
  between operations  1.5 us (2%)
    ppermute x8, starting transfers between devices, from_partners(): lax.ppermute(grad, 'tile', [(i, i ^ bit) for i in range(n_tile)])  20 us
    pallas_call x7, Pallas kernels, call(): pl.pallas_call(wrapped, out_shape=out_shape, in_specs=[sm if i in smem el...  19.1 us
    ppermute x8, waiting for transfers between devices, from_partners(): lax.ppermute(grad, 'tile', [(i, i ^ bit) for i in range(n_tile)])  9.78 us
    ppermute x2, waiting for transfers between devices, depth_pair(): peer = lax.ppermute(x, 'depth', [(i, i ^ bit) for i in range(n_depth)])  4.8 us
    ppermute x4, starting transfers between devices, move(): return lax.ppermute(x, 'tile', pairs)  2.63 us
    ppermute x2, starting transfers between devices, depth_pair(): peer = lax.ppermute(x, 'depth', [(i, i ^ bit) for i in range(n_depth)])  2.12 us
    unnamed x20, local copies, waits for them, and re-layouts  1.85 us
    ppermute x2, waiting for transfers between devices, move(): return lax.ppermute(x, ('tile', 'depth'), both)  1.55 us
  transfers between devices with their start and end apart: 16, of which 6 were waited for; matrix products, arithmetic and copies ran while one was open for 0% of the time, Pallas kernels for 2%

profile of v5, /device:TPU:0, one launch (start us, length us, event | category | flops | bytes accessed | tf_op | source)
XLA Modules:
  0.0 64.1 jit_solution(4313500817327062977)
XLA Ops:
  0.6 0.0 copy-start
  0.6 0.9 %copy-done = f32[2,128,128]{2,1,0:T(8,128)S(1)} copy-done((f32[2,128,128]{2,1,0:T(8,128)S(1)}, f32[2,128,128]{2,1,0:T(8,128)}, u32[]{:S(2)}) %copy-start) | copy-done | bytes 131096
  1.5 0.9 %copy-done.3 = s32[2,128,128]{2,1,0:T(8,128)S(1)} copy-done((s32[2,128,128]{2,1,0:T(8,128)S(1)}, s32[2,128,128]{2,1,0:T(8,128)}, u32[]{:S(2)}) %copy-start.3) | copy-done | bytes 131096
  2.4 0.2 shard_map.113
  2.7 0.5 collective-permute-start
  3.2 0.7 %collective-permute-start.1 = (f32[48,256]{1,0:T(8,128)S(1)}, f32[48,256]{1,0:T(8,128)S(1)}, u32[]{:S(2)}, u32[]{:S(2)}) collective-permute-start(f32[48,256]{1,0:T(8,128)S(1)} %get-tuple-element.11), channel_id=1, source_target_pairs={{2,4},{4,2},{6,8},{8,6},{10,12},{12,10},{14,16},{16,14},{18,20},{2... | collective-permute-start | bytes 147464 | tf_op jit(solution)/shard_map/ppermute | solution.py:473
  3.9 0.0 copy-start.1
  3.9 0.0 copy-start.4
  3.9 0.0 copy-start.5
  3.9 0.0 copy-start.6
  3.9 1.4 %shard_map.114.refs_6_.refs_10_ = f32[12,4,96,128]{3,2,1,0:T(8,128)S(1)} custom-call(f32[2,6,25,1,25]{4,3,2,1,0:T(1,128)S(1)} %bitcast.5, bf16[1408,256]{1,0:T(8,128)(2,1)S(1)} %copy-done.7), custom_call_target="tpu_custom_call" | custom-call | flops 3000000000 | bytes 4000000 | tf_op jit(solution)/shard_map/pallas_call | solution.py:204
  6.0 0.0 copy-start.8
  6.0 0.0 copy-start.9
  6.0 0.0 collective-permute-done.refs_4_
  6.0 0.0 collective-permute-done.1.refs_5_
  6.1 7.6 %shard_map.115 = (f32[256,128]{1,0:T(8,128)S(1)}, f32[2,4,96,128]{3,2,1,0:T(8,128)S(1)}, f32[160,256]{1,0:T(8,128)S(1)}) custom-call(f32[1,6]{1,0:T(1,128)S(1)} %copy-done.5, f32[1]{0:T(128)S(6)} %copy.12.refs_1_, f32[256,128]{1,0:T(8,128)S(1)} %bitcast.4, s32[256,128]{1,0:T(8,128)S(1)} %bitcast.7, f32[48,256]{1,0:T(8,128)S(1)} %collective-permute-done.refs_4_, ...), custom_call_target="tpu_custom_call" | custom-call | flops 10000000000 | tf_op jit(solution)/shard_map/pallas_call | solution.py:204
  13.7 7.2 %collective-permute-start.5 = (f32[256,128]{1,0:T(8,128)S(1)}, f32[256,128]{1,0:T(8,128)S(1)}, u32[]{:S(2)}, u32[]{:S(2)}) collective-permute-start(f32[256,128]{1,0:T(8,128)S(1)} %get-tuple-element.12.refs_1_), channel_id=1, source_target_pairs={{0,16},{2,18},{4,20},{6,22},{8,24},{10,26},{12,28},{14,30},{16,0},... | collective-permute-start | bytes 393224 | tf_op jit(solution)/shard_map/ppermute | solution.py:491
  20.9 1.6 %collective-permute-start.4 = (f32[256,128]{1,0:T(8,128)S(1)}, f32[256,128]{1,0:T(8,128)S(1)}, u32[]{:S(2)}, u32[]{:S(2)}) collective-permute-start(f32[256,128]{1,0:T(8,128)S(1)} %get-tuple-element.12.refs_1_), channel_id=1, source_target_pairs={{0,8},{2,10},{4,12},{6,14},{8,0},{10,2},{12,4},{14,6},{16,24},{18,... | collective-permute-start | bytes 393224 | tf_op jit(solution)/shard_map/ppermute | solution.py:491
  22.5 0.5 collective-permute-start.3
  23.0 0.0 collective-permute-start.2
  23.0 0.1 pad_add_fusion.refs_0_
  23.0 4.4 %collective-permute-done.5.refs_5_ = f32[256,128]{1,0:T(8,128)S(1)} collective-permute-done((f32[256,128]{1,0:T(8,128)S(1)}, f32[256,128]{1,0:T(8,128)S(1)}, u32[]{:S(2)}, u32[]{:S(2)}) %collective-permute-start.5) | collective-permute-done | bytes 131104 | tf_op jit(solution)/shard_map/ppermute | solution.py:491
  27.5 0.2 collective-permute-done.4.refs_4_
  27.7 0.0 collective-permute-done.3.refs_3_
  27.7 0.0 collective-permute-done.2.refs_2_
  27.7 0.9 %shard_map.116 = (f32[256,128]{1,0:T(8,128)S(1)}, f32[32,256]{1,0:T(8,128)S(1)}, f32[32,256]{1,0:T(8,128)S(1)}) custom-call(s32[4]{0:T(128)S(1)} %pad_add_fusion.refs_0_, f32[256,128]{1,0:T(8,128)S(1)} %get-tuple-element.12.refs_1_, f32[256,128]{1,0:T(8,128)S(1)} %collective-permute-done.2.refs_2_, f32[256,128]{1,0:T(8,128)S(1)} %collective-permute-done.3.refs_3_, ...), custom_call_target="tpu_custom_call" | custom-call | tf_op jit(solution)/shard_map/pallas_call | solution.py:204
  28.6 1.6 %collective-permute-start.6 = (f32[256,128]{1,0:T(8,128)S(1)}, f32[256,128]{1,0:T(8,128)S(1)}, u32[]{:S(2)}, u32[]{:S(2)}) collective-permute-start(f32[256,128]{1,0:T(8,128)S(1)} %get-tuple-element.13.refs_2_.refs_1_), channel_id=1, source_target_pairs={{0,1},{1,0},{2,3},{3,2},{4,5},{5,4},{6,7},{7,6},{8,9},{9,8},{10,11... | collective-permute-start | bytes 393224 | tf_op jit(solution)/shard_map/ppermute | solution.py:482
  30.1 0.0 collective-permute-start.8
  30.1 0.6 collective-permute-start.7
  30.7 0.7 %collective-permute-start.10 = (f32[32,256]{1,0:T(8,128)S(1)}, f32[32,256]{1,0:T(8,128)S(1)}, u32[]{:S(2)}, u32[]{:S(2)}) collective-permute-start(f32[32,256]{1,0:T(8,128)S(1)} %get-tuple-element.15), channel_id=1, source_target_pairs={{2,5},{3,4},{4,3},{5,2},{6,9},{7,8},{8,7},{9,6},{10,13},{11,12},{1... | collective-permute-start | bytes 98312 | tf_op jit(solution)/shard_map/ppermute | solution.py:475
  31.4 0.8 %collective-permute-start.9 = (f32[32,256]{1,0:T(8,128)S(1)}, f32[32,256]{1,0:T(8,128)S(1)}, u32[]{:S(2)}, u32[]{:S(2)}) collective-permute-start(f32[32,256]{1,0:T(8,128)S(1)} %get-tuple-element.15), channel_id=1, source_target_pairs={{2,4},{4,2},{6,8},{8,6},{10,12},{12,10},{14,16},{16,14},{18,20},{2... | collective-permute-start | bytes 98312 | tf_op jit(solution)/shard_map/ppermute | solution.py:473
  32.2 1.5 %collective-permute-done.8.refs_5_ = f32[32,256]{1,0:T(8,128)S(1)} collective-permute-done((f32[32,256]{1,0:T(8,128)S(1)}, f32[32,256]{1,0:T(8,128)S(1)}, u32[]{:S(2)}, u32[]{:S(2)}) %collective-permute-start.8) | collective-permute-done | bytes 32800 | tf_op jit(solution)/shard_map/ppermute | solution.py:475
  33.8 0.0 collective-permute-done.10.refs_7_
  33.8 0.0 collective-permute-done.9.refs_6_
  33.8 0.1 collective-permute-done.6.refs_3_.refs_2_
  33.9 7.6 %shard_map.117.refs_1_ = f32[256,128]{1,0:T(8,128)S(1)} custom-call(f32[1,6]{1,0:T(1,128)S(1)} %copy-done.5, f32[1]{0:T(128)S(6)} %copy.12.refs_1_, f32[256,128]{1,0:T(8,128)S(1)} %get-tuple-element.13.refs_2_.refs_1_, f32[256,128]{1,0:T(8,128)S(1)} %collective-permute-done.6.refs_3_.refs_2_, f32[32,256]{1,0:T(8,128)S(1)} %collective-permute-done.7.refs_4_, ...), custom_call_target="tpu_custom_call" | custom-call | flops 10000000000 | tf_op jit(solution)/shard_map/pallas_call | solution.py:204
  41.5 9.0 %collective-permute-start.14 = (f32[256,128]{1,0:T(8,128)S(1)}, f32[256,128]{1,0:T(8,128)S(1)}, u32[]{:S(2)}, u32[]{:S(2)}) collective-permute-start(f32[256,128]{1,0:T(8,128)S(1)} %shard_map.117.refs_1_), channel_id=1, source_target_pairs={{0,16},{2,18},{4,20},{6,22},{8,24},{10,26},{12,28},{14,30},{16,0},... | collective-permute-start | bytes 393224 | tf_op jit(solution)/shard_map/ppermute | solution.py:491
  50.5 0.7 %collective-permute-start.13 = (f32[256,128]{1,0:T(8,128)S(1)}, f32[256,128]{1,0:T(8,128)S(1)}, u32[]{:S(2)}, u32[]{:S(2)}) collective-permute-start(f32[256,128]{1,0:T(8,128)S(1)} %shard_map.117.refs_1_), channel_id=1, source_target_pairs={{0,8},{2,10},{4,12},{6,14},{8,0},{10,2},{12,4},{14,6},{16,24},{18,... | collective-permute-start | bytes 393224 | tf_op jit(solution)/shard_map/ppermute | solution.py:491
  51.2 0.7 %collective-permute-start.12 = (f32[256,128]{1,0:T(8,128)S(1)}, f32[256,128]{1,0:T(8,128)S(1)}, u32[]{:S(2)}, u32[]{:S(2)}) collective-permute-start(f32[256,128]{1,0:T(8,128)S(1)} %shard_map.117.refs_1_), channel_id=1, source_target_pairs={{0,4},{2,6},{4,0},{6,2},{8,12},{10,14},{12,8},{14,10},{16,20},{18,... | collective-permute-start | bytes 393224 | tf_op jit(solution)/shard_map/ppermute | solution.py:491
  51.9 0.3 collective-permute-start.11
  52.2 5.1 %collective-permute-done.14.refs_5_ = f32[256,128]{1,0:T(8,128)S(1)} collective-permute-done((f32[256,128]{1,0:T(8,128)S(1)}, f32[256,128]{1,0:T(8,128)S(1)}, u32[]{:S(2)}, u32[]{:S(2)}) %collective-permute-start.14) | collective-permute-done | bytes 131104 | tf_op jit(solution)/shard_map/ppermute | solution.py:491
  57.4 0.0 collective-permute-done.13.refs_4_
  57.4 0.0 collective-permute-done.12.refs_3_
  57.4 0.0 collective-permute-done.11.refs_2_
  57.4 0.7 %shard_map.118.refs_3_ = f32[256,128]{1,0:T(8,128)S(1)} custom-call(s32[4]{0:T(128)S(1)} %pad_add_fusion.refs_0_, f32[256,128]{1,0:T(8,128)S(1)} %shard_map.117.refs_1_, f32[256,128]{1,0:T(8,128)S(1)} %collective-permute-done.11.refs_2_, f32[256,128]{1,0:T(8,128)S(1)} %collective-permute-done.12.refs_3_, f32[256,128]{1,0:T(8,128)S(1)} %collective-permute-done.13.refs_4_, ...), custom_call_target="tpu_custom_call" | custom-call | tf_op jit(solution)/shard_map/pallas_call | solution.py:204
  58.1 0.6 collective-permute-start.15
  58.7 4.7 %collective-permute-done.15.refs_4_ = f32[256,128]{1,0:T(8,128)S(1)} collective-permute-done((f32[256,128]{1,0:T(8,128)S(1)}, f32[256,128]{1,0:T(8,128)S(1)}, u32[]{:S(2)}, u32[]{:S(2)}) %collective-permute-start.15) | collective-permute-done | bytes 131104 | tf_op jit(solution)/shard_map/ppermute | solution.py:482
  63.4 0.7 %shard_map.119 = (f32[2,128,128]{2,1,0:T(8,128)}, f32[2,128,128]{2,1,0:T(8,128)}) custom-call(f32[2,128,128]{2,1,0:T(8,128)S(1)} %copy-done.1, f32[256,128]{1,0:T(8,128)S(1)} %get-tuple-element.13.refs_2_.refs_1_, f32[256,128]{1,0:T(8,128)S(1)} %collective-permute-done.6.refs_3_.refs_2_, f32[256,128]{1,0:T(8,128)S(1)} %shard_map.118.refs_3_, ...), custom_call_target="tpu_custom_call" | custom-call | tf_op jit(solution)/shard_map/pallas_call | solution.py:204
  (12 shorter events, 0.0 us)
Async XLA Ops:
  0.6 0.9 %copy-start = (f32[2,128,128]{2,1,0:T(8,128)S(1)}, f32[2,128,128]{2,1,0:T(8,128)}, u32[]{:S(2)}) copy-start(f32[2,128,128]{2,1,0:T(8,128)} %refs_0_.5) | copy-start | bytes 393220
  1.5 0.9 %copy-start.3 = (s32[2,128,128]{2,1,0:T(8,128)S(1)}, s32[2,128,128]{2,1,0:T(8,128)}, u32[]{:S(2)}) copy-start(s32[2,128,128]{2,1,0:T(8,128)} %param.11) | copy-start | bytes 393220
  2.4 1.4 %copy-start.2 = (f32[2,1,6,25,25]{4,1,3,2,0:T(1,128)S(1)}, f32[2,1,6,25,25]{4,1,3,2,0:T(1,128)}, u32[]{:S(2)}) copy-start(f32[2,1,6,25,25]{4,1,3,2,0:T(1,128)} %param.12) | copy-start | bytes 90004
  2.4 1.4 %copy-start.7 = (bf16[1408,256]{1,0:T(8,128)(2,1)S(1)}, bf16[1408,256]{1,0:T(8,128)(2,1)}, u32[]{:S(2)}) copy-start(bf16[1408,256]{1,0:T(8,128)(2,1)} %constant.4.clone.refs_1_) | copy-start | bytes 2162692
  2.7 3.4 %collective-permute-start = (f32[48,256]{1,0:T(8,128)S(1)}, f32[48,256]{1,0:T(8,128)S(1)}, u32[]{:S(2)}, u32[]{:S(2)}) collective-permute-start(f32[48,256]{1,0:T(8,128)S(1)} %get-tuple-element.10), channel_id=1, source_target_pairs={{0,2},{2,0},{4,6},{6,4},{8,10},{10,8},{12,14},{14,12},{16,18},{18,... | collective-permute-start | bytes 147464 | tf_op jit(solution)/shard_map/ppermute | solution.py:473
  3.2 2.8 %collective-permute-start.1 = (f32[48,256]{1,0:T(8,128)S(1)}, f32[48,256]{1,0:T(8,128)S(1)}, u32[]{:S(2)}, u32[]{:S(2)}) collective-permute-start(f32[48,256]{1,0:T(8,128)S(1)} %get-tuple-element.11), channel_id=1, source_target_pairs={{2,4},{4,2},{6,8},{8,6},{10,12},{12,10},{14,16},{16,14},{18,20},{2... | collective-permute-start | bytes 147464 | tf_op jit(solution)/shard_map/ppermute | solution.py:473
  3.9 2.2 %copy-start.1 = (f32[2,128,128]{2,1,0:T(8,128)S(1)}, f32[2,128,128]{2,1,0:T(8,128)}, u32[]{:S(2)}) copy-start(f32[2,128,128]{2,1,0:T(8,128)} %refs_0_.5) | copy-start | bytes 393220
  3.9 2.2 %copy-start.4 = (s32[2,128,128]{2,1,0:T(8,128)S(1)}, s32[2,128,128]{2,1,0:T(8,128)}, u32[]{:S(2)}) copy-start(s32[2,128,128]{2,1,0:T(8,128)} %param.11) | copy-start | bytes 393220
  3.9 2.2 %copy-start.5 = (f32[1,6]{1,0:T(1,128)S(1)}, f32[1,6]{1,0:T(1,128)}, u32[]{:S(2)}) copy-start(f32[1,6]{1,0:T(1,128)} %refs_0_.4) | copy-start | bytes 76
  3.9 2.2 %copy-start.6 = (bf16[3712,256]{1,0:T(8,128)(2,1)S(1)}, bf16[3712,256]{1,0:T(8,128)(2,1)}, u32[]{:S(2)}) copy-start(bf16[3712,256]{1,0:T(8,128)(2,1)} %constant.5.clone.refs_7_.refs_11_) | copy-start | bytes 5701636
  6.0 17.0 %copy-start.8 = (s32[2]{0:T(128)S(1)}, s32[2]{0:T(128)}, u32[]{:S(2)}) copy-start(s32[2]{0:T(128)} %param.16) | copy-start | bytes 28
  6.0 16.9 %copy-start.9 = (s32[2]{0:T(128)S(1)}, s32[2]{0:T(128)}, u32[]{:S(2)}) copy-start(s32[2]{0:T(128)} %param.15) | copy-start | bytes 28
  13.7 13.8 %collective-permute-start.5 = (f32[256,128]{1,0:T(8,128)S(1)}, f32[256,128]{1,0:T(8,128)S(1)}, u32[]{:S(2)}, u32[]{:S(2)}) collective-permute-start(f32[256,128]{1,0:T(8,128)S(1)} %get-tuple-element.12.refs_1_), channel_id=1, source_target_pairs={{0,16},{2,18},{4,20},{6,22},{8,24},{10,26},{12,28},{14,30},{16,0},... | collective-permute-start | bytes 393224 | tf_op jit(solution)/shard_map/ppermute | solution.py:491
  20.9 6.8 %collective-permute-start.4 = (f32[256,128]{1,0:T(8,128)S(1)}, f32[256,128]{1,0:T(8,128)S(1)}, u32[]{:S(2)}, u32[]{:S(2)}) collective-permute-start(f32[256,128]{1,0:T(8,128)S(1)} %get-tuple-element.12.refs_1_), channel_id=1, source_target_pairs={{0,8},{2,10},{4,12},{6,14},{8,0},{10,2},{12,4},{14,6},{16,24},{18,... | collective-permute-start | bytes 393224 | tf_op jit(solution)/shard_map/ppermute | solution.py:491
  22.5 5.2 %collective-permute-start.3 = (f32[256,128]{1,0:T(8,128)S(1)}, f32[256,128]{1,0:T(8,128)S(1)}, u32[]{:S(2)}, u32[]{:S(2)}) collective-permute-start(f32[256,128]{1,0:T(8,128)S(1)} %get-tuple-element.12.refs_1_), channel_id=1, source_target_pairs={{0,4},{2,6},{4,0},{6,2},{8,12},{10,14},{12,8},{14,10},{16,20},{18,... | collective-permute-start | bytes 393224 | tf_op jit(solution)/shard_map/ppermute | solution.py:491
  23.0 4.7 %collective-permute-start.2 = (f32[256,128]{1,0:T(8,128)S(1)}, f32[256,128]{1,0:T(8,128)S(1)}, u32[]{:S(2)}, u32[]{:S(2)}) collective-permute-start(f32[256,128]{1,0:T(8,128)S(1)} %get-tuple-element.12.refs_1_), channel_id=1, source_target_pairs={{0,2},{2,0},{4,6},{6,4},{8,10},{10,8},{12,14},{14,12},{16,18},{18,... | collective-permute-start | bytes 393224 | tf_op jit(solution)/shard_map/ppermute | solution.py:491
  28.6 5.4 %collective-permute-start.6 = (f32[256,128]{1,0:T(8,128)S(1)}, f32[256,128]{1,0:T(8,128)S(1)}, u32[]{:S(2)}, u32[]{:S(2)}) collective-permute-start(f32[256,128]{1,0:T(8,128)S(1)} %get-tuple-element.13.refs_2_.refs_1_), channel_id=1, source_target_pairs={{0,1},{1,0},{2,3},{3,2},{4,5},{5,4},{6,7},{7,6},{8,9},{9,8},{10,11... | collective-permute-start | bytes 393224 | tf_op jit(solution)/shard_map/ppermute | solution.py:482
  30.1 3.7 %collective-permute-start.8 = (f32[32,256]{1,0:T(8,128)S(1)}, f32[32,256]{1,0:T(8,128)S(1)}, u32[]{:S(2)}, u32[]{:S(2)}) collective-permute-start(f32[32,256]{1,0:T(8,128)S(1)} %get-tuple-element.14), channel_id=1, source_target_pairs={{0,3},{1,2},{2,1},{3,0},{4,7},{5,6},{6,5},{7,4},{8,11},{9,10},{10,... | collective-permute-start | bytes 98312 | tf_op jit(solution)/shard_map/ppermute | solution.py:475
  30.1 3.7 %collective-permute-start.7 = (f32[32,256]{1,0:T(8,128)S(1)}, f32[32,256]{1,0:T(8,128)S(1)}, u32[]{:S(2)}, u32[]{:S(2)}) collective-permute-start(f32[32,256]{1,0:T(8,128)S(1)} %get-tuple-element.14), channel_id=1, source_target_pairs={{0,2},{2,0},{4,6},{6,4},{8,10},{10,8},{12,14},{14,12},{16,18},{18,... | collective-permute-start | bytes 98312 | tf_op jit(solution)/shard_map/ppermute | solution.py:473
  30.7 3.1 %collective-permute-start.10 = (f32[32,256]{1,0:T(8,128)S(1)}, f32[32,256]{1,0:T(8,128)S(1)}, u32[]{:S(2)}, u32[]{:S(2)}) collective-permute-start(f32[32,256]{1,0:T(8,128)S(1)} %get-tuple-element.15), channel_id=1, source_target_pairs={{2,5},{3,4},{4,3},{5,2},{6,9},{7,8},{8,7},{9,6},{10,13},{11,12},{1... | collective-permute-start | bytes 98312 | tf_op jit(solution)/shard_map/ppermute | solution.py:475
  31.4 2.4 %collective-permute-start.9 = (f32[32,256]{1,0:T(8,128)S(1)}, f32[32,256]{1,0:T(8,128)S(1)}, u32[]{:S(2)}, u32[]{:S(2)}) collective-permute-start(f32[32,256]{1,0:T(8,128)S(1)} %get-tuple-element.15), channel_id=1, source_target_pairs={{2,4},{4,2},{6,8},{8,6},{10,12},{12,10},{14,16},{16,14},{18,20},{2... | collective-permute-start | bytes 98312 | tf_op jit(solution)/shard_map/ppermute | solution.py:473
  41.5 15.9 %collective-permute-start.14 = (f32[256,128]{1,0:T(8,128)S(1)}, f32[256,128]{1,0:T(8,128)S(1)}, u32[]{:S(2)}, u32[]{:S(2)}) collective-permute-start(f32[256,128]{1,0:T(8,128)S(1)} %shard_map.117.refs_1_), channel_id=1, source_target_pairs={{0,16},{2,18},{4,20},{6,22},{8,24},{10,26},{12,28},{14,30},{16,0},... | collective-permute-start | bytes 393224 | tf_op jit(solution)/shard_map/ppermute | solution.py:491
  50.5 6.9 %collective-permute-start.13 = (f32[256,128]{1,0:T(8,128)S(1)}, f32[256,128]{1,0:T(8,128)S(1)}, u32[]{:S(2)}, u32[]{:S(2)}) collective-permute-start(f32[256,128]{1,0:T(8,128)S(1)} %shard_map.117.refs_1_), channel_id=1, source_target_pairs={{0,8},{2,10},{4,12},{6,14},{8,0},{10,2},{12,4},{14,6},{16,24},{18,... | collective-permute-start | bytes 393224 | tf_op jit(solution)/shard_map/ppermute | solution.py:491
  51.2 6.2 %collective-permute-start.12 = (f32[256,128]{1,0:T(8,128)S(1)}, f32[256,128]{1,0:T(8,128)S(1)}, u32[]{:S(2)}, u32[]{:S(2)}) collective-permute-start(f32[256,128]{1,0:T(8,128)S(1)} %shard_map.117.refs_1_), channel_id=1, source_target_pairs={{0,4},{2,6},{4,0},{6,2},{8,12},{10,14},{12,8},{14,10},{16,20},{18,... | collective-permute-start | bytes 393224 | tf_op jit(solution)/shard_map/ppermute | solution.py:491
  51.9 5.4 %collective-permute-start.11 = (f32[256,128]{1,0:T(8,128)S(1)}, f32[256,128]{1,0:T(8,128)S(1)}, u32[]{:S(2)}, u32[]{:S(2)}) collective-permute-start(f32[256,128]{1,0:T(8,128)S(1)} %shard_map.117.refs_1_), channel_id=1, source_target_pairs={{0,2},{2,0},{4,6},{6,4},{8,10},{10,8},{12,14},{14,12},{16,18},{18,... | collective-permute-start | bytes 393224 | tf_op jit(solution)/shard_map/ppermute | solution.py:491
  58.1 5.3 %collective-permute-start.15 = (f32[256,128]{1,0:T(8,128)S(1)}, f32[256,128]{1,0:T(8,128)S(1)}, u32[]{:S(2)}, u32[]{:S(2)}) collective-permute-start(f32[256,128]{1,0:T(8,128)S(1)} %shard_map.118.refs_3_), channel_id=1, source_target_pairs={{0,1},{1,0},{2,3},{3,2},{4,5},{5,4},{6,7},{7,6},{8,9},{9,8},{10,11... | collective-permute-start | bytes 393224 | tf_op jit(solution)/shard_map/ppermute | solution.py:482

commit v6 on v5

--- a/solution.py
+++ b/solution.py
@@ -81,7 +81,15 @@
 
 def pack(parts):
     rows, where, at = [], {}, 0
+    pieces = []
     for name, a in parts:
+        if a.shape[1] <= 256:
+            pieces.append((name, a))
+            continue
+        cuts = range(0, a.shape[1], 256)
+        where[name] = len(cuts)
+        pieces += [(f"{name}.{i}", a[:, c : c + 256]) for i, c in enumerate(cuts)]
+    for name, a in pieces:
         height = -(-a.shape[0] // 16) * 16
         block = np.zeros((height, 256), np.float64)
         block[: a.shape[0], : a.shape[1]] = a
@@ -96,7 +104,8 @@
     for name, a in parts:
         hi, lo = np_split(a)
         if name in ("x2", "x3", "x4"):
-            both.append((name, np.concatenate([hi.astype(np.float64), lo.astype(np.float64)])))
+            hi, lo = hi.astype(np.float64), lo.astype(np.float64)
+            both.append((name, np.concatenate([hi, lo, hi], axis=1)))
             continue
         both += [(name + "_hi", hi.astype(np.float64)), (name + "_lo", lo.astype(np.float64))]
     return both
@@ -120,7 +129,7 @@
     y3_hi, y3_lo = (a.astype(np.float64) for a in np_split(y_lanes(core_rows)))
     grad = pack_split(parts)
     grad += [("y2", np.concatenate([y2_hi, y2_lo], axis=1))]
-    grad += [("y3_dup", np.concatenate([y3_hi, y3_hi])), ("y3_lo", y3_lo)]
+    grad += [("y3", np.concatenate([y3_hi, y3_hi, y3_lo]))]
     own = np.zeros((ROWS, CORE))
     own[np.arange(CORE) + WIDE - ROW0, np.arange(CORE)] = 1
     halo = np.zeros((ROWS, 256))
@@ -156,12 +165,6 @@
     return mul(a_hi, b_hi) + (mul(a_lo, b_hi) + mul(a_hi, b_lo))
 
 
-def dot_stacked(table, b_hi, b_lo):
-    rows = table.shape[0] // 2
-    both = dot(table, b_hi)
-    return both[:rows] + (both[rows:] + dot(table[:rows], b_lo))
-
-
 def signed(spec):
     cc, cs = spec[:XB, :YB], spec[:XB, YB:]
     sc, ss = spec[XB:, :YB], spec[XB:, YB:]
@@ -182,6 +185,8 @@
     where = tables()[group][1]
 
     def table(name, half=None):
+        if isinstance(where[name], int):
+            return jnp.concatenate([table(f"{name}.{i}") for i in range(where[name])], axis=1)
         at, height, width = where[name]
         lanes = slice(0, width) if half is None else slice(128 * half, 128 * half + 128)
         return ref[at : at + height, lanes]
@@ -284,7 +289,7 @@
 
 
 def gradient_body(kern, last, f_ref, tgt_ref, h_ref, w_ref, thr_ref, tb, g_ref, work):
-    fld, inten, tot, a_hi, a_lo, b_hi, b_lo = work
+    fld, inten, tot, a_hi, a_lo, b_cat, c_cat = work
     chains = [(t, k) for t in range(2) for k in range(kern)]
     rounds = range(len(chains) + 2)
 
@@ -311,7 +316,7 @@
                 a_lo[slot, rows] = p_lo
         if old:
             slot = (i - 2) % 2
-            field = dot_stacked(tb("x2"), b_hi[slot], b_lo[slot])
+            field = dot(tb("x2"), b_cat[slot])
             t, k = old
             fld[t, k] = field
             re, im = field[:, :CORE], field[:, CORE:]
@@ -321,8 +326,8 @@
             slot = (i - 1) % 2
             z = z_one[:, :CORE] + (z_one[:, CORE:] + z_two)
             z_hi, z_lo = split(jnp.concatenate([z[: 2 * XB], z[2 * XB :]], axis=1))
-            b_hi[slot] = z_hi
-            b_lo[slot] = z_lo
+            for j, piece in enumerate((z_hi, z_hi, z_lo)):
+                b_cat[slot, 2 * XB * j : 2 * XB * j + 2 * XB] = piece
 
     tile = lax.axis_index("tile")
     first = jnp.where(tile == 0, WIDE, HALO) - ROW0
@@ -338,7 +343,7 @@
         new, mid, old = at(i), at(i - 1), at(i - 2)
         if mid:
             slot = (i - 1) % 2
-            w_now = dot_stacked(tb("x3"), b_hi[slot, :ROWS], b_lo[slot, :ROWS])
+            w_now = dot(tb("x3"), b_cat[slot, : 3 * ROWS])
         if new:
             t, k = new
             slot = i % 2
@@ -347,13 +352,12 @@
             r_hi, r_lo = split(
                 jnp.concatenate([scaled * field[:, :CORE], scaled * field[:, CORE:]], axis=1)
             )
-            b_hi[slot, :ROWS] = r_hi
-            b_lo[slot, :ROWS] = r_lo
+            for j, piece in enumerate((r_hi, r_hi, r_lo)):
+                b_cat[slot, ROWS * j : ROWS * j + ROWS] = piece
         if old:
             slot = (i - 2) % 2
             t, k = old
-            cat = a_hi[slot]
-            specs = dot(cat, tb("y3_dup")) + dot(cat[:, :CORE], tb("y3_lo"))
+            specs = dot(c_cat[slot], tb("y3"))
             acc = [0.0] * 4 if k == 0 else [tot[t, j] for j in range(4)]
             for part in range(2):
                 spec = specs[2 * XB * part : 2 * XB * part + 2 * XB]
@@ -373,8 +377,8 @@
             for part in range(2):
                 rows = slice(2 * XB * part, 2 * XB * part + 2 * XB)
                 lanes = slice(CORE * part, CORE * part + CORE)
-                a_hi[slot, rows, :CORE] = w_hi[:, lanes]
-                a_hi[slot, rows, CORE:] = w_lo[:, lanes]
+                for j, piece in enumerate((w_hi, w_lo, w_hi)):
+                    c_cat[slot, rows, CORE * j : CORE * j + CORE] = piece[:, lanes]
 
     lane = lax.broadcasted_iota(jnp.int32, (1, 2 * YB), 1)
     bin_at = lax.rem(lane, YB)
@@ -383,7 +387,7 @@
     out = None
     for t in range(2):
         r_hi, r_lo = split(even_odd(*(tot[t, j] for j in range(4))))
-        u_hi, u_lo = split(weight * dot_stacked(tb("x4"), r_hi, r_lo))
+        u_hi, u_lo = split(weight * dot(tb("x4"), jnp.concatenate([r_hi, r_hi, r_lo], axis=0)))
         term = dot3(tb(f"by{t}_hi"), tb(f"by{t}_lo"), u_hi, u_lo, dot_nt)
         out = term if out is None else out + term
     g_ref[...] = out
@@ -506,8 +510,8 @@
         pltpu.VMEM((2, 4, XB, YB), f32),
         pltpu.VMEM((2, 4 * XB, 2 * YB), bf16),
         pltpu.VMEM((2, 4 * XB, 2 * YB), bf16),
-        pltpu.VMEM((2, 2 * XB, 2 * CORE), bf16),
-        pltpu.VMEM((2, 2 * XB, 2 * CORE), bf16),
+        pltpu.VMEM((2, 6 * XB, 2 * CORE), bf16),
+        pltpu.VMEM((2, 4 * XB, 3 * CORE), bf16),
     ]
 
     edge = jax.ShapeDtypeStruct((EDGE, tiles_dev * core), f32)

time: 64.3 us -> 63.6 us (0.989)
  Pallas kernels: 19.1 us -> 18.4 us
    pallas_call x7, Pallas kernels: 19.1 us -> 18.4 us  [call(): pl.pallas_call(wrapped, out_shape=out_shape, in_specs=[sm if i in smem el...]
where the time goes in v6:
time: 63.6 us; the launch traced here: 63.4 us
  starting transfers between devices  25.4 us (40%)
  Pallas kernels  18.4 us (29%)
  waiting for transfers between devices  16.1 us (25%)
  local copies, waits for them, and re-layouts  1.85 us (3%)
  between operations  1.5 us (2%)
    ppermute x8, starting transfers between devices, from_partners(): lax.ppermute(grad, 'tile', [(i, i ^ bit) for i in range(n_tile)])  20 us
    pallas_call x7, Pallas kernels, call(): pl.pallas_call(wrapped, out_shape=out_shape, in_specs=[sm if i in smem el...  18.4 us
    ppermute x8, waiting for transfers between devices, from_partners(): lax.ppermute(grad, 'tile', [(i, i ^ bit) for i in range(n_tile)])  9.77 us
    ppermute x2, waiting for transfers between devices, depth_pair(): peer = lax.ppermute(x, 'depth', [(i, i ^ bit) for i in range(n_depth)])  4.79 us
    ppermute x4, starting transfers between devices, move(): return lax.ppermute(x, 'tile', pairs)  2.63 us
    ppermute x2, starting transfers between devices, depth_pair(): peer = lax.ppermute(x, 'depth', [(i, i ^ bit) for i in range(n_depth)])  2.12 us
    unnamed x20, local copies, waits for them, and re-layouts  1.85 us
    ppermute x2, waiting for transfers between devices, move(): return lax.ppermute(x, ('tile', 'depth'), both)  1.55 us
  transfers between devices with their start and end apart: 16, of which 6 were waited for; matrix products, arithmetic and copies ran while one was open for 0% of the time, Pallas kernels for 2%

profile of v6, /device:TPU:0, one launch (start us, length us, event | category | flops | bytes accessed | tf_op | source)
XLA Modules:
  0.0 63.4 jit_solution(7639319147414732432)
XLA Ops:
  0.6 0.0 copy-start
  0.6 0.9 %copy-done = f32[2,128,128]{2,1,0:T(8,128)S(1)} copy-done((f32[2,128,128]{2,1,0:T(8,128)S(1)}, f32[2,128,128]{2,1,0:T(8,128)}, u32[]{:S(2)}) %copy-start) | copy-done | bytes 131096
  1.5 0.9 %copy-done.3 = s32[2,128,128]{2,1,0:T(8,128)S(1)} copy-done((s32[2,128,128]{2,1,0:T(8,128)S(1)}, s32[2,128,128]{2,1,0:T(8,128)}, u32[]{:S(2)}) %copy-start.3) | copy-done | bytes 131096
  2.4 0.2 shard_map.113
  2.7 0.5 collective-permute-start
  3.2 0.7 %collective-permute-start.1 = (f32[48,256]{1,0:T(8,128)S(1)}, f32[48,256]{1,0:T(8,128)S(1)}, u32[]{:S(2)}, u32[]{:S(2)}) collective-permute-start(f32[48,256]{1,0:T(8,128)S(1)} %get-tuple-element.11), channel_id=1, source_target_pairs={{2,4},{4,2},{6,8},{8,6},{10,12},{12,10},{14,16},{16,14},{18,20},{2... | collective-permute-start | bytes 147464 | tf_op jit(solution)/shard_map/ppermute | solution.py:477
  3.9 0.0 copy-start.1
  3.9 0.0 copy-start.4
  3.9 0.0 copy-start.5
  3.9 0.0 copy-start.6
  3.9 1.4 %shard_map.114.refs_6_.refs_10_ = f32[12,4,96,128]{3,2,1,0:T(8,128)S(1)} custom-call(f32[2,6,25,1,25]{4,3,2,1,0:T(1,128)S(1)} %bitcast.5, bf16[1408,256]{1,0:T(8,128)(2,1)S(1)} %copy-done.7), custom_call_target="tpu_custom_call" | custom-call | flops 3000000000 | bytes 4000000 | tf_op jit(solution)/shard_map/pallas_call | solution.py:209
  6.0 0.0 copy-start.8
  6.0 0.0 copy-start.9
  6.0 0.0 collective-permute-done.refs_4_
  6.0 0.0 collective-permute-done.1.refs_5_
  6.1 7.3 %shard_map.115 = (f32[256,128]{1,0:T(8,128)S(1)}, f32[2,4,96,128]{3,2,1,0:T(8,128)S(1)}, f32[160,256]{1,0:T(8,128)S(1)}) custom-call(f32[1,6]{1,0:T(1,128)S(1)} %copy-done.5, f32[1]{0:T(128)S(6)} %copy.12.refs_1_, f32[256,128]{1,0:T(8,128)S(1)} %bitcast.4, s32[256,128]{1,0:T(8,128)S(1)} %bitcast.7, f32[48,256]{1,0:T(8,128)S(1)} %collective-permute-done.refs_4_, ...), custom_call_target="tpu_custom_call" | custom-call | flops 10000000000 | tf_op jit(solution)/shard_map/pallas_call | solution.py:209
  13.4 7.2 %collective-permute-start.5 = (f32[256,128]{1,0:T(8,128)S(1)}, f32[256,128]{1,0:T(8,128)S(1)}, u32[]{:S(2)}, u32[]{:S(2)}) collective-permute-start(f32[256,128]{1,0:T(8,128)S(1)} %get-tuple-element.12.refs_1_), channel_id=1, source_target_pairs={{0,16},{2,18},{4,20},{6,22},{8,24},{10,26},{12,28},{14,30},{16,0},... | collective-permute-start | bytes 393224 | tf_op jit(solution)/shard_map/ppermute | solution.py:495
  20.6 1.6 %collective-permute-start.4 = (f32[256,128]{1,0:T(8,128)S(1)}, f32[256,128]{1,0:T(8,128)S(1)}, u32[]{:S(2)}, u32[]{:S(2)}) collective-permute-start(f32[256,128]{1,0:T(8,128)S(1)} %get-tuple-element.12.refs_1_), channel_id=1, source_target_pairs={{0,8},{2,10},{4,12},{6,14},{8,0},{10,2},{12,4},{14,6},{16,24},{18,... | collective-permute-start | bytes 393224 | tf_op jit(solution)/shard_map/ppermute | solution.py:495
  22.2 0.5 collective-permute-start.3
  22.7 0.0 collective-permute-start.2
  22.7 0.1 pad_add_fusion.refs_0_
  22.8 4.4 %collective-permute-done.5.refs_5_ = f32[256,128]{1,0:T(8,128)S(1)} collective-permute-done((f32[256,128]{1,0:T(8,128)S(1)}, f32[256,128]{1,0:T(8,128)S(1)}, u32[]{:S(2)}, u32[]{:S(2)}) %collective-permute-start.5) | collective-permute-done | bytes 131104 | tf_op jit(solution)/shard_map/ppermute | solution.py:495
  27.2 0.2 collective-permute-done.4.refs_4_
  27.4 0.0 collective-permute-done.2.refs_2_
  27.4 0.9 %shard_map.116 = (f32[256,128]{1,0:T(8,128)S(1)}, f32[32,256]{1,0:T(8,128)S(1)}, f32[32,256]{1,0:T(8,128)S(1)}) custom-call(s32[4]{0:T(128)S(1)} %pad_add_fusion.refs_0_, f32[256,128]{1,0:T(8,128)S(1)} %get-tuple-element.12.refs_1_, f32[256,128]{1,0:T(8,128)S(1)} %collective-permute-done.2.refs_2_, f32[256,128]{1,0:T(8,128)S(1)} %collective-permute-done.3.refs_3_, ...), custom_call_target="tpu_custom_call" | custom-call | tf_op jit(solution)/shard_map/pallas_call | solution.py:209
  28.3 1.6 %collective-permute-start.6 = (f32[256,128]{1,0:T(8,128)S(1)}, f32[256,128]{1,0:T(8,128)S(1)}, u32[]{:S(2)}, u32[]{:S(2)}) collective-permute-start(f32[256,128]{1,0:T(8,128)S(1)} %get-tuple-element.13.refs_2_.refs_1_), channel_id=1, source_target_pairs={{0,1},{1,0},{2,3},{3,2},{4,5},{5,4},{6,7},{7,6},{8,9},{9,8},{10,11... | collective-permute-start | bytes 393224 | tf_op jit(solution)/shard_map/ppermute | solution.py:486
  29.8 0.0 collective-permute-start.8
  29.8 0.6 collective-permute-start.7
  30.5 0.7 %collective-permute-start.10 = (f32[32,256]{1,0:T(8,128)S(1)}, f32[32,256]{1,0:T(8,128)S(1)}, u32[]{:S(2)}, u32[]{:S(2)}) collective-permute-start(f32[32,256]{1,0:T(8,128)S(1)} %get-tuple-element.15), channel_id=1, source_target_pairs={{2,5},{3,4},{4,3},{5,2},{6,9},{7,8},{8,7},{9,6},{10,13},{11,12},{1... | collective-permute-start | bytes 98312 | tf_op jit(solution)/shard_map/ppermute | solution.py:479
  31.1 0.8 %collective-permute-start.9 = (f32[32,256]{1,0:T(8,128)S(1)}, f32[32,256]{1,0:T(8,128)S(1)}, u32[]{:S(2)}, u32[]{:S(2)}) collective-permute-start(f32[32,256]{1,0:T(8,128)S(1)} %get-tuple-element.15), channel_id=1, source_target_pairs={{2,4},{4,2},{6,8},{8,6},{10,12},{12,10},{14,16},{16,14},{18,20},{2... | collective-permute-start | bytes 98312 | tf_op jit(solution)/shard_map/ppermute | solution.py:477
  32.0 1.5 %collective-permute-done.8.refs_5_ = f32[32,256]{1,0:T(8,128)S(1)} collective-permute-done((f32[32,256]{1,0:T(8,128)S(1)}, f32[32,256]{1,0:T(8,128)S(1)}, u32[]{:S(2)}, u32[]{:S(2)}) %collective-permute-start.8) | collective-permute-done | bytes 32800 | tf_op jit(solution)/shard_map/ppermute | solution.py:479
  33.5 0.0 collective-permute-done.7.refs_4_
  33.5 0.0 collective-permute-done.10.refs_7_
  33.5 0.0 collective-permute-done.9.refs_6_
  33.5 0.1 collective-permute-done.6.refs_3_.refs_2_
  33.6 7.2 %shard_map.117.refs_1_ = f32[256,128]{1,0:T(8,128)S(1)} custom-call(f32[1,6]{1,0:T(1,128)S(1)} %copy-done.5, f32[1]{0:T(128)S(6)} %copy.12.refs_1_, f32[256,128]{1,0:T(8,128)S(1)} %get-tuple-element.13.refs_2_.refs_1_, f32[256,128]{1,0:T(8,128)S(1)} %collective-permute-done.6.refs_3_.refs_2_, f32[32,256]{1,0:T(8,128)S(1)} %collective-permute-done.7.refs_4_, ...), custom_call_target="tpu_custom_call" | custom-call | flops 10000000000 | tf_op jit(solution)/shard_map/pallas_call | solution.py:209
  40.8 9.0 %collective-permute-start.14 = (f32[256,128]{1,0:T(8,128)S(1)}, f32[256,128]{1,0:T(8,128)S(1)}, u32[]{:S(2)}, u32[]{:S(2)}) collective-permute-start(f32[256,128]{1,0:T(8,128)S(1)} %shard_map.117.refs_1_), channel_id=1, source_target_pairs={{0,16},{2,18},{4,20},{6,22},{8,24},{10,26},{12,28},{14,30},{16,0},... | collective-permute-start | bytes 393224 | tf_op jit(solution)/shard_map/ppermute | solution.py:495
  49.8 0.7 %collective-permute-start.13 = (f32[256,128]{1,0:T(8,128)S(1)}, f32[256,128]{1,0:T(8,128)S(1)}, u32[]{:S(2)}, u32[]{:S(2)}) collective-permute-start(f32[256,128]{1,0:T(8,128)S(1)} %shard_map.117.refs_1_), channel_id=1, source_target_pairs={{0,8},{2,10},{4,12},{6,14},{8,0},{10,2},{12,4},{14,6},{16,24},{18,... | collective-permute-start | bytes 393224 | tf_op jit(solution)/shard_map/ppermute | solution.py:495
  50.5 0.7 %collective-permute-start.12 = (f32[256,128]{1,0:T(8,128)S(1)}, f32[256,128]{1,0:T(8,128)S(1)}, u32[]{:S(2)}, u32[]{:S(2)}) collective-permute-start(f32[256,128]{1,0:T(8,128)S(1)} %shard_map.117.refs_1_), channel_id=1, source_target_pairs={{0,4},{2,6},{4,0},{6,2},{8,12},{10,14},{12,8},{14,10},{16,20},{18,... | collective-permute-start | bytes 393224 | tf_op jit(solution)/shard_map/ppermute | solution.py:495
  51.2 0.3 collective-permute-start.11
  51.5 5.1 %collective-permute-done.14.refs_5_ = f32[256,128]{1,0:T(8,128)S(1)} collective-permute-done((f32[256,128]{1,0:T(8,128)S(1)}, f32[256,128]{1,0:T(8,128)S(1)}, u32[]{:S(2)}, u32[]{:S(2)}) %collective-permute-start.14) | collective-permute-done | bytes 131104 | tf_op jit(solution)/shard_map/ppermute | solution.py:495
  56.7 0.0 collective-permute-done.13.refs_4_
  56.7 0.0 collective-permute-done.12.refs_3_
  56.7 0.0 collective-permute-done.11.refs_2_
  56.7 0.7 %shard_map.118.refs_3_ = f32[256,128]{1,0:T(8,128)S(1)} custom-call(s32[4]{0:T(128)S(1)} %pad_add_fusion.refs_0_, f32[256,128]{1,0:T(8,128)S(1)} %shard_map.117.refs_1_, f32[256,128]{1,0:T(8,128)S(1)} %collective-permute-done.11.refs_2_, f32[256,128]{1,0:T(8,128)S(1)} %collective-permute-done.12.refs_3_, f32[256,128]{1,0:T(8,128)S(1)} %collective-permute-done.13.refs_4_, ...), custom_call_target="tpu_custom_call" | custom-call | tf_op jit(solution)/shard_map/pallas_call | solution.py:209
  57.4 0.6 collective-permute-start.15
  58.0 4.7 %collective-permute-done.15.refs_4_ = f32[256,128]{1,0:T(8,128)S(1)} collective-permute-done((f32[256,128]{1,0:T(8,128)S(1)}, f32[256,128]{1,0:T(8,128)S(1)}, u32[]{:S(2)}, u32[]{:S(2)}) %collective-permute-start.15) | collective-permute-done | bytes 131104 | tf_op jit(solution)/shard_map/ppermute | solution.py:486
  62.6 0.7 %shard_map.119 = (f32[2,128,128]{2,1,0:T(8,128)}, f32[2,128,128]{2,1,0:T(8,128)}) custom-call(f32[2,128,128]{2,1,0:T(8,128)S(1)} %copy-done.1, f32[256,128]{1,0:T(8,128)S(1)} %get-tuple-element.13.refs_2_.refs_1_, f32[256,128]{1,0:T(8,128)S(1)} %collective-permute-done.6.refs_3_.refs_2_, f32[256,128]{1,0:T(8,128)S(1)} %shard_map.118.refs_3_, ...), custom_call_target="tpu_custom_call" | custom-call | tf_op jit(solution)/shard_map/pallas_call | solution.py:209
  (12 shorter events, 0.0 us)
Async XLA Ops:
  0.6 0.9 %copy-start = (f32[2,128,128]{2,1,0:T(8,128)S(1)}, f32[2,128,128]{2,1,0:T(8,128)}, u32[]{:S(2)}) copy-start(f32[2,128,128]{2,1,0:T(8,128)} %refs_0_.5) | copy-start | bytes 393220
  1.5 0.9 %copy-start.3 = (s32[2,128,128]{2,1,0:T(8,128)S(1)}, s32[2,128,128]{2,1,0:T(8,128)}, u32[]{:S(2)}) copy-start(s32[2,128,128]{2,1,0:T(8,128)} %param.11) | copy-start | bytes 393220
  2.4 1.4 %copy-start.2 = (f32[2,1,6,25,25]{4,1,3,2,0:T(1,128)S(1)}, f32[2,1,6,25,25]{4,1,3,2,0:T(1,128)}, u32[]{:S(2)}) copy-start(f32[2,1,6,25,25]{4,1,3,2,0:T(1,128)} %param.12) | copy-start | bytes 90004
  2.4 1.4 %copy-start.7 = (bf16[1408,256]{1,0:T(8,128)(2,1)S(1)}, bf16[1408,256]{1,0:T(8,128)(2,1)}, u32[]{:S(2)}) copy-start(bf16[1408,256]{1,0:T(8,128)(2,1)} %constant.4.clone.refs_1_) | copy-start | bytes 2162692
  2.7 3.4 %collective-permute-start = (f32[48,256]{1,0:T(8,128)S(1)}, f32[48,256]{1,0:T(8,128)S(1)}, u32[]{:S(2)}, u32[]{:S(2)}) collective-permute-start(f32[48,256]{1,0:T(8,128)S(1)} %get-tuple-element.10), channel_id=1, source_target_pairs={{0,2},{2,0},{4,6},{6,4},{8,10},{10,8},{12,14},{14,12},{16,18},{18,... | collective-permute-start | bytes 147464 | tf_op jit(solution)/shard_map/ppermute | solution.py:477
  3.2 2.8 %collective-permute-start.1 = (f32[48,256]{1,0:T(8,128)S(1)}, f32[48,256]{1,0:T(8,128)S(1)}, u32[]{:S(2)}, u32[]{:S(2)}) collective-permute-start(f32[48,256]{1,0:T(8,128)S(1)} %get-tuple-element.11), channel_id=1, source_target_pairs={{2,4},{4,2},{6,8},{8,6},{10,12},{12,10},{14,16},{16,14},{18,20},{2... | collective-permute-start | bytes 147464 | tf_op jit(solution)/shard_map/ppermute | solution.py:477
  3.9 2.2 %copy-start.1 = (f32[2,128,128]{2,1,0:T(8,128)S(1)}, f32[2,128,128]{2,1,0:T(8,128)}, u32[]{:S(2)}) copy-start(f32[2,128,128]{2,1,0:T(8,128)} %refs_0_.5) | copy-start | bytes 393220
  3.9 2.2 %copy-start.4 = (s32[2,128,128]{2,1,0:T(8,128)S(1)}, s32[2,128,128]{2,1,0:T(8,128)}, u32[]{:S(2)}) copy-start(s32[2,128,128]{2,1,0:T(8,128)} %param.11) | copy-start | bytes 393220
  3.9 2.2 %copy-start.5 = (f32[1,6]{1,0:T(1,128)S(1)}, f32[1,6]{1,0:T(1,128)}, u32[]{:S(2)}) copy-start(f32[1,6]{1,0:T(1,128)} %refs_0_.4) | copy-start | bytes 76
  3.9 2.2 %copy-start.6 = (bf16[4000,256]{1,0:T(8,128)(2,1)S(1)}, bf16[4000,256]{1,0:T(8,128)(2,1)}, u32[]{:S(2)}) copy-start(bf16[4000,256]{1,0:T(8,128)(2,1)} %constant.5.clone.refs_7_.refs_11_) | copy-start | bytes 6144004
  6.0 16.7 %copy-start.8 = (s32[2]{0:T(128)S(1)}, s32[2]{0:T(128)}, u32[]{:S(2)}) copy-start(s32[2]{0:T(128)} %param.16) | copy-start | bytes 28
  6.0 16.7 %copy-start.9 = (s32[2]{0:T(128)S(1)}, s32[2]{0:T(128)}, u32[]{:S(2)}) copy-start(s32[2]{0:T(128)} %param.15) | copy-start | bytes 28
  13.4 13.8 %collective-permute-start.5 = (f32[256,128]{1,0:T(8,128)S(1)}, f32[256,128]{1,0:T(8,128)S(1)}, u32[]{:S(2)}, u32[]{:S(2)}) collective-permute-start(f32[256,128]{1,0:T(8,128)S(1)} %get-tuple-element.12.refs_1_), channel_id=1, source_target_pairs={{0,16},{2,18},{4,20},{6,22},{8,24},{10,26},{12,28},{14,30},{16,0},... | collective-permute-start | bytes 393224 | tf_op jit(solution)/shard_map/ppermute | solution.py:495
  20.6 6.8 %collective-permute-start.4 = (f32[256,128]{1,0:T(8,128)S(1)}, f32[256,128]{1,0:T(8,128)S(1)}, u32[]{:S(2)}, u32[]{:S(2)}) collective-permute-start(f32[256,128]{1,0:T(8,128)S(1)} %get-tuple-element.12.refs_1_), channel_id=1, source_target_pairs={{0,8},{2,10},{4,12},{6,14},{8,0},{10,2},{12,4},{14,6},{16,24},{18,... | collective-permute-start | bytes 393224 | tf_op jit(solution)/shard_map/ppermute | solution.py:495
  22.2 5.2 %collective-permute-start.3 = (f32[256,128]{1,0:T(8,128)S(1)}, f32[256,128]{1,0:T(8,128)S(1)}, u32[]{:S(2)}, u32[]{:S(2)}) collective-permute-start(f32[256,128]{1,0:T(8,128)S(1)} %get-tuple-element.12.refs_1_), channel_id=1, source_target_pairs={{0,4},{2,6},{4,0},{6,2},{8,12},{10,14},{12,8},{14,10},{16,20},{18,... | collective-permute-start | bytes 393224 | tf_op jit(solution)/shard_map/ppermute | solution.py:495
  22.7 4.7 %collective-permute-start.2 = (f32[256,128]{1,0:T(8,128)S(1)}, f32[256,128]{1,0:T(8,128)S(1)}, u32[]{:S(2)}, u32[]{:S(2)}) collective-permute-start(f32[256,128]{1,0:T(8,128)S(1)} %get-tuple-element.12.refs_1_), channel_id=1, source_target_pairs={{0,2},{2,0},{4,6},{6,4},{8,10},{10,8},{12,14},{14,12},{16,18},{18,... | collective-permute-start | bytes 393224 | tf_op jit(solution)/shard_map/ppermute | solution.py:495
  28.3 5.4 %collective-permute-start.6 = (f32[256,128]{1,0:T(8,128)S(1)}, f32[256,128]{1,0:T(8,128)S(1)}, u32[]{:S(2)}, u32[]{:S(2)}) collective-permute-start(f32[256,128]{1,0:T(8,128)S(1)} %get-tuple-element.13.refs_2_.refs_1_), channel_id=1, source_target_pairs={{0,1},{1,0},{2,3},{3,2},{4,5},{5,4},{6,7},{7,6},{8,9},{9,8},{10,11... | collective-permute-start | bytes 393224 | tf_op jit(solution)/shard_map/ppermute | solution.py:486
  29.8 3.7 %collective-permute-start.8 = (f32[32,256]{1,0:T(8,128)S(1)}, f32[32,256]{1,0:T(8,128)S(1)}, u32[]{:S(2)}, u32[]{:S(2)}) collective-permute-start(f32[32,256]{1,0:T(8,128)S(1)} %get-tuple-element.14), channel_id=1, source_target_pairs={{0,3},{1,2},{2,1},{3,0},{4,7},{5,6},{6,5},{7,4},{8,11},{9,10},{10,... | collective-permute-start | bytes 98312 | tf_op jit(solution)/shard_map/ppermute | solution.py:479
  29.8 3.7 %collective-permute-start.7 = (f32[32,256]{1,0:T(8,128)S(1)}, f32[32,256]{1,0:T(8,128)S(1)}, u32[]{:S(2)}, u32[]{:S(2)}) collective-permute-start(f32[32,256]{1,0:T(8,128)S(1)} %get-tuple-element.14), channel_id=1, source_target_pairs={{0,2},{2,0},{4,6},{6,4},{8,10},{10,8},{12,14},{14,12},{16,18},{18,... | collective-permute-start | bytes 98312 | tf_op jit(solution)/shard_map/ppermute | solution.py:477
  30.5 3.1 %collective-permute-start.10 = (f32[32,256]{1,0:T(8,128)S(1)}, f32[32,256]{1,0:T(8,128)S(1)}, u32[]{:S(2)}, u32[]{:S(2)}) collective-permute-start(f32[32,256]{1,0:T(8,128)S(1)} %get-tuple-element.15), channel_id=1, source_target_pairs={{2,5},{3,4},{4,3},{5,2},{6,9},{7,8},{8,7},{9,6},{10,13},{11,12},{1... | collective-permute-start | bytes 98312 | tf_op jit(solution)/shard_map/ppermute | solution.py:479
  31.1 2.4 %collective-permute-start.9 = (f32[32,256]{1,0:T(8,128)S(1)}, f32[32,256]{1,0:T(8,128)S(1)}, u32[]{:S(2)}, u32[]{:S(2)}) collective-permute-start(f32[32,256]{1,0:T(8,128)S(1)} %get-tuple-element.15), channel_id=1, source_target_pairs={{2,4},{4,2},{6,8},{8,6},{10,12},{12,10},{14,16},{16,14},{18,20},{2... | collective-permute-start | bytes 98312 | tf_op jit(solution)/shard_map/ppermute | solution.py:477
  40.8 15.9 %collective-permute-start.14 = (f32[256,128]{1,0:T(8,128)S(1)}, f32[256,128]{1,0:T(8,128)S(1)}, u32[]{:S(2)}, u32[]{:S(2)}) collective-permute-start(f32[256,128]{1,0:T(8,128)S(1)} %shard_map.117.refs_1_), channel_id=1, source_target_pairs={{0,16},{2,18},{4,20},{6,22},{8,24},{10,26},{12,28},{14,30},{16,0},... | collective-permute-start | bytes 393224 | tf_op jit(solution)/shard_map/ppermute | solution.py:495
  49.8 6.8 %collective-permute-start.13 = (f32[256,128]{1,0:T(8,128)S(1)}, f32[256,128]{1,0:T(8,128)S(1)}, u32[]{:S(2)}, u32[]{:S(2)}) collective-permute-start(f32[256,128]{1,0:T(8,128)S(1)} %shard_map.117.refs_1_), channel_id=1, source_target_pairs={{0,8},{2,10},{4,12},{6,14},{8,0},{10,2},{12,4},{14,6},{16,24},{18,... | collective-permute-start | bytes 393224 | tf_op jit(solution)/shard_map/ppermute | solution.py:495
  50.5 6.1 %collective-permute-start.12 = (f32[256,128]{1,0:T(8,128)S(1)}, f32[256,128]{1,0:T(8,128)S(1)}, u32[]{:S(2)}, u32[]{:S(2)}) collective-permute-start(f32[256,128]{1,0:T(8,128)S(1)} %shard_map.117.refs_1_), channel_id=1, source_target_pairs={{0,4},{2,6},{4,0},{6,2},{8,12},{10,14},{12,8},{14,10},{16,20},{18,... | collective-permute-start | bytes 393224 | tf_op jit(solution)/shard_map/ppermute | solution.py:495
  51.2 5.4 %collective-permute-start.11 = (f32[256,128]{1,0:T(8,128)S(1)}, f32[256,128]{1,0:T(8,128)S(1)}, u32[]{:S(2)}, u32[]{:S(2)}) collective-permute-start(f32[256,128]{1,0:T(8,128)S(1)} %shard_map.117.refs_1_), channel_id=1, source_target_pairs={{0,2},{2,0},{4,6},{6,4},{8,10},{10,8},{12,14},{14,12},{16,18},{18,... | collective-permute-start | bytes 393224 | tf_op jit(solution)/shard_map/ppermute | solution.py:495
  57.4 5.2 %collective-permute-start.15 = (f32[256,128]{1,0:T(8,128)S(1)}, f32[256,128]{1,0:T(8,128)S(1)}, u32[]{:S(2)}, u32[]{:S(2)}) collective-permute-start(f32[256,128]{1,0:T(8,128)S(1)} %shard_map.118.refs_3_), channel_id=1, source_target_pairs={{0,1},{1,0},{2,3},{3,2},{4,5},{5,4},{6,7},{7,6},{8,9},{9,8},{10,11... | collective-permute-start | bytes 393224 | tf_op jit(solution)/shard_map/ppermute | solution.py:486

commit v7 on v6

--- a/solution.py
+++ b/solution.py
@@ -251,7 +251,7 @@
     send_edges(*edges_of(EDGE, mask_ref[...], target), a_ref, b_ref)
 
 
-def spectra_kernel(kern, ker_ref, tb, h_ref, hs_ref):
+def spectra_kernel(kern, w_ref, ker_ref, tb, h_ref, hs_ref):
     hs_ref[...] = jnp.zeros_like(hs_ref)
     for k in range(kern):
         for part in range(2):
@@ -263,8 +263,9 @@
     for c in range(2 * kern):
         lanes = slice(128 * (c // 4), 128 * (c // 4) + 128)
         spec = dot3(z_hi[:, lanes], z_lo[:, lanes], tb(f"ky{c % 4}_hi"), tb(f"ky{c % 4}_lo"))
+        root = jnp.sqrt(jnp.full((1, YB), w_ref[0, c // 2], f32))
         for j, comp in enumerate(signed(spec)):
-            h_ref[c, j] = comp
+            h_ref[c, j] = root * comp
 
 
 def sides(from_a, from_b, tb):
@@ -288,113 +289,120 @@
             f_ref[t, j] = comp if base is None else base[t, j] - STEP_RATE * comp
 
 
-def gradient_body(kern, last, f_ref, tgt_ref, h_ref, w_ref, thr_ref, tb, g_ref, work):
-    fld, inten, tot, a_hi, a_lo, b_cat, c_cat = work
+def gradient_body(kern, last, f_ref, tgt_ref, h_ref, thr_ref, tb, g_ref, work):
+    fld, inten, tot, a_hi, a_lo, b_cat, r_cat, w_cat = work
     chains = [(t, k) for t in range(2) for k in range(kern)]
-    rounds = range(len(chains) + 2)
+    lag = kern + 2
 
     def at(i):
         return chains[i] if 0 <= i < len(chains) else None
-
-    for i in rounds:
-        new, mid, old = at(i), at(i - 1), at(i - 2)
-        if mid:
-            slot = (i - 1) % 2
-            z_one = dot(a_hi[slot], tb("y2"))
-            z_two = dot(a_lo[slot], tb("y2", 0))
-        if new:
-            t, k = new
-            slot = i % 2
-            for part in range(2):
-                hpr, hpi, hmr, hmi = (h_ref[2 * k + part, j] for j in range(4))
-                fpr, fpi, fmr, fmi = (f_ref[t, j] for j in range(4))
-                pr, pi = hpr * fpr - hpi * fpi, hpr * fpi + hpi * fpr
-                mr, mi = hmr * fmr - hmi * fmi, hmr * fmi + hmi * fmr
-                p_hi, p_lo = split(even_odd(pr, pi, mr, mi))
-                rows = slice(2 * XB * part, 2 * XB * part + 2 * XB)
-                a_hi[slot, rows] = p_hi
-                a_lo[slot, rows] = p_lo
-        if old:
-            slot = (i - 2) % 2
-            field = dot(tb("x2"), b_cat[slot])
-            t, k = old
-            fld[t, k] = field
-            re, im = field[:, :CORE], field[:, CORE:]
-            power = w_ref[0, k] * (re * re + im * im)
-            inten[t] = power if k == 0 else inten[t] + power
-        if mid:
-            slot = (i - 1) % 2
-            z = z_one[:, :CORE] + (z_one[:, CORE:] + z_two)
-            z_hi, z_lo = split(jnp.concatenate([z[: 2 * XB], z[2 * XB :]], axis=1))
-            for j, piece in enumerate((z_hi, z_hi, z_lo)):
-                b_cat[slot, 2 * XB * j : 2 * XB * j + 2 * XB] = piece
 
     tile = lax.axis_index("tile")
     first = jnp.where(tile == 0, WIDE, HALO) - ROW0
     end = jnp.where(tile == last, WIDE + CORE, WIDE + CORE + HALO) - ROW0
     row = lax.broadcasted_iota(jnp.int32, (ROWS, CORE), 0)
     inside = (row >= first) & (row < end)
-    for t in range(2):
+    lane = lax.broadcasted_iota(jnp.int32, (1, 2 * YB), 1)
+    bin_at = lax.rem(lane, YB)
+    weight = jnp.where((bin_at == 0) | (bin_at == NU - 1), 1.0, 2.0) / (NX * NY)
+    weight = jnp.where(lane < YB, weight, -weight)
+
+    def spectra_of(t, k, part):
+        return [h_ref[2 * k + part, j] for j in range(4)], [f_ref[t, j] for j in range(4)]
+
+    def products(t, k, slot):
+        for part in range(2):
+            (hpr, hpi, hmr, hmi), (fpr, fpi, fmr, fmi) = spectra_of(t, k, part)
+            pr, pi = hpr * fpr - hpi * fpi, hpr * fpi + hpi * fpr
+            mr, mi = hmr * fmr - hmi * fmi, hmr * fmi + hmi * fmr
+            p_hi, p_lo = split(even_odd(pr, pi, mr, mi))
+            rows = slice(2 * XB * part, 2 * XB * part + 2 * XB)
+            a_hi[slot, rows] = p_hi
+            a_lo[slot, rows] = p_lo
+
+    def store_three(ref, slot, pieces, height):
+        for j, piece in enumerate(pieces):
+            ref[slot, height * j : height * j + height] = piece
+
+    def field_of(t, k, slot):
+        field = dot(tb("x2"), b_cat[slot])
+        fld[t, k] = field
+        re, im = field[:, :CORE], field[:, CORE:]
+        power = re * re + im * im
+        inten[t] = power if k == 0 else inten[t] + power
+
+    def slope_of(t):
         resist = jax.nn.sigmoid(STEEPNESS * (inten[t] - thr_ref[0]))
         target = tgt_ref[:, CORE * t : CORE * t + CORE]
         slope = 2.0 * (resist - target) * STEEPNESS * resist * (1.0 - resist)
         inten[t] = jnp.where(inside, 2.0 * slope, 0.0)
-    for i in rounds:
+
+    def scaled_field(t, k, slot):
+        slope, field = inten[t], fld[t, k]
+        r_hi, r_lo = split(
+            jnp.concatenate([slope * field[:, :CORE], slope * field[:, CORE:]], axis=1)
+        )
+        store_three(r_cat, slot, (r_hi, r_hi, r_lo), ROWS)
+
+    def add_back(t, k, slot):
+        specs = dot(w_cat[slot], tb("y3"))
+        acc = [0.0] * 4 if k == 0 else [tot[t, j] for j in range(4)]
+        for part in range(2):
+            spec = specs[2 * XB * part : 2 * XB * part + 2 * XB]
+            cc, cs = spec[:XB, :YB], spec[:XB, YB:]
+            sc, ss = spec[XB:, :YB], spec[XB:, YB:]
+            bpr, neg, bmr, bmi = cc - ss, cs + sc, cc + ss, sc - cs
+            hpr, hpi, hmr, hmi = (h_ref[2 * k + part, j] for j in range(4))
+            acc[0] = acc[0] + (hpr * bpr - hpi * neg)
+            acc[1] = acc[1] - (hpr * neg + hpi * bpr)
+            acc[2] = acc[2] + (hmr * bmr + hmi * bmi)
+            acc[3] = acc[3] + (hmr * bmi - hmi * bmr)
+        for j in range(4):
+            tot[t, j] = acc[j]
+
+    def finish(t):
+        r_hi, r_lo = split(even_odd(*(tot[t, j] for j in range(4))))
+        u = dot(tb("x4"), jnp.concatenate([r_hi, r_hi, r_lo], axis=0))
+        u_hi, u_lo = split(weight * u)
+        term = dot3(tb(f"by{t}_hi"), tb(f"by{t}_lo"), u_hi, u_lo, dot_nt)
+        g_ref[...] = term if t == 0 else g_ref[...] + term
+
+    for i in range(len(chains) + lag + 2):
         new, mid, old = at(i), at(i - 1), at(i - 2)
+        back, back_mid, back_old = at(i - lag), at(i - lag - 1), at(i - lag - 2)
+        slot, other = i % 2, (i + 1) % 2
         if mid:
-            slot = (i - 1) % 2
-            w_now = dot(tb("x3"), b_cat[slot, : 3 * ROWS])
+            z_one = dot(a_hi[other], tb("y2"))
+            z_two = dot(a_lo[other], tb("y2", 0))
         if new:
-            t, k = new
-            slot = i % 2
-            scaled = w_ref[0, k] * inten[t]
-            field = fld[t, k]
-            r_hi, r_lo = split(
-                jnp.concatenate([scaled * field[:, :CORE], scaled * field[:, CORE:]], axis=1)
-            )
-            for j, piece in enumerate((r_hi, r_hi, r_lo)):
-                b_cat[slot, ROWS * j : ROWS * j + ROWS] = piece
+            products(*new, slot)
+        if back_mid:
+            w_now = dot(tb("x3"), r_cat[other])
+        if back:
+            scaled_field(*back, slot)
         if old:
-            slot = (i - 2) % 2
-            t, k = old
-            specs = dot(c_cat[slot], tb("y3"))
-            acc = [0.0] * 4 if k == 0 else [tot[t, j] for j in range(4)]
-            for part in range(2):
-                spec = specs[2 * XB * part : 2 * XB * part + 2 * XB]
-                cc, cs = spec[:XB, :YB], spec[:XB, YB:]
-                sc, ss = spec[XB:, :YB], spec[XB:, YB:]
-                bpr, neg, bmr, bmi = cc - ss, cs + sc, cc + ss, sc - cs
-                hpr, hpi, hmr, hmi = (h_ref[2 * k + part, j] for j in range(4))
-                acc[0] = acc[0] + (hpr * bpr - hpi * neg)
-                acc[1] = acc[1] - (hpr * neg + hpi * bpr)
-                acc[2] = acc[2] + (hmr * bmr + hmi * bmi)
-                acc[3] = acc[3] + (hmr * bmi - hmi * bmr)
-            for j in range(4):
-                tot[t, j] = acc[j]
+            field_of(*old, slot)
+        if back_old:
+            add_back(*back_old, slot)
         if mid:
-            slot = (i - 1) % 2
+            z = z_one[:, :CORE] + (z_one[:, CORE:] + z_two)
+            z_hi, z_lo = split(jnp.concatenate([z[: 2 * XB], z[2 * XB :]], axis=1))
+            store_three(b_cat, other, (z_hi, z_hi, z_lo), 2 * XB)
+        if back_mid:
             w_hi, w_lo = split(w_now)
             for part in range(2):
                 rows = slice(2 * XB * part, 2 * XB * part + 2 * XB)
                 lanes = slice(CORE * part, CORE * part + CORE)
                 for j, piece in enumerate((w_hi, w_lo, w_hi)):
-                    c_cat[slot, rows, CORE * j : CORE * j + CORE] = piece[:, lanes]
-
-    lane = lax.broadcasted_iota(jnp.int32, (1, 2 * YB), 1)
-    bin_at = lax.rem(lane, YB)
-    weight = jnp.where((bin_at == 0) | (bin_at == NU - 1), 1.0, 2.0) / (NX * NY)
-    weight = jnp.where(lane < YB, weight, -weight)
-    out = None
-    for t in range(2):
-        r_hi, r_lo = split(even_odd(*(tot[t, j] for j in range(4))))
-        u_hi, u_lo = split(weight * dot(tb("x4"), jnp.concatenate([r_hi, r_hi, r_lo], axis=0)))
-        term = dot3(tb(f"by{t}_hi"), tb(f"by{t}_lo"), u_hi, u_lo, dot_nt)
-        out = term if out is None else out + term
-    g_ref[...] = out
+                    w_cat[other, rows, CORE * j : CORE * j + CORE] = piece[:, lanes]
+        if old and old[1] == kern - 1:
+            slope_of(old[0])
+        if back_old and back_old[1] == kern - 1:
+            finish(back_old[0])
 
 
 def first_kernel(
-    kern, last, w_ref, thr_ref, mask_ref, target_ref, a_ref, b_ref, h_ref, tb,
+    kern, last, thr_ref, mask_ref, target_ref, a_ref, b_ref, h_ref, tb,
     g_ref, f_ref, tgt_ref, *work,
 ):
     m_hi, m_lo = split(mask_ref[...])
@@ -406,11 +414,11 @@
         + dot(tb("sel_halo", 0)[:, :EDGE], left)
         + dot(tb("sel_halo", 1)[:, :EDGE], right)
     )
-    gradient_body(kern, last, f_ref, tgt_ref, h_ref, w_ref, thr_ref, tb, g_ref, work)
+    gradient_body(kern, last, f_ref, tgt_ref, h_ref, thr_ref, tb, g_ref, work)
 
 
 def later_kernel(
-    kern, last, w_ref, thr_ref, mine_ref, peer_ref, a_ref, a2_ref, b_ref, b2_ref, f_in_ref, tgt_ref,
+    kern, last, thr_ref, mine_ref, peer_ref, a_ref, a2_ref, b_ref, b2_ref, f_in_ref, tgt_ref,
     h_ref, tb, g_ref, f_ref, *work,
 ):
     s_hi, s_lo = split(mine_ref[...] + peer_ref[...])
@@ -419,7 +427,7 @@
     v, _, _ = sides(from_a, from_b, tb)
     v = v + dot3(tb("cx_own_hi"), tb("cx_own_lo"), s_hi, s_lo, dot_nt)
     to_spectrum(v, tb, f_ref, f_in_ref)
-    gradient_body(kern, last, f_ref, tgt_ref, h_ref, w_ref, thr_ref, tb, g_ref, work)
+    gradient_body(kern, last, f_ref, tgt_ref, h_ref, thr_ref, tb, g_ref, work)
 
 
 def match_kernel(n_got, table_ref, own_ref, *refs):
@@ -511,6 +519,7 @@
         pltpu.VMEM((2, 4 * XB, 2 * YB), bf16),
         pltpu.VMEM((2, 4 * XB, 2 * YB), bf16),
         pltpu.VMEM((2, 6 * XB, 2 * CORE), bf16),
+        pltpu.VMEM((2, 3 * ROWS, 2 * CORE), bf16),
         pltpu.VMEM((2, 4 * XB, 3 * CORE), bf16),
     ]
 
@@ -523,19 +532,20 @@
     (spectra,) = call(
         functools.partial(spectra_kernel, kern),
         "spec",
-        [kernels.transpose(0, 2, 3, 1, 4)],
+        [socs_weights, kernels.transpose(0, 2, 3, 1, 4)],
         [jax.ShapeDtypeStruct((2 * kern, 4, XB, YB), f32)],
         [pltpu.VMEM((32 * 2 * kern, 128), f32)],
+        smem=(0,),
         flops=3 * 10**9,
         nbytes=4 * 10**6,
     )
     grad, freq_now, goals = call(
         functools.partial(first_kernel, kern, n_tile - 1),
         "grad",
-        [socs_weights, thresholds, mask_rows, target_rows, from_a, from_b, spectra],
+        [thresholds, mask_rows, target_rows, from_a, from_b, spectra],
         [strip, freq, goal],
         scratch,
-        smem=(0, 1),
+        smem=(0,),
         flops=10**10,
     )
     moves = []
@@ -563,10 +573,10 @@
         grad, *rest = call(
             functools.partial(later_kernel, kern, n_tile - 1),
             "grad",
-            [socs_weights, thresholds, *moves[-2:], *rims, freq_now, goals, spectra],
+            [thresholds, *moves[-2:], *rims, freq_now, goals, spectra],
             [strip, freq] if kept else [strip],
             scratch if kept else [pltpu.VMEM(freq.shape, f32)] + scratch,
-            smem=(0, 1),
+            smem=(0,),
             flops=10**10,
         )
         freq_now = rest[0] if kept else None

time: 63.6 us -> 62.9 us (0.989)
  transfers between devices with their start and end apart: 16 -> 16, of which waited for: 6 -> 6; matrix products, arithmetic and copies ran while one was open for 0% -> 0% of each run, Pallas kernels for 2% -> 3%
where the time goes in v7:
time: 62.9 us; the launch traced here: 62.7 us
  starting transfers between devices  24.9 us (40%)
  Pallas kernels  18.2 us (29%)
  waiting for transfers between devices  16.1 us (26%)
  local copies, waits for them, and re-layouts  1.85 us (3%)
  between operations  1.5 us (2%)
    ppermute x8, starting transfers between devices, from_partners(): lax.ppermute(grad, 'tile', [(i, i ^ bit) for i in range(n_tile)])  19.4 us
    pallas_call x7, Pallas kernels, call(): pl.pallas_call(wrapped, out_shape=out_shape, in_specs=[sm if i in smem el...  18.2 us
    ppermute x8, waiting for transfers between devices, from_partners(): lax.ppermute(grad, 'tile', [(i, i ^ bit) for i in range(n_tile)])  9.78 us
    ppermute x2, waiting for transfers between devices, depth_pair(): peer = lax.ppermute(x, 'depth', [(i, i ^ bit) for i in range(n_depth)])  4.79 us
    ppermute x4, starting transfers between devices, move(): return lax.ppermute(x, 'tile', pairs)  2.63 us
    ppermute x2, starting transfers between devices, depth_pair(): peer = lax.ppermute(x, 'depth', [(i, i ^ bit) for i in range(n_depth)])  2.13 us
    unnamed x20, local copies, waits for them, and re-layouts  1.85 us
    ppermute x2, waiting for transfers between devices, move(): return lax.ppermute(x, ('tile', 'depth'), both)  1.55 us
  transfers between devices with their start and end apart: 16, of which 6 were waited for; matrix products, arithmetic and copies ran while one was open for 0% of the time, Pallas kernels for 3%

profile of v7, /device:TPU:0, one launch (start us, length us, event | category | flops | bytes accessed | tf_op | source)
XLA Modules:
  0.0 62.7 jit_solution(8904027048659136400)
XLA Ops:
  0.6 0.0 copy-start
  0.6 0.9 %copy-done = f32[2,128,128]{2,1,0:T(8,128)S(1)} copy-done((f32[2,128,128]{2,1,0:T(8,128)S(1)}, f32[2,128,128]{2,1,0:T(8,128)}, u32[]{:S(2)}) %copy-start) | copy-done | bytes 131096
  1.5 0.9 %copy-done.3 = s32[2,128,128]{2,1,0:T(8,128)S(1)} copy-done((s32[2,128,128]{2,1,0:T(8,128)S(1)}, s32[2,128,128]{2,1,0:T(8,128)}, u32[]{:S(2)}) %copy-start.3) | copy-done | bytes 131096
  2.4 0.2 shard_map.113
  2.7 0.5 collective-permute-start
  3.2 0.7 %collective-permute-start.1 = (f32[48,256]{1,0:T(8,128)S(1)}, f32[48,256]{1,0:T(8,128)S(1)}, u32[]{:S(2)}, u32[]{:S(2)}) collective-permute-start(f32[48,256]{1,0:T(8,128)S(1)} %get-tuple-element.11), channel_id=1, source_target_pairs={{2,4},{4,2},{6,8},{8,6},{10,12},{12,10},{14,16},{16,14},{18,20},{2... | collective-permute-start | bytes 147464 | tf_op jit(solution)/shard_map/ppermute | solution.py:485
  3.9 0.0 copy-start.1
  3.9 0.0 copy-start.4
  3.9 0.0 copy-start.6
  3.9 2.0 %shard_map.114.refs_5_.refs_9_ = f32[12,4,96,128]{3,2,1,0:T(8,128)S(1)} custom-call(f32[1,6]{1,0:T(1,128)S(1)} %copy-done.5, f32[2,6,25,1,25]{4,3,2,1,0:T(1,128)S(1)} %bitcast.5, bf16[1408,256]{1,0:T(8,128)(2,1)S(1)} %copy-done.7), custom_call_target="tpu_custom_call" | custom-call | flops 3000000000 | bytes 4000000 | tf_op jit(solution)/shard_map/pallas_call | solution.py:209
  6.6 0.0 copy-start.8
  6.6 0.0 copy-start.9
  6.6 0.0 collective-permute-done.refs_3_
  6.6 0.0 collective-permute-done.1.refs_4_
  6.6 6.9 %shard_map.115 = (f32[256,128]{1,0:T(8,128)S(1)}, f32[2,4,96,128]{3,2,1,0:T(8,128)S(1)}, f32[160,256]{1,0:T(8,128)S(1)}) custom-call(f32[1]{0:T(128)S(6)} %copy.12.refs_0_, f32[256,128]{1,0:T(8,128)S(1)} %bitcast.4, s32[256,128]{1,0:T(8,128)S(1)} %bitcast.7, f32[48,256]{1,0:T(8,128)S(1)} %collective-permute-done.refs_3_, ...), custom_call_target="tpu_custom_call" | custom-call | flops 10000000000 | tf_op jit(solution)/shard_map/pallas_call | solution.py:209
  13.5 6.7 %collective-permute-start.5 = (f32[256,128]{1,0:T(8,128)S(1)}, f32[256,128]{1,0:T(8,128)S(1)}, u32[]{:S(2)}, u32[]{:S(2)}) collective-permute-start(f32[256,128]{1,0:T(8,128)S(1)} %get-tuple-element.12.refs_1_), channel_id=1, source_target_pairs={{0,16},{2,18},{4,20},{6,22},{8,24},{10,26},{12,28},{14,30},{16,0},... | collective-permute-start | bytes 393224 | tf_op jit(solution)/shard_map/ppermute | solution.py:503
  20.2 1.6 %collective-permute-start.4 = (f32[256,128]{1,0:T(8,128)S(1)}, f32[256,128]{1,0:T(8,128)S(1)}, u32[]{:S(2)}, u32[]{:S(2)}) collective-permute-start(f32[256,128]{1,0:T(8,128)S(1)} %get-tuple-element.12.refs_1_), channel_id=1, source_target_pairs={{0,8},{2,10},{4,12},{6,14},{8,0},{10,2},{12,4},{14,6},{16,24},{18,... | collective-permute-start | bytes 393224 | tf_op jit(solution)/shard_map/ppermute | solution.py:503
  21.8 0.5 collective-permute-start.3
  22.3 0.0 collective-permute-start.2
  22.3 0.1 pad_add_fusion.refs_0_
  22.4 4.4 %collective-permute-done.5.refs_5_ = f32[256,128]{1,0:T(8,128)S(1)} collective-permute-done((f32[256,128]{1,0:T(8,128)S(1)}, f32[256,128]{1,0:T(8,128)S(1)}, u32[]{:S(2)}, u32[]{:S(2)}) %collective-permute-start.5) | collective-permute-done | bytes 131104 | tf_op jit(solution)/shard_map/ppermute | solution.py:503
  26.8 0.2 collective-permute-done.4.refs_4_
  27.0 0.0 collective-permute-done.3.refs_3_
  27.0 0.0 collective-permute-done.2.refs_2_
  27.0 0.9 %shard_map.116 = (f32[256,128]{1,0:T(8,128)S(1)}, f32[32,256]{1,0:T(8,128)S(1)}, f32[32,256]{1,0:T(8,128)S(1)}) custom-call(s32[4]{0:T(128)S(1)} %pad_add_fusion.refs_0_, f32[256,128]{1,0:T(8,128)S(1)} %get-tuple-element.12.refs_1_, f32[256,128]{1,0:T(8,128)S(1)} %collective-permute-done.2.refs_2_, f32[256,128]{1,0:T(8,128)S(1)} %collective-permute-done.3.refs_3_, ...), custom_call_target="tpu_custom_call" | custom-call | tf_op jit(solution)/shard_map/pallas_call | solution.py:209
  27.9 1.6 %collective-permute-start.6 = (f32[256,128]{1,0:T(8,128)S(1)}, f32[256,128]{1,0:T(8,128)S(1)}, u32[]{:S(2)}, u32[]{:S(2)}) collective-permute-start(f32[256,128]{1,0:T(8,128)S(1)} %get-tuple-element.13.refs_1_), channel_id=1, source_target_pairs={{0,1},{1,0},{2,3},{3,2},{4,5},{5,4},{6,7},{7,6},{8,9},{9,8},{10,11... | collective-permute-start | bytes 393224 | tf_op jit(solution)/shard_map/ppermute | solution.py:494
  29.4 0.0 collective-permute-start.8
  29.4 0.6 collective-permute-start.7
  30.0 0.7 %collective-permute-start.10 = (f32[32,256]{1,0:T(8,128)S(1)}, f32[32,256]{1,0:T(8,128)S(1)}, u32[]{:S(2)}, u32[]{:S(2)}) collective-permute-start(f32[32,256]{1,0:T(8,128)S(1)} %get-tuple-element.15), channel_id=1, source_target_pairs={{2,5},{3,4},{4,3},{5,2},{6,9},{7,8},{8,7},{9,6},{10,13},{11,12},{1... | collective-permute-start | bytes 98312 | tf_op jit(solution)/shard_map/ppermute | solution.py:487
  30.7 0.8 %collective-permute-start.9 = (f32[32,256]{1,0:T(8,128)S(1)}, f32[32,256]{1,0:T(8,128)S(1)}, u32[]{:S(2)}, u32[]{:S(2)}) collective-permute-start(f32[32,256]{1,0:T(8,128)S(1)} %get-tuple-element.15), channel_id=1, source_target_pairs={{2,4},{4,2},{6,8},{8,6},{10,12},{12,10},{14,16},{16,14},{18,20},{2... | collective-permute-start | bytes 98312 | tf_op jit(solution)/shard_map/ppermute | solution.py:485
  31.6 1.5 %collective-permute-done.8.refs_4_ = f32[32,256]{1,0:T(8,128)S(1)} collective-permute-done((f32[32,256]{1,0:T(8,128)S(1)}, f32[32,256]{1,0:T(8,128)S(1)}, u32[]{:S(2)}, u32[]{:S(2)}) %collective-permute-start.8) | collective-permute-done | bytes 32800 | tf_op jit(solution)/shard_map/ppermute | solution.py:487
  33.1 0.0 collective-permute-done.7.refs_3_
  33.1 0.0 collective-permute-done.10.refs_6_
  33.1 0.0 collective-permute-done.9.refs_5_
  33.1 0.1 collective-permute-done.6.refs_2_
  33.2 6.8 %shard_map.117.refs_1_ = f32[256,128]{1,0:T(8,128)S(1)} custom-call(f32[1]{0:T(128)S(6)} %copy.12.refs_0_, f32[256,128]{1,0:T(8,128)S(1)} %get-tuple-element.13.refs_1_, f32[256,128]{1,0:T(8,128)S(1)} %collective-permute-done.6.refs_2_, f32[32,256]{1,0:T(8,128)S(1)} %collective-permute-done.7.refs_3_, f32[32,256]{1,0:T(8,128)S(1)} %collective-permute-done.8.refs_4_, ...), custom_call_target="tpu_custom_call" | custom-call | flops 10000000000 | tf_op jit(solution)/shard_map/pallas_call | solution.py:209
  40.1 9.0 %collective-permute-start.14 = (f32[256,128]{1,0:T(8,128)S(1)}, f32[256,128]{1,0:T(8,128)S(1)}, u32[]{:S(2)}, u32[]{:S(2)}) collective-permute-start(f32[256,128]{1,0:T(8,128)S(1)} %shard_map.117.refs_1_), channel_id=1, source_target_pairs={{0,16},{2,18},{4,20},{6,22},{8,24},{10,26},{12,28},{14,30},{16,0},... | collective-permute-start | bytes 393224 | tf_op jit(solution)/shard_map/ppermute | solution.py:503
  49.1 0.7 %collective-permute-start.13 = (f32[256,128]{1,0:T(8,128)S(1)}, f32[256,128]{1,0:T(8,128)S(1)}, u32[]{:S(2)}, u32[]{:S(2)}) collective-permute-start(f32[256,128]{1,0:T(8,128)S(1)} %shard_map.117.refs_1_), channel_id=1, source_target_pairs={{0,8},{2,10},{4,12},{6,14},{8,0},{10,2},{12,4},{14,6},{16,24},{18,... | collective-permute-start | bytes 393224 | tf_op jit(solution)/shard_map/ppermute | solution.py:503
  49.8 0.7 %collective-permute-start.12 = (f32[256,128]{1,0:T(8,128)S(1)}, f32[256,128]{1,0:T(8,128)S(1)}, u32[]{:S(2)}, u32[]{:S(2)}) collective-permute-start(f32[256,128]{1,0:T(8,128)S(1)} %shard_map.117.refs_1_), channel_id=1, source_target_pairs={{0,4},{2,6},{4,0},{6,2},{8,12},{10,14},{12,8},{14,10},{16,20},{18,... | collective-permute-start | bytes 393224 | tf_op jit(solution)/shard_map/ppermute | solution.py:503
  50.5 0.3 collective-permute-start.11
  50.8 5.1 %collective-permute-done.14.refs_5_ = f32[256,128]{1,0:T(8,128)S(1)} collective-permute-done((f32[256,128]{1,0:T(8,128)S(1)}, f32[256,128]{1,0:T(8,128)S(1)}, u32[]{:S(2)}, u32[]{:S(2)}) %collective-permute-start.14) | collective-permute-done | bytes 131104 | tf_op jit(solution)/shard_map/ppermute | solution.py:503
  55.9 0.0 collective-permute-done.13.refs_4_
  55.9 0.0 collective-permute-done.12.refs_3_
  55.9 0.0 collective-permute-done.11.refs_2_
  55.9 0.7 %shard_map.118.refs_3_ = f32[256,128]{1,0:T(8,128)S(1)} custom-call(s32[4]{0:T(128)S(1)} %pad_add_fusion.refs_0_, f32[256,128]{1,0:T(8,128)S(1)} %shard_map.117.refs_1_, f32[256,128]{1,0:T(8,128)S(1)} %collective-permute-done.11.refs_2_, f32[256,128]{1,0:T(8,128)S(1)} %collective-permute-done.12.refs_3_, f32[256,128]{1,0:T(8,128)S(1)} %collective-permute-done.13.refs_4_, ...), custom_call_target="tpu_custom_call" | custom-call | tf_op jit(solution)/shard_map/pallas_call | solution.py:209
  56.7 0.6 collective-permute-start.15
  57.2 4.7 %collective-permute-done.15.refs_4_ = f32[256,128]{1,0:T(8,128)S(1)} collective-permute-done((f32[256,128]{1,0:T(8,128)S(1)}, f32[256,128]{1,0:T(8,128)S(1)}, u32[]{:S(2)}, u32[]{:S(2)}) %collective-permute-start.15) | collective-permute-done | bytes 131104 | tf_op jit(solution)/shard_map/ppermute | solution.py:494
  61.9 0.7 %shard_map.119 = (f32[2,128,128]{2,1,0:T(8,128)}, f32[2,128,128]{2,1,0:T(8,128)}) custom-call(f32[2,128,128]{2,1,0:T(8,128)S(1)} %copy-done.1, f32[256,128]{1,0:T(8,128)S(1)} %get-tuple-element.13.refs_1_, f32[256,128]{1,0:T(8,128)S(1)} %collective-permute-done.6.refs_2_, f32[256,128]{1,0:T(8,128)S(1)} %shard_map.118.refs_3_, ...), custom_call_target="tpu_custom_call" | custom-call | tf_op jit(solution)/shard_map/pallas_call | solution.py:209
  (12 shorter events, 0.0 us)
Async XLA Ops:
  0.6 0.9 %copy-start = (f32[2,128,128]{2,1,0:T(8,128)S(1)}, f32[2,128,128]{2,1,0:T(8,128)}, u32[]{:S(2)}) copy-start(f32[2,128,128]{2,1,0:T(8,128)} %refs_0_.5) | copy-start | bytes 393220
  1.5 0.9 %copy-start.3 = (s32[2,128,128]{2,1,0:T(8,128)S(1)}, s32[2,128,128]{2,1,0:T(8,128)}, u32[]{:S(2)}) copy-start(s32[2,128,128]{2,1,0:T(8,128)} %param.11) | copy-start | bytes 393220
  2.4 1.4 %copy-start.2 = (f32[2,1,6,25,25]{4,1,3,2,0:T(1,128)S(1)}, f32[2,1,6,25,25]{4,1,3,2,0:T(1,128)}, u32[]{:S(2)}) copy-start(f32[2,1,6,25,25]{4,1,3,2,0:T(1,128)} %param.12) | copy-start | bytes 90004
  2.4 1.4 %copy-start.5 = (f32[1,6]{1,0:T(1,128)S(1)}, f32[1,6]{1,0:T(1,128)}, u32[]{:S(2)}) copy-start(f32[1,6]{1,0:T(1,128)} %refs_0_.4) | copy-start | bytes 76
  2.4 1.4 %copy-start.7 = (bf16[1408,256]{1,0:T(8,128)(2,1)S(1)}, bf16[1408,256]{1,0:T(8,128)(2,1)}, u32[]{:S(2)}) copy-start(bf16[1408,256]{1,0:T(8,128)(2,1)} %constant.4.clone.refs_2_) | copy-start | bytes 2162692
  2.7 3.9 %collective-permute-start = (f32[48,256]{1,0:T(8,128)S(1)}, f32[48,256]{1,0:T(8,128)S(1)}, u32[]{:S(2)}, u32[]{:S(2)}) collective-permute-start(f32[48,256]{1,0:T(8,128)S(1)} %get-tuple-element.10), channel_id=1, source_target_pairs={{0,2},{2,0},{4,6},{6,4},{8,10},{10,8},{12,14},{14,12},{16,18},{18,... | collective-permute-start | bytes 147464 | tf_op jit(solution)/shard_map/ppermute | solution.py:485
  3.2 3.4 %collective-permute-start.1 = (f32[48,256]{1,0:T(8,128)S(1)}, f32[48,256]{1,0:T(8,128)S(1)}, u32[]{:S(2)}, u32[]{:S(2)}) collective-permute-start(f32[48,256]{1,0:T(8,128)S(1)} %get-tuple-element.11), channel_id=1, source_target_pairs={{2,4},{4,2},{6,8},{8,6},{10,12},{12,10},{14,16},{16,14},{18,20},{2... | collective-permute-start | bytes 147464 | tf_op jit(solution)/shard_map/ppermute | solution.py:485
  3.9 2.7 %copy-start.1 = (f32[2,128,128]{2,1,0:T(8,128)S(1)}, f32[2,128,128]{2,1,0:T(8,128)}, u32[]{:S(2)}) copy-start(f32[2,128,128]{2,1,0:T(8,128)} %refs_0_.5) | copy-start | bytes 393220
  3.9 2.7 %copy-start.4 = (s32[2,128,128]{2,1,0:T(8,128)S(1)}, s32[2,128,128]{2,1,0:T(8,128)}, u32[]{:S(2)}) copy-start(s32[2,128,128]{2,1,0:T(8,128)} %param.11) | copy-start | bytes 393220
  3.9 2.7 %copy-start.6 = (bf16[4000,256]{1,0:T(8,128)(2,1)S(1)}, bf16[4000,256]{1,0:T(8,128)(2,1)}, u32[]{:S(2)}) copy-start(bf16[4000,256]{1,0:T(8,128)(2,1)} %constant.5.clone.refs_6_.refs_10_) | copy-start | bytes 6144004
  6.6 15.7 %copy-start.8 = (s32[2]{0:T(128)S(1)}, s32[2]{0:T(128)}, u32[]{:S(2)}) copy-start(s32[2]{0:T(128)} %param.16) | copy-start | bytes 28
  6.6 15.7 %copy-start.9 = (s32[2]{0:T(128)S(1)}, s32[2]{0:T(128)}, u32[]{:S(2)}) copy-start(s32[2]{0:T(128)} %param.15) | copy-start | bytes 28
  13.5 13.2 %collective-permute-start.5 = (f32[256,128]{1,0:T(8,128)S(1)}, f32[256,128]{1,0:T(8,128)S(1)}, u32[]{:S(2)}, u32[]{:S(2)}) collective-permute-start(f32[256,128]{1,0:T(8,128)S(1)} %get-tuple-element.12.refs_1_), channel_id=1, source_target_pairs={{0,16},{2,18},{4,20},{6,22},{8,24},{10,26},{12,28},{14,30},{16,0},... | collective-permute-start | bytes 393224 | tf_op jit(solution)/shard_map/ppermute | solution.py:503
  20.2 6.8 %collective-permute-start.4 = (f32[256,128]{1,0:T(8,128)S(1)}, f32[256,128]{1,0:T(8,128)S(1)}, u32[]{:S(2)}, u32[]{:S(2)}) collective-permute-start(f32[256,128]{1,0:T(8,128)S(1)} %get-tuple-element.12.refs_1_), channel_id=1, source_target_pairs={{0,8},{2,10},{4,12},{6,14},{8,0},{10,2},{12,4},{14,6},{16,24},{18,... | collective-permute-start | bytes 393224 | tf_op jit(solution)/shard_map/ppermute | solution.py:503
  21.8 5.2 %collective-permute-start.3 = (f32[256,128]{1,0:T(8,128)S(1)}, f32[256,128]{1,0:T(8,128)S(1)}, u32[]{:S(2)}, u32[]{:S(2)}) collective-permute-start(f32[256,128]{1,0:T(8,128)S(1)} %get-tuple-element.12.refs_1_), channel_id=1, source_target_pairs={{0,4},{2,6},{4,0},{6,2},{8,12},{10,14},{12,8},{14,10},{16,20},{18,... | collective-permute-start | bytes 393224 | tf_op jit(solution)/shard_map/ppermute | solution.py:503
  22.3 4.7 %collective-permute-start.2 = (f32[256,128]{1,0:T(8,128)S(1)}, f32[256,128]{1,0:T(8,128)S(1)}, u32[]{:S(2)}, u32[]{:S(2)}) collective-permute-start(f32[256,128]{1,0:T(8,128)S(1)} %get-tuple-element.12.refs_1_), channel_id=1, source_target_pairs={{0,2},{2,0},{4,6},{6,4},{8,10},{10,8},{12,14},{14,12},{16,18},{18,... | collective-permute-start | bytes 393224 | tf_op jit(solution)/shard_map/ppermute | solution.py:503
  27.9 5.4 %collective-permute-start.6 = (f32[256,128]{1,0:T(8,128)S(1)}, f32[256,128]{1,0:T(8,128)S(1)}, u32[]{:S(2)}, u32[]{:S(2)}) collective-permute-start(f32[256,128]{1,0:T(8,128)S(1)} %get-tuple-element.13.refs_1_), channel_id=1, source_target_pairs={{0,1},{1,0},{2,3},{3,2},{4,5},{5,4},{6,7},{7,6},{8,9},{9,8},{10,11... | collective-permute-start | bytes 393224 | tf_op jit(solution)/shard_map/ppermute | solution.py:494
  29.4 3.7 %collective-permute-start.8 = (f32[32,256]{1,0:T(8,128)S(1)}, f32[32,256]{1,0:T(8,128)S(1)}, u32[]{:S(2)}, u32[]{:S(2)}) collective-permute-start(f32[32,256]{1,0:T(8,128)S(1)} %get-tuple-element.14), channel_id=1, source_target_pairs={{0,3},{1,2},{2,1},{3,0},{4,7},{5,6},{6,5},{7,4},{8,11},{9,10},{10,... | collective-permute-start | bytes 98312 | tf_op jit(solution)/shard_map/ppermute | solution.py:487
  29.4 3.7 %collective-permute-start.7 = (f32[32,256]{1,0:T(8,128)S(1)}, f32[32,256]{1,0:T(8,128)S(1)}, u32[]{:S(2)}, u32[]{:S(2)}) collective-permute-start(f32[32,256]{1,0:T(8,128)S(1)} %get-tuple-element.14), channel_id=1, source_target_pairs={{0,2},{2,0},{4,6},{6,4},{8,10},{10,8},{12,14},{14,12},{16,18},{18,... | collective-permute-start | bytes 98312 | tf_op jit(solution)/shard_map/ppermute | solution.py:485
  30.0 3.1 %collective-permute-start.10 = (f32[32,256]{1,0:T(8,128)S(1)}, f32[32,256]{1,0:T(8,128)S(1)}, u32[]{:S(2)}, u32[]{:S(2)}) collective-permute-start(f32[32,256]{1,0:T(8,128)S(1)} %get-tuple-element.15), channel_id=1, source_target_pairs={{2,5},{3,4},{4,3},{5,2},{6,9},{7,8},{8,7},{9,6},{10,13},{11,12},{1... | collective-permute-start | bytes 98312 | tf_op jit(solution)/shard_map/ppermute | solution.py:487
  30.7 2.4 %collective-permute-start.9 = (f32[32,256]{1,0:T(8,128)S(1)}, f32[32,256]{1,0:T(8,128)S(1)}, u32[]{:S(2)}, u32[]{:S(2)}) collective-permute-start(f32[32,256]{1,0:T(8,128)S(1)} %get-tuple-element.15), channel_id=1, source_target_pairs={{2,4},{4,2},{6,8},{8,6},{10,12},{12,10},{14,16},{16,14},{18,20},{2... | collective-permute-start | bytes 98312 | tf_op jit(solution)/shard_map/ppermute | solution.py:485
  40.1 15.9 %collective-permute-start.14 = (f32[256,128]{1,0:T(8,128)S(1)}, f32[256,128]{1,0:T(8,128)S(1)}, u32[]{:S(2)}, u32[]{:S(2)}) collective-permute-start(f32[256,128]{1,0:T(8,128)S(1)} %shard_map.117.refs_1_), channel_id=1, source_target_pairs={{0,16},{2,18},{4,20},{6,22},{8,24},{10,26},{12,28},{14,30},{16,0},... | collective-permute-start | bytes 393224 | tf_op jit(solution)/shard_map/ppermute | solution.py:503
  49.1 6.9 %collective-permute-start.13 = (f32[256,128]{1,0:T(8,128)S(1)}, f32[256,128]{1,0:T(8,128)S(1)}, u32[]{:S(2)}, u32[]{:S(2)}) collective-permute-start(f32[256,128]{1,0:T(8,128)S(1)} %shard_map.117.refs_1_), channel_id=1, source_target_pairs={{0,8},{2,10},{4,12},{6,14},{8,0},{10,2},{12,4},{14,6},{16,24},{18,... | collective-permute-start | bytes 393224 | tf_op jit(solution)/shard_map/ppermute | solution.py:503
  49.8 6.2 %collective-permute-start.12 = (f32[256,128]{1,0:T(8,128)S(1)}, f32[256,128]{1,0:T(8,128)S(1)}, u32[]{:S(2)}, u32[]{:S(2)}) collective-permute-start(f32[256,128]{1,0:T(8,128)S(1)} %shard_map.117.refs_1_), channel_id=1, source_target_pairs={{0,4},{2,6},{4,0},{6,2},{8,12},{10,14},{12,8},{14,10},{16,20},{18,... | collective-permute-start | bytes 393224 | tf_op jit(solution)/shard_map/ppermute | solution.py:503
  50.5 5.4 %collective-permute-start.11 = (f32[256,128]{1,0:T(8,128)S(1)}, f32[256,128]{1,0:T(8,128)S(1)}, u32[]{:S(2)}, u32[]{:S(2)}) collective-permute-start(f32[256,128]{1,0:T(8,128)S(1)} %shard_map.117.refs_1_), channel_id=1, source_target_pairs={{0,2},{2,0},{4,6},{6,4},{8,10},{10,8},{12,14},{14,12},{16,18},{18,... | collective-permute-start | bytes 393224 | tf_op jit(solution)/shard_map/ppermute | solution.py:503
  56.7 5.3 %collective-permute-start.15 = (f32[256,128]{1,0:T(8,128)S(1)}, f32[256,128]{1,0:T(8,128)S(1)}, u32[]{:S(2)}, u32[]{:S(2)}) collective-permute-start(f32[256,128]{1,0:T(8,128)S(1)} %shard_map.118.refs_3_), channel_id=1, source_target_pairs={{0,1},{1,0},{2,3},{3,2},{4,5},{5,4},{6,7},{7,6},{8,9},{9,8},{10,11... | collective-permute-start | bytes 393224 | tf_op jit(solution)/shard_map/ppermute | solution.py:494

commit v8 on v7

--- a/solution.py
+++ b/solution.py
@@ -25,6 +25,7 @@
 NV = NX // 2 + 1
 ROWS = 160
 ROW0 = 8
+CHUNK = 16
 EDGE = 48
 WIDE_PAD = 32
 VMEM_LIMIT = 24 * 1024 * 1024
@@ -307,29 +308,44 @@
     weight = jnp.where((bin_at == 0) | (bin_at == NU - 1), 1.0, 2.0) / (NX * NY)
     weight = jnp.where(lane < YB, weight, -weight)
 
-    def spectra_of(t, k, part):
-        return [h_ref[2 * k + part, j] for j in range(4)], [f_ref[t, j] for j in range(4)]
+    def chunks(height):
+        return [slice(r, r + CHUNK) for r in range(0, height, CHUNK)]
+
+    def put(ref, slot, starts, pieces):
+        for at_row, piece in zip(starts, pieces):
+            ref[slot, at_row : at_row + CHUNK] = piece
 
     def products(t, k, slot):
         for part in range(2):
-            (hpr, hpi, hmr, hmi), (fpr, fpi, fmr, fmi) = spectra_of(t, k, part)
-            pr, pi = hpr * fpr - hpi * fpi, hpr * fpi + hpi * fpr
-            mr, mi = hmr * fmr - hmi * fmi, hmr * fmi + hmi * fmr
-            p_hi, p_lo = split(even_odd(pr, pi, mr, mi))
-            rows = slice(2 * XB * part, 2 * XB * part + 2 * XB)
-            a_hi[slot, rows] = p_hi
-            a_lo[slot, rows] = p_lo
-
-    def store_three(ref, slot, pieces, height):
-        for j, piece in enumerate(pieces):
-            ref[slot, height * j : height * j + height] = piece
+            for rows in chunks(XB):
+                hpr, hpi, hmr, hmi = (h_ref[2 * k + part, j, rows] for j in range(4))
+                fpr, fpi, fmr, fmi = (f_ref[t, j, rows] for j in range(4))
+                pr, pi = hpr * fpr - hpi * fpi, hpr * fpi + hpi * fpr
+                mr, mi = hmr * fmr - hmi * fmi, hmr * fmi + hmi * fmr
+                starts = [2 * XB * part + rows.start, 2 * XB * part + XB + rows.start]
+                top = split(jnp.concatenate([pr + mr, pi + mi], axis=1))
+                low = split(jnp.concatenate([mi - pi, pr - mr], axis=1))
+                put(a_hi, slot, starts, (top[0], low[0]))
+                put(a_lo, slot, starts, (top[1], low[1]))
+
+    def y_done(z_one, z_two, slot):
+        for rows in chunks(2 * XB):
+            z = []
+            for part in range(2):
+                here = slice(2 * XB * part + rows.start, 2 * XB * part + rows.stop)
+                z.append(z_one[here, :CORE] + (z_one[here, CORE:] + z_two[here]))
+            z_hi, z_lo = split(jnp.concatenate(z, axis=1))
+            starts = [2 * XB * j + rows.start for j in range(3)]
+            put(b_cat, slot, starts, (z_hi, z_hi, z_lo))
 
     def field_of(t, k, slot):
-        field = dot(tb("x2"), b_cat[slot])
-        fld[t, k] = field
-        re, im = field[:, :CORE], field[:, CORE:]
-        power = re * re + im * im
-        inten[t] = power if k == 0 else inten[t] + power
+        whole = dot(tb("x2"), b_cat[slot])
+        for rows in chunks(ROWS):
+            field = whole[rows]
+            fld[t, k, rows] = field
+            re, im = field[:, :CORE], field[:, CORE:]
+            power = re * re + im * im
+            inten[t, rows] = power if k == 0 else inten[t, rows] + power
 
     def slope_of(t):
         resist = jax.nn.sigmoid(STEEPNESS * (inten[t] - thr_ref[0]))
@@ -338,27 +354,40 @@
         inten[t] = jnp.where(inside, 2.0 * slope, 0.0)
 
     def scaled_field(t, k, slot):
-        slope, field = inten[t], fld[t, k]
-        r_hi, r_lo = split(
-            jnp.concatenate([slope * field[:, :CORE], slope * field[:, CORE:]], axis=1)
-        )
-        store_three(r_cat, slot, (r_hi, r_hi, r_lo), ROWS)
+        for rows in chunks(ROWS):
+            slope, field = inten[t, rows], fld[t, k, rows]
+            r_hi, r_lo = split(
+                jnp.concatenate([slope * field[:, :CORE], slope * field[:, CORE:]], axis=1)
+            )
+            starts = [ROWS * j + rows.start for j in range(3)]
+            put(r_cat, slot, starts, (r_hi, r_hi, r_lo))
+
+    def x_back_done(w_now, slot):
+        for rows in chunks(2 * XB):
+            w_hi, w_lo = split(w_now[rows])
+            for part in range(2):
+                here = slice(2 * XB * part + rows.start, 2 * XB * part + rows.stop)
+                lanes = slice(CORE * part, CORE * part + CORE)
+                for j, piece in enumerate((w_hi, w_lo, w_hi)):
+                    w_cat[slot, here, CORE * j : CORE * j + CORE] = piece[:, lanes]
 
     def add_back(t, k, slot):
         specs = dot(w_cat[slot], tb("y3"))
-        acc = [0.0] * 4 if k == 0 else [tot[t, j] for j in range(4)]
-        for part in range(2):
-            spec = specs[2 * XB * part : 2 * XB * part + 2 * XB]
-            cc, cs = spec[:XB, :YB], spec[:XB, YB:]
-            sc, ss = spec[XB:, :YB], spec[XB:, YB:]
-            bpr, neg, bmr, bmi = cc - ss, cs + sc, cc + ss, sc - cs
-            hpr, hpi, hmr, hmi = (h_ref[2 * k + part, j] for j in range(4))
-            acc[0] = acc[0] + (hpr * bpr - hpi * neg)
-            acc[1] = acc[1] - (hpr * neg + hpi * bpr)
-            acc[2] = acc[2] + (hmr * bmr + hmi * bmi)
-            acc[3] = acc[3] + (hmr * bmi - hmi * bmr)
-        for j in range(4):
-            tot[t, j] = acc[j]
+        for rows in chunks(XB):
+            acc = [0.0] * 4 if k == 0 else [tot[t, j, rows] for j in range(4)]
+            for part in range(2):
+                base = 2 * XB * part + rows.start
+                cos_rows, sin_rows = slice(base, base + CHUNK), slice(base + XB, base + XB + CHUNK)
+                cc, cs = specs[cos_rows, :YB], specs[cos_rows, YB:]
+                sc, ss = specs[sin_rows, :YB], specs[sin_rows, YB:]
+                bpr, neg, bmr, bmi = cc - ss, cs + sc, cc + ss, sc - cs
+                hpr, hpi, hmr, hmi = (h_ref[2 * k + part, j, rows] for j in range(4))
+                acc[0] = acc[0] + (hpr * bpr - hpi * neg)
+                acc[1] = acc[1] - (hpr * neg + hpi * bpr)
+                acc[2] = acc[2] + (hmr * bmr + hmi * bmi)
+                acc[3] = acc[3] + (hmr * bmi - hmi * bmr)
+            for j in range(4):
+                tot[t, j, rows] = acc[j]
 
     def finish(t):
         r_hi, r_lo = split(even_odd(*(tot[t, j] for j in range(4))))
@@ -385,16 +414,9 @@
         if back_old:
             add_back(*back_old, slot)
         if mid:
-            z = z_one[:, :CORE] + (z_one[:, CORE:] + z_two)
-            z_hi, z_lo = split(jnp.concatenate([z[: 2 * XB], z[2 * XB :]], axis=1))
-            store_three(b_cat, other, (z_hi, z_hi, z_lo), 2 * XB)
+            y_done(z_one, z_two, other)
         if back_mid:
-            w_hi, w_lo = split(w_now)
-            for part in range(2):
-                rows = slice(2 * XB * part, 2 * XB * part + 2 * XB)
-                lanes = slice(CORE * part, CORE * part + CORE)
-                for j, piece in enumerate((w_hi, w_lo, w_hi)):
-                    w_cat[other, rows, CORE * j : CORE * j + CORE] = piece[:, lanes]
+            x_back_done(w_now, other)
         if old and old[1] == kern - 1:
             slope_of(old[0])
         if back_old and back_old[1] == kern - 1:

time: 62.9 us -> 62.8 us (level)
  no operation moved by 1% of the time
where the time goes in v8:
time: 62.8 us; the launch traced here: 62.6 us
  starting transfers between devices  24.9 us (40%)
  Pallas kernels  18.2 us (29%)
  waiting for transfers between devices  16.1 us (26%)
  local copies, waits for them, and re-layouts  1.85 us (3%)
  between operations  1.5 us (2%)
    ppermute x8, starting transfers between devices, from_partners(): lax.ppermute(grad, 'tile', [(i, i ^ bit) for i in range(n_tile)])  19.4 us
    pallas_call x7, Pallas kernels, call(): pl.pallas_call(wrapped, out_shape=out_shape, in_specs=[sm if i in smem el...  18.2 us
    ppermute x8, waiting for transfers between devices, from_partners(): lax.ppermute(grad, 'tile', [(i, i ^ bit) for i in range(n_tile)])  9.78 us
    ppermute x2, waiting for transfers between devices, depth_pair(): peer = lax.ppermute(x, 'depth', [(i, i ^ bit) for i in range(n_depth)])  4.79 us
    ppermute x4, starting transfers between devices, move(): return lax.ppermute(x, 'tile', pairs)  2.63 us
    ppermute x2, starting transfers between devices, depth_pair(): peer = lax.ppermute(x, 'depth', [(i, i ^ bit) for i in range(n_depth)])  2.12 us
    unnamed x20, local copies, waits for them, and re-layouts  1.85 us
    ppermute x2, waiting for transfers between devices, move(): return lax.ppermute(x, ('tile', 'depth'), both)  1.55 us
  transfers between devices with their start and end apart: 16, of which 6 were waited for; matrix products, arithmetic and copies ran while one was open for 0% of the time, Pallas kernels for 3%

profile of v8, /device:TPU:0, one launch (start us, length us, event | category | flops | bytes accessed | tf_op | source)
XLA Modules:
  0.0 62.6 jit_solution(11504787104944830528)
XLA Ops:
  0.6 0.0 copy-start
  0.6 0.9 %copy-done = f32[2,128,128]{2,1,0:T(8,128)S(1)} copy-done((f32[2,128,128]{2,1,0:T(8,128)S(1)}, f32[2,128,128]{2,1,0:T(8,128)}, u32[]{:S(2)}) %copy-start) | copy-done | bytes 131096
  1.5 0.9 %copy-done.3 = s32[2,128,128]{2,1,0:T(8,128)S(1)} copy-done((s32[2,128,128]{2,1,0:T(8,128)S(1)}, s32[2,128,128]{2,1,0:T(8,128)}, u32[]{:S(2)}) %copy-start.3) | copy-done | bytes 131096
  2.4 0.2 shard_map.113
  2.7 0.5 collective-permute-start
  3.2 0.7 %collective-permute-start.1 = (f32[48,256]{1,0:T(8,128)S(1)}, f32[48,256]{1,0:T(8,128)S(1)}, u32[]{:S(2)}, u32[]{:S(2)}) collective-permute-start(f32[48,256]{1,0:T(8,128)S(1)} %get-tuple-element.11), channel_id=1, source_target_pairs={{2,4},{4,2},{6,8},{8,6},{10,12},{12,10},{14,16},{16,14},{18,20},{2... | collective-permute-start | bytes 147464 | tf_op jit(solution)/shard_map/ppermute | solution.py:507
  3.9 0.0 copy-start.1
  3.9 0.0 copy-start.4
  3.9 0.0 copy-start.6
  3.9 2.0 %shard_map.114.refs_5_.refs_9_ = f32[12,4,96,128]{3,2,1,0:T(8,128)S(1)} custom-call(f32[1,6]{1,0:T(1,128)S(1)} %copy-done.5, f32[2,6,25,1,25]{4,3,2,1,0:T(1,128)S(1)} %bitcast.5, bf16[1408,256]{1,0:T(8,128)(2,1)S(1)} %copy-done.7), custom_call_target="tpu_custom_call" | custom-call | flops 3000000000 | bytes 4000000 | tf_op jit(solution)/shard_map/pallas_call | solution.py:210
  6.6 0.0 copy-start.8
  6.6 0.0 copy-start.9
  6.6 0.0 collective-permute-done.refs_3_
  6.6 0.0 collective-permute-done.1.refs_4_
  6.6 6.9 %shard_map.115 = (f32[256,128]{1,0:T(8,128)S(1)}, f32[2,4,96,128]{3,2,1,0:T(8,128)S(1)}, f32[160,256]{1,0:T(8,128)S(1)}) custom-call(f32[1]{0:T(128)S(6)} %copy.12.refs_0_, f32[256,128]{1,0:T(8,128)S(1)} %bitcast.4, s32[256,128]{1,0:T(8,128)S(1)} %bitcast.7, f32[48,256]{1,0:T(8,128)S(1)} %collective-permute-done.refs_3_, ...), custom_call_target="tpu_custom_call" | custom-call | flops 10000000000 | tf_op jit(solution)/shard_map/pallas_call | solution.py:210
  13.6 6.7 %collective-permute-start.5 = (f32[256,128]{1,0:T(8,128)S(1)}, f32[256,128]{1,0:T(8,128)S(1)}, u32[]{:S(2)}, u32[]{:S(2)}) collective-permute-start(f32[256,128]{1,0:T(8,128)S(1)} %get-tuple-element.12.refs_1_), channel_id=1, source_target_pairs={{0,16},{2,18},{4,20},{6,22},{8,24},{10,26},{12,28},{14,30},{16,0},... | collective-permute-start | bytes 393224 | tf_op jit(solution)/shard_map/ppermute | solution.py:525
  20.2 1.6 %collective-permute-start.4 = (f32[256,128]{1,0:T(8,128)S(1)}, f32[256,128]{1,0:T(8,128)S(1)}, u32[]{:S(2)}, u32[]{:S(2)}) collective-permute-start(f32[256,128]{1,0:T(8,128)S(1)} %get-tuple-element.12.refs_1_), channel_id=1, source_target_pairs={{0,8},{2,10},{4,12},{6,14},{8,0},{10,2},{12,4},{14,6},{16,24},{18,... | collective-permute-start | bytes 393224 | tf_op jit(solution)/shard_map/ppermute | solution.py:525
  21.8 0.5 collective-permute-start.3
  22.3 0.0 collective-permute-start.2
  22.3 0.1 pad_add_fusion.refs_0_
  22.4 4.4 %collective-permute-done.5.refs_5_ = f32[256,128]{1,0:T(8,128)S(1)} collective-permute-done((f32[256,128]{1,0:T(8,128)S(1)}, f32[256,128]{1,0:T(8,128)S(1)}, u32[]{:S(2)}, u32[]{:S(2)}) %collective-permute-start.5) | collective-permute-done | bytes 131104 | tf_op jit(solution)/shard_map/ppermute | solution.py:525
  26.8 0.2 collective-permute-done.4.refs_4_
  27.0 0.0 collective-permute-done.3.refs_3_
  27.0 0.0 collective-permute-done.2.refs_2_
  27.0 0.9 %shard_map.116 = (f32[256,128]{1,0:T(8,128)S(1)}, f32[32,256]{1,0:T(8,128)S(1)}, f32[32,256]{1,0:T(8,128)S(1)}) custom-call(s32[4]{0:T(128)S(1)} %pad_add_fusion.refs_0_, f32[256,128]{1,0:T(8,128)S(1)} %get-tuple-element.12.refs_1_, f32[256,128]{1,0:T(8,128)S(1)} %collective-permute-done.2.refs_2_, f32[256,128]{1,0:T(8,128)S(1)} %collective-permute-done.3.refs_3_, ...), custom_call_target="tpu_custom_call" | custom-call | tf_op jit(solution)/shard_map/pallas_call | solution.py:210
  27.9 1.6 %collective-permute-start.6 = (f32[256,128]{1,0:T(8,128)S(1)}, f32[256,128]{1,0:T(8,128)S(1)}, u32[]{:S(2)}, u32[]{:S(2)}) collective-permute-start(f32[256,128]{1,0:T(8,128)S(1)} %get-tuple-element.13.refs_1_), channel_id=1, source_target_pairs={{0,1},{1,0},{2,3},{3,2},{4,5},{5,4},{6,7},{7,6},{8,9},{9,8},{10,11... | collective-permute-start | bytes 393224 | tf_op jit(solution)/shard_map/ppermute | solution.py:516
  29.4 0.0 collective-permute-start.8
  29.4 0.6 collective-permute-start.7
  30.1 0.7 %collective-permute-start.10 = (f32[32,256]{1,0:T(8,128)S(1)}, f32[32,256]{1,0:T(8,128)S(1)}, u32[]{:S(2)}, u32[]{:S(2)}) collective-permute-start(f32[32,256]{1,0:T(8,128)S(1)} %get-tuple-element.15), channel_id=1, source_target_pairs={{2,5},{3,4},{4,3},{5,2},{6,9},{7,8},{8,7},{9,6},{10,13},{11,12},{1... | collective-permute-start | bytes 98312 | tf_op jit(solution)/shard_map/ppermute | solution.py:509
  30.7 0.8 %collective-permute-start.9 = (f32[32,256]{1,0:T(8,128)S(1)}, f32[32,256]{1,0:T(8,128)S(1)}, u32[]{:S(2)}, u32[]{:S(2)}) collective-permute-start(f32[32,256]{1,0:T(8,128)S(1)} %get-tuple-element.15), channel_id=1, source_target_pairs={{2,4},{4,2},{6,8},{8,6},{10,12},{12,10},{14,16},{16,14},{18,20},{2... | collective-permute-start | bytes 98312 | tf_op jit(solution)/shard_map/ppermute | solution.py:507
  31.6 1.5 %collective-permute-done.8.refs_4_ = f32[32,256]{1,0:T(8,128)S(1)} collective-permute-done((f32[32,256]{1,0:T(8,128)S(1)}, f32[32,256]{1,0:T(8,128)S(1)}, u32[]{:S(2)}, u32[]{:S(2)}) %collective-permute-start.8) | collective-permute-done | bytes 32800 | tf_op jit(solution)/shard_map/ppermute | solution.py:509
  33.1 0.0 collective-permute-done.7.refs_3_
  33.1 0.0 collective-permute-done.10.refs_6_
  33.1 0.0 collective-permute-done.9.refs_5_
  33.1 0.1 collective-permute-done.6.refs_2_
  33.2 6.8 %shard_map.117.refs_1_ = f32[256,128]{1,0:T(8,128)S(1)} custom-call(f32[1]{0:T(128)S(6)} %copy.12.refs_0_, f32[256,128]{1,0:T(8,128)S(1)} %get-tuple-element.13.refs_1_, f32[256,128]{1,0:T(8,128)S(1)} %collective-permute-done.6.refs_2_, f32[32,256]{1,0:T(8,128)S(1)} %collective-permute-done.7.refs_3_, f32[32,256]{1,0:T(8,128)S(1)} %collective-permute-done.8.refs_4_, ...), custom_call_target="tpu_custom_call" | custom-call | flops 10000000000 | tf_op jit(solution)/shard_map/pallas_call | solution.py:210
  40.0 9.0 %collective-permute-start.14 = (f32[256,128]{1,0:T(8,128)S(1)}, f32[256,128]{1,0:T(8,128)S(1)}, u32[]{:S(2)}, u32[]{:S(2)}) collective-permute-start(f32[256,128]{1,0:T(8,128)S(1)} %shard_map.117.refs_1_), channel_id=1, source_target_pairs={{0,16},{2,18},{4,20},{6,22},{8,24},{10,26},{12,28},{14,30},{16,0},... | collective-permute-start | bytes 393224 | tf_op jit(solution)/shard_map/ppermute | solution.py:525
  49.0 0.7 %collective-permute-start.13 = (f32[256,128]{1,0:T(8,128)S(1)}, f32[256,128]{1,0:T(8,128)S(1)}, u32[]{:S(2)}, u32[]{:S(2)}) collective-permute-start(f32[256,128]{1,0:T(8,128)S(1)} %shard_map.117.refs_1_), channel_id=1, source_target_pairs={{0,8},{2,10},{4,12},{6,14},{8,0},{10,2},{12,4},{14,6},{16,24},{18,... | collective-permute-start | bytes 393224 | tf_op jit(solution)/shard_map/ppermute | solution.py:525
  49.7 0.7 %collective-permute-start.12 = (f32[256,128]{1,0:T(8,128)S(1)}, f32[256,128]{1,0:T(8,128)S(1)}, u32[]{:S(2)}, u32[]{:S(2)}) collective-permute-start(f32[256,128]{1,0:T(8,128)S(1)} %shard_map.117.refs_1_), channel_id=1, source_target_pairs={{0,4},{2,6},{4,0},{6,2},{8,12},{10,14},{12,8},{14,10},{16,20},{18,... | collective-permute-start | bytes 393224 | tf_op jit(solution)/shard_map/ppermute | solution.py:525
  50.5 0.3 collective-permute-start.11
  50.8 5.1 %collective-permute-done.14.refs_5_ = f32[256,128]{1,0:T(8,128)S(1)} collective-permute-done((f32[256,128]{1,0:T(8,128)S(1)}, f32[256,128]{1,0:T(8,128)S(1)}, u32[]{:S(2)}, u32[]{:S(2)}) %collective-permute-start.14) | collective-permute-done | bytes 131104 | tf_op jit(solution)/shard_map/ppermute | solution.py:525
  55.9 0.0 collective-permute-done.13.refs_4_
  55.9 0.0 collective-permute-done.12.refs_3_
  55.9 0.0 collective-permute-done.11.refs_2_
  55.9 0.7 %shard_map.118.refs_3_ = f32[256,128]{1,0:T(8,128)S(1)} custom-call(s32[4]{0:T(128)S(1)} %pad_add_fusion.refs_0_, f32[256,128]{1,0:T(8,128)S(1)} %shard_map.117.refs_1_, f32[256,128]{1,0:T(8,128)S(1)} %collective-permute-done.11.refs_2_, f32[256,128]{1,0:T(8,128)S(1)} %collective-permute-done.12.refs_3_, f32[256,128]{1,0:T(8,128)S(1)} %collective-permute-done.13.refs_4_, ...), custom_call_target="tpu_custom_call" | custom-call | tf_op jit(solution)/shard_map/pallas_call | solution.py:210
  56.6 0.6 collective-permute-start.15
  57.2 4.7 %collective-permute-done.15.refs_4_ = f32[256,128]{1,0:T(8,128)S(1)} collective-permute-done((f32[256,128]{1,0:T(8,128)S(1)}, f32[256,128]{1,0:T(8,128)S(1)}, u32[]{:S(2)}, u32[]{:S(2)}) %collective-permute-start.15) | collective-permute-done | bytes 131104 | tf_op jit(solution)/shard_map/ppermute | solution.py:516
  61.9 0.7 %shard_map.119 = (f32[2,128,128]{2,1,0:T(8,128)}, f32[2,128,128]{2,1,0:T(8,128)}) custom-call(f32[2,128,128]{2,1,0:T(8,128)S(1)} %copy-done.1, f32[256,128]{1,0:T(8,128)S(1)} %get-tuple-element.13.refs_1_, f32[256,128]{1,0:T(8,128)S(1)} %collective-permute-done.6.refs_2_, f32[256,128]{1,0:T(8,128)S(1)} %shard_map.118.refs_3_, ...), custom_call_target="tpu_custom_call" | custom-call | tf_op jit(solution)/shard_map/pallas_call | solution.py:210
  (12 shorter events, 0.0 us)
Async XLA Ops:
  0.6 0.9 %copy-start = (f32[2,128,128]{2,1,0:T(8,128)S(1)}, f32[2,128,128]{2,1,0:T(8,128)}, u32[]{:S(2)}) copy-start(f32[2,128,128]{2,1,0:T(8,128)} %refs_0_.5) | copy-start | bytes 393220
  1.5 0.9 %copy-start.3 = (s32[2,128,128]{2,1,0:T(8,128)S(1)}, s32[2,128,128]{2,1,0:T(8,128)}, u32[]{:S(2)}) copy-start(s32[2,128,128]{2,1,0:T(8,128)} %param.11) | copy-start | bytes 393220
  2.4 1.4 %copy-start.2 = (f32[2,1,6,25,25]{4,1,3,2,0:T(1,128)S(1)}, f32[2,1,6,25,25]{4,1,3,2,0:T(1,128)}, u32[]{:S(2)}) copy-start(f32[2,1,6,25,25]{4,1,3,2,0:T(1,128)} %param.12) | copy-start | bytes 90004
  2.4 1.4 %copy-start.5 = (f32[1,6]{1,0:T(1,128)S(1)}, f32[1,6]{1,0:T(1,128)}, u32[]{:S(2)}) copy-start(f32[1,6]{1,0:T(1,128)} %refs_0_.4) | copy-start | bytes 76
  2.4 1.4 %copy-start.7 = (bf16[1408,256]{1,0:T(8,128)(2,1)S(1)}, bf16[1408,256]{1,0:T(8,128)(2,1)}, u32[]{:S(2)}) copy-start(bf16[1408,256]{1,0:T(8,128)(2,1)} %constant.4.clone.refs_2_) | copy-start | bytes 2162692
  2.7 3.9 %collective-permute-start = (f32[48,256]{1,0:T(8,128)S(1)}, f32[48,256]{1,0:T(8,128)S(1)}, u32[]{:S(2)}, u32[]{:S(2)}) collective-permute-start(f32[48,256]{1,0:T(8,128)S(1)} %get-tuple-element.10), channel_id=1, source_target_pairs={{0,2},{2,0},{4,6},{6,4},{8,10},{10,8},{12,14},{14,12},{16,18},{18,... | collective-permute-start | bytes 147464 | tf_op jit(solution)/shard_map/ppermute | solution.py:507
  3.2 3.4 %collective-permute-start.1 = (f32[48,256]{1,0:T(8,128)S(1)}, f32[48,256]{1,0:T(8,128)S(1)}, u32[]{:S(2)}, u32[]{:S(2)}) collective-permute-start(f32[48,256]{1,0:T(8,128)S(1)} %get-tuple-element.11), channel_id=1, source_target_pairs={{2,4},{4,2},{6,8},{8,6},{10,12},{12,10},{14,16},{16,14},{18,20},{2... | collective-permute-start | bytes 147464 | tf_op jit(solution)/shard_map/ppermute | solution.py:507
  3.9 2.7 %copy-start.1 = (f32[2,128,128]{2,1,0:T(8,128)S(1)}, f32[2,128,128]{2,1,0:T(8,128)}, u32[]{:S(2)}) copy-start(f32[2,128,128]{2,1,0:T(8,128)} %refs_0_.5) | copy-start | bytes 393220
  3.9 2.7 %copy-start.4 = (s32[2,128,128]{2,1,0:T(8,128)S(1)}, s32[2,128,128]{2,1,0:T(8,128)}, u32[]{:S(2)}) copy-start(s32[2,128,128]{2,1,0:T(8,128)} %param.11) | copy-start | bytes 393220
  3.9 2.7 %copy-start.6 = (bf16[4000,256]{1,0:T(8,128)(2,1)S(1)}, bf16[4000,256]{1,0:T(8,128)(2,1)}, u32[]{:S(2)}) copy-start(bf16[4000,256]{1,0:T(8,128)(2,1)} %constant.5.clone.refs_6_.refs_10_) | copy-start | bytes 6144004
  6.6 15.7 %copy-start.8 = (s32[2]{0:T(128)S(1)}, s32[2]{0:T(128)}, u32[]{:S(2)}) copy-start(s32[2]{0:T(128)} %param.16) | copy-start | bytes 28
  6.6 15.7 %copy-start.9 = (s32[2]{0:T(128)S(1)}, s32[2]{0:T(128)}, u32[]{:S(2)}) copy-start(s32[2]{0:T(128)} %param.15) | copy-start | bytes 28
  13.6 13.2 %collective-permute-start.5 = (f32[256,128]{1,0:T(8,128)S(1)}, f32[256,128]{1,0:T(8,128)S(1)}, u32[]{:S(2)}, u32[]{:S(2)}) collective-permute-start(f32[256,128]{1,0:T(8,128)S(1)} %get-tuple-element.12.refs_1_), channel_id=1, source_target_pairs={{0,16},{2,18},{4,20},{6,22},{8,24},{10,26},{12,28},{14,30},{16,0},... | collective-permute-start | bytes 393224 | tf_op jit(solution)/shard_map/ppermute | solution.py:525
  20.2 6.8 %collective-permute-start.4 = (f32[256,128]{1,0:T(8,128)S(1)}, f32[256,128]{1,0:T(8,128)S(1)}, u32[]{:S(2)}, u32[]{:S(2)}) collective-permute-start(f32[256,128]{1,0:T(8,128)S(1)} %get-tuple-element.12.refs_1_), channel_id=1, source_target_pairs={{0,8},{2,10},{4,12},{6,14},{8,0},{10,2},{12,4},{14,6},{16,24},{18,... | collective-permute-start | bytes 393224 | tf_op jit(solution)/shard_map/ppermute | solution.py:525
  21.8 5.2 %collective-permute-start.3 = (f32[256,128]{1,0:T(8,128)S(1)}, f32[256,128]{1,0:T(8,128)S(1)}, u32[]{:S(2)}, u32[]{:S(2)}) collective-permute-start(f32[256,128]{1,0:T(8,128)S(1)} %get-tuple-element.12.refs_1_), channel_id=1, source_target_pairs={{0,4},{2,6},{4,0},{6,2},{8,12},{10,14},{12,8},{14,10},{16,20},{18,... | collective-permute-start | bytes 393224 | tf_op jit(solution)/shard_map/ppermute | solution.py:525
  22.3 4.7 %collective-permute-start.2 = (f32[256,128]{1,0:T(8,128)S(1)}, f32[256,128]{1,0:T(8,128)S(1)}, u32[]{:S(2)}, u32[]{:S(2)}) collective-permute-start(f32[256,128]{1,0:T(8,128)S(1)} %get-tuple-element.12.refs_1_), channel_id=1, source_target_pairs={{0,2},{2,0},{4,6},{6,4},{8,10},{10,8},{12,14},{14,12},{16,18},{18,... | collective-permute-start | bytes 393224 | tf_op jit(solution)/shard_map/ppermute | solution.py:525
  27.9 5.4 %collective-permute-start.6 = (f32[256,128]{1,0:T(8,128)S(1)}, f32[256,128]{1,0:T(8,128)S(1)}, u32[]{:S(2)}, u32[]{:S(2)}) collective-permute-start(f32[256,128]{1,0:T(8,128)S(1)} %get-tuple-element.13.refs_1_), channel_id=1, source_target_pairs={{0,1},{1,0},{2,3},{3,2},{4,5},{5,4},{6,7},{7,6},{8,9},{9,8},{10,11... | collective-permute-start | bytes 393224 | tf_op jit(solution)/shard_map/ppermute | solution.py:516
  29.4 3.7 %collective-permute-start.8 = (f32[32,256]{1,0:T(8,128)S(1)}, f32[32,256]{1,0:T(8,128)S(1)}, u32[]{:S(2)}, u32[]{:S(2)}) collective-permute-start(f32[32,256]{1,0:T(8,128)S(1)} %get-tuple-element.14), channel_id=1, source_target_pairs={{0,3},{1,2},{2,1},{3,0},{4,7},{5,6},{6,5},{7,4},{8,11},{9,10},{10,... | collective-permute-start | bytes 98312 | tf_op jit(solution)/shard_map/ppermute | solution.py:509
  29.4 3.7 %collective-permute-start.7 = (f32[32,256]{1,0:T(8,128)S(1)}, f32[32,256]{1,0:T(8,128)S(1)}, u32[]{:S(2)}, u32[]{:S(2)}) collective-permute-start(f32[32,256]{1,0:T(8,128)S(1)} %get-tuple-element.14), channel_id=1, source_target_pairs={{0,2},{2,0},{4,6},{6,4},{8,10},{10,8},{12,14},{14,12},{16,18},{18,... | collective-permute-start | bytes 98312 | tf_op jit(solution)/shard_map/ppermute | solution.py:507
  30.1 3.1 %collective-permute-start.10 = (f32[32,256]{1,0:T(8,128)S(1)}, f32[32,256]{1,0:T(8,128)S(1)}, u32[]{:S(2)}, u32[]{:S(2)}) collective-permute-start(f32[32,256]{1,0:T(8,128)S(1)} %get-tuple-element.15), channel_id=1, source_target_pairs={{2,5},{3,4},{4,3},{5,2},{6,9},{7,8},{8,7},{9,6},{10,13},{11,12},{1... | collective-permute-start | bytes 98312 | tf_op jit(solution)/shard_map/ppermute | solution.py:509
  30.7 2.4 %collective-permute-start.9 = (f32[32,256]{1,0:T(8,128)S(1)}, f32[32,256]{1,0:T(8,128)S(1)}, u32[]{:S(2)}, u32[]{:S(2)}) collective-permute-start(f32[32,256]{1,0:T(8,128)S(1)} %get-tuple-element.15), channel_id=1, source_target_pairs={{2,4},{4,2},{6,8},{8,6},{10,12},{12,10},{14,16},{16,14},{18,20},{2... | collective-permute-start | bytes 98312 | tf_op jit(solution)/shard_map/ppermute | solution.py:507
  40.0 15.9 %collective-permute-start.14 = (f32[256,128]{1,0:T(8,128)S(1)}, f32[256,128]{1,0:T(8,128)S(1)}, u32[]{:S(2)}, u32[]{:S(2)}) collective-permute-start(f32[256,128]{1,0:T(8,128)S(1)} %shard_map.117.refs_1_), channel_id=1, source_target_pairs={{0,16},{2,18},{4,20},{6,22},{8,24},{10,26},{12,28},{14,30},{16,0},... | collective-permute-start | bytes 393224 | tf_op jit(solution)/shard_map/ppermute | solution.py:525
  49.0 6.9 %collective-permute-start.13 = (f32[256,128]{1,0:T(8,128)S(1)}, f32[256,128]{1,0:T(8,128)S(1)}, u32[]{:S(2)}, u32[]{:S(2)}) collective-permute-start(f32[256,128]{1,0:T(8,128)S(1)} %shard_map.117.refs_1_), channel_id=1, source_target_pairs={{0,8},{2,10},{4,12},{6,14},{8,0},{10,2},{12,4},{14,6},{16,24},{18,... | collective-permute-start | bytes 393224 | tf_op jit(solution)/shard_map/ppermute | solution.py:525
  49.7 6.2 %collective-permute-start.12 = (f32[256,128]{1,0:T(8,128)S(1)}, f32[256,128]{1,0:T(8,128)S(1)}, u32[]{:S(2)}, u32[]{:S(2)}) collective-permute-start(f32[256,128]{1,0:T(8,128)S(1)} %shard_map.117.refs_1_), channel_id=1, source_target_pairs={{0,4},{2,6},{4,0},{6,2},{8,12},{10,14},{12,8},{14,10},{16,20},{18,... | collective-permute-start | bytes 393224 | tf_op jit(solution)/shard_map/ppermute | solution.py:525
  50.5 5.4 %collective-permute-start.11 = (f32[256,128]{1,0:T(8,128)S(1)}, f32[256,128]{1,0:T(8,128)S(1)}, u32[]{:S(2)}, u32[]{:S(2)}) collective-permute-start(f32[256,128]{1,0:T(8,128)S(1)} %shard_map.117.refs_1_), channel_id=1, source_target_pairs={{0,2},{2,0},{4,6},{6,4},{8,10},{10,8},{12,14},{14,12},{16,18},{18,... | collective-permute-start | bytes 393224 | tf_op jit(solution)/shard_map/ppermute | solution.py:525
  56.6 5.3 %collective-permute-start.15 = (f32[256,128]{1,0:T(8,128)S(1)}, f32[256,128]{1,0:T(8,128)S(1)}, u32[]{:S(2)}, u32[]{:S(2)}) collective-permute-start(f32[256,128]{1,0:T(8,128)S(1)} %shard_map.118.refs_3_), channel_id=1, source_target_pairs={{0,1},{1,0},{2,3},{3,2},{4,5},{5,4},{6,7},{7,6},{8,9},{9,8},{10,11... | collective-permute-start | bytes 393224 | tf_op jit(solution)/shard_map/ppermute | solution.py:516

commit v9 on v8

--- a/solution.py
+++ b/solution.py
@@ -292,8 +292,10 @@
 
 def gradient_body(kern, last, f_ref, tgt_ref, h_ref, thr_ref, tb, g_ref, work):
     fld, inten, tot, a_hi, a_lo, b_cat, r_cat, w_cat = work
-    chains = [(t, k) for t in range(2) for k in range(kern)]
-    lag = kern + 2
+    group = 2 if kern % 2 == 0 else 1
+    count = kern // group
+    chains = [(t, c) for t in range(2) for c in range(count)]
+    lag = count + 2
 
     def at(i):
         return chains[i] if 0 <= i < len(chains) else None
@@ -315,10 +317,10 @@
         for at_row, piece in zip(starts, pieces):
             ref[slot, at_row : at_row + CHUNK] = piece
 
-    def products(t, k, slot):
-        for part in range(2):
+    def products(t, c, slot):
+        for part in range(2 * group):
             for rows in chunks(XB):
-                hpr, hpi, hmr, hmi = (h_ref[2 * k + part, j, rows] for j in range(4))
+                hpr, hpi, hmr, hmi = (h_ref[2 * group * c + part, j, rows] for j in range(4))
                 fpr, fpi, fmr, fmi = (f_ref[t, j, rows] for j in range(4))
                 pr, pi = hpr * fpr - hpi * fpi, hpr * fpi + hpi * fpr
                 mr, mi = hmr * fmr - hmi * fmi, hmr * fmi + hmi * fmr
@@ -329,23 +331,26 @@
                 put(a_lo, slot, starts, (top[1], low[1]))
 
     def y_done(z_one, z_two, slot):
-        for rows in chunks(2 * XB):
-            z = []
-            for part in range(2):
-                here = slice(2 * XB * part + rows.start, 2 * XB * part + rows.stop)
-                z.append(z_one[here, :CORE] + (z_one[here, CORE:] + z_two[here]))
-            z_hi, z_lo = split(jnp.concatenate(z, axis=1))
-            starts = [2 * XB * j + rows.start for j in range(3)]
-            put(b_cat, slot, starts, (z_hi, z_hi, z_lo))
-
-    def field_of(t, k, slot):
-        whole = dot(tb("x2"), b_cat[slot])
-        for rows in chunks(ROWS):
-            field = whole[rows]
-            fld[t, k, rows] = field
-            re, im = field[:, :CORE], field[:, CORE:]
-            power = re * re + im * im
-            inten[t, rows] = power if k == 0 else inten[t, rows] + power
+        for g in range(group):
+            for rows in chunks(2 * XB):
+                z = []
+                for part in range(2 * g, 2 * g + 2):
+                    here = slice(2 * XB * part + rows.start, 2 * XB * part + rows.stop)
+                    z.append(z_one[here, :CORE] + (z_one[here, CORE:] + z_two[here]))
+                z_hi, z_lo = split(jnp.concatenate(z, axis=1))
+                starts = [2 * XB * j + rows.start for j in range(3)]
+                put(b_cat, 2 * g + slot, starts, (z_hi, z_hi, z_lo))
+
+    def field_of(t, c, slot):
+        for g in range(group):
+            k = group * c + g
+            whole = dot(tb("x2"), b_cat[2 * g + slot])
+            for rows in chunks(ROWS):
+                field = whole[rows]
+                fld[t, k, rows] = field
+                re, im = field[:, :CORE], field[:, CORE:]
+                power = re * re + im * im
+                inten[t, rows] = power if k == 0 else inten[t, rows] + power
 
     def slope_of(t):
         resist = jax.nn.sigmoid(STEEPNESS * (inten[t] - thr_ref[0]))
@@ -353,35 +358,37 @@
         slope = 2.0 * (resist - target) * STEEPNESS * resist * (1.0 - resist)
         inten[t] = jnp.where(inside, 2.0 * slope, 0.0)
 
-    def scaled_field(t, k, slot):
-        for rows in chunks(ROWS):
-            slope, field = inten[t, rows], fld[t, k, rows]
-            r_hi, r_lo = split(
-                jnp.concatenate([slope * field[:, :CORE], slope * field[:, CORE:]], axis=1)
-            )
-            starts = [ROWS * j + rows.start for j in range(3)]
-            put(r_cat, slot, starts, (r_hi, r_hi, r_lo))
-
-    def x_back_done(w_now, slot):
+    def scaled_field(t, c, slot):
+        for g in range(group):
+            for rows in chunks(ROWS):
+                slope, field = inten[t, rows], fld[t, group * c + g, rows]
+                r_hi, r_lo = split(
+                    jnp.concatenate([slope * field[:, :CORE], slope * field[:, CORE:]], axis=1)
+                )
+                starts = [ROWS * j + rows.start for j in range(3)]
+                put(r_cat, 2 * g + slot, starts, (r_hi, r_hi, r_lo))
+
+    def x_back_done(w_now, g, slot):
         for rows in chunks(2 * XB):
             w_hi, w_lo = split(w_now[rows])
             for part in range(2):
-                here = slice(2 * XB * part + rows.start, 2 * XB * part + rows.stop)
+                base = 2 * XB * (2 * g + part)
+                here = slice(base + rows.start, base + rows.stop)
                 lanes = slice(CORE * part, CORE * part + CORE)
                 for j, piece in enumerate((w_hi, w_lo, w_hi)):
                     w_cat[slot, here, CORE * j : CORE * j + CORE] = piece[:, lanes]
 
-    def add_back(t, k, slot):
+    def add_back(t, c, slot):
         specs = dot(w_cat[slot], tb("y3"))
         for rows in chunks(XB):
-            acc = [0.0] * 4 if k == 0 else [tot[t, j, rows] for j in range(4)]
-            for part in range(2):
+            acc = [0.0] * 4 if c == 0 else [tot[t, j, rows] for j in range(4)]
+            for part in range(2 * group):
                 base = 2 * XB * part + rows.start
                 cos_rows, sin_rows = slice(base, base + CHUNK), slice(base + XB, base + XB + CHUNK)
                 cc, cs = specs[cos_rows, :YB], specs[cos_rows, YB:]
                 sc, ss = specs[sin_rows, :YB], specs[sin_rows, YB:]
                 bpr, neg, bmr, bmi = cc - ss, cs + sc, cc + ss, sc - cs
-                hpr, hpi, hmr, hmi = (h_ref[2 * k + part, j, rows] for j in range(4))
+                hpr, hpi, hmr, hmi = (h_ref[2 * group * c + part, j, rows] for j in range(4))
                 acc[0] = acc[0] + (hpr * bpr - hpi * neg)
                 acc[1] = acc[1] - (hpr * neg + hpi * bpr)
                 acc[2] = acc[2] + (hmr * bmr + hmi * bmi)
@@ -406,7 +413,7 @@
         if new:
             products(*new, slot)
         if back_mid:
-            w_now = dot(tb("x3"), r_cat[other])
+            w_now = [dot(tb("x3"), r_cat[2 * g + other]) for g in range(group)]
         if back:
             scaled_field(*back, slot)
         if old:
@@ -416,10 +423,11 @@
         if mid:
             y_done(z_one, z_two, other)
         if back_mid:
-            x_back_done(w_now, other)
-        if old and old[1] == kern - 1:
+            for g in range(group):
+                x_back_done(w_now[g], g, other)
+        if old and old[1] == count - 1:
             slope_of(old[0])
-        if back_old and back_old[1] == kern - 1:
+        if back_old and back_old[1] == count - 1:
             finish(back_old[0])
 
 
@@ -534,15 +542,16 @@
     freq = jax.ShapeDtypeStruct((2, 4, XB, YB), f32)
     goal = jax.ShapeDtypeStruct((ROWS, 2 * CORE), f32)
     tiles = jax.ShapeDtypeStruct((tiles_dev, core, core), f32)
+    group = 2 if kern % 2 == 0 else 1
     scratch = [
         pltpu.VMEM((2, kern, ROWS, 2 * CORE), f32),
         pltpu.VMEM((2, ROWS, CORE), f32),
         pltpu.VMEM((2, 4, XB, YB), f32),
-        pltpu.VMEM((2, 4 * XB, 2 * YB), bf16),
-        pltpu.VMEM((2, 4 * XB, 2 * YB), bf16),
-        pltpu.VMEM((2, 6 * XB, 2 * CORE), bf16),
-        pltpu.VMEM((2, 3 * ROWS, 2 * CORE), bf16),
-        pltpu.VMEM((2, 4 * XB, 3 * CORE), bf16),
+        pltpu.VMEM((2, group * 4 * XB, 2 * YB), bf16),
+        pltpu.VMEM((2, group * 4 * XB, 2 * YB), bf16),
+        pltpu.VMEM((2 * group, 6 * XB, 2 * CORE), bf16),
+        pltpu.VMEM((2 * group, 3 * ROWS, 2 * CORE), bf16),
+        pltpu.VMEM((2, group * 4 * XB, 3 * CORE), bf16),
     ]
 
     edge = jax.ShapeDtypeStruct((EDGE, tiles_dev * core), f32)

time: 62.8 us -> 62.7 us (level)
  no operation moved by 1% of the time
where the time goes in v9:
time: 62.7 us; the launch traced here: 62.5 us
  starting transfers between devices  24.8 us (40%)
  Pallas kernels  18.1 us (29%)
  waiting for transfers between devices  16.1 us (26%)
  local copies, waits for them, and re-layouts  1.85 us (3%)
  between operations  1.5 us (2%)
    ppermute x8, starting transfers between devices, from_partners(): lax.ppermute(grad, 'tile', [(i, i ^ bit) for i in range(n_tile)])  19.4 us
    pallas_call x7, Pallas kernels, call(): pl.pallas_call(wrapped, out_shape=out_shape, in_specs=[sm if i in smem el...  18.1 us
    ppermute x8, waiting for transfers between devices, from_partners(): lax.ppermute(grad, 'tile', [(i, i ^ bit) for i in range(n_tile)])  9.78 us
    ppermute x2, waiting for transfers between devices, depth_pair(): peer = lax.ppermute(x, 'depth', [(i, i ^ bit) for i in range(n_depth)])  4.79 us
    ppermute x4, starting transfers between devices, move(): return lax.ppermute(x, 'tile', pairs)  2.63 us
    ppermute x2, starting transfers between devices, depth_pair(): peer = lax.ppermute(x, 'depth', [(i, i ^ bit) for i in range(n_depth)])  2.12 us
    unnamed x20, local copies, waits for them, and re-layouts  1.85 us
    ppermute x2, waiting for transfers between devices, move(): return lax.ppermute(x, ('tile', 'depth'), both)  1.55 us
  transfers between devices with their start and end apart: 16, of which 6 were waited for; matrix products, arithmetic and copies ran while one was open for 0% of the time, Pallas kernels for 3%

profile of v9, /device:TPU:0, one launch (start us, length us, event | category | flops | bytes accessed | tf_op | source)
XLA Modules:
  0.0 62.5 jit_solution(9452502311427758715)
XLA Ops:
  0.6 0.0 copy-start
  0.6 0.9 %copy-done = f32[2,128,128]{2,1,0:T(8,128)S(1)} copy-done((f32[2,128,128]{2,1,0:T(8,128)S(1)}, f32[2,128,128]{2,1,0:T(8,128)}, u32[]{:S(2)}) %copy-start) | copy-done | bytes 131096
  1.5 0.9 %copy-done.3 = s32[2,128,128]{2,1,0:T(8,128)S(1)} copy-done((s32[2,128,128]{2,1,0:T(8,128)S(1)}, s32[2,128,128]{2,1,0:T(8,128)}, u32[]{:S(2)}) %copy-start.3) | copy-done | bytes 131096
  2.4 0.2 shard_map.113
  2.7 0.5 collective-permute-start
  3.2 0.7 %collective-permute-start.1 = (f32[48,256]{1,0:T(8,128)S(1)}, f32[48,256]{1,0:T(8,128)S(1)}, u32[]{:S(2)}, u32[]{:S(2)}) collective-permute-start(f32[48,256]{1,0:T(8,128)S(1)} %get-tuple-element.11), channel_id=1, source_target_pairs={{2,4},{4,2},{6,8},{8,6},{10,12},{12,10},{14,16},{16,14},{18,20},{2... | collective-permute-start | bytes 147464 | tf_op jit(solution)/shard_map/ppermute | solution.py:515
  3.9 0.0 copy-start.1
  3.9 0.0 copy-start.4
  3.9 0.0 copy-start.6
  3.9 2.0 %shard_map.114.refs_5_.refs_9_ = f32[12,4,96,128]{3,2,1,0:T(8,128)S(1)} custom-call(f32[1,6]{1,0:T(1,128)S(1)} %copy-done.5, f32[2,6,25,1,25]{4,3,2,1,0:T(1,128)S(1)} %bitcast.5, bf16[1408,256]{1,0:T(8,128)(2,1)S(1)} %copy-done.7), custom_call_target="tpu_custom_call" | custom-call | flops 3000000000 | bytes 4000000 | tf_op jit(solution)/shard_map/pallas_call | solution.py:210
  6.6 0.0 copy-start.8
  6.6 0.0 copy-start.9
  6.6 0.0 collective-permute-done.refs_3_
  6.6 0.0 collective-permute-done.1.refs_4_
  6.6 6.8 %shard_map.115 = (f32[256,128]{1,0:T(8,128)S(1)}, f32[2,4,96,128]{3,2,1,0:T(8,128)S(1)}, f32[160,256]{1,0:T(8,128)S(1)}) custom-call(f32[1]{0:T(128)S(6)} %copy.12.refs_0_, f32[256,128]{1,0:T(8,128)S(1)} %bitcast.4, s32[256,128]{1,0:T(8,128)S(1)} %bitcast.7, f32[48,256]{1,0:T(8,128)S(1)} %collective-permute-done.refs_3_, ...), custom_call_target="tpu_custom_call" | custom-call | flops 10000000000 | tf_op jit(solution)/shard_map/pallas_call | solution.py:210
  13.4 6.7 %collective-permute-start.5 = (f32[256,128]{1,0:T(8,128)S(1)}, f32[256,128]{1,0:T(8,128)S(1)}, u32[]{:S(2)}, u32[]{:S(2)}) collective-permute-start(f32[256,128]{1,0:T(8,128)S(1)} %get-tuple-element.12.refs_1_), channel_id=1, source_target_pairs={{0,16},{2,18},{4,20},{6,22},{8,24},{10,26},{12,28},{14,30},{16,0},... | collective-permute-start | bytes 393224 | tf_op jit(solution)/shard_map/ppermute | solution.py:533
  20.1 1.6 %collective-permute-start.4 = (f32[256,128]{1,0:T(8,128)S(1)}, f32[256,128]{1,0:T(8,128)S(1)}, u32[]{:S(2)}, u32[]{:S(2)}) collective-permute-start(f32[256,128]{1,0:T(8,128)S(1)} %get-tuple-element.12.refs_1_), channel_id=1, source_target_pairs={{0,8},{2,10},{4,12},{6,14},{8,0},{10,2},{12,4},{14,6},{16,24},{18,... | collective-permute-start | bytes 393224 | tf_op jit(solution)/shard_map/ppermute | solution.py:533
  21.7 0.5 collective-permute-start.3
  22.2 0.0 collective-permute-start.2
  22.2 0.1 pad_add_fusion.refs_0_
  22.3 4.4 %collective-permute-done.5.refs_5_ = f32[256,128]{1,0:T(8,128)S(1)} collective-permute-done((f32[256,128]{1,0:T(8,128)S(1)}, f32[256,128]{1,0:T(8,128)S(1)}, u32[]{:S(2)}, u32[]{:S(2)}) %collective-permute-start.5) | collective-permute-done | bytes 131104 | tf_op jit(solution)/shard_map/ppermute | solution.py:533
  26.7 0.2 collective-permute-done.4.refs_4_
  26.9 0.0 collective-permute-done.3.refs_3_
  26.9 0.0 collective-permute-done.2.refs_2_
  26.9 0.9 %shard_map.116 = (f32[256,128]{1,0:T(8,128)S(1)}, f32[32,256]{1,0:T(8,128)S(1)}, f32[32,256]{1,0:T(8,128)S(1)}) custom-call(s32[4]{0:T(128)S(1)} %pad_add_fusion.refs_0_, f32[256,128]{1,0:T(8,128)S(1)} %get-tuple-element.12.refs_1_, f32[256,128]{1,0:T(8,128)S(1)} %collective-permute-done.2.refs_2_, f32[256,128]{1,0:T(8,128)S(1)} %collective-permute-done.3.refs_3_, ...), custom_call_target="tpu_custom_call" | custom-call | tf_op jit(solution)/shard_map/pallas_call | solution.py:210
  27.8 1.6 %collective-permute-start.6 = (f32[256,128]{1,0:T(8,128)S(1)}, f32[256,128]{1,0:T(8,128)S(1)}, u32[]{:S(2)}, u32[]{:S(2)}) collective-permute-start(f32[256,128]{1,0:T(8,128)S(1)} %get-tuple-element.13.refs_1_), channel_id=1, source_target_pairs={{0,1},{1,0},{2,3},{3,2},{4,5},{5,4},{6,7},{7,6},{8,9},{9,8},{10,11... | collective-permute-start | bytes 393224 | tf_op jit(solution)/shard_map/ppermute | solution.py:524
  29.3 0.0 collective-permute-start.8
  29.3 0.6 collective-permute-start.7
  29.9 0.7 %collective-permute-start.10 = (f32[32,256]{1,0:T(8,128)S(1)}, f32[32,256]{1,0:T(8,128)S(1)}, u32[]{:S(2)}, u32[]{:S(2)}) collective-permute-start(f32[32,256]{1,0:T(8,128)S(1)} %get-tuple-element.15), channel_id=1, source_target_pairs={{2,5},{3,4},{4,3},{5,2},{6,9},{7,8},{8,7},{9,6},{10,13},{11,12},{1... | collective-permute-start | bytes 98312 | tf_op jit(solution)/shard_map/ppermute | solution.py:517
  30.6 0.8 %collective-permute-start.9 = (f32[32,256]{1,0:T(8,128)S(1)}, f32[32,256]{1,0:T(8,128)S(1)}, u32[]{:S(2)}, u32[]{:S(2)}) collective-permute-start(f32[32,256]{1,0:T(8,128)S(1)} %get-tuple-element.15), channel_id=1, source_target_pairs={{2,4},{4,2},{6,8},{8,6},{10,12},{12,10},{14,16},{16,14},{18,20},{2... | collective-permute-start | bytes 98312 | tf_op jit(solution)/shard_map/ppermute | solution.py:515
  31.5 1.5 %collective-permute-done.8.refs_4_ = f32[32,256]{1,0:T(8,128)S(1)} collective-permute-done((f32[32,256]{1,0:T(8,128)S(1)}, f32[32,256]{1,0:T(8,128)S(1)}, u32[]{:S(2)}, u32[]{:S(2)}) %collective-permute-start.8) | collective-permute-done | bytes 32800 | tf_op jit(solution)/shard_map/ppermute | solution.py:517
  33.0 0.0 collective-permute-done.7.refs_3_
  33.0 0.0 collective-permute-done.10.refs_6_
  33.0 0.0 collective-permute-done.9.refs_5_
  33.0 0.1 collective-permute-done.6.refs_2_
  33.1 6.8 %shard_map.117.refs_1_ = f32[256,128]{1,0:T(8,128)S(1)} custom-call(f32[1]{0:T(128)S(6)} %copy.12.refs_0_, f32[256,128]{1,0:T(8,128)S(1)} %get-tuple-element.13.refs_1_, f32[256,128]{1,0:T(8,128)S(1)} %collective-permute-done.6.refs_2_, f32[32,256]{1,0:T(8,128)S(1)} %collective-permute-done.7.refs_3_, f32[32,256]{1,0:T(8,128)S(1)} %collective-permute-done.8.refs_4_, ...), custom_call_target="tpu_custom_call" | custom-call | flops 10000000000 | tf_op jit(solution)/shard_map/pallas_call | solution.py:210
  39.9 9.0 %collective-permute-start.14 = (f32[256,128]{1,0:T(8,128)S(1)}, f32[256,128]{1,0:T(8,128)S(1)}, u32[]{:S(2)}, u32[]{:S(2)}) collective-permute-start(f32[256,128]{1,0:T(8,128)S(1)} %shard_map.117.refs_1_), channel_id=1, source_target_pairs={{0,16},{2,18},{4,20},{6,22},{8,24},{10,26},{12,28},{14,30},{16,0},... | collective-permute-start | bytes 393224 | tf_op jit(solution)/shard_map/ppermute | solution.py:533
  48.9 0.7 %collective-permute-start.13 = (f32[256,128]{1,0:T(8,128)S(1)}, f32[256,128]{1,0:T(8,128)S(1)}, u32[]{:S(2)}, u32[]{:S(2)}) collective-permute-start(f32[256,128]{1,0:T(8,128)S(1)} %shard_map.117.refs_1_), channel_id=1, source_target_pairs={{0,8},{2,10},{4,12},{6,14},{8,0},{10,2},{12,4},{14,6},{16,24},{18,... | collective-permute-start | bytes 393224 | tf_op jit(solution)/shard_map/ppermute | solution.py:533
  49.6 0.7 %collective-permute-start.12 = (f32[256,128]{1,0:T(8,128)S(1)}, f32[256,128]{1,0:T(8,128)S(1)}, u32[]{:S(2)}, u32[]{:S(2)}) collective-permute-start(f32[256,128]{1,0:T(8,128)S(1)} %shard_map.117.refs_1_), channel_id=1, source_target_pairs={{0,4},{2,6},{4,0},{6,2},{8,12},{10,14},{12,8},{14,10},{16,20},{18,... | collective-permute-start | bytes 393224 | tf_op jit(solution)/shard_map/ppermute | solution.py:533
  50.3 0.3 collective-permute-start.11
  50.6 5.1 %collective-permute-done.14.refs_5_ = f32[256,128]{1,0:T(8,128)S(1)} collective-permute-done((f32[256,128]{1,0:T(8,128)S(1)}, f32[256,128]{1,0:T(8,128)S(1)}, u32[]{:S(2)}, u32[]{:S(2)}) %collective-permute-start.14) | collective-permute-done | bytes 131104 | tf_op jit(solution)/shard_map/ppermute | solution.py:533
  55.7 0.0 collective-permute-done.13.refs_4_
  55.7 0.0 collective-permute-done.12.refs_3_
  55.8 0.0 collective-permute-done.11.refs_2_
  55.8 0.7 %shard_map.118.refs_3_ = f32[256,128]{1,0:T(8,128)S(1)} custom-call(s32[4]{0:T(128)S(1)} %pad_add_fusion.refs_0_, f32[256,128]{1,0:T(8,128)S(1)} %shard_map.117.refs_1_, f32[256,128]{1,0:T(8,128)S(1)} %collective-permute-done.11.refs_2_, f32[256,128]{1,0:T(8,128)S(1)} %collective-permute-done.12.refs_3_, f32[256,128]{1,0:T(8,128)S(1)} %collective-permute-done.13.refs_4_, ...), custom_call_target="tpu_custom_call" | custom-call | tf_op jit(solution)/shard_map/pallas_call | solution.py:210
  56.5 0.6 collective-permute-start.15
  57.1 4.7 %collective-permute-done.15.refs_4_ = f32[256,128]{1,0:T(8,128)S(1)} collective-permute-done((f32[256,128]{1,0:T(8,128)S(1)}, f32[256,128]{1,0:T(8,128)S(1)}, u32[]{:S(2)}, u32[]{:S(2)}) %collective-permute-start.15) | collective-permute-done | bytes 131104 | tf_op jit(solution)/shard_map/ppermute | solution.py:524
  61.7 0.7 %shard_map.119 = (f32[2,128,128]{2,1,0:T(8,128)}, f32[2,128,128]{2,1,0:T(8,128)}) custom-call(f32[2,128,128]{2,1,0:T(8,128)S(1)} %copy-done.1, f32[256,128]{1,0:T(8,128)S(1)} %get-tuple-element.13.refs_1_, f32[256,128]{1,0:T(8,128)S(1)} %collective-permute-done.6.refs_2_, f32[256,128]{1,0:T(8,128)S(1)} %shard_map.118.refs_3_, ...), custom_call_target="tpu_custom_call" | custom-call | tf_op jit(solution)/shard_map/pallas_call | solution.py:210
  (12 shorter events, 0.0 us)
Async XLA Ops:
  0.6 0.9 %copy-start = (f32[2,128,128]{2,1,0:T(8,128)S(1)}, f32[2,128,128]{2,1,0:T(8,128)}, u32[]{:S(2)}) copy-start(f32[2,128,128]{2,1,0:T(8,128)} %refs_0_.5) | copy-start | bytes 393220
  1.5 0.9 %copy-start.3 = (s32[2,128,128]{2,1,0:T(8,128)S(1)}, s32[2,128,128]{2,1,0:T(8,128)}, u32[]{:S(2)}) copy-start(s32[2,128,128]{2,1,0:T(8,128)} %param.11) | copy-start | bytes 393220
  2.4 1.4 %copy-start.2 = (f32[2,1,6,25,25]{4,1,3,2,0:T(1,128)S(1)}, f32[2,1,6,25,25]{4,1,3,2,0:T(1,128)}, u32[]{:S(2)}) copy-start(f32[2,1,6,25,25]{4,1,3,2,0:T(1,128)} %param.12) | copy-start | bytes 90004
  2.4 1.4 %copy-start.5 = (f32[1,6]{1,0:T(1,128)S(1)}, f32[1,6]{1,0:T(1,128)}, u32[]{:S(2)}) copy-start(f32[1,6]{1,0:T(1,128)} %refs_0_.4) | copy-start | bytes 76
  2.4 1.4 %copy-start.7 = (bf16[1408,256]{1,0:T(8,128)(2,1)S(1)}, bf16[1408,256]{1,0:T(8,128)(2,1)}, u32[]{:S(2)}) copy-start(bf16[1408,256]{1,0:T(8,128)(2,1)} %constant.4.clone.refs_2_) | copy-start | bytes 2162692
  2.7 3.9 %collective-permute-start = (f32[48,256]{1,0:T(8,128)S(1)}, f32[48,256]{1,0:T(8,128)S(1)}, u32[]{:S(2)}, u32[]{:S(2)}) collective-permute-start(f32[48,256]{1,0:T(8,128)S(1)} %get-tuple-element.10), channel_id=1, source_target_pairs={{0,2},{2,0},{4,6},{6,4},{8,10},{10,8},{12,14},{14,12},{16,18},{18,... | collective-permute-start | bytes 147464 | tf_op jit(solution)/shard_map/ppermute | solution.py:515
  3.2 3.4 %collective-permute-start.1 = (f32[48,256]{1,0:T(8,128)S(1)}, f32[48,256]{1,0:T(8,128)S(1)}, u32[]{:S(2)}, u32[]{:S(2)}) collective-permute-start(f32[48,256]{1,0:T(8,128)S(1)} %get-tuple-element.11), channel_id=1, source_target_pairs={{2,4},{4,2},{6,8},{8,6},{10,12},{12,10},{14,16},{16,14},{18,20},{2... | collective-permute-start | bytes 147464 | tf_op jit(solution)/shard_map/ppermute | solution.py:515
  3.9 2.7 %copy-start.1 = (f32[2,128,128]{2,1,0:T(8,128)S(1)}, f32[2,128,128]{2,1,0:T(8,128)}, u32[]{:S(2)}) copy-start(f32[2,128,128]{2,1,0:T(8,128)} %refs_0_.5) | copy-start | bytes 393220
  3.9 2.7 %copy-start.4 = (s32[2,128,128]{2,1,0:T(8,128)S(1)}, s32[2,128,128]{2,1,0:T(8,128)}, u32[]{:S(2)}) copy-start(s32[2,128,128]{2,1,0:T(8,128)} %param.11) | copy-start | bytes 393220
  3.9 2.7 %copy-start.6 = (bf16[4000,256]{1,0:T(8,128)(2,1)S(1)}, bf16[4000,256]{1,0:T(8,128)(2,1)}, u32[]{:S(2)}) copy-start(bf16[4000,256]{1,0:T(8,128)(2,1)} %constant.5.clone.refs_6_.refs_10_) | copy-start | bytes 6144004
  6.6 15.6 %copy-start.8 = (s32[2]{0:T(128)S(1)}, s32[2]{0:T(128)}, u32[]{:S(2)}) copy-start(s32[2]{0:T(128)} %param.16) | copy-start | bytes 28
  6.6 15.6 %copy-start.9 = (s32[2]{0:T(128)S(1)}, s32[2]{0:T(128)}, u32[]{:S(2)}) copy-start(s32[2]{0:T(128)} %param.15) | copy-start | bytes 28
  13.4 13.2 %collective-permute-start.5 = (f32[256,128]{1,0:T(8,128)S(1)}, f32[256,128]{1,0:T(8,128)S(1)}, u32[]{:S(2)}, u32[]{:S(2)}) collective-permute-start(f32[256,128]{1,0:T(8,128)S(1)} %get-tuple-element.12.refs_1_), channel_id=1, source_target_pairs={{0,16},{2,18},{4,20},{6,22},{8,24},{10,26},{12,28},{14,30},{16,0},... | collective-permute-start | bytes 393224 | tf_op jit(solution)/shard_map/ppermute | solution.py:533
  20.1 6.8 %collective-permute-start.4 = (f32[256,128]{1,0:T(8,128)S(1)}, f32[256,128]{1,0:T(8,128)S(1)}, u32[]{:S(2)}, u32[]{:S(2)}) collective-permute-start(f32[256,128]{1,0:T(8,128)S(1)} %get-tuple-element.12.refs_1_), channel_id=1, source_target_pairs={{0,8},{2,10},{4,12},{6,14},{8,0},{10,2},{12,4},{14,6},{16,24},{18,... | collective-permute-start | bytes 393224 | tf_op jit(solution)/shard_map/ppermute | solution.py:533
  21.7 5.2 %collective-permute-start.3 = (f32[256,128]{1,0:T(8,128)S(1)}, f32[256,128]{1,0:T(8,128)S(1)}, u32[]{:S(2)}, u32[]{:S(2)}) collective-permute-start(f32[256,128]{1,0:T(8,128)S(1)} %get-tuple-element.12.refs_1_), channel_id=1, source_target_pairs={{0,4},{2,6},{4,0},{6,2},{8,12},{10,14},{12,8},{14,10},{16,20},{18,... | collective-permute-start | bytes 393224 | tf_op jit(solution)/shard_map/ppermute | solution.py:533
  22.2 4.7 %collective-permute-start.2 = (f32[256,128]{1,0:T(8,128)S(1)}, f32[256,128]{1,0:T(8,128)S(1)}, u32[]{:S(2)}, u32[]{:S(2)}) collective-permute-start(f32[256,128]{1,0:T(8,128)S(1)} %get-tuple-element.12.refs_1_), channel_id=1, source_target_pairs={{0,2},{2,0},{4,6},{6,4},{8,10},{10,8},{12,14},{14,12},{16,18},{18,... | collective-permute-start | bytes 393224 | tf_op jit(solution)/shard_map/ppermute | solution.py:533
  27.8 5.4 %collective-permute-start.6 = (f32[256,128]{1,0:T(8,128)S(1)}, f32[256,128]{1,0:T(8,128)S(1)}, u32[]{:S(2)}, u32[]{:S(2)}) collective-permute-start(f32[256,128]{1,0:T(8,128)S(1)} %get-tuple-element.13.refs_1_), channel_id=1, source_target_pairs={{0,1},{1,0},{2,3},{3,2},{4,5},{5,4},{6,7},{7,6},{8,9},{9,8},{10,11... | collective-permute-start | bytes 393224 | tf_op jit(solution)/shard_map/ppermute | solution.py:524
  29.3 3.7 %collective-permute-start.8 = (f32[32,256]{1,0:T(8,128)S(1)}, f32[32,256]{1,0:T(8,128)S(1)}, u32[]{:S(2)}, u32[]{:S(2)}) collective-permute-start(f32[32,256]{1,0:T(8,128)S(1)} %get-tuple-element.14), channel_id=1, source_target_pairs={{0,3},{1,2},{2,1},{3,0},{4,7},{5,6},{6,5},{7,4},{8,11},{9,10},{10,... | collective-permute-start | bytes 98312 | tf_op jit(solution)/shard_map/ppermute | solution.py:517
  29.3 3.7 %collective-permute-start.7 = (f32[32,256]{1,0:T(8,128)S(1)}, f32[32,256]{1,0:T(8,128)S(1)}, u32[]{:S(2)}, u32[]{:S(2)}) collective-permute-start(f32[32,256]{1,0:T(8,128)S(1)} %get-tuple-element.14), channel_id=1, source_target_pairs={{0,2},{2,0},{4,6},{6,4},{8,10},{10,8},{12,14},{14,12},{16,18},{18,... | collective-permute-start | bytes 98312 | tf_op jit(solution)/shard_map/ppermute | solution.py:515
  29.9 3.1 %collective-permute-start.10 = (f32[32,256]{1,0:T(8,128)S(1)}, f32[32,256]{1,0:T(8,128)S(1)}, u32[]{:S(2)}, u32[]{:S(2)}) collective-permute-start(f32[32,256]{1,0:T(8,128)S(1)} %get-tuple-element.15), channel_id=1, source_target_pairs={{2,5},{3,4},{4,3},{5,2},{6,9},{7,8},{8,7},{9,6},{10,13},{11,12},{1... | collective-permute-start | bytes 98312 | tf_op jit(solution)/shard_map/ppermute | solution.py:517
  30.6 2.4 %collective-permute-start.9 = (f32[32,256]{1,0:T(8,128)S(1)}, f32[32,256]{1,0:T(8,128)S(1)}, u32[]{:S(2)}, u32[]{:S(2)}) collective-permute-start(f32[32,256]{1,0:T(8,128)S(1)} %get-tuple-element.15), channel_id=1, source_target_pairs={{2,4},{4,2},{6,8},{8,6},{10,12},{12,10},{14,16},{16,14},{18,20},{2... | collective-permute-start | bytes 98312 | tf_op jit(solution)/shard_map/ppermute | solution.py:515
  39.9 15.9 %collective-permute-start.14 = (f32[256,128]{1,0:T(8,128)S(1)}, f32[256,128]{1,0:T(8,128)S(1)}, u32[]{:S(2)}, u32[]{:S(2)}) collective-permute-start(f32[256,128]{1,0:T(8,128)S(1)} %shard_map.117.refs_1_), channel_id=1, source_target_pairs={{0,16},{2,18},{4,20},{6,22},{8,24},{10,26},{12,28},{14,30},{16,0},... | collective-permute-start | bytes 393224 | tf_op jit(solution)/shard_map/ppermute | solution.py:533
  48.9 6.9 %collective-permute-start.13 = (f32[256,128]{1,0:T(8,128)S(1)}, f32[256,128]{1,0:T(8,128)S(1)}, u32[]{:S(2)}, u32[]{:S(2)}) collective-permute-start(f32[256,128]{1,0:T(8,128)S(1)} %shard_map.117.refs_1_), channel_id=1, source_target_pairs={{0,8},{2,10},{4,12},{6,14},{8,0},{10,2},{12,4},{14,6},{16,24},{18,... | collective-permute-start | bytes 393224 | tf_op jit(solution)/shard_map/ppermute | solution.py:533
  49.6 6.2 %collective-permute-start.12 = (f32[256,128]{1,0:T(8,128)S(1)}, f32[256,128]{1,0:T(8,128)S(1)}, u32[]{:S(2)}, u32[]{:S(2)}) collective-permute-start(f32[256,128]{1,0:T(8,128)S(1)} %shard_map.117.refs_1_), channel_id=1, source_target_pairs={{0,4},{2,6},{4,0},{6,2},{8,12},{10,14},{12,8},{14,10},{16,20},{18,... | collective-permute-start | bytes 393224 | tf_op jit(solution)/shard_map/ppermute | solution.py:533
  50.3 5.4 %collective-permute-start.11 = (f32[256,128]{1,0:T(8,128)S(1)}, f32[256,128]{1,0:T(8,128)S(1)}, u32[]{:S(2)}, u32[]{:S(2)}) collective-permute-start(f32[256,128]{1,0:T(8,128)S(1)} %shard_map.117.refs_1_), channel_id=1, source_target_pairs={{0,2},{2,0},{4,6},{6,4},{8,10},{10,8},{12,14},{14,12},{16,18},{18,... | collective-permute-start | bytes 393224 | tf_op jit(solution)/shard_map/ppermute | solution.py:533
  56.5 5.2 %collective-permute-start.15 = (f32[256,128]{1,0:T(8,128)S(1)}, f32[256,128]{1,0:T(8,128)S(1)}, u32[]{:S(2)}, u32[]{:S(2)}) collective-permute-start(f32[256,128]{1,0:T(8,128)S(1)} %shard_map.118.refs_3_), channel_id=1, source_target_pairs={{0,1},{1,0},{2,3},{3,2},{4,5},{5,4},{6,7},{7,6},{8,9},{9,8},{10,11... | collective-permute-start | bytes 393224 | tf_op jit(solution)/shard_map/ppermute | solution.py:524

commit v10 on v9

--- a/solution.py
+++ b/solution.py
@@ -269,8 +269,10 @@
             h_ref[c, j] = root * comp
 
 
-def sides(from_a, from_b, tb):
+def sides(last, from_a, from_b, tb):
     even = is_even()
+    tile = lax.axis_index("tile")
+    from_b = jnp.where((tile == 0) | (tile == last), 0.0, from_b)
     l_hi, l_lo = split(jnp.where(even, from_b, from_a))
     r_hi, r_lo = split(jnp.where(even, from_a, from_b))
     height = l_hi.shape[0]
@@ -436,7 +438,7 @@
     g_ref, f_ref, tgt_ref, *work,
 ):
     m_hi, m_lo = split(mask_ref[...])
-    v, left, right = sides(a_ref[...], b_ref[...], tb)
+    v, left, right = sides(last, a_ref[...], b_ref[...], tb)
     v = v + dot3(tb("cx_own_hi"), tb("cx_own_lo"), m_hi, m_lo, dot_nt)
     to_spectrum(v, tb, f_ref, None)
     tgt_ref[...] = (
@@ -454,7 +456,7 @@
     s_hi, s_lo = split(mine_ref[...] + peer_ref[...])
     from_a = a_ref[...] + a2_ref[...]
     from_b = b_ref[...] + b2_ref[...]
-    v, _, _ = sides(from_a, from_b, tb)
+    v, _, _ = sides(last, from_a, from_b, tb)
     v = v + dot3(tb("cx_own_hi"), tb("cx_own_lo"), s_hi, s_lo, dot_nt)
     to_spectrum(v, tb, f_ref, f_in_ref)
     gradient_body(kern, last, f_ref, tgt_ref, h_ref, thr_ref, tb, g_ref, work)
@@ -508,6 +510,7 @@
     assert tiles_dev == 2 and core == CORE
     pairs_a = [(i, i ^ 1) for i in range(n_tile)]
     pairs_b = [p for i in range(1, n_tile - 1, 2) for p in ((i, i + 1), (i + 1, i))]
+    pairs_b += [(0, 0), (n_tile - 1, n_tile - 1)]
 
     def swap_edges(send_a, send_b, cross=False):
         def move(x, pairs):

time: 62.7 us -> 60.7 us (0.968)
  starting transfers between devices: 24.8 us -> 23 us
    ppermute x8, starting transfers between devices: 19.4 us -> 16.8 us  [from_partners(): lax.ppermute(grad, 'tile', [(i, i ^ bit) for i in range(n_tile)])]
    ppermute x2, starting transfers between devices: 0.65 us -> 1.52 us  [move(): return lax.ppermute(x, ('tile', 'depth'), both)]
where the time goes in v10:
time: 60.7 us; the launch traced here: 60.5 us
  starting transfers between devices  23 us (38%)
  Pallas kernels  18.1 us (30%)
  waiting for transfers between devices  16 us (26%)
  local copies, waits for them, and re-layouts  1.85 us (3%)
  between operations  1.49 us (2%)
    pallas_call x7, Pallas kernels, call(): pl.pallas_call(wrapped, out_shape=out_shape, in_specs=[sm if i in smem el...  18.1 us
    ppermute x8, starting transfers between devices, from_partners(): lax.ppermute(grad, 'tile', [(i, i ^ bit) for i in range(n_tile)])  16.8 us
    ppermute x8, waiting for transfers between devices, from_partners(): lax.ppermute(grad, 'tile', [(i, i ^ bit) for i in range(n_tile)])  9.78 us
    ppermute x2, waiting for transfers between devices, depth_pair(): peer = lax.ppermute(x, 'depth', [(i, i ^ bit) for i in range(n_depth)])  4.68 us
    ppermute x4, starting transfers between devices, move(): return lax.ppermute(x, 'tile', pairs)  2.62 us
    ppermute x2, starting transfers between devices, depth_pair(): peer = lax.ppermute(x, 'depth', [(i, i ^ bit) for i in range(n_depth)])  2.13 us
    unnamed x20, local copies, waits for them, and re-layouts  1.85 us
    ppermute x2, waiting for transfers between devices, move(): return lax.ppermute(x, ('tile', 'depth'), both)  1.55 us
  transfers between devices with their start and end apart: 16, of which 6 were waited for; matrix products, arithmetic and copies ran while one was open for 0% of the time, Pallas kernels for 3%

profile of v10, /device:TPU:0, one launch (start us, length us, event | category | flops | bytes accessed | tf_op | source)
XLA Modules:
  0.0 60.5 jit_solution(4942896537546256085)
XLA Ops:
  0.6 0.0 copy-start
  0.6 0.9 %copy-done = f32[2,128,128]{2,1,0:T(8,128)S(1)} copy-done((f32[2,128,128]{2,1,0:T(8,128)S(1)}, f32[2,128,128]{2,1,0:T(8,128)}, u32[]{:S(2)}) %copy-start) | copy-done | bytes 131096
  1.5 0.9 %copy-done.3 = s32[2,128,128]{2,1,0:T(8,128)S(1)} copy-done((s32[2,128,128]{2,1,0:T(8,128)S(1)}, s32[2,128,128]{2,1,0:T(8,128)}, u32[]{:S(2)}) %copy-start.3) | copy-done | bytes 131096
  2.4 0.2 shard_map.113
  2.7 0.5 collective-permute-start
  3.2 0.7 %collective-permute-start.1 = (f32[48,256]{1,0:T(8,128)S(1)}, f32[48,256]{1,0:T(8,128)S(1)}, u32[]{:S(2)}, u32[]{:S(2)}) collective-permute-start(f32[48,256]{1,0:T(8,128)S(1)} %get-tuple-element.11), channel_id=1, source_target_pairs={{2,4},{4,2},{6,8},{8,6},{10,12},{12,10},{14,16},{16,14},{18,20},{2... | collective-permute-start | bytes 147464 | tf_op jit(solution)/shard_map/ppermute | solution.py:518
  3.9 0.0 copy-start.1
  3.9 0.0 copy-start.4
  3.9 0.0 copy-start.6
  3.9 2.0 %shard_map.114.refs_5_.refs_9_ = f32[12,4,96,128]{3,2,1,0:T(8,128)S(1)} custom-call(f32[1,6]{1,0:T(1,128)S(1)} %copy-done.5, f32[2,6,25,1,25]{4,3,2,1,0:T(1,128)S(1)} %bitcast.5, bf16[1408,256]{1,0:T(8,128)(2,1)S(1)} %copy-done.7), custom_call_target="tpu_custom_call" | custom-call | flops 3000000000 | bytes 4000000 | tf_op jit(solution)/shard_map/pallas_call | solution.py:210
  6.6 0.0 copy-start.8
  6.6 0.0 copy-start.9
  6.6 0.0 collective-permute-done.refs_3_
  6.6 0.0 collective-permute-done.1.refs_4_
  6.6 6.8 %shard_map.115 = (f32[256,128]{1,0:T(8,128)S(1)}, f32[2,4,96,128]{3,2,1,0:T(8,128)S(1)}, f32[160,256]{1,0:T(8,128)S(1)}) custom-call(f32[1]{0:T(128)S(6)} %copy.12.refs_0_, f32[256,128]{1,0:T(8,128)S(1)} %bitcast.4, s32[256,128]{1,0:T(8,128)S(1)} %bitcast.7, f32[48,256]{1,0:T(8,128)S(1)} %collective-permute-done.refs_3_, ...), custom_call_target="tpu_custom_call" | custom-call | flops 10000000000 | tf_op jit(solution)/shard_map/pallas_call | solution.py:210
  13.4 6.7 %collective-permute-start.5 = (f32[256,128]{1,0:T(8,128)S(1)}, f32[256,128]{1,0:T(8,128)S(1)}, u32[]{:S(2)}, u32[]{:S(2)}) collective-permute-start(f32[256,128]{1,0:T(8,128)S(1)} %get-tuple-element.12.refs_1_), channel_id=1, source_target_pairs={{0,16},{2,18},{4,20},{6,22},{8,24},{10,26},{12,28},{14,30},{16,0},... | collective-permute-start | bytes 393224 | tf_op jit(solution)/shard_map/ppermute | solution.py:536
  20.1 1.6 %collective-permute-start.4 = (f32[256,128]{1,0:T(8,128)S(1)}, f32[256,128]{1,0:T(8,128)S(1)}, u32[]{:S(2)}, u32[]{:S(2)}) collective-permute-start(f32[256,128]{1,0:T(8,128)S(1)} %get-tuple-element.12.refs_1_), channel_id=1, source_target_pairs={{0,8},{2,10},{4,12},{6,14},{8,0},{10,2},{12,4},{14,6},{16,24},{18,... | collective-permute-start | bytes 393224 | tf_op jit(solution)/shard_map/ppermute | solution.py:536
  21.7 0.5 collective-permute-start.3
  22.2 0.0 collective-permute-start.2
  22.2 0.1 pad_add_fusion.refs_0_
  22.2 4.4 %collective-permute-done.5.refs_5_ = f32[256,128]{1,0:T(8,128)S(1)} collective-permute-done((f32[256,128]{1,0:T(8,128)S(1)}, f32[256,128]{1,0:T(8,128)S(1)}, u32[]{:S(2)}, u32[]{:S(2)}) %collective-permute-start.5) | collective-permute-done | bytes 131104 | tf_op jit(solution)/shard_map/ppermute | solution.py:536
  26.7 0.2 collective-permute-done.4.refs_4_
  26.9 0.0 collective-permute-done.3.refs_3_
  26.9 0.0 collective-permute-done.2.refs_2_
  26.9 0.9 %shard_map.116 = (f32[256,128]{1,0:T(8,128)S(1)}, f32[32,256]{1,0:T(8,128)S(1)}, f32[32,256]{1,0:T(8,128)S(1)}) custom-call(s32[4]{0:T(128)S(1)} %pad_add_fusion.refs_0_, f32[256,128]{1,0:T(8,128)S(1)} %get-tuple-element.12.refs_1_, f32[256,128]{1,0:T(8,128)S(1)} %collective-permute-done.2.refs_2_, f32[256,128]{1,0:T(8,128)S(1)} %collective-permute-done.3.refs_3_, ...), custom_call_target="tpu_custom_call" | custom-call | tf_op jit(solution)/shard_map/pallas_call | solution.py:210
  27.8 1.6 %collective-permute-start.6 = (f32[256,128]{1,0:T(8,128)S(1)}, f32[256,128]{1,0:T(8,128)S(1)}, u32[]{:S(2)}, u32[]{:S(2)}) collective-permute-start(f32[256,128]{1,0:T(8,128)S(1)} %get-tuple-element.13.refs_1_), channel_id=1, source_target_pairs={{0,1},{1,0},{2,3},{3,2},{4,5},{5,4},{6,7},{7,6},{8,9},{9,8},{10,11... | collective-permute-start | bytes 393224 | tf_op jit(solution)/shard_map/ppermute | solution.py:527
  29.3 0.0 collective-permute-start.8
  29.3 0.6 %collective-permute-start.7 = (f32[32,256]{1,0:T(8,128)S(1)}, f32[32,256]{1,0:T(8,128)S(1)}, u32[]{:S(2)}, u32[]{:S(2)}) collective-permute-start(f32[32,256]{1,0:T(8,128)S(1)} %get-tuple-element.14), channel_id=1, source_target_pairs={{0,2},{2,0},{4,6},{6,4},{8,10},{10,8},{12,14},{14,12},{16,18},{18,... | collective-permute-start | bytes 98312 | tf_op jit(solution)/shard_map/ppermute | solution.py:518
  29.9 1.5 %collective-permute-start.10 = (f32[32,256]{1,0:T(8,128)S(1)}, f32[32,256]{1,0:T(8,128)S(1)}, u32[]{:S(2)}, u32[]{:S(2)}) collective-permute-start(f32[32,256]{1,0:T(8,128)S(1)} %get-tuple-element.15), channel_id=1, source_target_pairs={{2,5},{3,4},{4,3},{5,2},{6,9},{7,8},{8,7},{9,6},{10,13},{11,12},{1... | collective-permute-start | bytes 98312 | tf_op jit(solution)/shard_map/ppermute | solution.py:520
  31.5 0.8 %collective-permute-start.9 = (f32[32,256]{1,0:T(8,128)S(1)}, f32[32,256]{1,0:T(8,128)S(1)}, u32[]{:S(2)}, u32[]{:S(2)}) collective-permute-start(f32[32,256]{1,0:T(8,128)S(1)} %get-tuple-element.15), channel_id=1, source_target_pairs={{2,4},{4,2},{6,8},{8,6},{10,12},{12,10},{14,16},{16,14},{18,20},{2... | collective-permute-start | bytes 98312 | tf_op jit(solution)/shard_map/ppermute | solution.py:518
  32.3 0.7 %collective-permute-done.8.refs_4_ = f32[32,256]{1,0:T(8,128)S(1)} collective-permute-done((f32[32,256]{1,0:T(8,128)S(1)}, f32[32,256]{1,0:T(8,128)S(1)}, u32[]{:S(2)}, u32[]{:S(2)}) %collective-permute-start.8) | collective-permute-done | bytes 32800 | tf_op jit(solution)/shard_map/ppermute | solution.py:520
  33.0 0.0 collective-permute-done.7.refs_3_
  33.0 0.9 %collective-permute-done.10.refs_6_ = f32[32,256]{1,0:T(8,128)S(1)} collective-permute-done((f32[32,256]{1,0:T(8,128)S(1)}, f32[32,256]{1,0:T(8,128)S(1)}, u32[]{:S(2)}, u32[]{:S(2)}) %collective-permute-start.10) | collective-permute-done | bytes 32800 | tf_op jit(solution)/shard_map/ppermute | solution.py:520
  33.8 0.0 collective-permute-done.9.refs_5_
  33.9 0.0 collective-permute-done.6.refs_2_
  33.9 6.8 %shard_map.117.refs_1_ = f32[256,128]{1,0:T(8,128)S(1)} custom-call(f32[1]{0:T(128)S(6)} %copy.12.refs_0_, f32[256,128]{1,0:T(8,128)S(1)} %get-tuple-element.13.refs_1_, f32[256,128]{1,0:T(8,128)S(1)} %collective-permute-done.6.refs_2_, f32[32,256]{1,0:T(8,128)S(1)} %collective-permute-done.7.refs_3_, f32[32,256]{1,0:T(8,128)S(1)} %collective-permute-done.8.refs_4_, ...), custom_call_target="tpu_custom_call" | custom-call | flops 10000000000 | tf_op jit(solution)/shard_map/pallas_call | solution.py:210
  40.6 6.3 %collective-permute-start.14 = (f32[256,128]{1,0:T(8,128)S(1)}, f32[256,128]{1,0:T(8,128)S(1)}, u32[]{:S(2)}, u32[]{:S(2)}) collective-permute-start(f32[256,128]{1,0:T(8,128)S(1)} %shard_map.117.refs_1_), channel_id=1, source_target_pairs={{0,16},{2,18},{4,20},{6,22},{8,24},{10,26},{12,28},{14,30},{16,0},... | collective-permute-start | bytes 393224 | tf_op jit(solution)/shard_map/ppermute | solution.py:536
  47.0 0.7 %collective-permute-start.13 = (f32[256,128]{1,0:T(8,128)S(1)}, f32[256,128]{1,0:T(8,128)S(1)}, u32[]{:S(2)}, u32[]{:S(2)}) collective-permute-start(f32[256,128]{1,0:T(8,128)S(1)} %shard_map.117.refs_1_), channel_id=1, source_target_pairs={{0,8},{2,10},{4,12},{6,14},{8,0},{10,2},{12,4},{14,6},{16,24},{18,... | collective-permute-start | bytes 393224 | tf_op jit(solution)/shard_map/ppermute | solution.py:536
  47.7 0.7 %collective-permute-start.12 = (f32[256,128]{1,0:T(8,128)S(1)}, f32[256,128]{1,0:T(8,128)S(1)}, u32[]{:S(2)}, u32[]{:S(2)}) collective-permute-start(f32[256,128]{1,0:T(8,128)S(1)} %shard_map.117.refs_1_), channel_id=1, source_target_pairs={{0,4},{2,6},{4,0},{6,2},{8,12},{10,14},{12,8},{14,10},{16,20},{18,... | collective-permute-start | bytes 393224 | tf_op jit(solution)/shard_map/ppermute | solution.py:536
  48.4 0.3 collective-permute-start.11
  48.7 5.1 %collective-permute-done.14.refs_5_ = f32[256,128]{1,0:T(8,128)S(1)} collective-permute-done((f32[256,128]{1,0:T(8,128)S(1)}, f32[256,128]{1,0:T(8,128)S(1)}, u32[]{:S(2)}, u32[]{:S(2)}) %collective-permute-start.14) | collective-permute-done | bytes 131104 | tf_op jit(solution)/shard_map/ppermute | solution.py:536
  53.8 0.0 collective-permute-done.13.refs_4_
  53.8 0.0 collective-permute-done.12.refs_3_
  53.8 0.0 collective-permute-done.11.refs_2_
  53.8 0.7 %shard_map.118.refs_3_ = f32[256,128]{1,0:T(8,128)S(1)} custom-call(s32[4]{0:T(128)S(1)} %pad_add_fusion.refs_0_, f32[256,128]{1,0:T(8,128)S(1)} %shard_map.117.refs_1_, f32[256,128]{1,0:T(8,128)S(1)} %collective-permute-done.11.refs_2_, f32[256,128]{1,0:T(8,128)S(1)} %collective-permute-done.12.refs_3_, f32[256,128]{1,0:T(8,128)S(1)} %collective-permute-done.13.refs_4_, ...), custom_call_target="tpu_custom_call" | custom-call | tf_op jit(solution)/shard_map/pallas_call | solution.py:210
  54.6 0.6 collective-permute-start.15
  55.1 4.7 %collective-permute-done.15.refs_4_ = f32[256,128]{1,0:T(8,128)S(1)} collective-permute-done((f32[256,128]{1,0:T(8,128)S(1)}, f32[256,128]{1,0:T(8,128)S(1)}, u32[]{:S(2)}, u32[]{:S(2)}) %collective-permute-start.15) | collective-permute-done | bytes 131104 | tf_op jit(solution)/shard_map/ppermute | solution.py:527
  59.8 0.7 %shard_map.119 = (f32[2,128,128]{2,1,0:T(8,128)}, f32[2,128,128]{2,1,0:T(8,128)}) custom-call(f32[2,128,128]{2,1,0:T(8,128)S(1)} %copy-done.1, f32[256,128]{1,0:T(8,128)S(1)} %get-tuple-element.13.refs_1_, f32[256,128]{1,0:T(8,128)S(1)} %collective-permute-done.6.refs_2_, f32[256,128]{1,0:T(8,128)S(1)} %shard_map.118.refs_3_, ...), custom_call_target="tpu_custom_call" | custom-call | tf_op jit(solution)/shard_map/pallas_call | solution.py:210
  (12 shorter events, 0.0 us)
Async XLA Ops:
  0.6 0.9 %copy-start = (f32[2,128,128]{2,1,0:T(8,128)S(1)}, f32[2,128,128]{2,1,0:T(8,128)}, u32[]{:S(2)}) copy-start(f32[2,128,128]{2,1,0:T(8,128)} %refs_0_.5) | copy-start | bytes 393220
  1.5 0.9 %copy-start.3 = (s32[2,128,128]{2,1,0:T(8,128)S(1)}, s32[2,128,128]{2,1,0:T(8,128)}, u32[]{:S(2)}) copy-start(s32[2,128,128]{2,1,0:T(8,128)} %param.11) | copy-start | bytes 393220
  2.4 1.4 %copy-start.2 = (f32[2,1,6,25,25]{4,1,3,2,0:T(1,128)S(1)}, f32[2,1,6,25,25]{4,1,3,2,0:T(1,128)}, u32[]{:S(2)}) copy-start(f32[2,1,6,25,25]{4,1,3,2,0:T(1,128)} %param.12) | copy-start | bytes 90004
  2.4 1.4 %copy-start.5 = (f32[1,6]{1,0:T(1,128)S(1)}, f32[1,6]{1,0:T(1,128)}, u32[]{:S(2)}) copy-start(f32[1,6]{1,0:T(1,128)} %refs_0_.4) | copy-start | bytes 76
  2.4 1.4 %copy-start.7 = (bf16[1408,256]{1,0:T(8,128)(2,1)S(1)}, bf16[1408,256]{1,0:T(8,128)(2,1)}, u32[]{:S(2)}) copy-start(bf16[1408,256]{1,0:T(8,128)(2,1)} %constant.4.clone.refs_2_) | copy-start | bytes 2162692
  2.7 3.9 %collective-permute-start = (f32[48,256]{1,0:T(8,128)S(1)}, f32[48,256]{1,0:T(8,128)S(1)}, u32[]{:S(2)}, u32[]{:S(2)}) collective-permute-start(f32[48,256]{1,0:T(8,128)S(1)} %get-tuple-element.10), channel_id=1, source_target_pairs={{0,2},{2,0},{4,6},{6,4},{8,10},{10,8},{12,14},{14,12},{16,18},{18,... | collective-permute-start | bytes 147464 | tf_op jit(solution)/shard_map/ppermute | solution.py:518
  3.2 3.4 %collective-permute-start.1 = (f32[48,256]{1,0:T(8,128)S(1)}, f32[48,256]{1,0:T(8,128)S(1)}, u32[]{:S(2)}, u32[]{:S(2)}) collective-permute-start(f32[48,256]{1,0:T(8,128)S(1)} %get-tuple-element.11), channel_id=1, source_target_pairs={{2,4},{4,2},{6,8},{8,6},{10,12},{12,10},{14,16},{16,14},{18,20},{2... | collective-permute-start | bytes 147464 | tf_op jit(solution)/shard_map/ppermute | solution.py:518
  3.9 2.7 %copy-start.1 = (f32[2,128,128]{2,1,0:T(8,128)S(1)}, f32[2,128,128]{2,1,0:T(8,128)}, u32[]{:S(2)}) copy-start(f32[2,128,128]{2,1,0:T(8,128)} %refs_0_.5) | copy-start | bytes 393220
  3.9 2.7 %copy-start.4 = (s32[2,128,128]{2,1,0:T(8,128)S(1)}, s32[2,128,128]{2,1,0:T(8,128)}, u32[]{:S(2)}) copy-start(s32[2,128,128]{2,1,0:T(8,128)} %param.11) | copy-start | bytes 393220
  3.9 2.7 %copy-start.6 = (bf16[4000,256]{1,0:T(8,128)(2,1)S(1)}, bf16[4000,256]{1,0:T(8,128)(2,1)}, u32[]{:S(2)}) copy-start(bf16[4000,256]{1,0:T(8,128)(2,1)} %constant.5.clone.refs_6_.refs_10_) | copy-start | bytes 6144004
  6.6 15.6 %copy-start.8 = (s32[2]{0:T(128)S(1)}, s32[2]{0:T(128)}, u32[]{:S(2)}) copy-start(s32[2]{0:T(128)} %param.16) | copy-start | bytes 28
  6.6 15.6 %copy-start.9 = (s32[2]{0:T(128)S(1)}, s32[2]{0:T(128)}, u32[]{:S(2)}) copy-start(s32[2]{0:T(128)} %param.15) | copy-start | bytes 28
  13.4 13.2 %collective-permute-start.5 = (f32[256,128]{1,0:T(8,128)S(1)}, f32[256,128]{1,0:T(8,128)S(1)}, u32[]{:S(2)}, u32[]{:S(2)}) collective-permute-start(f32[256,128]{1,0:T(8,128)S(1)} %get-tuple-element.12.refs_1_), channel_id=1, source_target_pairs={{0,16},{2,18},{4,20},{6,22},{8,24},{10,26},{12,28},{14,30},{16,0},... | collective-permute-start | bytes 393224 | tf_op jit(solution)/shard_map/ppermute | solution.py:536
  20.1 6.8 %collective-permute-start.4 = (f32[256,128]{1,0:T(8,128)S(1)}, f32[256,128]{1,0:T(8,128)S(1)}, u32[]{:S(2)}, u32[]{:S(2)}) collective-permute-start(f32[256,128]{1,0:T(8,128)S(1)} %get-tuple-element.12.refs_1_), channel_id=1, source_target_pairs={{0,8},{2,10},{4,12},{6,14},{8,0},{10,2},{12,4},{14,6},{16,24},{18,... | collective-permute-start | bytes 393224 | tf_op jit(solution)/shard_map/ppermute | solution.py:536
  21.7 5.2 %collective-permute-start.3 = (f32[256,128]{1,0:T(8,128)S(1)}, f32[256,128]{1,0:T(8,128)S(1)}, u32[]{:S(2)}, u32[]{:S(2)}) collective-permute-start(f32[256,128]{1,0:T(8,128)S(1)} %get-tuple-element.12.refs_1_), channel_id=1, source_target_pairs={{0,4},{2,6},{4,0},{6,2},{8,12},{10,14},{12,8},{14,10},{16,20},{18,... | collective-permute-start | bytes 393224 | tf_op jit(solution)/shard_map/ppermute | solution.py:536
  22.2 4.7 %collective-permute-start.2 = (f32[256,128]{1,0:T(8,128)S(1)}, f32[256,128]{1,0:T(8,128)S(1)}, u32[]{:S(2)}, u32[]{:S(2)}) collective-permute-start(f32[256,128]{1,0:T(8,128)S(1)} %get-tuple-element.12.refs_1_), channel_id=1, source_target_pairs={{0,2},{2,0},{4,6},{6,4},{8,10},{10,8},{12,14},{14,12},{16,18},{18,... | collective-permute-start | bytes 393224 | tf_op jit(solution)/shard_map/ppermute | solution.py:536
  27.8 6.1 %collective-permute-start.6 = (f32[256,128]{1,0:T(8,128)S(1)}, f32[256,128]{1,0:T(8,128)S(1)}, u32[]{:S(2)}, u32[]{:S(2)}) collective-permute-start(f32[256,128]{1,0:T(8,128)S(1)} %get-tuple-element.13.refs_1_), channel_id=1, source_target_pairs={{0,1},{1,0},{2,3},{3,2},{4,5},{5,4},{6,7},{7,6},{8,9},{9,8},{10,11... | collective-permute-start | bytes 393224 | tf_op jit(solution)/shard_map/ppermute | solution.py:527
  29.3 3.7 %collective-permute-start.8 = (f32[32,256]{1,0:T(8,128)S(1)}, f32[32,256]{1,0:T(8,128)S(1)}, u32[]{:S(2)}, u32[]{:S(2)}) collective-permute-start(f32[32,256]{1,0:T(8,128)S(1)} %get-tuple-element.14), channel_id=1, source_target_pairs={{0,3},{1,2},{2,1},{3,0},{4,7},{5,6},{6,5},{7,4},{8,11},{9,10},{10,... | collective-permute-start | bytes 98312 | tf_op jit(solution)/shard_map/ppermute | solution.py:520
  29.3 3.7 %collective-permute-start.7 = (f32[32,256]{1,0:T(8,128)S(1)}, f32[32,256]{1,0:T(8,128)S(1)}, u32[]{:S(2)}, u32[]{:S(2)}) collective-permute-start(f32[32,256]{1,0:T(8,128)S(1)} %get-tuple-element.14), channel_id=1, source_target_pairs={{0,2},{2,0},{4,6},{6,4},{8,10},{10,8},{12,14},{14,12},{16,18},{18,... | collective-permute-start | bytes 98312 | tf_op jit(solution)/shard_map/ppermute | solution.py:518
  29.9 3.9 %collective-permute-start.10 = (f32[32,256]{1,0:T(8,128)S(1)}, f32[32,256]{1,0:T(8,128)S(1)}, u32[]{:S(2)}, u32[]{:S(2)}) collective-permute-start(f32[32,256]{1,0:T(8,128)S(1)} %get-tuple-element.15), channel_id=1, source_target_pairs={{2,5},{3,4},{4,3},{5,2},{6,9},{7,8},{8,7},{9,6},{10,13},{11,12},{1... | collective-permute-start | bytes 98312 | tf_op jit(solution)/shard_map/ppermute | solution.py:520
  31.5 2.4 %collective-permute-start.9 = (f32[32,256]{1,0:T(8,128)S(1)}, f32[32,256]{1,0:T(8,128)S(1)}, u32[]{:S(2)}, u32[]{:S(2)}) collective-permute-start(f32[32,256]{1,0:T(8,128)S(1)} %get-tuple-element.15), channel_id=1, source_target_pairs={{2,4},{4,2},{6,8},{8,6},{10,12},{12,10},{14,16},{16,14},{18,20},{2... | collective-permute-start | bytes 98312 | tf_op jit(solution)/shard_map/ppermute | solution.py:518
  40.6 13.2 %collective-permute-start.14 = (f32[256,128]{1,0:T(8,128)S(1)}, f32[256,128]{1,0:T(8,128)S(1)}, u32[]{:S(2)}, u32[]{:S(2)}) collective-permute-start(f32[256,128]{1,0:T(8,128)S(1)} %shard_map.117.refs_1_), channel_id=1, source_target_pairs={{0,16},{2,18},{4,20},{6,22},{8,24},{10,26},{12,28},{14,30},{16,0},... | collective-permute-start | bytes 393224 | tf_op jit(solution)/shard_map/ppermute | solution.py:536
  47.0 6.8 %collective-permute-start.13 = (f32[256,128]{1,0:T(8,128)S(1)}, f32[256,128]{1,0:T(8,128)S(1)}, u32[]{:S(2)}, u32[]{:S(2)}) collective-permute-start(f32[256,128]{1,0:T(8,128)S(1)} %shard_map.117.refs_1_), channel_id=1, source_target_pairs={{0,8},{2,10},{4,12},{6,14},{8,0},{10,2},{12,4},{14,6},{16,24},{18,... | collective-permute-start | bytes 393224 | tf_op jit(solution)/shard_map/ppermute | solution.py:536
  47.7 6.1 %collective-permute-start.12 = (f32[256,128]{1,0:T(8,128)S(1)}, f32[256,128]{1,0:T(8,128)S(1)}, u32[]{:S(2)}, u32[]{:S(2)}) collective-permute-start(f32[256,128]{1,0:T(8,128)S(1)} %shard_map.117.refs_1_), channel_id=1, source_target_pairs={{0,4},{2,6},{4,0},{6,2},{8,12},{10,14},{12,8},{14,10},{16,20},{18,... | collective-permute-start | bytes 393224 | tf_op jit(solution)/shard_map/ppermute | solution.py:536
  48.4 5.4 %collective-permute-start.11 = (f32[256,128]{1,0:T(8,128)S(1)}, f32[256,128]{1,0:T(8,128)S(1)}, u32[]{:S(2)}, u32[]{:S(2)}) collective-permute-start(f32[256,128]{1,0:T(8,128)S(1)} %shard_map.117.refs_1_), channel_id=1, source_target_pairs={{0,2},{2,0},{4,6},{6,4},{8,10},{10,8},{12,14},{14,12},{16,18},{18,... | collective-permute-start | bytes 393224 | tf_op jit(solution)/shard_map/ppermute | solution.py:536
  54.6 5.2 %collective-permute-start.15 = (f32[256,128]{1,0:T(8,128)S(1)}, f32[256,128]{1,0:T(8,128)S(1)}, u32[]{:S(2)}, u32[]{:S(2)}) collective-permute-start(f32[256,128]{1,0:T(8,128)S(1)} %shard_map.118.refs_3_), channel_id=1, source_target_pairs={{0,1},{1,0},{2,3},{3,2},{4,5},{5,4},{6,7},{7,6},{8,9},{9,8},{10,11... | collective-permute-start | bytes 393224 | tf_op jit(solution)/shard_map/ppermute | solution.py:527

commit v11 on v9

--- a/solution.py
+++ b/solution.py
@@ -269,8 +269,13 @@
             h_ref[c, j] = root * comp
 
 
-def sides(from_a, from_b, tb):
+def sides(masks, near, tb):
     even = is_even()
+    tile = lax.axis_index("tile")
+    differ = lax.bitwise_xor(tile, jnp.where(even, tile - 1, tile + 1))
+    from_a, from_b = near[0], jnp.zeros_like(near[0])
+    for mask, got in zip(masks, near[1:]):
+        from_b = jnp.where(differ == mask, got, from_b)
     l_hi, l_lo = split(jnp.where(even, from_b, from_a))
     r_hi, r_lo = split(jnp.where(even, from_a, from_b))
     height = l_hi.shape[0]
@@ -431,12 +436,11 @@
             finish(back_old[0])
 
 
-def first_kernel(
-    kern, last, thr_ref, mask_ref, target_ref, a_ref, b_ref, h_ref, tb,
-    g_ref, f_ref, tgt_ref, *work,
-):
+def first_kernel(kern, last, masks, thr_ref, mask_ref, target_ref, *refs):
+    near, refs = refs[: 1 + len(masks)], refs[1 + len(masks) :]
+    h_ref, tb, g_ref, f_ref, tgt_ref, *work = refs
     m_hi, m_lo = split(mask_ref[...])
-    v, left, right = sides(a_ref[...], b_ref[...], tb)
+    v, left, right = sides(masks, [x[...] for x in near], tb)
     v = v + dot3(tb("cx_own_hi"), tb("cx_own_lo"), m_hi, m_lo, dot_nt)
     to_spectrum(v, tb, f_ref, None)
     tgt_ref[...] = (
@@ -447,14 +451,12 @@
     gradient_body(kern, last, f_ref, tgt_ref, h_ref, thr_ref, tb, g_ref, work)
 
 
-def later_kernel(
-    kern, last, thr_ref, mine_ref, peer_ref, a_ref, a2_ref, b_ref, b2_ref, f_in_ref, tgt_ref,
-    h_ref, tb, g_ref, f_ref, *work,
-):
+def later_kernel(kern, last, masks, thr_ref, mine_ref, peer_ref, *refs):
+    count = 1 + len(masks)
+    near, far, refs = refs[:count], refs[count : 2 * count], refs[2 * count :]
+    f_in_ref, tgt_ref, h_ref, tb, g_ref, f_ref, *work = refs
     s_hi, s_lo = split(mine_ref[...] + peer_ref[...])
-    from_a = a_ref[...] + a2_ref[...]
-    from_b = b_ref[...] + b2_ref[...]
-    v, _, _ = sides(from_a, from_b, tb)
+    v, _, _ = sides(masks, [x[...] + y[...] for x, y in zip(near, far)], tb)
     v = v + dot3(tb("cx_own_hi"), tb("cx_own_lo"), s_hi, s_lo, dot_nt)
     to_spectrum(v, tb, f_ref, f_in_ref)
     gradient_body(kern, last, f_ref, tgt_ref, h_ref, thr_ref, tb, g_ref, work)
@@ -506,17 +508,17 @@
     tiles_dev, core, _ = mask_tiles.shape
     kern = kernels.shape[2]
     assert tiles_dev == 2 and core == CORE
-    pairs_a = [(i, i ^ 1) for i in range(n_tile)]
-    pairs_b = [p for i in range(1, n_tile - 1, 2) for p in ((i, i + 1), (i + 1, i))]
+    bits = [1 << b for b in range(n_tile.bit_length() - 1)]
+    masks = [2 * bit - 1 for bit in bits[1:]]
 
     def swap_edges(send_a, send_b, cross=False):
-        def move(x, pairs):
+        def move(x, mask):
             if not cross:
-                return lax.ppermute(x, "tile", pairs)
-            both = [(2 * i + p, 2 * j + 1 - p) for i, j in pairs for p in range(2)]
+                return lax.ppermute(x, "tile", [(i, i ^ mask) for i in range(n_tile)])
+            both = [(2 * i + p, 2 * (i ^ mask) + 1 - p) for i in range(n_tile) for p in range(2)]
             return lax.ppermute(x, ("tile", "depth"), both)
 
-        return move(send_b, pairs_b), move(send_a, pairs_a)
+        return [move(send_a, 1)] + [move(send_b, mask) for mask in masks]
 
     def depth_pair(x):
         bit = 1
@@ -528,7 +530,6 @@
             x = x + peer
 
     def from_partners(grad):
-        bits = [1 << b for b in range(n_tile.bit_length() - 1)]
         got = [
             lax.ppermute(grad, "tile", [(i, i ^ bit) for i in range(n_tile)])
             for bit in reversed(bits)
@@ -558,7 +559,7 @@
     send_a, send_b = call(
         edges_kernel, None, [mask_rows, target_rows], [edge, edge], flops=3 * 10**9
     )
-    from_b, from_a = swap_edges(send_a, send_b)
+    near = swap_edges(send_a, send_b)
     table = jnp.concatenate([partner_table, mirror_flags])
     (spectra,) = call(
         functools.partial(spectra_kernel, kern),
@@ -571,9 +572,9 @@
         nbytes=4 * 10**6,
     )
     grad, freq_now, goals = call(
-        functools.partial(first_kernel, kern, n_tile - 1),
+        functools.partial(first_kernel, kern, n_tile - 1, masks),
         "grad",
-        [thresholds, mask_rows, target_rows, from_a, from_b, spectra],
+        [thresholds, mask_rows, target_rows, *near, spectra],
         [strip, freq, goal],
         scratch,
         smem=(0,),
@@ -592,19 +593,17 @@
         if step == STEPS:
             moves += depth_pair(outs[0])
             break
+        near = swap_edges(*outs[1:])
         if n_depth == 2:
-            from_b, from_a = swap_edges(*outs[1:])
-            far_b, far_a = swap_edges(*outs[1:], cross=True)
-            rims = (from_a, far_a, from_b, far_b)
+            far = swap_edges(*outs[1:], cross=True)
         else:
-            from_b, from_a = swap_edges(*outs[1:])
-            rims = depth_pair(from_a) + depth_pair(from_b)
+            near, far = zip(*(depth_pair(x) for x in near))
         moves += depth_pair(outs[0])
         kept = step + 1 < STEPS
         grad, *rest = call(
-            functools.partial(later_kernel, kern, n_tile - 1),
+            functools.partial(later_kernel, kern, n_tile - 1, masks),
             "grad",
-            [thresholds, *moves[-2:], *rims, freq_now, goals, spectra],
+            [thresholds, *moves[-2:], *near, *far, freq_now, goals, spectra],
             [strip, freq] if kept else [strip],
             scratch if kept else [pltpu.VMEM(freq.shape, f32)] + scratch,
             smem=(0,),

time: 62.7 us -> 68.6 us (1.094)
  starting transfers between devices: 24.8 us -> 28 us
  waiting for transfers between devices: 16.1 us -> 19 us
    ppermute x8, starting transfers between devices: 19.4 us -> 8.13 us  [from_partners(): lax.ppermute(grad, 'tile', [(i, i ^ bit) for i in range(n_tile)])]
    ppermute x4 -> x8, starting transfers between devices: 2.63 us -> 11.1 us  [move(): return lax.ppermute(x, 'tile', [(i, i ^ mask) for i in range(n_tile)])]
    ppermute x2 -> x4, starting transfers between devices: 0.65 us -> 5.71 us  [move(): return lax.ppermute(x, ('tile', 'depth'), both)]
    ppermute x4 -> x8, waiting for transfers between devices: 0.01 us -> 3.81 us  [move(): return lax.ppermute(x, 'tile', [(i, i ^ mask) for i in range(n_tile)])]
    ppermute x2, waiting for transfers between devices: 4.79 us -> 3.54 us  [depth_pair(): peer = lax.ppermute(x, 'depth', [(i, i ^ bit) for i in range(n_depth)])]
    ppermute x8, waiting for transfers between devices: 9.78 us -> 11 us  [from_partners(): lax.ppermute(grad, 'tile', [(i, i ^ bit) for i in range(n_tile)])]
    ppermute x2, starting transfers between devices: 2.12 us -> 3.05 us  [depth_pair(): peer = lax.ppermute(x, 'depth', [(i, i ^ bit) for i in range(n_depth)])]
    ppermute x2 -> x4, waiting for transfers between devices: 1.55 us -> 0.65 us  [move(): return lax.ppermute(x, ('tile', 'depth'), both)]
  transfers between devices with their start and end apart: 16 -> 22, of which waited for: 6 -> 8; matrix products, arithmetic and copies ran while one was open for 0% -> 0% of each run, Pallas kernels for 3% -> 3%
where the time goes in v11:
time: 68.6 us; the launch traced here: 68.4 us
  starting transfers between devices  28 us (41%)
  waiting for transfers between devices  19 us (28%)
  Pallas kernels  18.1 us (26%)
  local copies, waits for them, and re-layouts  1.84 us (3%)
  between operations  1.45 us (2%)
    pallas_call x7, Pallas kernels, call(): pl.pallas_call(wrapped, out_shape=out_shape, in_specs=[sm if i in smem el...  18.1 us
    ppermute x8, starting transfers between devices, move(): return lax.ppermute(x, 'tile', [(i, i ^ mask) for i in range(n_tile)])  11.1 us
    ppermute x8, waiting for transfers between devices, from_partners(): lax.ppermute(grad, 'tile', [(i, i ^ bit) for i in range(n_tile)])  11 us
    ppermute x8, starting transfers between devices, from_partners(): lax.ppermute(grad, 'tile', [(i, i ^ bit) for i in range(n_tile)])  8.13 us
    ppermute x4, starting transfers between devices, move(): return lax.ppermute(x, ('tile', 'depth'), both)  5.71 us
    ppermute x8, waiting for transfers between devices, move(): return lax.ppermute(x, 'tile', [(i, i ^ mask) for i in range(n_tile)])  3.81 us
    ppermute x2, waiting for transfers between devices, depth_pair(): peer = lax.ppermute(x, 'depth', [(i, i ^ bit) for i in range(n_depth)])  3.54 us
    ppermute x2, starting transfers between devices, depth_pair(): peer = lax.ppermute(x, 'depth', [(i, i ^ bit) for i in range(n_depth)])  3.05 us
  transfers between devices with their start and end apart: 22, of which 8 were waited for; matrix products, arithmetic and copies ran while one was open for 0% of the time, Pallas kernels for 3%

profile of v11, /device:TPU:0, one launch (start us, length us, event | category | flops | bytes accessed | tf_op | source)
XLA Modules:
  0.0 68.4 jit_solution(1779956454542256413)
XLA Ops:
  0.6 0.0 copy-start
  0.6 0.9 %copy-done = f32[2,128,128]{2,1,0:T(8,128)S(1)} copy-done((f32[2,128,128]{2,1,0:T(8,128)S(1)}, f32[2,128,128]{2,1,0:T(8,128)}, u32[]{:S(2)}) %copy-start) | copy-done | bytes 131096
  1.5 0.9 %copy-done.3 = s32[2,128,128]{2,1,0:T(8,128)S(1)} copy-done((s32[2,128,128]{2,1,0:T(8,128)S(1)}, s32[2,128,128]{2,1,0:T(8,128)}, u32[]{:S(2)}) %copy-start.3) | copy-done | bytes 131096
  2.4 0.2 shard_map.113
  2.7 5.5 %collective-permute-start.3 = (f32[48,256]{1,0:T(8,128)S(1)}, f32[48,256]{1,0:T(8,128)S(1)}, u32[]{:S(2)}, u32[]{:S(2)}) collective-permute-start(f32[48,256]{1,0:T(8,128)S(1)} %get-tuple-element.11), channel_id=1, source_target_pairs={{0,30},{2,28},{4,26},{6,24},{8,22},{10,20},{12,18},{14,16},{16,14}... | collective-permute-start | bytes 147464 | tf_op jit(solution)/shard_map/ppermute | solution.py:517
  8.2 0.0 collective-permute-start.2
  8.2 0.8 %collective-permute-start.1 = (f32[48,256]{1,0:T(8,128)S(1)}, f32[48,256]{1,0:T(8,128)S(1)}, u32[]{:S(2)}, u32[]{:S(2)}) collective-permute-start(f32[48,256]{1,0:T(8,128)S(1)} %get-tuple-element.11), channel_id=1, source_target_pairs={{0,6},{2,4},{4,2},{6,0},{8,14},{10,12},{12,10},{14,8},{16,22},{18,... | collective-permute-start | bytes 147464 | tf_op jit(solution)/shard_map/ppermute | solution.py:517
  9.0 0.6 collective-permute-start
  9.6 0.0 copy-start.4
  9.6 0.0 copy-start.6
  9.6 2.0 %shard_map.114.refs_7_.refs_13_ = f32[12,4,96,128]{3,2,1,0:T(8,128)S(1)} custom-call(f32[1,6]{1,0:T(1,128)S(1)} %copy-done.5, f32[2,6,25,1,25]{4,3,2,1,0:T(1,128)S(1)} %bitcast.5, bf16[1408,256]{1,0:T(8,128)(2,1)S(1)} %copy-done.7), custom_call_target="tpu_custom_call" | custom-call | flops 3000000000 | bytes 4000000 | tf_op jit(solution)/shard_map/pallas_call | solution.py:210
  12.2 0.0 copy-start.8
  12.3 0.0 copy-start.9
  12.3 0.0 collective-permute-done.3.refs_6_
  12.3 0.4 collective-permute-done.2.refs_5_
  12.7 0.0 collective-permute-done.1.refs_4_
  12.7 6.8 %shard_map.115 = (f32[256,128]{1,0:T(8,128)S(1)}, f32[2,4,96,128]{3,2,1,0:T(8,128)S(1)}, f32[160,256]{1,0:T(8,128)S(1)}) custom-call(f32[1]{0:T(128)S(6)} %copy.12.refs_0_, f32[256,128]{1,0:T(8,128)S(1)} %bitcast.4, s32[256,128]{1,0:T(8,128)S(1)} %bitcast.7, f32[48,256]{1,0:T(8,128)S(1)} %collective-permute-done.refs_3_, ...), custom_call_target="tpu_custom_call" | custom-call | flops 10000000000 | tf_op jit(solution)/shard_map/pallas_call | solution.py:210
  19.5 1.1 %collective-permute-start.7 = (f32[256,128]{1,0:T(8,128)S(1)}, f32[256,128]{1,0:T(8,128)S(1)}, u32[]{:S(2)}, u32[]{:S(2)}) collective-permute-start(f32[256,128]{1,0:T(8,128)S(1)} %get-tuple-element.12.refs_1_), channel_id=1, source_target_pairs={{0,16},{2,18},{4,20},{6,22},{8,24},{10,26},{12,28},{14,30},{16,0},... | collective-permute-start | bytes 393224 | tf_op jit(solution)/shard_map/ppermute | solution.py:534
  20.6 2.3 %collective-permute-start.6 = (f32[256,128]{1,0:T(8,128)S(1)}, f32[256,128]{1,0:T(8,128)S(1)}, u32[]{:S(2)}, u32[]{:S(2)}) collective-permute-start(f32[256,128]{1,0:T(8,128)S(1)} %get-tuple-element.12.refs_1_), channel_id=1, source_target_pairs={{0,8},{2,10},{4,12},{6,14},{8,0},{10,2},{12,4},{14,6},{16,24},{18,... | collective-permute-start | bytes 393224 | tf_op jit(solution)/shard_map/ppermute | solution.py:534
  22.9 1.0 %collective-permute-start.5 = (f32[256,128]{1,0:T(8,128)S(1)}, f32[256,128]{1,0:T(8,128)S(1)}, u32[]{:S(2)}, u32[]{:S(2)}) collective-permute-start(f32[256,128]{1,0:T(8,128)S(1)} %get-tuple-element.12.refs_1_), channel_id=1, source_target_pairs={{0,4},{2,6},{4,0},{6,2},{8,12},{10,14},{12,8},{14,10},{16,20},{18,... | collective-permute-start | bytes 393224 | tf_op jit(solution)/shard_map/ppermute | solution.py:534
  23.9 0.0 collective-permute-start.4
  23.9 0.1 pad_add_fusion.refs_0_
  24.0 5.5 %collective-permute-done.7.refs_5_ = f32[256,128]{1,0:T(8,128)S(1)} collective-permute-done((f32[256,128]{1,0:T(8,128)S(1)}, f32[256,128]{1,0:T(8,128)S(1)}, u32[]{:S(2)}, u32[]{:S(2)}) %collective-permute-start.7) | collective-permute-done | bytes 131104 | tf_op jit(solution)/shard_map/ppermute | solution.py:534
  29.4 0.0 collective-permute-done.4.refs_2_
  29.4 0.9 %shard_map.116 = (f32[256,128]{1,0:T(8,128)S(1)}, f32[32,256]{1,0:T(8,128)S(1)}, f32[32,256]{1,0:T(8,128)S(1)}) custom-call(s32[4]{0:T(128)S(1)} %pad_add_fusion.refs_0_, f32[256,128]{1,0:T(8,128)S(1)} %get-tuple-element.12.refs_1_, f32[256,128]{1,0:T(8,128)S(1)} %collective-permute-done.4.refs_2_, f32[256,128]{1,0:T(8,128)S(1)} %collective-permute-done.5.refs_3_, ...), custom_call_target="tpu_custom_call" | custom-call | tf_op jit(solution)/shard_map/pallas_call | solution.py:210
  30.3 1.6 %collective-permute-start.8 = (f32[256,128]{1,0:T(8,128)S(1)}, f32[256,128]{1,0:T(8,128)S(1)}, u32[]{:S(2)}, u32[]{:S(2)}) collective-permute-start(f32[256,128]{1,0:T(8,128)S(1)} %get-tuple-element.13.refs_1_), channel_id=1, source_target_pairs={{0,1},{1,0},{2,3},{3,2},{4,5},{5,4},{6,7},{7,6},{8,9},{9,8},{10,11... | collective-permute-start | bytes 393224 | tf_op jit(solution)/shard_map/ppermute | solution.py:526
  31.9 0.0 collective-permute-start.13
  31.9 0.6 collective-permute-start.9
  32.5 4.1 %collective-permute-start.16 = (f32[32,256]{1,0:T(8,128)S(1)}, f32[32,256]{1,0:T(8,128)S(1)}, u32[]{:S(2)}, u32[]{:S(2)}) collective-permute-start(f32[32,256]{1,0:T(8,128)S(1)} %get-tuple-element.15), channel_id=1, source_target_pairs={{0,31},{1,30},{2,29},{3,28},{4,27},{5,26},{6,25},{7,24},{8,23},{9,... | collective-permute-start | bytes 98312 | tf_op jit(solution)/shard_map/ppermute | solution.py:519
  36.6 1.6 %collective-permute-start.14 = (f32[32,256]{1,0:T(8,128)S(1)}, f32[32,256]{1,0:T(8,128)S(1)}, u32[]{:S(2)}, u32[]{:S(2)}) collective-permute-start(f32[32,256]{1,0:T(8,128)S(1)} %get-tuple-element.15), channel_id=1, source_target_pairs={{0,7},{1,6},{2,5},{3,4},{4,3},{5,2},{6,1},{7,0},{8,15},{9,14},{10,... | collective-permute-start | bytes 98312 | tf_op jit(solution)/shard_map/ppermute | solution.py:519
  38.2 0.0 collective-permute-done.9.refs_3_
  38.2 1.1 %collective-permute-start.12 = (f32[32,256]{1,0:T(8,128)S(1)}, f32[32,256]{1,0:T(8,128)S(1)}, u32[]{:S(2)}, u32[]{:S(2)}) collective-permute-start(f32[32,256]{1,0:T(8,128)S(1)} %get-tuple-element.15), channel_id=1, source_target_pairs={{0,30},{2,28},{4,26},{6,24},{8,22},{10,20},{12,18},{14,16},{16,14}... | collective-permute-start | bytes 98312 | tf_op jit(solution)/shard_map/ppermute | solution.py:517
  39.3 0.3 collective-permute-done.16.refs_10_
  39.6 1.9 %collective-permute-start.11 = (f32[32,256]{1,0:T(8,128)S(1)}, f32[32,256]{1,0:T(8,128)S(1)}, u32[]{:S(2)}, u32[]{:S(2)}) collective-permute-start(f32[32,256]{1,0:T(8,128)S(1)} %get-tuple-element.15), channel_id=1, source_target_pairs={{0,14},{2,12},{4,10},{6,8},{8,6},{10,4},{12,2},{14,0},{16,30},{18,... | collective-permute-start | bytes 98312 | tf_op jit(solution)/shard_map/ppermute | solution.py:517
  41.5 0.3 collective-permute-done.15.refs_9_
  41.8 0.6 collective-permute-start.10
  42.5 0.0 collective-permute-done.14.refs_8_
  42.5 1.8 %collective-permute-done.12.refs_6_ = f32[32,256]{1,0:T(8,128)S(1)} collective-permute-done((f32[32,256]{1,0:T(8,128)S(1)}, f32[32,256]{1,0:T(8,128)S(1)}, u32[]{:S(2)}, u32[]{:S(2)}) %collective-permute-start.12) | collective-permute-done | bytes 32800 | tf_op jit(solution)/shard_map/ppermute | solution.py:517
  44.3 1.6 %collective-permute-done.10.refs_4_ = f32[32,256]{1,0:T(8,128)S(1)} collective-permute-done((f32[32,256]{1,0:T(8,128)S(1)}, f32[32,256]{1,0:T(8,128)S(1)}, u32[]{:S(2)}, u32[]{:S(2)}) %collective-permute-start.10) | collective-permute-done | bytes 32800 | tf_op jit(solution)/shard_map/ppermute | solution.py:517
  45.9 6.8 %shard_map.117.refs_1_ = f32[256,128]{1,0:T(8,128)S(1)} custom-call(f32[1]{0:T(128)S(6)} %copy.12.refs_0_, f32[256,128]{1,0:T(8,128)S(1)} %get-tuple-element.13.refs_1_, f32[256,128]{1,0:T(8,128)S(1)} %collective-permute-done.8.refs_2_, f32[32,256]{1,0:T(8,128)S(1)} %collective-permute-done.9.refs_3_, f32[32,256]{1,0:T(8,128)S(1)} %collective-permute-done.10.refs_4_, ...), custom_call_target="tpu_custom_call" | custom-call | flops 10000000000 | tf_op jit(solution)/shard_map/pallas_call | solution.py:210
  52.6 1.6 %collective-permute-start.20 = (f32[256,128]{1,0:T(8,128)S(1)}, f32[256,128]{1,0:T(8,128)S(1)}, u32[]{:S(2)}, u32[]{:S(2)}) collective-permute-start(f32[256,128]{1,0:T(8,128)S(1)} %shard_map.117.refs_1_), channel_id=1, source_target_pairs={{0,16},{2,18},{4,20},{6,22},{8,24},{10,26},{12,28},{14,30},{16,0},... | collective-permute-start | bytes 393224 | tf_op jit(solution)/shard_map/ppermute | solution.py:534
  54.2 0.8 %collective-permute-start.19 = (f32[256,128]{1,0:T(8,128)S(1)}, f32[256,128]{1,0:T(8,128)S(1)}, u32[]{:S(2)}, u32[]{:S(2)}) collective-permute-start(f32[256,128]{1,0:T(8,128)S(1)} %shard_map.117.refs_1_), channel_id=1, source_target_pairs={{0,8},{2,10},{4,12},{6,14},{8,0},{10,2},{12,4},{14,6},{16,24},{18,... | collective-permute-start | bytes 393224 | tf_op jit(solution)/shard_map/ppermute | solution.py:534
  55.0 1.4 %collective-permute-start.18 = (f32[256,128]{1,0:T(8,128)S(1)}, f32[256,128]{1,0:T(8,128)S(1)}, u32[]{:S(2)}, u32[]{:S(2)}) collective-permute-start(f32[256,128]{1,0:T(8,128)S(1)} %shard_map.117.refs_1_), channel_id=1, source_target_pairs={{0,4},{2,6},{4,0},{6,2},{8,12},{10,14},{12,8},{14,10},{16,20},{18,... | collective-permute-start | bytes 393224 | tf_op jit(solution)/shard_map/ppermute | solution.py:534
  56.4 5.5 %collective-permute-done.20.refs_5_ = f32[256,128]{1,0:T(8,128)S(1)} collective-permute-done((f32[256,128]{1,0:T(8,128)S(1)}, f32[256,128]{1,0:T(8,128)S(1)}, u32[]{:S(2)}, u32[]{:S(2)}) %collective-permute-start.20) | collective-permute-done | bytes 131104 | tf_op jit(solution)/shard_map/ppermute | solution.py:534
  61.9 0.7 %shard_map.118.refs_3_ = f32[256,128]{1,0:T(8,128)S(1)} custom-call(s32[4]{0:T(128)S(1)} %pad_add_fusion.refs_0_, f32[256,128]{1,0:T(8,128)S(1)} %shard_map.117.refs_1_, f32[256,128]{1,0:T(8,128)S(1)} %collective-permute-done.17.refs_2_, f32[256,128]{1,0:T(8,128)S(1)} %collective-permute-done.18.refs_3_, f32[256,128]{1,0:T(8,128)S(1)} %collective-permute-done.19.refs_4_, ...), custom_call_target="tpu_custom_call" | custom-call | tf_op jit(solution)/shard_map/pallas_call | solution.py:210
  62.7 1.5 %collective-permute-start.21 = (f32[256,128]{1,0:T(8,128)S(1)}, f32[256,128]{1,0:T(8,128)S(1)}, u32[]{:S(2)}, u32[]{:S(2)}) collective-permute-start(f32[256,128]{1,0:T(8,128)S(1)} %shard_map.118.refs_3_), channel_id=1, source_target_pairs={{0,1},{1,0},{2,3},{3,2},{4,5},{5,4},{6,7},{7,6},{8,9},{9,8},{10,11... | collective-permute-start | bytes 393224 | tf_op jit(solution)/shard_map/ppermute | solution.py:526
  64.2 3.5 %collective-permute-done.21.refs_4_ = f32[256,128]{1,0:T(8,128)S(1)} collective-permute-done((f32[256,128]{1,0:T(8,128)S(1)}, f32[256,128]{1,0:T(8,128)S(1)}, u32[]{:S(2)}, u32[]{:S(2)}) %collective-permute-start.21) | collective-permute-done | bytes 131104 | tf_op jit(solution)/shard_map/ppermute | solution.py:526
  67.7 0.7 %shard_map.119 = (f32[2,128,128]{2,1,0:T(8,128)}, f32[2,128,128]{2,1,0:T(8,128)}) custom-call(f32[2,128,128]{2,1,0:T(8,128)S(1)} %copy-done.1, f32[256,128]{1,0:T(8,128)S(1)} %get-tuple-element.13.refs_1_, f32[256,128]{1,0:T(8,128)S(1)} %collective-permute-done.8.refs_2_, f32[256,128]{1,0:T(8,128)S(1)} %shard_map.118.refs_3_, ...), custom_call_target="tpu_custom_call" | custom-call | tf_op jit(solution)/shard_map/pallas_call | solution.py:210
  (24 shorter events, 0.1 us)
Async XLA Ops:
  0.6 0.9 %copy-start = (f32[2,128,128]{2,1,0:T(8,128)S(1)}, f32[2,128,128]{2,1,0:T(8,128)}, u32[]{:S(2)}) copy-start(f32[2,128,128]{2,1,0:T(8,128)} %refs_0_.5) | copy-start | bytes 393220
  1.5 0.9 %copy-start.3 = (s32[2,128,128]{2,1,0:T(8,128)S(1)}, s32[2,128,128]{2,1,0:T(8,128)}, u32[]{:S(2)}) copy-start(s32[2,128,128]{2,1,0:T(8,128)} %param.11) | copy-start | bytes 393220
  2.4 7.1 %copy-start.2 = (f32[2,1,6,25,25]{4,1,3,2,0:T(1,128)S(1)}, f32[2,1,6,25,25]{4,1,3,2,0:T(1,128)}, u32[]{:S(2)}) copy-start(f32[2,1,6,25,25]{4,1,3,2,0:T(1,128)} %param.12) | copy-start | bytes 90004
  2.4 7.1 %copy-start.5 = (f32[1,6]{1,0:T(1,128)S(1)}, f32[1,6]{1,0:T(1,128)}, u32[]{:S(2)}) copy-start(f32[1,6]{1,0:T(1,128)} %refs_0_.4) | copy-start | bytes 76
  2.4 7.1 %copy-start.7 = (bf16[1408,256]{1,0:T(8,128)(2,1)S(1)}, bf16[1408,256]{1,0:T(8,128)(2,1)}, u32[]{:S(2)}) copy-start(bf16[1408,256]{1,0:T(8,128)(2,1)} %constant.4.clone.refs_2_) | copy-start | bytes 2162692
  2.7 9.6 %collective-permute-start.3 = (f32[48,256]{1,0:T(8,128)S(1)}, f32[48,256]{1,0:T(8,128)S(1)}, u32[]{:S(2)}, u32[]{:S(2)}) collective-permute-start(f32[48,256]{1,0:T(8,128)S(1)} %get-tuple-element.11), channel_id=1, source_target_pairs={{0,30},{2,28},{4,26},{6,24},{8,22},{10,20},{12,18},{14,16},{16,14}... | collective-permute-start | bytes 147464 | tf_op jit(solution)/shard_map/ppermute | solution.py:517
  8.2 4.5 %collective-permute-start.2 = (f32[48,256]{1,0:T(8,128)S(1)}, f32[48,256]{1,0:T(8,128)S(1)}, u32[]{:S(2)}, u32[]{:S(2)}) collective-permute-start(f32[48,256]{1,0:T(8,128)S(1)} %get-tuple-element.11), channel_id=1, source_target_pairs={{0,14},{2,12},{4,10},{6,8},{8,6},{10,4},{12,2},{14,0},{16,30},{18,... | collective-permute-start | bytes 147464 | tf_op jit(solution)/shard_map/ppermute | solution.py:517
  8.2 4.5 %collective-permute-start.1 = (f32[48,256]{1,0:T(8,128)S(1)}, f32[48,256]{1,0:T(8,128)S(1)}, u32[]{:S(2)}, u32[]{:S(2)}) collective-permute-start(f32[48,256]{1,0:T(8,128)S(1)} %get-tuple-element.11), channel_id=1, source_target_pairs={{0,6},{2,4},{4,2},{6,0},{8,14},{10,12},{12,10},{14,8},{16,22},{18,... | collective-permute-start | bytes 147464 | tf_op jit(solution)/shard_map/ppermute | solution.py:517
  9.0 3.3 %collective-permute-start = (f32[48,256]{1,0:T(8,128)S(1)}, f32[48,256]{1,0:T(8,128)S(1)}, u32[]{:S(2)}, u32[]{:S(2)}) collective-permute-start(f32[48,256]{1,0:T(8,128)S(1)} %get-tuple-element.10), channel_id=1, source_target_pairs={{0,2},{2,0},{4,6},{6,4},{8,10},{10,8},{12,14},{14,12},{16,18},{18,... | collective-permute-start | bytes 147464 | tf_op jit(solution)/shard_map/ppermute | solution.py:517
  9.6 3.1 %copy-start.1 = (f32[2,128,128]{2,1,0:T(8,128)S(1)}, f32[2,128,128]{2,1,0:T(8,128)}, u32[]{:S(2)}) copy-start(f32[2,128,128]{2,1,0:T(8,128)} %refs_0_.5) | copy-start | bytes 393220
  9.6 3.1 %copy-start.4 = (s32[2,128,128]{2,1,0:T(8,128)S(1)}, s32[2,128,128]{2,1,0:T(8,128)}, u32[]{:S(2)}) copy-start(s32[2,128,128]{2,1,0:T(8,128)} %param.11) | copy-start | bytes 393220
  9.6 3.1 %copy-start.6 = (bf16[4000,256]{1,0:T(8,128)(2,1)S(1)}, bf16[4000,256]{1,0:T(8,128)(2,1)}, u32[]{:S(2)}) copy-start(bf16[4000,256]{1,0:T(8,128)(2,1)} %constant.5.clone.refs_8_.refs_14_) | copy-start | bytes 6144004
  12.2 11.6 %copy-start.8 = (s32[2]{0:T(128)S(1)}, s32[2]{0:T(128)}, u32[]{:S(2)}) copy-start(s32[2]{0:T(128)} %param.16) | copy-start | bytes 28
  12.3 11.6 %copy-start.9 = (s32[2]{0:T(128)S(1)}, s32[2]{0:T(128)}, u32[]{:S(2)}) copy-start(s32[2]{0:T(128)} %param.15) | copy-start | bytes 28
  19.5 9.9 %collective-permute-start.7 = (f32[256,128]{1,0:T(8,128)S(1)}, f32[256,128]{1,0:T(8,128)S(1)}, u32[]{:S(2)}, u32[]{:S(2)}) collective-permute-start(f32[256,128]{1,0:T(8,128)S(1)} %get-tuple-element.12.refs_1_), channel_id=1, source_target_pairs={{0,16},{2,18},{4,20},{6,22},{8,24},{10,26},{12,28},{14,30},{16,0},... | collective-permute-start | bytes 393224 | tf_op jit(solution)/shard_map/ppermute | solution.py:534
  20.6 8.8 %collective-permute-start.6 = (f32[256,128]{1,0:T(8,128)S(1)}, f32[256,128]{1,0:T(8,128)S(1)}, u32[]{:S(2)}, u32[]{:S(2)}) collective-permute-start(f32[256,128]{1,0:T(8,128)S(1)} %get-tuple-element.12.refs_1_), channel_id=1, source_target_pairs={{0,8},{2,10},{4,12},{6,14},{8,0},{10,2},{12,4},{14,6},{16,24},{18,... | collective-permute-start | bytes 393224 | tf_op jit(solution)/shard_map/ppermute | solution.py:534
  22.9 6.6 %collective-permute-start.5 = (f32[256,128]{1,0:T(8,128)S(1)}, f32[256,128]{1,0:T(8,128)S(1)}, u32[]{:S(2)}, u32[]{:S(2)}) collective-permute-start(f32[256,128]{1,0:T(8,128)S(1)} %get-tuple-element.12.refs_1_), channel_id=1, source_target_pairs={{0,4},{2,6},{4,0},{6,2},{8,12},{10,14},{12,8},{14,10},{16,20},{18,... | collective-permute-start | bytes 393224 | tf_op jit(solution)/shard_map/ppermute | solution.py:534
  23.9 5.6 %collective-permute-start.4 = (f32[256,128]{1,0:T(8,128)S(1)}, f32[256,128]{1,0:T(8,128)S(1)}, u32[]{:S(2)}, u32[]{:S(2)}) collective-permute-start(f32[256,128]{1,0:T(8,128)S(1)} %get-tuple-element.12.refs_1_), channel_id=1, source_target_pairs={{0,2},{2,0},{4,6},{6,4},{8,10},{10,8},{12,14},{14,12},{16,18},{18,... | collective-permute-start | bytes 393224 | tf_op jit(solution)/shard_map/ppermute | solution.py:534
  30.3 15.5 %collective-permute-start.8 = (f32[256,128]{1,0:T(8,128)S(1)}, f32[256,128]{1,0:T(8,128)S(1)}, u32[]{:S(2)}, u32[]{:S(2)}) collective-permute-start(f32[256,128]{1,0:T(8,128)S(1)} %get-tuple-element.13.refs_1_), channel_id=1, source_target_pairs={{0,1},{1,0},{2,3},{3,2},{4,5},{5,4},{6,7},{7,6},{8,9},{9,8},{10,11... | collective-permute-start | bytes 393224 | tf_op jit(solution)/shard_map/ppermute | solution.py:526
  31.9 4.7 %collective-permute-start.13 = (f32[32,256]{1,0:T(8,128)S(1)}, f32[32,256]{1,0:T(8,128)S(1)}, u32[]{:S(2)}, u32[]{:S(2)}) collective-permute-start(f32[32,256]{1,0:T(8,128)S(1)} %get-tuple-element.14), channel_id=1, source_target_pairs={{0,3},{1,2},{2,1},{3,0},{4,7},{5,6},{6,5},{7,4},{8,11},{9,10},{10,... | collective-permute-start | bytes 98312 | tf_op jit(solution)/shard_map/ppermute | solution.py:519
  31.9 6.3 %collective-permute-start.9 = (f32[32,256]{1,0:T(8,128)S(1)}, f32[32,256]{1,0:T(8,128)S(1)}, u32[]{:S(2)}, u32[]{:S(2)}) collective-permute-start(f32[32,256]{1,0:T(8,128)S(1)} %get-tuple-element.14), channel_id=1, source_target_pairs={{0,2},{2,0},{4,6},{6,4},{8,10},{10,8},{12,14},{14,12},{16,18},{18,... | collective-permute-start | bytes 98312 | tf_op jit(solution)/shard_map/ppermute | solution.py:517
  32.5 7.1 %collective-permute-start.16 = (f32[32,256]{1,0:T(8,128)S(1)}, f32[32,256]{1,0:T(8,128)S(1)}, u32[]{:S(2)}, u32[]{:S(2)}) collective-permute-start(f32[32,256]{1,0:T(8,128)S(1)} %get-tuple-element.15), channel_id=1, source_target_pairs={{0,31},{1,30},{2,29},{3,28},{4,27},{5,26},{6,25},{7,24},{8,23},{9,... | collective-permute-start | bytes 98312 | tf_op jit(solution)/shard_map/ppermute | solution.py:519
  36.6 5.2 %collective-permute-start.15 = (f32[32,256]{1,0:T(8,128)S(1)}, f32[32,256]{1,0:T(8,128)S(1)}, u32[]{:S(2)}, u32[]{:S(2)}) collective-permute-start(f32[32,256]{1,0:T(8,128)S(1)} %get-tuple-element.15), channel_id=1, source_target_pairs={{0,15},{1,14},{2,13},{3,12},{4,11},{5,10},{6,9},{7,8},{8,7},{9,6},... | collective-permute-start | bytes 98312 | tf_op jit(solution)/shard_map/ppermute | solution.py:519
  36.6 5.8 %collective-permute-start.14 = (f32[32,256]{1,0:T(8,128)S(1)}, f32[32,256]{1,0:T(8,128)S(1)}, u32[]{:S(2)}, u32[]{:S(2)}) collective-permute-start(f32[32,256]{1,0:T(8,128)S(1)} %get-tuple-element.15), channel_id=1, source_target_pairs={{0,7},{1,6},{2,5},{3,4},{4,3},{5,2},{6,1},{7,0},{8,15},{9,14},{10,... | collective-permute-start | bytes 98312 | tf_op jit(solution)/shard_map/ppermute | solution.py:519
  38.2 6.1 %collective-permute-start.12 = (f32[32,256]{1,0:T(8,128)S(1)}, f32[32,256]{1,0:T(8,128)S(1)}, u32[]{:S(2)}, u32[]{:S(2)}) collective-permute-start(f32[32,256]{1,0:T(8,128)S(1)} %get-tuple-element.15), channel_id=1, source_target_pairs={{0,30},{2,28},{4,26},{6,24},{8,22},{10,20},{12,18},{14,16},{16,14}... | collective-permute-start | bytes 98312 | tf_op jit(solution)/shard_map/ppermute | solution.py:517
  39.6 4.7 %collective-permute-start.11 = (f32[32,256]{1,0:T(8,128)S(1)}, f32[32,256]{1,0:T(8,128)S(1)}, u32[]{:S(2)}, u32[]{:S(2)}) collective-permute-start(f32[32,256]{1,0:T(8,128)S(1)} %get-tuple-element.15), channel_id=1, source_target_pairs={{0,14},{2,12},{4,10},{6,8},{8,6},{10,4},{12,2},{14,0},{16,30},{18,... | collective-permute-start | bytes 98312 | tf_op jit(solution)/shard_map/ppermute | solution.py:517
  41.8 4.0 %collective-permute-start.10 = (f32[32,256]{1,0:T(8,128)S(1)}, f32[32,256]{1,0:T(8,128)S(1)}, u32[]{:S(2)}, u32[]{:S(2)}) collective-permute-start(f32[32,256]{1,0:T(8,128)S(1)} %get-tuple-element.15), channel_id=1, source_target_pairs={{0,6},{2,4},{4,2},{6,0},{8,14},{10,12},{12,10},{14,8},{16,22},{18,... | collective-permute-start | bytes 98312 | tf_op jit(solution)/shard_map/ppermute | solution.py:517
  52.6 9.3 %collective-permute-start.20 = (f32[256,128]{1,0:T(8,128)S(1)}, f32[256,128]{1,0:T(8,128)S(1)}, u32[]{:S(2)}, u32[]{:S(2)}) collective-permute-start(f32[256,128]{1,0:T(8,128)S(1)} %shard_map.117.refs_1_), channel_id=1, source_target_pairs={{0,16},{2,18},{4,20},{6,22},{8,24},{10,26},{12,28},{14,30},{16,0},... | collective-permute-start | bytes 393224 | tf_op jit(solution)/shard_map/ppermute | solution.py:534
  54.2 7.7 %collective-permute-start.19 = (f32[256,128]{1,0:T(8,128)S(1)}, f32[256,128]{1,0:T(8,128)S(1)}, u32[]{:S(2)}, u32[]{:S(2)}) collective-permute-start(f32[256,128]{1,0:T(8,128)S(1)} %shard_map.117.refs_1_), channel_id=1, source_target_pairs={{0,8},{2,10},{4,12},{6,14},{8,0},{10,2},{12,4},{14,6},{16,24},{18,... | collective-permute-start | bytes 393224 | tf_op jit(solution)/shard_map/ppermute | solution.py:534
  55.0 6.9 %collective-permute-start.18 = (f32[256,128]{1,0:T(8,128)S(1)}, f32[256,128]{1,0:T(8,128)S(1)}, u32[]{:S(2)}, u32[]{:S(2)}) collective-permute-start(f32[256,128]{1,0:T(8,128)S(1)} %shard_map.117.refs_1_), channel_id=1, source_target_pairs={{0,4},{2,6},{4,0},{6,2},{8,12},{10,14},{12,8},{14,10},{16,20},{18,... | collective-permute-start | bytes 393224 | tf_op jit(solution)/shard_map/ppermute | solution.py:534
  56.4 5.5 %collective-permute-start.17 = (f32[256,128]{1,0:T(8,128)S(1)}, f32[256,128]{1,0:T(8,128)S(1)}, u32[]{:S(2)}, u32[]{:S(2)}) collective-permute-start(f32[256,128]{1,0:T(8,128)S(1)} %shard_map.117.refs_1_), channel_id=1, source_target_pairs={{0,2},{2,0},{4,6},{6,4},{8,10},{10,8},{12,14},{14,12},{16,18},{18,... | collective-permute-start | bytes 393224 | tf_op jit(solution)/shard_map/ppermute | solution.py:534
  62.7 5.0 %collective-permute-start.21 = (f32[256,128]{1,0:T(8,128)S(1)}, f32[256,128]{1,0:T(8,128)S(1)}, u32[]{:S(2)}, u32[]{:S(2)}) collective-permute-start(f32[256,128]{1,0:T(8,128)S(1)} %shard_map.118.refs_3_), channel_id=1, source_target_pairs={{0,1},{1,0},{2,3},{3,2},{4,5},{5,4},{6,7},{7,6},{8,9},{9,8},{10,11... | collective-permute-start | bytes 393224 | tf_op jit(solution)/shard_map/ppermute | solution.py:526

commit v12 on v10

--- a/solution.py
+++ b/solution.py
@@ -247,9 +247,11 @@
     return both
 
 
-def edges_kernel(mask_ref, target_ref, a_ref, b_ref):
-    target = target_ref[...].astype(f32).astype(bf16)
-    send_edges(*edges_of(EDGE, mask_ref[...], target), a_ref, b_ref)
+def edges_kernel(both_ref, a_ref, b_ref):
+    both = both_ref[...]
+    target = jnp.where(both >= 2.0, 1.0, 0.0)
+    mask = both - 2.0 * target
+    send_edges(*edges_of(EDGE, mask, target.astype(bf16)), a_ref, b_ref)
 
 
 def spectra_kernel(kern, w_ref, ker_ref, tb, h_ref, hs_ref):
@@ -559,7 +561,11 @@
 
     edge = jax.ShapeDtypeStruct((EDGE, tiles_dev * core), f32)
     send_a, send_b = call(
-        edges_kernel, None, [mask_rows, target_rows], [edge, edge], flops=3 * 10**9
+        edges_kernel,
+        None,
+        [mask_rows + 2.0 * target_rows.astype(f32)],
+        [edge, edge],
+        flops=3 * 10**9,
     )
     from_b, from_a = swap_edges(send_a, send_b)
     table = jnp.concatenate([partner_table, mirror_flags])

time: 60.7 us -> 60 us (0.988)
  local copies, waits for them, and re-layouts: 1.85 us -> 0.05 us
  other arithmetic: 0.08 us -> 1.06 us
    unnamed x20 -> x16, local copies, waits for them, and re-layouts: 1.85 us -> 0.05 us
    add x0 -> x1, other arithmetic: none -> 0.99 us  [per_device(): mask_rows + 2.0 * target_rows.astype(f32)]
where the time goes in v12:
time: 60 us; the launch traced here: 59.8 us
  starting transfers between devices  23.1 us (38%)
  Pallas kernels  18.1 us (30%)
  waiting for transfers between devices  16.1 us (27%)
  between operations  1.49 us (2%)
  other arithmetic  1.06 us (2%)
    pallas_call x7, Pallas kernels, call(): pl.pallas_call(wrapped, out_shape=out_shape, in_specs=[sm if i in smem el...  18.1 us
    ppermute x8, starting transfers between devices, from_partners(): lax.ppermute(grad, 'tile', [(i, i ^ bit) for i in range(n_tile)])  16.8 us
    ppermute x8, waiting for transfers between devices, from_partners(): lax.ppermute(grad, 'tile', [(i, i ^ bit) for i in range(n_tile)])  9.79 us
    ppermute x2, waiting for transfers between devices, depth_pair(): peer = lax.ppermute(x, 'depth', [(i, i ^ bit) for i in range(n_depth)])  4.7 us
    ppermute x4, starting transfers between devices, move(): return lax.ppermute(x, 'tile', pairs)  2.63 us
    ppermute x2, starting transfers between devices, depth_pair(): peer = lax.ppermute(x, 'depth', [(i, i ^ bit) for i in range(n_depth)])  2.11 us
    ppermute x2, waiting for transfers between devices, move(): return lax.ppermute(x, ('tile', 'depth'), both)  1.56 us
    ppermute x2, starting transfers between devices, move(): return lax.ppermute(x, ('tile', 'depth'), both)  1.52 us
  transfers between devices with their start and end apart: 16, of which 6 were waited for; matrix products, arithmetic and copies ran while one was open for 0% of the time, Pallas kernels for 3%

profile of v12, /device:TPU:0, one launch (start us, length us, event | category | flops | bytes accessed | tf_op | source)
XLA Modules:
  0.0 59.8 jit_solution(4900881317172511124)
XLA Ops:
  0.6 1.0 %multiply_add_fusion.refs_0_ = f32[256,128]{1,0:T(8,128)S(1)} fusion(s32[2,128,128]{2,1,0:T(8,128)} %param.11, f32[2,128,128]{2,1,0:T(8,128)} %refs_0_.5), kind=kLoop, calls=%fused_computation | loop fusion | flops 98304 | bytes 393216 | tf_op jit(solution)/shard_map/add | solution.py:566
  1.6 0.0 copy-start.2
  1.6 0.0 copy-start.3
  1.6 0.0 copy-start.5
  1.7 0.3 shard_map.113
  1.9 0.5 collective-permute-start
  2.4 0.7 %collective-permute-start.1 = (f32[48,256]{1,0:T(8,128)S(1)}, f32[48,256]{1,0:T(8,128)S(1)}, u32[]{:S(2)}, u32[]{:S(2)}) collective-permute-start(f32[48,256]{1,0:T(8,128)S(1)} %get-tuple-element.11), channel_id=1, source_target_pairs={{2,4},{4,2},{6,8},{8,6},{10,12},{12,10},{14,16},{16,14},{18,20},{2... | collective-permute-start | bytes 147464 | tf_op jit(solution)/shard_map/ppermute | solution.py:520
  3.1 0.0 copy-start
  3.1 0.0 copy-start.1
  3.1 0.0 copy-start.4
  3.2 2.0 %shard_map.114.refs_5_.refs_9_ = f32[12,4,96,128]{3,2,1,0:T(8,128)S(1)} custom-call(f32[1,6]{1,0:T(1,128)S(1)} %copy-done.3, f32[2,6,25,1,25]{4,3,2,1,0:T(1,128)S(1)} %bitcast.7, bf16[1408,256]{1,0:T(8,128)(2,1)S(1)} %copy-done.5), custom_call_target="tpu_custom_call" | custom-call | flops 3000000000 | bytes 4000000 | tf_op jit(solution)/shard_map/pallas_call | solution.py:210
  5.8 0.0 collective-permute-done.refs_3_
  5.8 0.0 collective-permute-done.1.refs_4_
  5.8 0.0 copy-start.6
  5.8 0.0 copy-start.7
  5.9 6.8 %shard_map.115 = (f32[256,128]{1,0:T(8,128)S(1)}, f32[2,4,96,128]{3,2,1,0:T(8,128)S(1)}, f32[160,256]{1,0:T(8,128)S(1)}) custom-call(f32[1]{0:T(128)S(6)} %copy.12.refs_0_, f32[256,128]{1,0:T(8,128)S(1)} %bitcast.5, s32[256,128]{1,0:T(8,128)S(1)} %bitcast.6, f32[48,256]{1,0:T(8,128)S(1)} %collective-permute-done.refs_3_, ...), custom_call_target="tpu_custom_call" | custom-call | flops 10000000000 | tf_op jit(solution)/shard_map/pallas_call | solution.py:210
  12.7 6.7 %collective-permute-start.5 = (f32[256,128]{1,0:T(8,128)S(1)}, f32[256,128]{1,0:T(8,128)S(1)}, u32[]{:S(2)}, u32[]{:S(2)}) collective-permute-start(f32[256,128]{1,0:T(8,128)S(1)} %get-tuple-element.12.refs_1_), channel_id=1, source_target_pairs={{0,16},{2,18},{4,20},{6,22},{8,24},{10,26},{12,28},{14,30},{16,0},... | collective-permute-start | bytes 393224 | tf_op jit(solution)/shard_map/ppermute | solution.py:538
  19.3 1.6 %collective-permute-start.4 = (f32[256,128]{1,0:T(8,128)S(1)}, f32[256,128]{1,0:T(8,128)S(1)}, u32[]{:S(2)}, u32[]{:S(2)}) collective-permute-start(f32[256,128]{1,0:T(8,128)S(1)} %get-tuple-element.12.refs_1_), channel_id=1, source_target_pairs={{0,8},{2,10},{4,12},{6,14},{8,0},{10,2},{12,4},{14,6},{16,24},{18,... | collective-permute-start | bytes 393224 | tf_op jit(solution)/shard_map/ppermute | solution.py:538
  20.9 0.5 collective-permute-start.3
  21.4 0.0 collective-permute-start.2
  21.4 0.1 pad_add_fusion.refs_0_
  21.5 4.4 %collective-permute-done.5.refs_5_ = f32[256,128]{1,0:T(8,128)S(1)} collective-permute-done((f32[256,128]{1,0:T(8,128)S(1)}, f32[256,128]{1,0:T(8,128)S(1)}, u32[]{:S(2)}, u32[]{:S(2)}) %collective-permute-start.5) | collective-permute-done | bytes 131104 | tf_op jit(solution)/shard_map/ppermute | solution.py:538
  25.9 0.2 collective-permute-done.4.refs_4_
  26.1 0.0 collective-permute-done.3.refs_3_
  26.1 0.0 collective-permute-done.2.refs_2_
  26.1 0.9 %shard_map.116 = (f32[256,128]{1,0:T(8,128)S(1)}, f32[32,256]{1,0:T(8,128)S(1)}, f32[32,256]{1,0:T(8,128)S(1)}) custom-call(s32[4]{0:T(128)S(1)} %pad_add_fusion.refs_0_, f32[256,128]{1,0:T(8,128)S(1)} %get-tuple-element.12.refs_1_, f32[256,128]{1,0:T(8,128)S(1)} %collective-permute-done.2.refs_2_, f32[256,128]{1,0:T(8,128)S(1)} %collective-permute-done.3.refs_3_, ...), custom_call_target="tpu_custom_call" | custom-call | tf_op jit(solution)/shard_map/pallas_call | solution.py:210
  27.0 1.6 %collective-permute-start.6 = (f32[256,128]{1,0:T(8,128)S(1)}, f32[256,128]{1,0:T(8,128)S(1)}, u32[]{:S(2)}, u32[]{:S(2)}) collective-permute-start(f32[256,128]{1,0:T(8,128)S(1)} %get-tuple-element.13.refs_1_), channel_id=1, source_target_pairs={{0,1},{1,0},{2,3},{3,2},{4,5},{5,4},{6,7},{7,6},{8,9},{9,8},{10,11... | collective-permute-start | bytes 393224 | tf_op jit(solution)/shard_map/ppermute | solution.py:529
  28.6 0.0 collective-permute-start.8
  28.6 0.6 %collective-permute-start.7 = (f32[32,256]{1,0:T(8,128)S(1)}, f32[32,256]{1,0:T(8,128)S(1)}, u32[]{:S(2)}, u32[]{:S(2)}) collective-permute-start(f32[32,256]{1,0:T(8,128)S(1)} %get-tuple-element.14), channel_id=1, source_target_pairs={{0,2},{2,0},{4,6},{6,4},{8,10},{10,8},{12,14},{14,12},{16,18},{18,... | collective-permute-start | bytes 98312 | tf_op jit(solution)/shard_map/ppermute | solution.py:520
  29.2 1.5 %collective-permute-start.10 = (f32[32,256]{1,0:T(8,128)S(1)}, f32[32,256]{1,0:T(8,128)S(1)}, u32[]{:S(2)}, u32[]{:S(2)}) collective-permute-start(f32[32,256]{1,0:T(8,128)S(1)} %get-tuple-element.15), channel_id=1, source_target_pairs={{2,5},{3,4},{4,3},{5,2},{6,9},{7,8},{8,7},{9,6},{10,13},{11,12},{1... | collective-permute-start | bytes 98312 | tf_op jit(solution)/shard_map/ppermute | solution.py:522
  30.7 0.8 %collective-permute-start.9 = (f32[32,256]{1,0:T(8,128)S(1)}, f32[32,256]{1,0:T(8,128)S(1)}, u32[]{:S(2)}, u32[]{:S(2)}) collective-permute-start(f32[32,256]{1,0:T(8,128)S(1)} %get-tuple-element.15), channel_id=1, source_target_pairs={{2,4},{4,2},{6,8},{8,6},{10,12},{12,10},{14,16},{16,14},{18,20},{2... | collective-permute-start | bytes 98312 | tf_op jit(solution)/shard_map/ppermute | solution.py:520
  31.5 0.7 %collective-permute-done.8.refs_4_ = f32[32,256]{1,0:T(8,128)S(1)} collective-permute-done((f32[32,256]{1,0:T(8,128)S(1)}, f32[32,256]{1,0:T(8,128)S(1)}, u32[]{:S(2)}, u32[]{:S(2)}) %collective-permute-start.8) | collective-permute-done | bytes 32800 | tf_op jit(solution)/shard_map/ppermute | solution.py:522
  32.2 0.0 collective-permute-done.7.refs_3_
  32.2 0.9 %collective-permute-done.10.refs_6_ = f32[32,256]{1,0:T(8,128)S(1)} collective-permute-done((f32[32,256]{1,0:T(8,128)S(1)}, f32[32,256]{1,0:T(8,128)S(1)}, u32[]{:S(2)}, u32[]{:S(2)}) %collective-permute-start.10) | collective-permute-done | bytes 32800 | tf_op jit(solution)/shard_map/ppermute | solution.py:522
  33.1 0.0 collective-permute-done.9.refs_5_
  33.1 0.0 collective-permute-done.6.refs_2_
  33.1 6.8 %shard_map.117.refs_1_ = f32[256,128]{1,0:T(8,128)S(1)} custom-call(f32[1]{0:T(128)S(6)} %copy.12.refs_0_, f32[256,128]{1,0:T(8,128)S(1)} %get-tuple-element.13.refs_1_, f32[256,128]{1,0:T(8,128)S(1)} %collective-permute-done.6.refs_2_, f32[32,256]{1,0:T(8,128)S(1)} %collective-permute-done.7.refs_3_, f32[32,256]{1,0:T(8,128)S(1)} %collective-permute-done.8.refs_4_, ...), custom_call_target="tpu_custom_call" | custom-call | flops 10000000000 | tf_op jit(solution)/shard_map/pallas_call | solution.py:210
  39.9 6.3 %collective-permute-start.14 = (f32[256,128]{1,0:T(8,128)S(1)}, f32[256,128]{1,0:T(8,128)S(1)}, u32[]{:S(2)}, u32[]{:S(2)}) collective-permute-start(f32[256,128]{1,0:T(8,128)S(1)} %shard_map.117.refs_1_), channel_id=1, source_target_pairs={{0,16},{2,18},{4,20},{6,22},{8,24},{10,26},{12,28},{14,30},{16,0},... | collective-permute-start | bytes 393224 | tf_op jit(solution)/shard_map/ppermute | solution.py:538
  46.2 0.7 %collective-permute-start.13 = (f32[256,128]{1,0:T(8,128)S(1)}, f32[256,128]{1,0:T(8,128)S(1)}, u32[]{:S(2)}, u32[]{:S(2)}) collective-permute-start(f32[256,128]{1,0:T(8,128)S(1)} %shard_map.117.refs_1_), channel_id=1, source_target_pairs={{0,8},{2,10},{4,12},{6,14},{8,0},{10,2},{12,4},{14,6},{16,24},{18,... | collective-permute-start | bytes 393224 | tf_op jit(solution)/shard_map/ppermute | solution.py:538
  46.9 0.7 %collective-permute-start.12 = (f32[256,128]{1,0:T(8,128)S(1)}, f32[256,128]{1,0:T(8,128)S(1)}, u32[]{:S(2)}, u32[]{:S(2)}) collective-permute-start(f32[256,128]{1,0:T(8,128)S(1)} %shard_map.117.refs_1_), channel_id=1, source_target_pairs={{0,4},{2,6},{4,0},{6,2},{8,12},{10,14},{12,8},{14,10},{16,20},{18,... | collective-permute-start | bytes 393224 | tf_op jit(solution)/shard_map/ppermute | solution.py:538
  47.6 0.3 collective-permute-start.11
  47.9 5.1 %collective-permute-done.14.refs_5_ = f32[256,128]{1,0:T(8,128)S(1)} collective-permute-done((f32[256,128]{1,0:T(8,128)S(1)}, f32[256,128]{1,0:T(8,128)S(1)}, u32[]{:S(2)}, u32[]{:S(2)}) %collective-permute-start.14) | collective-permute-done | bytes 131104 | tf_op jit(solution)/shard_map/ppermute | solution.py:538
  53.1 0.0 collective-permute-done.13.refs_4_
  53.1 0.0 collective-permute-done.12.refs_3_
  53.1 0.7 %shard_map.118.refs_3_ = f32[256,128]{1,0:T(8,128)S(1)} custom-call(s32[4]{0:T(128)S(1)} %pad_add_fusion.refs_0_, f32[256,128]{1,0:T(8,128)S(1)} %shard_map.117.refs_1_, f32[256,128]{1,0:T(8,128)S(1)} %collective-permute-done.11.refs_2_, f32[256,128]{1,0:T(8,128)S(1)} %collective-permute-done.12.refs_3_, f32[256,128]{1,0:T(8,128)S(1)} %collective-permute-done.13.refs_4_, ...), custom_call_target="tpu_custom_call" | custom-call | tf_op jit(solution)/shard_map/pallas_call | solution.py:210
  53.8 0.6 collective-permute-start.15
  54.4 4.7 %collective-permute-done.15.refs_4_ = f32[256,128]{1,0:T(8,128)S(1)} collective-permute-done((f32[256,128]{1,0:T(8,128)S(1)}, f32[256,128]{1,0:T(8,128)S(1)}, u32[]{:S(2)}, u32[]{:S(2)}) %collective-permute-start.15) | collective-permute-done | bytes 131104 | tf_op jit(solution)/shard_map/ppermute | solution.py:529
  59.1 0.7 %shard_map.119 = (f32[2,128,128]{2,1,0:T(8,128)}, f32[2,128,128]{2,1,0:T(8,128)}) custom-call(f32[2,128,128]{2,1,0:T(8,128)S(1)} %copy-done, f32[256,128]{1,0:T(8,128)S(1)} %get-tuple-element.13.refs_1_, f32[256,128]{1,0:T(8,128)S(1)} %collective-permute-done.6.refs_2_, f32[256,128]{1,0:T(8,128)S(1)} %shard_map.118.refs_3_, ...), custom_call_target="tpu_custom_call" | custom-call | tf_op jit(solution)/shard_map/pallas_call | solution.py:210
  (9 shorter events, 0.0 us)
Async XLA Ops:
  1.6 1.5 %copy-start.2 = (f32[2,1,6,25,25]{4,1,3,2,0:T(1,128)S(1)}, f32[2,1,6,25,25]{4,1,3,2,0:T(1,128)}, u32[]{:S(2)}) copy-start(f32[2,1,6,25,25]{4,1,3,2,0:T(1,128)} %param.12) | copy-start | bytes 90004
  1.6 1.5 %copy-start.3 = (f32[1,6]{1,0:T(1,128)S(1)}, f32[1,6]{1,0:T(1,128)}, u32[]{:S(2)}) copy-start(f32[1,6]{1,0:T(1,128)} %refs_0_.4) | copy-start | bytes 76
  1.6 1.5 %copy-start.5 = (bf16[1408,256]{1,0:T(8,128)(2,1)S(1)}, bf16[1408,256]{1,0:T(8,128)(2,1)}, u32[]{:S(2)}) copy-start(bf16[1408,256]{1,0:T(8,128)(2,1)} %constant.6.clone.refs_2_) | copy-start | bytes 2162692
  1.9 3.9 %collective-permute-start = (f32[48,256]{1,0:T(8,128)S(1)}, f32[48,256]{1,0:T(8,128)S(1)}, u32[]{:S(2)}, u32[]{:S(2)}) collective-permute-start(f32[48,256]{1,0:T(8,128)S(1)} %get-tuple-element.10), channel_id=1, source_target_pairs={{0,2},{2,0},{4,6},{6,4},{8,10},{10,8},{12,14},{14,12},{16,18},{18,... | collective-permute-start | bytes 147464 | tf_op jit(solution)/shard_map/ppermute | solution.py:520
  2.4 3.4 %collective-permute-start.1 = (f32[48,256]{1,0:T(8,128)S(1)}, f32[48,256]{1,0:T(8,128)S(1)}, u32[]{:S(2)}, u32[]{:S(2)}) collective-permute-start(f32[48,256]{1,0:T(8,128)S(1)} %get-tuple-element.11), channel_id=1, source_target_pairs={{2,4},{4,2},{6,8},{8,6},{10,12},{12,10},{14,16},{16,14},{18,20},{2... | collective-permute-start | bytes 147464 | tf_op jit(solution)/shard_map/ppermute | solution.py:520
  3.1 2.7 %copy-start = (f32[2,128,128]{2,1,0:T(8,128)S(1)}, f32[2,128,128]{2,1,0:T(8,128)}, u32[]{:S(2)}) copy-start(f32[2,128,128]{2,1,0:T(8,128)} %refs_0_.5) | copy-start | bytes 393220
  3.1 2.7 %copy-start.1 = (s32[2,128,128]{2,1,0:T(8,128)S(1)}, s32[2,128,128]{2,1,0:T(8,128)}, u32[]{:S(2)}) copy-start(s32[2,128,128]{2,1,0:T(8,128)} %param.11) | copy-start | bytes 393220
  3.1 2.7 %copy-start.4 = (bf16[4000,256]{1,0:T(8,128)(2,1)S(1)}, bf16[4000,256]{1,0:T(8,128)(2,1)}, u32[]{:S(2)}) copy-start(bf16[4000,256]{1,0:T(8,128)(2,1)} %constant.7.clone.refs_6_.refs_10_) | copy-start | bytes 6144004
  5.8 15.6 %copy-start.6 = (s32[2]{0:T(128)S(1)}, s32[2]{0:T(128)}, u32[]{:S(2)}) copy-start(s32[2]{0:T(128)} %param.16) | copy-start | bytes 28
  5.8 15.6 %copy-start.7 = (s32[2]{0:T(128)S(1)}, s32[2]{0:T(128)}, u32[]{:S(2)}) copy-start(s32[2]{0:T(128)} %param.15) | copy-start | bytes 28
  12.7 13.3 %collective-permute-start.5 = (f32[256,128]{1,0:T(8,128)S(1)}, f32[256,128]{1,0:T(8,128)S(1)}, u32[]{:S(2)}, u32[]{:S(2)}) collective-permute-start(f32[256,128]{1,0:T(8,128)S(1)} %get-tuple-element.12.refs_1_), channel_id=1, source_target_pairs={{0,16},{2,18},{4,20},{6,22},{8,24},{10,26},{12,28},{14,30},{16,0},... | collective-permute-start | bytes 393224 | tf_op jit(solution)/shard_map/ppermute | solution.py:538
  19.3 6.8 %collective-permute-start.4 = (f32[256,128]{1,0:T(8,128)S(1)}, f32[256,128]{1,0:T(8,128)S(1)}, u32[]{:S(2)}, u32[]{:S(2)}) collective-permute-start(f32[256,128]{1,0:T(8,128)S(1)} %get-tuple-element.12.refs_1_), channel_id=1, source_target_pairs={{0,8},{2,10},{4,12},{6,14},{8,0},{10,2},{12,4},{14,6},{16,24},{18,... | collective-permute-start | bytes 393224 | tf_op jit(solution)/shard_map/ppermute | solution.py:538
  20.9 5.2 %collective-permute-start.3 = (f32[256,128]{1,0:T(8,128)S(1)}, f32[256,128]{1,0:T(8,128)S(1)}, u32[]{:S(2)}, u32[]{:S(2)}) collective-permute-start(f32[256,128]{1,0:T(8,128)S(1)} %get-tuple-element.12.refs_1_), channel_id=1, source_target_pairs={{0,4},{2,6},{4,0},{6,2},{8,12},{10,14},{12,8},{14,10},{16,20},{18,... | collective-permute-start | bytes 393224 | tf_op jit(solution)/shard_map/ppermute | solution.py:538
  21.4 4.7 %collective-permute-start.2 = (f32[256,128]{1,0:T(8,128)S(1)}, f32[256,128]{1,0:T(8,128)S(1)}, u32[]{:S(2)}, u32[]{:S(2)}) collective-permute-start(f32[256,128]{1,0:T(8,128)S(1)} %get-tuple-element.12.refs_1_), channel_id=1, source_target_pairs={{0,2},{2,0},{4,6},{6,4},{8,10},{10,8},{12,14},{14,12},{16,18},{18,... | collective-permute-start | bytes 393224 | tf_op jit(solution)/shard_map/ppermute | solution.py:538
  27.0 6.1 %collective-permute-start.6 = (f32[256,128]{1,0:T(8,128)S(1)}, f32[256,128]{1,0:T(8,128)S(1)}, u32[]{:S(2)}, u32[]{:S(2)}) collective-permute-start(f32[256,128]{1,0:T(8,128)S(1)} %get-tuple-element.13.refs_1_), channel_id=1, source_target_pairs={{0,1},{1,0},{2,3},{3,2},{4,5},{5,4},{6,7},{7,6},{8,9},{9,8},{10,11... | collective-permute-start | bytes 393224 | tf_op jit(solution)/shard_map/ppermute | solution.py:529
  28.6 3.7 %collective-permute-start.8 = (f32[32,256]{1,0:T(8,128)S(1)}, f32[32,256]{1,0:T(8,128)S(1)}, u32[]{:S(2)}, u32[]{:S(2)}) collective-permute-start(f32[32,256]{1,0:T(8,128)S(1)} %get-tuple-element.14), channel_id=1, source_target_pairs={{0,3},{1,2},{2,1},{3,0},{4,7},{5,6},{6,5},{7,4},{8,11},{9,10},{10,... | collective-permute-start | bytes 98312 | tf_op jit(solution)/shard_map/ppermute | solution.py:522
  28.6 3.7 %collective-permute-start.7 = (f32[32,256]{1,0:T(8,128)S(1)}, f32[32,256]{1,0:T(8,128)S(1)}, u32[]{:S(2)}, u32[]{:S(2)}) collective-permute-start(f32[32,256]{1,0:T(8,128)S(1)} %get-tuple-element.14), channel_id=1, source_target_pairs={{0,2},{2,0},{4,6},{6,4},{8,10},{10,8},{12,14},{14,12},{16,18},{18,... | collective-permute-start | bytes 98312 | tf_op jit(solution)/shard_map/ppermute | solution.py:520
  29.2 3.9 %collective-permute-start.10 = (f32[32,256]{1,0:T(8,128)S(1)}, f32[32,256]{1,0:T(8,128)S(1)}, u32[]{:S(2)}, u32[]{:S(2)}) collective-permute-start(f32[32,256]{1,0:T(8,128)S(1)} %get-tuple-element.15), channel_id=1, source_target_pairs={{2,5},{3,4},{4,3},{5,2},{6,9},{7,8},{8,7},{9,6},{10,13},{11,12},{1... | collective-permute-start | bytes 98312 | tf_op jit(solution)/shard_map/ppermute | solution.py:522
  30.7 2.4 %collective-permute-start.9 = (f32[32,256]{1,0:T(8,128)S(1)}, f32[32,256]{1,0:T(8,128)S(1)}, u32[]{:S(2)}, u32[]{:S(2)}) collective-permute-start(f32[32,256]{1,0:T(8,128)S(1)} %get-tuple-element.15), channel_id=1, source_target_pairs={{2,4},{4,2},{6,8},{8,6},{10,12},{12,10},{14,16},{16,14},{18,20},{2... | collective-permute-start | bytes 98312 | tf_op jit(solution)/shard_map/ppermute | solution.py:520
  39.9 13.2 %collective-permute-start.14 = (f32[256,128]{1,0:T(8,128)S(1)}, f32[256,128]{1,0:T(8,128)S(1)}, u32[]{:S(2)}, u32[]{:S(2)}) collective-permute-start(f32[256,128]{1,0:T(8,128)S(1)} %shard_map.117.refs_1_), channel_id=1, source_target_pairs={{0,16},{2,18},{4,20},{6,22},{8,24},{10,26},{12,28},{14,30},{16,0},... | collective-permute-start | bytes 393224 | tf_op jit(solution)/shard_map/ppermute | solution.py:538
  46.2 6.9 %collective-permute-start.13 = (f32[256,128]{1,0:T(8,128)S(1)}, f32[256,128]{1,0:T(8,128)S(1)}, u32[]{:S(2)}, u32[]{:S(2)}) collective-permute-start(f32[256,128]{1,0:T(8,128)S(1)} %shard_map.117.refs_1_), channel_id=1, source_target_pairs={{0,8},{2,10},{4,12},{6,14},{8,0},{10,2},{12,4},{14,6},{16,24},{18,... | collective-permute-start | bytes 393224 | tf_op jit(solution)/shard_map/ppermute | solution.py:538
  46.9 6.2 %collective-permute-start.12 = (f32[256,128]{1,0:T(8,128)S(1)}, f32[256,128]{1,0:T(8,128)S(1)}, u32[]{:S(2)}, u32[]{:S(2)}) collective-permute-start(f32[256,128]{1,0:T(8,128)S(1)} %shard_map.117.refs_1_), channel_id=1, source_target_pairs={{0,4},{2,6},{4,0},{6,2},{8,12},{10,14},{12,8},{14,10},{16,20},{18,... | collective-permute-start | bytes 393224 | tf_op jit(solution)/shard_map/ppermute | solution.py:538
  47.6 5.4 %collective-permute-start.11 = (f32[256,128]{1,0:T(8,128)S(1)}, f32[256,128]{1,0:T(8,128)S(1)}, u32[]{:S(2)}, u32[]{:S(2)}) collective-permute-start(f32[256,128]{1,0:T(8,128)S(1)} %shard_map.117.refs_1_), channel_id=1, source_target_pairs={{0,2},{2,0},{4,6},{6,4},{8,10},{10,8},{12,14},{14,12},{16,18},{18,... | collective-permute-start | bytes 393224 | tf_op jit(solution)/shard_map/ppermute | solution.py:538
  53.8 5.3 %collective-permute-start.15 = (f32[256,128]{1,0:T(8,128)S(1)}, f32[256,128]{1,0:T(8,128)S(1)}, u32[]{:S(2)}, u32[]{:S(2)}) collective-permute-start(f32[256,128]{1,0:T(8,128)S(1)} %shard_map.118.refs_3_), channel_id=1, source_target_pairs={{0,1},{1,0},{2,3},{3,2},{4,5},{5,4},{6,7},{7,6},{8,9},{9,8},{10,11... | collective-permute-start | bytes 393224 | tf_op jit(solution)/shard_map/ppermute | solution.py:529

commit v13 on v12

--- a/solution.py
+++ b/solution.py
@@ -26,6 +26,7 @@
 ROWS = 160
 ROW0 = 8
 CHUNK = 16
+SPILL = 16
 EDGE = 48
 WIDE_PAD = 32
 VMEM_LIMIT = 24 * 1024 * 1024
@@ -294,25 +295,29 @@
             f_ref[t, j] = comp if base is None else base[t, j] - STEP_RATE * comp
 
 
-def gradient_body(kern, last, f_ref, tgt_ref, h_ref, thr_ref, tb, g_ref, work):
-    fld, inten, tot, a_hi, a_lo, b_cat, r_cat, w_cat = work
-    group = 2 if kern % 2 == 0 else 1
+def group_of(kern):
+    return 2 if kern % 2 == 0 else 1
+
+
+def gradient_body(kern, field_tiles, back_tiles, field_refs, back_refs, fld, inten, h_ref, tb):
+    if field_tiles:
+        last, f_ref, tgt_ref, thr_ref, a_hi, a_lo, b_cat = field_refs
+    finish, tot, r_cat, w_cat = back_refs
+    group = group_of(kern)
     count = kern // group
-    chains = [(t, c) for t in range(2) for c in range(count)]
-    lag = count + 2
-
-    def at(i):
-        return chains[i] if 0 <= i < len(chains) else None
-
-    tile = lax.axis_index("tile")
-    first = jnp.where(tile == 0, WIDE, HALO) - ROW0
-    end = jnp.where(tile == last, WIDE + CORE, WIDE + CORE + HALO) - ROW0
-    row = lax.broadcasted_iota(jnp.int32, (ROWS, CORE), 0)
-    inside = (row >= first) & (row < end)
-    lane = lax.broadcasted_iota(jnp.int32, (1, 2 * YB), 1)
-    bin_at = lax.rem(lane, YB)
-    weight = jnp.where((bin_at == 0) | (bin_at == NU - 1), 1.0, 2.0) / (NX * NY)
-    weight = jnp.where(lane < YB, weight, -weight)
+    chains = [(t, c) for t in field_tiles for c in range(count)]
+    backs = [(t, c) for t in back_tiles for c in range(count)]
+    lag = count + 2 if field_tiles else 0
+
+    def pick(i, listed):
+        return listed[i] if 0 <= i < len(listed) else None
+
+    if field_tiles:
+        tile = lax.axis_index("tile")
+        first = jnp.where(tile == 0, WIDE, HALO) - ROW0
+        end = jnp.where(tile == last, WIDE + CORE, WIDE + CORE + HALO) - ROW0
+        row = lax.broadcasted_iota(jnp.int32, (ROWS, CORE), 0)
+        inside = (row >= first) & (row < end)
 
     def chunks(height):
         return [slice(r, r + CHUNK) for r in range(0, height, CHUNK)]
@@ -351,21 +356,21 @@
             whole = dot(tb("x2"), b_cat[2 * g + slot])
             for rows in chunks(ROWS):
                 field = whole[rows]
-                fld[t, k, rows] = field
+                fld[t][k, rows] = field
                 re, im = field[:, :CORE], field[:, CORE:]
                 power = re * re + im * im
-                inten[t, rows] = power if k == 0 else inten[t, rows] + power
+                inten[t][rows] = power if k == 0 else inten[t][rows] + power
 
     def slope_of(t):
-        resist = jax.nn.sigmoid(STEEPNESS * (inten[t] - thr_ref[0]))
+        resist = jax.nn.sigmoid(STEEPNESS * (inten[t][...] - thr_ref[0]))
         target = tgt_ref[:, CORE * t : CORE * t + CORE]
         slope = 2.0 * (resist - target) * STEEPNESS * resist * (1.0 - resist)
-        inten[t] = jnp.where(inside, 2.0 * slope, 0.0)
+        inten[t][...] = jnp.where(inside, 2.0 * slope, 0.0)
 
     def scaled_field(t, c, slot):
         for g in range(group):
             for rows in chunks(ROWS):
-                slope, field = inten[t, rows], fld[t, group * c + g, rows]
+                slope, field = inten[t][rows], fld[t][group * c + g, rows]
                 r_hi, r_lo = split(
                     jnp.concatenate([slope * field[:, :CORE], slope * field[:, CORE:]], axis=1)
                 )
@@ -385,7 +390,7 @@
     def add_back(t, c, slot):
         specs = dot(w_cat[slot], tb("y3"))
         for rows in chunks(XB):
-            acc = [0.0] * 4 if c == 0 else [tot[t, j, rows] for j in range(4)]
+            acc = [0.0] * 4 if c == 0 else [tot[j, rows] for j in range(4)]
             for part in range(2 * group):
                 base = 2 * XB * part + rows.start
                 cos_rows, sin_rows = slice(base, base + CHUNK), slice(base + XB, base + XB + CHUNK)
@@ -398,18 +403,11 @@
                 acc[2] = acc[2] + (hmr * bmr + hmi * bmi)
                 acc[3] = acc[3] + (hmr * bmi - hmi * bmr)
             for j in range(4):
-                tot[t, j, rows] = acc[j]
-
-    def finish(t):
-        r_hi, r_lo = split(even_odd(*(tot[t, j] for j in range(4))))
-        u = dot(tb("x4"), jnp.concatenate([r_hi, r_hi, r_lo], axis=0))
-        u_hi, u_lo = split(weight * u)
-        term = dot3(tb(f"by{t}_hi"), tb(f"by{t}_lo"), u_hi, u_lo, dot_nt)
-        g_ref[...] = term if t == 0 else g_ref[...] + term
-
-    for i in range(len(chains) + lag + 2):
-        new, mid, old = at(i), at(i - 1), at(i - 2)
-        back, back_mid, back_old = at(i - lag), at(i - lag - 1), at(i - lag - 2)
+                tot[j, rows] = acc[j]
+
+    for i in range(max(len(chains) + 2, len(backs) + lag + 2)):
+        new, mid, old = (pick(i - j, chains) for j in range(3))
+        back, back_mid, back_old = (pick(i - lag - j, backs) for j in range(3))
         slot, other = i % 2, (i + 1) % 2
         if mid:
             z_one = dot(a_hi[other], tb("y2"))
@@ -432,12 +430,54 @@
         if old and old[1] == count - 1:
             slope_of(old[0])
         if back_old and back_old[1] == count - 1:
-            finish(back_old[0])
+            finish()
+
+
+def strip_part(t, rows, tot, tb):
+    lane = lax.broadcasted_iota(jnp.int32, (1, 2 * YB), 1)
+    bin_at = lax.rem(lane, YB)
+    weight = jnp.where((bin_at == 0) | (bin_at == NU - 1), 1.0, 2.0) / (NX * NY)
+    weight = jnp.where(lane < YB, weight, -weight)
+    r_hi, r_lo = split(even_odd(*(tot[j] for j in range(4))))
+    u = dot(tb("x4"), jnp.concatenate([r_hi, r_hi, r_lo], axis=0))
+    u_hi, u_lo = split(weight * u)
+    return dot3(tb(f"by{t}_hi")[rows], tb(f"by{t}_lo")[rows], u_hi, u_lo, dot_nt)
+
+
+def upper_part(kern, last, f_ref, tgt_ref, h_ref, thr_ref, tb, outs, work):
+    own_ref, spill_ref, fld1, slope1 = outs
+    fld0, slope0, tot, a_hi, a_lo, b_cat, r_cat, w_cat = work
+
+    def finish():
+        term = strip_part(0, slice(0, CORE + SPILL), tot, tb)
+        own_ref[...] = term[:CORE]
+        spill_ref[...] = term[CORE:]
+
+    field_refs = (last, f_ref, tgt_ref, thr_ref, a_hi, a_lo, b_cat)
+    back_refs = (finish, tot, r_cat, w_cat)
+    fld, inten = (fld0, fld1), (slope0, slope1)
+    gradient_body(kern, (0, 1), (0,), field_refs, back_refs, fld, inten, h_ref, tb)
+
+
+def lower_kernel(
+    kern, own_ref, spill_ref, fld1, slope1, h_ref, tb, all_ref, late_ref, tot, r_cat, w_cat
+):
+    def finish():
+        term = strip_part(1, slice(CORE - SPILL, 2 * CORE), tot, tb)
+        join = term[SPILL : 2 * SPILL] + spill_ref[...]
+        late_ref[...] = jnp.concatenate([term[:SPILL], join, term[2 * SPILL :]], axis=0)
+        all_ref[: CORE - SPILL] = own_ref[: CORE - SPILL]
+        all_ref[CORE - SPILL : CORE] = own_ref[CORE - SPILL :] + term[:SPILL]
+        all_ref[CORE : CORE + SPILL] = join
+        all_ref[CORE + SPILL :] = term[2 * SPILL :]
+
+    back_refs = (finish, tot, r_cat, w_cat)
+    gradient_body(kern, (), (1,), None, back_refs, (None, fld1), (None, slope1), h_ref, tb)
 
 
 def first_kernel(
     kern, last, thr_ref, mask_ref, target_ref, a_ref, b_ref, h_ref, tb,
-    g_ref, f_ref, tgt_ref, *work,
+    own_ref, spill_ref, fld1, slope1, f_ref, tgt_ref, *work,
 ):
     m_hi, m_lo = split(mask_ref[...])
     v, left, right = sides(last, a_ref[...], b_ref[...], tb)
@@ -448,12 +488,13 @@
         + dot(tb("sel_halo", 0)[:, :EDGE], left)
         + dot(tb("sel_halo", 1)[:, :EDGE], right)
     )
-    gradient_body(kern, last, f_ref, tgt_ref, h_ref, thr_ref, tb, g_ref, work)
+    outs = (own_ref, spill_ref, fld1, slope1)
+    upper_part(kern, last, f_ref, tgt_ref, h_ref, thr_ref, tb, outs, work)
 
 
 def later_kernel(
     kern, last, thr_ref, mine_ref, peer_ref, a_ref, a2_ref, b_ref, b2_ref, f_in_ref, tgt_ref,
-    h_ref, tb, g_ref, f_ref, *work,
+    h_ref, tb, own_ref, spill_ref, fld1, slope1, f_ref, *work,
 ):
     s_hi, s_lo = split(mine_ref[...] + peer_ref[...])
     from_a = a_ref[...] + a2_ref[...]
@@ -461,19 +502,31 @@
     v, _, _ = sides(last, from_a, from_b, tb)
     v = v + dot3(tb("cx_own_hi"), tb("cx_own_lo"), s_hi, s_lo, dot_nt)
     to_spectrum(v, tb, f_ref, f_in_ref)
-    gradient_body(kern, last, f_ref, tgt_ref, h_ref, thr_ref, tb, g_ref, work)
-
-
-def match_kernel(n_got, table_ref, own_ref, *refs):
-    got_refs, (out_ref, *edge_refs) = refs[:n_got], refs[n_got:]
+    outs = (own_ref, spill_ref, fld1, slope1)
+    upper_part(kern, last, f_ref, tgt_ref, h_ref, thr_ref, tb, outs, work)
+
+
+def match_kernel(n_got, n_split, table_ref, own_ref, *refs):
+    got_refs, refs = refs[:n_got], refs[n_got:]
+    split_refs, (out_ref, *edge_refs) = refs[: 2 * n_split], refs[2 * n_split :]
+
+    def received(b, t):
+        if b < n_got:
+            return got_refs[b][CORE * t : CORE * t + CORE]
+        early, late = split_refs[2 * (b - n_got) : 2 * (b - n_got) + 2]
+        if t == 1:
+            return late[SPILL:]
+        tail = early[CORE - SPILL :] + late[:SPILL]
+        return jnp.concatenate([early[: CORE - SPILL], tail], axis=0)
+
     device = lax.axis_index("tile")
     other = []
     for t in range(2):
         rows = slice(CORE * t, CORE * t + CORE)
         bit = lax.bitwise_xor(table_ref[t], 2 * device + t)
         value = jnp.where(bit == 1, own_ref[CORE * (1 - t) : CORE * (2 - t)], own_ref[rows])
-        for b, got in enumerate(got_refs):
-            value = jnp.where(bit == 2 << b, got[rows], value)
+        for b in range(n_got + n_split):
+            value = jnp.where(bit == 2 << b, received(b, t), value)
         other.append(value)
     row = lax.broadcasted_iota(jnp.int32, (CORE, CORE), 0)
     lane = lax.broadcasted_iota(jnp.int32, (CORE, CORE), 1)
@@ -532,13 +585,26 @@
                 return x, peer
             x = x + peer
 
-    def from_partners(grad):
-        bits = [1 << b for b in range(n_tile.bit_length() - 1)]
-        got = [
-            lax.ppermute(grad, "tile", [(i, i ^ bit) for i in range(n_tile)])
-            for bit in reversed(bits)
-        ]
-        return got[::-1]
+    bits = [1 << b for b in range(n_tile.bit_length() - 1)]
+    n_split = min(2, len(bits))
+
+    def swap(x, bit):
+        return lax.ppermute(x, "tile", [(i, i ^ bit) for i in range(n_tile)])
+
+    def rest_of(own, spill, fields, slope):
+        far_bits = bits[len(bits) - n_split :]
+        early = [swap(own, bit) for bit in far_bits[::-1]][::-1]
+        grad, late = call(
+            functools.partial(lower_kernel, kern),
+            "grad",
+            [own, spill, fields, slope, spectra],
+            [strip, late_rows],
+            back_scratch,
+            flops=3 * 10**9,
+        )
+        late = [swap(late, bit) for bit in far_bits[::-1]][::-1]
+        near = [swap(grad, bit) for bit in bits[: len(bits) - n_split][::-1]][::-1]
+        return grad, near, [x for pair in zip(early, late) for x in pair]
 
     mask_rows = mask_tiles.reshape(tiles_dev * core, core)
     target_rows = target_tiles.reshape(tiles_dev * core, core)
@@ -547,16 +613,26 @@
     freq = jax.ShapeDtypeStruct((2, 4, XB, YB), f32)
     goal = jax.ShapeDtypeStruct((ROWS, 2 * CORE), f32)
     tiles = jax.ShapeDtypeStruct((tiles_dev, core, core), f32)
-    group = 2 if kern % 2 == 0 else 1
+    late_rows = jax.ShapeDtypeStruct((core + SPILL, core), f32)
+    group = group_of(kern)
+    fields = (kern, ROWS, 2 * CORE)
+    upper_outs = [
+        jax.ShapeDtypeStruct(shape, f32)
+        for shape in ((core, core), (SPILL, core), fields, (ROWS, CORE))
+    ]
+    back_scratch = [
+        pltpu.VMEM((4, XB, YB), f32),
+        pltpu.VMEM((2 * group, 3 * ROWS, 2 * CORE), bf16),
+        pltpu.VMEM((2, group * 4 * XB, 3 * CORE), bf16),
+    ]
     scratch = [
-        pltpu.VMEM((2, kern, ROWS, 2 * CORE), f32),
-        pltpu.VMEM((2, ROWS, CORE), f32),
-        pltpu.VMEM((2, 4, XB, YB), f32),
+        pltpu.VMEM(fields, f32),
+        pltpu.VMEM((ROWS, CORE), f32),
+        back_scratch[0],
         pltpu.VMEM((2, group * 4 * XB, 2 * YB), bf16),
         pltpu.VMEM((2, group * 4 * XB, 2 * YB), bf16),
         pltpu.VMEM((2 * group, 6 * XB, 2 * CORE), bf16),
-        pltpu.VMEM((2 * group, 3 * ROWS, 2 * CORE), bf16),
-        pltpu.VMEM((2, group * 4 * XB, 3 * CORE), bf16),
+        *back_scratch[1:],
     ]
 
     edge = jax.ShapeDtypeStruct((EDGE, tiles_dev * core), f32)
@@ -579,22 +655,22 @@
         flops=3 * 10**9,
         nbytes=4 * 10**6,
     )
-    grad, freq_now, goals = call(
+    *upper, freq_now, goals = call(
         functools.partial(first_kernel, kern, n_tile - 1),
         "grad",
         [thresholds, mask_rows, target_rows, from_a, from_b, spectra],
-        [strip, freq, goal],
+        [*upper_outs, freq, goal],
         scratch,
         smem=(0,),
         flops=10**10,
     )
     moves = []
     for step in range(1, STEPS + 1):
-        got = from_partners(grad)
+        grad, got, got_split = rest_of(*upper)
         outs = call(
-            functools.partial(match_kernel, len(got)),
+            functools.partial(match_kernel, len(got), n_split),
             None,
-            [table, grad, *got],
+            [table, grad, *got, *got_split],
             [strip, side, side] if step < STEPS else [strip],
             smem=(0,),
         )
@@ -610,16 +686,16 @@
             rims = depth_pair(from_a) + depth_pair(from_b)
         moves += depth_pair(outs[0])
         kept = step + 1 < STEPS
-        grad, *rest = call(
+        outs = call(
             functools.partial(later_kernel, kern, n_tile - 1),
             "grad",
             [thresholds, *moves[-2:], *rims, freq_now, goals, spectra],
-            [strip, freq] if kept else [strip],
+            [*upper_outs, freq] if kept else upper_outs,
             scratch if kept else [pltpu.VMEM(freq.shape, f32)] + scratch,
             smem=(0,),
             flops=10**10,
         )
-        freq_now = rest[0] if kept else None
+        upper, freq_now = outs[:4], outs[-1]
     final = functools.partial(final_kernel, STEPS)
     return tuple(call(final, None, [mask_tiles, *moves], [tiles, tiles]))
 

time: 60 us -> 64.4 us (1.073)
  starting transfers between devices: 23.1 us -> 26.5 us
    ppermute x8 -> x12, starting transfers between devices: 16.8 us -> 20.2 us  [swap(): return lax.ppermute(x, 'tile', [(i, i ^ bit) for i in range(n_tile)])]
    pallas_call x7 -> x9, Pallas kernels: 18.1 us -> 18.6 us  [call(): pl.pallas_call(wrapped, out_shape=out_shape, in_specs=[sm if i in smem el...]
    ppermute x8 -> x12, waiting for transfers between devices: 9.79 us -> 10.2 us  [swap(): return lax.ppermute(x, 'tile', [(i, i ^ bit) for i in range(n_tile)])]
  transfers between devices with their start and end apart: 16 -> 20, of which waited for: 6 -> 6; matrix products, arithmetic and copies ran while one was open for 0% -> 0% of each run, Pallas kernels for 3% -> 9%
where the time goes in v13:
time: 64.4 us; the launch traced here: 64.2 us
  starting transfers between devices  26.5 us (41%)
  Pallas kernels  18.6 us (29%)
  waiting for transfers between devices  16.4 us (25%)
  between operations  1.51 us (2%)
  other arithmetic  1.06 us (2%)
    ppermute x12, starting transfers between devices, swap(): return lax.ppermute(x, 'tile', [(i, i ^ bit) for i in range(n_tile)])  20.2 us
    pallas_call x9, Pallas kernels, call(): pl.pallas_call(wrapped, out_shape=out_shape, in_specs=[sm if i in smem el...  18.6 us
    ppermute x12, waiting for transfers between devices, swap(): return lax.ppermute(x, 'tile', [(i, i ^ bit) for i in range(n_tile)])  10.2 us
    ppermute x2, waiting for transfers between devices, depth_pair(): peer = lax.ppermute(x, 'depth', [(i, i ^ bit) for i in range(n_depth)])  4.46 us
    ppermute x4, starting transfers between devices, move(): return lax.ppermute(x, 'tile', pairs)  2.62 us
    ppermute x2, starting transfers between devices, depth_pair(): peer = lax.ppermute(x, 'depth', [(i, i ^ bit) for i in range(n_depth)])  2.13 us
    ppermute x2, waiting for transfers between devices, move(): return lax.ppermute(x, ('tile', 'depth'), both)  1.78 us
    ppermute x2, starting transfers between devices, move(): return lax.ppermute(x, ('tile', 'depth'), both)  1.52 us
  transfers between devices with their start and end apart: 20, of which 6 were waited for; matrix products, arithmetic and copies ran while one was open for 0% of the time, Pallas kernels for 9%

profile of v13, /device:TPU:0, one launch (start us, length us, event | category | flops | bytes accessed | tf_op | source)
XLA Modules:
  0.0 64.2 jit_solution(16008365178378609581)
XLA Ops:
  0.6 1.0 %multiply_add_fusion.refs_0_ = f32[256,128]{1,0:T(8,128)S(1)} fusion(s32[2,128,128]{2,1,0:T(8,128)} %param.13, f32[2,128,128]{2,1,0:T(8,128)} %refs_0_.5), kind=kLoop, calls=%fused_computation | loop fusion | flops 98304 | bytes 393216 | tf_op jit(solution)/shard_map/add | solution.py:642
  1.6 0.0 copy-start.2
  1.6 0.0 copy-start.3
  1.6 0.0 copy-start.5
  1.7 0.3 shard_map.131
  1.9 0.5 collective-permute-start
  2.4 0.7 %collective-permute-start.1 = (f32[48,256]{1,0:T(8,128)S(1)}, f32[48,256]{1,0:T(8,128)S(1)}, u32[]{:S(2)}, u32[]{:S(2)}) collective-permute-start(f32[48,256]{1,0:T(8,128)S(1)} %get-tuple-element.22), channel_id=1, source_target_pairs={{2,4},{4,2},{6,8},{8,6},{10,12},{12,10},{14,16},{16,14},{18,20},{2... | collective-permute-start | bytes 147464 | tf_op jit(solution)/shard_map/ppermute | solution.py:573
  3.1 0.0 copy-start
  3.1 0.0 copy-start.1
  3.1 0.0 copy-start.4
  3.2 2.0 %shard_map.132.refs_5_.refs_4_.refs_9_ = f32[12,4,96,128]{3,2,1,0:T(8,128)S(1)} custom-call(f32[1,6]{1,0:T(1,128)S(1)} %copy-done.3, f32[2,6,25,1,25]{4,3,2,1,0:T(1,128)S(1)} %bitcast.7, bf16[1408,256]{1,0:T(8,128)(2,1)S(1)} %copy-done.5), custom_call_target="tpu_custom_call" | custom-call | flops 3000000000 | bytes 4000000 | tf_op jit(solution)/shard_map/pallas_call | solution.py:211
  5.8 0.0 collective-permute-done.refs_3_
  5.8 5.3 %shard_map.133 = (f32[128,128]{1,0:T(8,128)S(1)}, f32[16,128]{1,0:T(8,128)S(1)}, f32[6,160,256]{2,1,0:T(8,128)S(1)}, f32[160,128]{1,0:T(8,128)S(1)}, f32[2,4,96,...) custom-call(f32[1]{0:T(128)S(6)} %copy.14.refs_0_, f32[256,128]{1,0:T(8,128)S(1)} %bitcast.5, s32[256,128]{1,0:T(8,128)S(1)} %bitcast.6, ...), custom_call_target="tpu_custom_call" | custom-call | flops 10000000000 | tf_op jit(solution)/shard_map/pallas_call | solution.py:211
  11.1 6.7 %collective-permute-start.6 = (f32[128,128]{1,0:T(8,128)S(1)}, f32[128,128]{1,0:T(8,128)S(1)}, u32[]{:S(2)}, u32[]{:S(2)}) collective-permute-start(f32[128,128]{1,0:T(8,128)S(1)} %get-tuple-element.23.refs_0_), channel_id=1, source_target_pairs={{0,16},{2,18},{4,20},{6,22},{8,24},{10,26},{12,28},{14,30},{16,0},... | collective-permute-start | bytes 196616 | tf_op jit(solution)/shard_map/ppermute | solution.py:592
  17.8 1.8 %shard_map.134 = (f32[256,128]{1,0:T(8,128)S(1)}, f32[144,128]{1,0:T(8,128)S(1)}) custom-call(f32[128,128]{1,0:T(8,128)S(1)} %get-tuple-element.23.refs_0_, f32[16,128]{1,0:T(8,128)S(1)} %get-tuple-element.24.refs_1_, f32[6,160,256]{2,1,0:T(8,128)S(1)} %get-tuple-element.25.refs_2_, f32[160,128]{1,0:T(8,128)S(1)} %get-tuple-element.26.refs_3_, ...), custom_call_target="tpu_custom_call" | custom-call | flops 3000000000 | tf_op jit(solution)/shard_map/pallas_call | solution.py:211
  19.6 0.6 collective-permute-start.3
  20.2 0.8 %collective-permute-start.2 = (f32[256,128]{1,0:T(8,128)S(1)}, f32[256,128]{1,0:T(8,128)S(1)}, u32[]{:S(2)}, u32[]{:S(2)}) collective-permute-start(f32[256,128]{1,0:T(8,128)S(1)} %get-tuple-element.27.refs_1_), channel_id=1, source_target_pairs={{0,2},{2,0},{4,6},{6,4},{8,10},{10,8},{12,14},{14,12},{16,18},{18,... | collective-permute-start | bytes 393224 | tf_op jit(solution)/shard_map/ppermute | solution.py:592
  21.0 0.8 %collective-permute-start.4 = (f32[128,128]{1,0:T(8,128)S(1)}, f32[128,128]{1,0:T(8,128)S(1)}, u32[]{:S(2)}, u32[]{:S(2)}) collective-permute-start(f32[128,128]{1,0:T(8,128)S(1)} %get-tuple-element.23.refs_0_), channel_id=1, source_target_pairs={{0,8},{2,10},{4,12},{6,14},{8,0},{10,2},{12,4},{14,6},{16,24},{18,... | collective-permute-start | bytes 196616 | tf_op jit(solution)/shard_map/ppermute | solution.py:592
  21.8 1.2 %collective-permute-start.7 = (f32[144,128]{1,0:T(8,128)S(1)}, f32[144,128]{1,0:T(8,128)S(1)}, u32[]{:S(2)}, u32[]{:S(2)}) collective-permute-start(f32[144,128]{1,0:T(8,128)S(1)} %get-tuple-element.28), channel_id=1, source_target_pairs={{0,16},{2,18},{4,20},{6,22},{8,24},{10,26},{12,28},{14,30},{16,0},... | collective-permute-start | bytes 221192 | tf_op jit(solution)/shard_map/ppermute | solution.py:592
  22.9 0.4 collective-permute-start.5
  23.4 0.1 pad_add_fusion.refs_0_
  23.4 2.5 %collective-permute-done.4.refs_4_ = f32[128,128]{1,0:T(8,128)S(1)} collective-permute-done((f32[128,128]{1,0:T(8,128)S(1)}, f32[128,128]{1,0:T(8,128)S(1)}, u32[]{:S(2)}, u32[]{:S(2)}) %collective-permute-start.4) | collective-permute-done | bytes 65568 | tf_op jit(solution)/shard_map/ppermute | solution.py:592
  26.0 2.7 %collective-permute-done.7.refs_7_ = f32[144,128]{1,0:T(8,128)S(1)} collective-permute-done((f32[144,128]{1,0:T(8,128)S(1)}, f32[144,128]{1,0:T(8,128)S(1)}, u32[]{:S(2)}, u32[]{:S(2)}) %collective-permute-start.7) | collective-permute-done | bytes 73760 | tf_op jit(solution)/shard_map/ppermute | solution.py:592
  28.6 0.0 collective-permute-done.5.refs_5_
  28.7 0.9 %shard_map.135 = (f32[256,128]{1,0:T(8,128)S(1)}, f32[32,256]{1,0:T(8,128)S(1)}, f32[32,256]{1,0:T(8,128)S(1)}) custom-call(s32[4]{0:T(128)S(1)} %pad_add_fusion.refs_0_, f32[256,128]{1,0:T(8,128)S(1)} %get-tuple-element.27.refs_1_, f32[256,128]{1,0:T(8,128)S(1)} %collective-permute-done.2.refs_2_, f32[256,128]{1,0:T(8,128)S(1)} %collective-permute-done.3.refs_3_, ...), custom_call_target="tpu_custom_call" | custom-call | tf_op jit(solution)/shard_map/pallas_call | solution.py:211
  29.5 1.6 %collective-permute-start.8 = (f32[256,128]{1,0:T(8,128)S(1)}, f32[256,128]{1,0:T(8,128)S(1)}, u32[]{:S(2)}, u32[]{:S(2)}) collective-permute-start(f32[256,128]{1,0:T(8,128)S(1)} %get-tuple-element.29.refs_1_), channel_id=1, source_target_pairs={{0,1},{1,0},{2,3},{3,2},{4,5},{5,4},{6,7},{7,6},{8,9},{9,8},{10,11... | collective-permute-start | bytes 393224 | tf_op jit(solution)/shard_map/ppermute | solution.py:582
  31.1 0.0 collective-permute-start.10
  31.1 0.6 collective-permute-start.9
  31.7 1.5 %collective-permute-start.12 = (f32[32,256]{1,0:T(8,128)S(1)}, f32[32,256]{1,0:T(8,128)S(1)}, u32[]{:S(2)}, u32[]{:S(2)}) collective-permute-start(f32[32,256]{1,0:T(8,128)S(1)} %get-tuple-element.31), channel_id=1, source_target_pairs={{2,5},{3,4},{4,3},{5,2},{6,9},{7,8},{8,7},{9,6},{10,13},{11,12},{1... | collective-permute-start | bytes 98312 | tf_op jit(solution)/shard_map/ppermute | solution.py:575
  33.2 0.8 %collective-permute-start.11 = (f32[32,256]{1,0:T(8,128)S(1)}, f32[32,256]{1,0:T(8,128)S(1)}, u32[]{:S(2)}, u32[]{:S(2)}) collective-permute-start(f32[32,256]{1,0:T(8,128)S(1)} %get-tuple-element.31), channel_id=1, source_target_pairs={{2,4},{4,2},{6,8},{8,6},{10,12},{12,10},{14,16},{16,14},{18,20},{2... | collective-permute-start | bytes 98312 | tf_op jit(solution)/shard_map/ppermute | solution.py:573
  34.1 0.7 %collective-permute-done.10.refs_4_ = f32[32,256]{1,0:T(8,128)S(1)} collective-permute-done((f32[32,256]{1,0:T(8,128)S(1)}, f32[32,256]{1,0:T(8,128)S(1)}, u32[]{:S(2)}, u32[]{:S(2)}) %collective-permute-start.10) | collective-permute-done | bytes 32800 | tf_op jit(solution)/shard_map/ppermute | solution.py:575
  34.8 0.0 collective-permute-done.9.refs_3_
  34.8 1.1 %collective-permute-done.12.refs_6_ = f32[32,256]{1,0:T(8,128)S(1)} collective-permute-done((f32[32,256]{1,0:T(8,128)S(1)}, f32[32,256]{1,0:T(8,128)S(1)}, u32[]{:S(2)}, u32[]{:S(2)}) %collective-permute-start.12) | collective-permute-done | bytes 32800 | tf_op jit(solution)/shard_map/ppermute | solution.py:575
  35.9 5.2 %shard_map.136 = (f32[128,128]{1,0:T(8,128)S(1)}, f32[16,128]{1,0:T(8,128)S(1)}, f32[6,160,256]{2,1,0:T(8,128)S(1)}, f32[160,128]{1,0:T(8,128)S(1)}) custom-call(f32[1]{0:T(128)S(6)} %copy.14.refs_0_, f32[256,128]{1,0:T(8,128)S(1)} %get-tuple-element.29.refs_1_, f32[256,128]{1,0:T(8,128)S(1)} %collective-permute-done.8.refs_2_, ...), custom_call_target="tpu_custom_call" | custom-call | flops 10000000000 | tf_op jit(solution)/shard_map/pallas_call | solution.py:211
  41.1 5.8 %collective-permute-start.17 = (f32[128,128]{1,0:T(8,128)S(1)}, f32[128,128]{1,0:T(8,128)S(1)}, u32[]{:S(2)}, u32[]{:S(2)}) collective-permute-start(f32[128,128]{1,0:T(8,128)S(1)} %get-tuple-element.34.refs_0_), channel_id=1, source_target_pairs={{0,16},{2,18},{4,20},{6,22},{8,24},{10,26},{12,28},{14,30},{16,0},... | collective-permute-start | bytes 196616 | tf_op jit(solution)/shard_map/ppermute | solution.py:592
  46.9 1.8 %shard_map.137 = (f32[256,128]{1,0:T(8,128)S(1)}, f32[144,128]{1,0:T(8,128)S(1)}) custom-call(f32[128,128]{1,0:T(8,128)S(1)} %get-tuple-element.34.refs_0_, f32[16,128]{1,0:T(8,128)S(1)} %get-tuple-element.35.refs_1_, f32[6,160,256]{2,1,0:T(8,128)S(1)} %get-tuple-element.36.refs_2_, f32[160,128]{1,0:T(8,128)S(1)} %get-tuple-element.37.refs_3_, ...), custom_call_target="tpu_custom_call" | custom-call | flops 3000000000 | tf_op jit(solution)/shard_map/pallas_call | solution.py:211
  48.7 0.1 collective-permute-start.14
  48.8 0.1 collective-permute-start.13
  48.8 1.8 %collective-permute-start.18 = (f32[144,128]{1,0:T(8,128)S(1)}, f32[144,128]{1,0:T(8,128)S(1)}, u32[]{:S(2)}, u32[]{:S(2)}) collective-permute-start(f32[144,128]{1,0:T(8,128)S(1)} %get-tuple-element.39), channel_id=1, source_target_pairs={{0,16},{2,18},{4,20},{6,22},{8,24},{10,26},{12,28},{14,30},{16,0},... | collective-permute-start | bytes 221192 | tf_op jit(solution)/shard_map/ppermute | solution.py:592
  50.7 0.8 %collective-permute-start.16 = (f32[144,128]{1,0:T(8,128)S(1)}, f32[144,128]{1,0:T(8,128)S(1)}, u32[]{:S(2)}, u32[]{:S(2)}) collective-permute-start(f32[144,128]{1,0:T(8,128)S(1)} %get-tuple-element.39), channel_id=1, source_target_pairs={{0,8},{2,10},{4,12},{6,14},{8,0},{10,2},{12,4},{14,6},{16,24},{18,... | collective-permute-start | bytes 221192 | tf_op jit(solution)/shard_map/ppermute | solution.py:592
  51.5 0.0 collective-permute-done.17.refs_6_
  51.5 1.2 %collective-permute-start.15 = (f32[128,128]{1,0:T(8,128)S(1)}, f32[128,128]{1,0:T(8,128)S(1)}, u32[]{:S(2)}, u32[]{:S(2)}) collective-permute-start(f32[128,128]{1,0:T(8,128)S(1)} %get-tuple-element.34.refs_0_), channel_id=1, source_target_pairs={{0,8},{2,10},{4,12},{6,14},{8,0},{10,2},{12,4},{14,6},{16,24},{18,... | collective-permute-start | bytes 196616 | tf_op jit(solution)/shard_map/ppermute | solution.py:592
  52.7 5.0 %collective-permute-done.15.refs_4_ = f32[128,128]{1,0:T(8,128)S(1)} collective-permute-done((f32[128,128]{1,0:T(8,128)S(1)}, f32[128,128]{1,0:T(8,128)S(1)}, u32[]{:S(2)}, u32[]{:S(2)}) %collective-permute-start.15) | collective-permute-done | bytes 65568 | tf_op jit(solution)/shard_map/ppermute | solution.py:592
  57.7 0.0 collective-permute-done.18.refs_7_
  57.7 0.7 %shard_map.138.refs_3_ = f32[256,128]{1,0:T(8,128)S(1)} custom-call(s32[4]{0:T(128)S(1)} %pad_add_fusion.refs_0_, f32[256,128]{1,0:T(8,128)S(1)} %get-tuple-element.38.refs_1_, f32[256,128]{1,0:T(8,128)S(1)} %collective-permute-done.13.refs_2_, f32[256,128]{1,0:T(8,128)S(1)} %collective-permute-done.14.refs_3_, ...), custom_call_target="tpu_custom_call" | custom-call | tf_op jit(solution)/shard_map/pallas_call | solution.py:211
  58.4 0.6 collective-permute-start.19
  59.0 4.5 %collective-permute-done.19.refs_4_ = f32[256,128]{1,0:T(8,128)S(1)} collective-permute-done((f32[256,128]{1,0:T(8,128)S(1)}, f32[256,128]{1,0:T(8,128)S(1)}, u32[]{:S(2)}, u32[]{:S(2)}) %collective-permute-start.19) | collective-permute-done | bytes 131104 | tf_op jit(solution)/shard_map/ppermute | solution.py:582
  63.5 0.7 %shard_map.139 = (f32[2,128,128]{2,1,0:T(8,128)}, f32[2,128,128]{2,1,0:T(8,128)}) custom-call(f32[2,128,128]{2,1,0:T(8,128)S(1)} %copy-done, f32[256,128]{1,0:T(8,128)S(1)} %get-tuple-element.29.refs_1_, f32[256,128]{1,0:T(8,128)S(1)} %collective-permute-done.8.refs_2_, f32[256,128]{1,0:T(8,128)S(1)} %shard_map.138.refs_3_, ...), custom_call_target="tpu_custom_call" | custom-call | tf_op jit(solution)/shard_map/pallas_call | solution.py:211
  (19 shorter events, 0.0 us)
Async XLA Ops:
  1.6 1.5 %copy-start.2 = (f32[2,1,6,25,25]{4,1,3,2,0:T(1,128)S(1)}, f32[2,1,6,25,25]{4,1,3,2,0:T(1,128)}, u32[]{:S(2)}) copy-start(f32[2,1,6,25,25]{4,1,3,2,0:T(1,128)} %param.14) | copy-start | bytes 90004
  1.6 1.5 %copy-start.3 = (f32[1,6]{1,0:T(1,128)S(1)}, f32[1,6]{1,0:T(1,128)}, u32[]{:S(2)}) copy-start(f32[1,6]{1,0:T(1,128)} %refs_0_.4) | copy-start | bytes 76
  1.6 1.5 %copy-start.5 = (bf16[1408,256]{1,0:T(8,128)(2,1)S(1)}, bf16[1408,256]{1,0:T(8,128)(2,1)}, u32[]{:S(2)}) copy-start(bf16[1408,256]{1,0:T(8,128)(2,1)} %constant.6.clone.refs_2_) | copy-start | bytes 2162692
  1.9 3.9 %collective-permute-start = (f32[48,256]{1,0:T(8,128)S(1)}, f32[48,256]{1,0:T(8,128)S(1)}, u32[]{:S(2)}, u32[]{:S(2)}) collective-permute-start(f32[48,256]{1,0:T(8,128)S(1)} %get-tuple-element.21), channel_id=1, source_target_pairs={{0,2},{2,0},{4,6},{6,4},{8,10},{10,8},{12,14},{14,12},{16,18},{18,... | collective-permute-start | bytes 147464 | tf_op jit(solution)/shard_map/ppermute | solution.py:573
  2.4 3.4 %collective-permute-start.1 = (f32[48,256]{1,0:T(8,128)S(1)}, f32[48,256]{1,0:T(8,128)S(1)}, u32[]{:S(2)}, u32[]{:S(2)}) collective-permute-start(f32[48,256]{1,0:T(8,128)S(1)} %get-tuple-element.22), channel_id=1, source_target_pairs={{2,4},{4,2},{6,8},{8,6},{10,12},{12,10},{14,16},{16,14},{18,20},{2... | collective-permute-start | bytes 147464 | tf_op jit(solution)/shard_map/ppermute | solution.py:573
  3.1 2.7 %copy-start = (f32[2,128,128]{2,1,0:T(8,128)S(1)}, f32[2,128,128]{2,1,0:T(8,128)}, u32[]{:S(2)}) copy-start(f32[2,128,128]{2,1,0:T(8,128)} %refs_0_.5) | copy-start | bytes 393220
  3.1 2.7 %copy-start.1 = (s32[2,128,128]{2,1,0:T(8,128)S(1)}, s32[2,128,128]{2,1,0:T(8,128)}, u32[]{:S(2)}) copy-start(s32[2,128,128]{2,1,0:T(8,128)} %param.13) | copy-start | bytes 393220
  3.1 2.7 %copy-start.4 = (bf16[4000,256]{1,0:T(8,128)(2,1)S(1)}, bf16[4000,256]{1,0:T(8,128)(2,1)}, u32[]{:S(2)}) copy-start(bf16[4000,256]{1,0:T(8,128)(2,1)} %constant.7.clone.refs_6_.refs_5_.refs_10_) | copy-start | bytes 6144004
  11.1 11.8 %collective-permute-start.6 = (f32[128,128]{1,0:T(8,128)S(1)}, f32[128,128]{1,0:T(8,128)S(1)}, u32[]{:S(2)}, u32[]{:S(2)}) collective-permute-start(f32[128,128]{1,0:T(8,128)S(1)} %get-tuple-element.23.refs_0_), channel_id=1, source_target_pairs={{0,16},{2,18},{4,20},{6,22},{8,24},{10,26},{12,28},{14,30},{16,0},... | collective-permute-start | bytes 196616 | tf_op jit(solution)/shard_map/ppermute | solution.py:592
  17.8 5.6 %copy-start.6 = (s32[2]{0:T(128)S(1)}, s32[2]{0:T(128)}, u32[]{:S(2)}) copy-start(s32[2]{0:T(128)} %param.18) | copy-start | bytes 28
  17.8 5.6 %copy-start.7 = (s32[2]{0:T(128)S(1)}, s32[2]{0:T(128)}, u32[]{:S(2)}) copy-start(s32[2]{0:T(128)} %param.17) | copy-start | bytes 28
  19.6 9.0 %collective-permute-start.3 = (f32[256,128]{1,0:T(8,128)S(1)}, f32[256,128]{1,0:T(8,128)S(1)}, u32[]{:S(2)}, u32[]{:S(2)}) collective-permute-start(f32[256,128]{1,0:T(8,128)S(1)} %get-tuple-element.27.refs_1_), channel_id=1, source_target_pairs={{0,4},{2,6},{4,0},{6,2},{8,12},{10,14},{12,8},{14,10},{16,20},{18,... | collective-permute-start | bytes 393224 | tf_op jit(solution)/shard_map/ppermute | solution.py:592
  20.2 8.5 %collective-permute-start.2 = (f32[256,128]{1,0:T(8,128)S(1)}, f32[256,128]{1,0:T(8,128)S(1)}, u32[]{:S(2)}, u32[]{:S(2)}) collective-permute-start(f32[256,128]{1,0:T(8,128)S(1)} %get-tuple-element.27.refs_1_), channel_id=1, source_target_pairs={{0,2},{2,0},{4,6},{6,4},{8,10},{10,8},{12,14},{14,12},{16,18},{18,... | collective-permute-start | bytes 393224 | tf_op jit(solution)/shard_map/ppermute | solution.py:592
  21.0 5.0 %collective-permute-start.4 = (f32[128,128]{1,0:T(8,128)S(1)}, f32[128,128]{1,0:T(8,128)S(1)}, u32[]{:S(2)}, u32[]{:S(2)}) collective-permute-start(f32[128,128]{1,0:T(8,128)S(1)} %get-tuple-element.23.refs_0_), channel_id=1, source_target_pairs={{0,8},{2,10},{4,12},{6,14},{8,0},{10,2},{12,4},{14,6},{16,24},{18,... | collective-permute-start | bytes 196616 | tf_op jit(solution)/shard_map/ppermute | solution.py:592
  21.8 6.9 %collective-permute-start.7 = (f32[144,128]{1,0:T(8,128)S(1)}, f32[144,128]{1,0:T(8,128)S(1)}, u32[]{:S(2)}, u32[]{:S(2)}) collective-permute-start(f32[144,128]{1,0:T(8,128)S(1)} %get-tuple-element.28), channel_id=1, source_target_pairs={{0,16},{2,18},{4,20},{6,22},{8,24},{10,26},{12,28},{14,30},{16,0},... | collective-permute-start | bytes 221192 | tf_op jit(solution)/shard_map/ppermute | solution.py:592
  22.9 5.7 %collective-permute-start.5 = (f32[144,128]{1,0:T(8,128)S(1)}, f32[144,128]{1,0:T(8,128)S(1)}, u32[]{:S(2)}, u32[]{:S(2)}) collective-permute-start(f32[144,128]{1,0:T(8,128)S(1)} %get-tuple-element.28), channel_id=1, source_target_pairs={{0,8},{2,10},{4,12},{6,14},{8,0},{10,2},{12,4},{14,6},{16,24},{18,... | collective-permute-start | bytes 221192 | tf_op jit(solution)/shard_map/ppermute | solution.py:592
  29.5 6.3 %collective-permute-start.8 = (f32[256,128]{1,0:T(8,128)S(1)}, f32[256,128]{1,0:T(8,128)S(1)}, u32[]{:S(2)}, u32[]{:S(2)}) collective-permute-start(f32[256,128]{1,0:T(8,128)S(1)} %get-tuple-element.29.refs_1_), channel_id=1, source_target_pairs={{0,1},{1,0},{2,3},{3,2},{4,5},{5,4},{6,7},{7,6},{8,9},{9,8},{10,11... | collective-permute-start | bytes 393224 | tf_op jit(solution)/shard_map/ppermute | solution.py:582
  31.1 3.7 %collective-permute-start.10 = (f32[32,256]{1,0:T(8,128)S(1)}, f32[32,256]{1,0:T(8,128)S(1)}, u32[]{:S(2)}, u32[]{:S(2)}) collective-permute-start(f32[32,256]{1,0:T(8,128)S(1)} %get-tuple-element.30), channel_id=1, source_target_pairs={{0,3},{1,2},{2,1},{3,0},{4,7},{5,6},{6,5},{7,4},{8,11},{9,10},{10,... | collective-permute-start | bytes 98312 | tf_op jit(solution)/shard_map/ppermute | solution.py:575
  31.1 3.7 %collective-permute-start.9 = (f32[32,256]{1,0:T(8,128)S(1)}, f32[32,256]{1,0:T(8,128)S(1)}, u32[]{:S(2)}, u32[]{:S(2)}) collective-permute-start(f32[32,256]{1,0:T(8,128)S(1)} %get-tuple-element.30), channel_id=1, source_target_pairs={{0,2},{2,0},{4,6},{6,4},{8,10},{10,8},{12,14},{14,12},{16,18},{18,... | collective-permute-start | bytes 98312 | tf_op jit(solution)/shard_map/ppermute | solution.py:573
  31.7 4.1 %collective-permute-start.12 = (f32[32,256]{1,0:T(8,128)S(1)}, f32[32,256]{1,0:T(8,128)S(1)}, u32[]{:S(2)}, u32[]{:S(2)}) collective-permute-start(f32[32,256]{1,0:T(8,128)S(1)} %get-tuple-element.31), channel_id=1, source_target_pairs={{2,5},{3,4},{4,3},{5,2},{6,9},{7,8},{8,7},{9,6},{10,13},{11,12},{1... | collective-permute-start | bytes 98312 | tf_op jit(solution)/shard_map/ppermute | solution.py:575
  33.2 2.6 %collective-permute-start.11 = (f32[32,256]{1,0:T(8,128)S(1)}, f32[32,256]{1,0:T(8,128)S(1)}, u32[]{:S(2)}, u32[]{:S(2)}) collective-permute-start(f32[32,256]{1,0:T(8,128)S(1)} %get-tuple-element.31), channel_id=1, source_target_pairs={{2,4},{4,2},{6,8},{8,6},{10,12},{12,10},{14,16},{16,14},{18,20},{2... | collective-permute-start | bytes 98312 | tf_op jit(solution)/shard_map/ppermute | solution.py:573
  41.1 10.4 %collective-permute-start.17 = (f32[128,128]{1,0:T(8,128)S(1)}, f32[128,128]{1,0:T(8,128)S(1)}, u32[]{:S(2)}, u32[]{:S(2)}) collective-permute-start(f32[128,128]{1,0:T(8,128)S(1)} %get-tuple-element.34.refs_0_), channel_id=1, source_target_pairs={{0,16},{2,18},{4,20},{6,22},{8,24},{10,26},{12,28},{14,30},{16,0},... | collective-permute-start | bytes 196616 | tf_op jit(solution)/shard_map/ppermute | solution.py:592
  48.7 9.0 %collective-permute-start.14 = (f32[256,128]{1,0:T(8,128)S(1)}, f32[256,128]{1,0:T(8,128)S(1)}, u32[]{:S(2)}, u32[]{:S(2)}) collective-permute-start(f32[256,128]{1,0:T(8,128)S(1)} %get-tuple-element.38.refs_1_), channel_id=1, source_target_pairs={{0,4},{2,6},{4,0},{6,2},{8,12},{10,14},{12,8},{14,10},{16,20},{18,... | collective-permute-start | bytes 393224 | tf_op jit(solution)/shard_map/ppermute | solution.py:592
  48.8 8.9 %collective-permute-start.13 = (f32[256,128]{1,0:T(8,128)S(1)}, f32[256,128]{1,0:T(8,128)S(1)}, u32[]{:S(2)}, u32[]{:S(2)}) collective-permute-start(f32[256,128]{1,0:T(8,128)S(1)} %get-tuple-element.38.refs_1_), channel_id=1, source_target_pairs={{0,2},{2,0},{4,6},{6,4},{8,10},{10,8},{12,14},{14,12},{16,18},{18,... | collective-permute-start | bytes 393224 | tf_op jit(solution)/shard_map/ppermute | solution.py:592
  48.8 8.8 %collective-permute-start.18 = (f32[144,128]{1,0:T(8,128)S(1)}, f32[144,128]{1,0:T(8,128)S(1)}, u32[]{:S(2)}, u32[]{:S(2)}) collective-permute-start(f32[144,128]{1,0:T(8,128)S(1)} %get-tuple-element.39), channel_id=1, source_target_pairs={{0,16},{2,18},{4,20},{6,22},{8,24},{10,26},{12,28},{14,30},{16,0},... | collective-permute-start | bytes 221192 | tf_op jit(solution)/shard_map/ppermute | solution.py:592
  50.7 7.0 %collective-permute-start.16 = (f32[144,128]{1,0:T(8,128)S(1)}, f32[144,128]{1,0:T(8,128)S(1)}, u32[]{:S(2)}, u32[]{:S(2)}) collective-permute-start(f32[144,128]{1,0:T(8,128)S(1)} %get-tuple-element.39), channel_id=1, source_target_pairs={{0,8},{2,10},{4,12},{6,14},{8,0},{10,2},{12,4},{14,6},{16,24},{18,... | collective-permute-start | bytes 221192 | tf_op jit(solution)/shard_map/ppermute | solution.py:592
  51.5 6.2 %collective-permute-start.15 = (f32[128,128]{1,0:T(8,128)S(1)}, f32[128,128]{1,0:T(8,128)S(1)}, u32[]{:S(2)}, u32[]{:S(2)}) collective-permute-start(f32[128,128]{1,0:T(8,128)S(1)} %get-tuple-element.34.refs_0_), channel_id=1, source_target_pairs={{0,8},{2,10},{4,12},{6,14},{8,0},{10,2},{12,4},{14,6},{16,24},{18,... | collective-permute-start | bytes 196616 | tf_op jit(solution)/shard_map/ppermute | solution.py:592
  58.4 5.0 %collective-permute-start.19 = (f32[256,128]{1,0:T(8,128)S(1)}, f32[256,128]{1,0:T(8,128)S(1)}, u32[]{:S(2)}, u32[]{:S(2)}) collective-permute-start(f32[256,128]{1,0:T(8,128)S(1)} %shard_map.138.refs_3_), channel_id=1, source_target_pairs={{0,1},{1,0},{2,3},{3,2},{4,5},{5,4},{6,7},{7,6},{8,9},{9,8},{10,11... | collective-permute-start | bytes 393224 | tf_op jit(solution)/shard_map/ppermute | solution.py:582

commit v14 on v12

--- a/solution.py
+++ b/solution.py
@@ -464,8 +464,7 @@
     gradient_body(kern, last, f_ref, tgt_ref, h_ref, thr_ref, tb, g_ref, work)
 
 
-def match_kernel(n_got, table_ref, own_ref, *refs):
-    got_refs, (out_ref, *edge_refs) = refs[:n_got], refs[n_got:]
+def match(table_ref, own_ref, got_refs):
     device = lax.axis_index("tile")
     other = []
     for t in range(2):
@@ -485,22 +484,26 @@
         rows = slice(CORE * t, CORE * t + CORE)
         value = jnp.where(table_ref[2 + t] == 1, turned[rows], other[t])
         tiles.append(0.5 * (own_ref[rows] + value))
-    matched = jnp.concatenate(tiles, axis=0)
+    return tiles
+
+
+def match_kernel(n_got, table_ref, own_ref, *refs):
+    got_refs, (out_ref, *edge_refs) = refs[:n_got], refs[n_got:]
+    matched = jnp.concatenate(match(table_ref, own_ref, got_refs), axis=0)
     out_ref[...] = matched
-    if edge_refs:
-        send_edges(*edges_of(WIDE_PAD, matched), *edge_refs)
-
-
-def final_kernel(n_moves, mask_ref, *refs):
+    send_edges(*edges_of(WIDE_PAD, matched), *edge_refs)
+
+
+def final_kernel(n_got, n_moves, table_ref, own_ref, *refs):
+    got_refs, mask_ref, refs = refs[:n_got], refs[n_got], refs[n_got + 1 :]
     moves, (mask_out, grad_out) = refs[: 2 * n_moves], refs[2 * n_moves :]
-    for t in range(2):
+    for t, step in enumerate(match(table_ref, own_ref, got_refs)):
         rows = slice(CORE * t, CORE * t + CORE)
         now = mask_ref[t]
         for mine, peer in zip(moves[::2], moves[1::2]):
-            step = mine[rows] + peer[rows]
-            now = now - STEP_RATE * step
+            now = now - STEP_RATE * (mine[rows] + peer[rows])
         grad_out[t] = step
-        mask_out[t] = now
+        mask_out[t] = now - STEP_RATE * step
 
 
 def per_device(
@@ -589,26 +592,22 @@
         flops=10**10,
     )
     moves = []
-    for step in range(1, STEPS + 1):
+    for step in range(1, STEPS):
         got = from_partners(grad)
-        outs = call(
+        move, *edges = call(
             functools.partial(match_kernel, len(got)),
             None,
             [table, grad, *got],
-            [strip, side, side] if step < STEPS else [strip],
+            [strip, side, side],
             smem=(0,),
         )
-        if step == STEPS:
-            moves += depth_pair(outs[0])
-            break
+        from_b, from_a = swap_edges(*edges)
         if n_depth == 2:
-            from_b, from_a = swap_edges(*outs[1:])
-            far_b, far_a = swap_edges(*outs[1:], cross=True)
+            far_b, far_a = swap_edges(*edges, cross=True)
             rims = (from_a, far_a, from_b, far_b)
         else:
-            from_b, from_a = swap_edges(*outs[1:])
             rims = depth_pair(from_a) + depth_pair(from_b)
-        moves += depth_pair(outs[0])
+        moves += depth_pair(move)
         kept = step + 1 < STEPS
         grad, *rest = call(
             functools.partial(later_kernel, kern, n_tile - 1),
@@ -620,8 +619,12 @@
             flops=10**10,
         )
         freq_now = rest[0] if kept else None
-    final = functools.partial(final_kernel, STEPS)
-    return tuple(call(final, None, [mask_tiles, *moves], [tiles, tiles]))
+    mine, peer = depth_pair(grad)
+    total = mine + peer
+    got = from_partners(total)
+    final = functools.partial(final_kernel, len(got), len(moves) // 2)
+    args = [table, total, *got, mask_tiles, *moves]
+    return tuple(call(final, None, args, [tiles, tiles], smem=(0,)))
 
 
 def solution(mesh):

time: 60 us -> 58.6 us (0.977)
  waiting for transfers between devices: 16.1 us -> 14 us
  starting transfers between devices: 23.1 us -> 23.8 us
    ppermute x2, waiting for transfers between devices: 4.7 us -> 3.46 us  [depth_pair(): peer = lax.ppermute(x, 'depth', [(i, i ^ bit) for i in range(n_depth)])]
    ppermute x2, starting transfers between devices: 2.11 us -> 3.12 us  [depth_pair(): peer = lax.ppermute(x, 'depth', [(i, i ^ bit) for i in range(n_depth)])]
    ppermute x8, waiting for transfers between devices: 9.79 us -> 8.92 us  [from_partners(): lax.ppermute(grad, 'tile', [(i, i ^ bit) for i in range(n_tile)])]
    pallas_call x7 -> x6, Pallas kernels: 18.1 us -> 18.1 us  [call(): pl.pallas_call(wrapped, out_shape=out_shape, in_specs=[sm if i in smem el...]
where the time goes in v14:
time: 58.6 us; the launch traced here: 58.4 us
  starting transfers between devices  23.8 us (41%)
  Pallas kernels  18.1 us (31%)
  waiting for transfers between devices  14 us (24%)
  between operations  1.48 us (3%)
  other arithmetic  1.08 us (2%)
    pallas_call x6, Pallas kernels, call(): pl.pallas_call(wrapped, out_shape=out_shape, in_specs=[sm if i in smem el...  18.1 us
    ppermute x8, starting transfers between devices, from_partners(): lax.ppermute(grad, 'tile', [(i, i ^ bit) for i in range(n_tile)])  16.5 us
    ppermute x8, waiting for transfers between devices, from_partners(): lax.ppermute(grad, 'tile', [(i, i ^ bit) for i in range(n_tile)])  8.92 us
    ppermute x2, waiting for transfers between devices, depth_pair(): peer = lax.ppermute(x, 'depth', [(i, i ^ bit) for i in range(n_depth)])  3.46 us
    ppermute x2, starting transfers between devices, depth_pair(): peer = lax.ppermute(x, 'depth', [(i, i ^ bit) for i in range(n_depth)])  3.12 us
    ppermute x4, starting transfers between devices, move(): return lax.ppermute(x, 'tile', pairs)  2.63 us
    ppermute x2, waiting for transfers between devices, move(): return lax.ppermute(x, ('tile', 'depth'), both)  1.56 us
    ppermute x2, starting transfers between devices, move(): return lax.ppermute(x, ('tile', 'depth'), both)  1.52 us
  transfers between devices with their start and end apart: 16, of which 6 were waited for; matrix products, arithmetic and copies ran while one was open for 0% of the time, Pallas kernels for 3%

profile of v14, /device:TPU:0, one launch (start us, length us, event | category | flops | bytes accessed | tf_op | source)
XLA Modules:
  0.0 58.4 jit_solution(9475447088907218347)
XLA Ops:
  0.6 1.0 %multiply_add_fusion.refs_0_ = f32[256,128]{1,0:T(8,128)S(1)} fusion(s32[2,128,128]{2,1,0:T(8,128)} %param.11, f32[2,128,128]{2,1,0:T(8,128)} %refs_6_.2), kind=kLoop, calls=%fused_computation | loop fusion | flops 98304 | bytes 393216 | tf_op jit(solution)/shard_map/add | solution.py:569
  1.6 0.0 copy-start.2
  1.6 0.0 copy-start.3
  1.6 0.0 copy-start.5
  1.7 0.3 shard_map.113
  1.9 0.5 collective-permute-start
  2.4 0.7 %collective-permute-start.1 = (f32[48,256]{1,0:T(8,128)S(1)}, f32[48,256]{1,0:T(8,128)S(1)}, u32[]{:S(2)}, u32[]{:S(2)}) collective-permute-start(f32[48,256]{1,0:T(8,128)S(1)} %get-tuple-element.11), channel_id=1, source_target_pairs={{2,4},{4,2},{6,8},{8,6},{10,12},{12,10},{14,16},{16,14},{18,20},{2... | collective-permute-start | bytes 147464 | tf_op jit(solution)/shard_map/ppermute | solution.py:523
  3.1 0.0 copy-start
  3.1 0.0 copy-start.1
  3.1 0.0 copy-start.4
  3.2 2.0 %shard_map.114.refs_5_.refs_9_ = f32[12,4,96,128]{3,2,1,0:T(8,128)S(1)} custom-call(f32[1,6]{1,0:T(1,128)S(1)} %copy-done.3, f32[2,6,25,1,25]{4,3,2,1,0:T(1,128)S(1)} %bitcast.7, bf16[1408,256]{1,0:T(8,128)(2,1)S(1)} %copy-done.5), custom_call_target="tpu_custom_call" | custom-call | flops 3000000000 | bytes 4000000 | tf_op jit(solution)/shard_map/pallas_call | solution.py:210
  5.8 0.0 collective-permute-done.refs_3_
  5.8 0.0 collective-permute-done.1.refs_4_
  5.8 0.0 copy-start.6
  5.8 0.0 copy-start.7
  5.9 6.8 %shard_map.115 = (f32[256,128]{1,0:T(8,128)S(1)}, f32[2,4,96,128]{3,2,1,0:T(8,128)S(1)}, f32[160,256]{1,0:T(8,128)S(1)}) custom-call(f32[1]{0:T(128)S(6)} %copy.12.refs_0_, f32[256,128]{1,0:T(8,128)S(1)} %bitcast.5, s32[256,128]{1,0:T(8,128)S(1)} %bitcast.6, f32[48,256]{1,0:T(8,128)S(1)} %collective-permute-done.refs_3_, ...), custom_call_target="tpu_custom_call" | custom-call | flops 10000000000 | tf_op jit(solution)/shard_map/pallas_call | solution.py:210
  12.7 6.7 %collective-permute-start.5 = (f32[256,128]{1,0:T(8,128)S(1)}, f32[256,128]{1,0:T(8,128)S(1)}, u32[]{:S(2)}, u32[]{:S(2)}) collective-permute-start(f32[256,128]{1,0:T(8,128)S(1)} %get-tuple-element.12.refs_1_), channel_id=1, source_target_pairs={{0,16},{2,18},{4,20},{6,22},{8,24},{10,26},{12,28},{14,30},{16,0},... | collective-permute-start | bytes 393224 | tf_op jit(solution)/shard_map/ppermute | solution.py:541
  19.3 1.6 %collective-permute-start.4 = (f32[256,128]{1,0:T(8,128)S(1)}, f32[256,128]{1,0:T(8,128)S(1)}, u32[]{:S(2)}, u32[]{:S(2)}) collective-permute-start(f32[256,128]{1,0:T(8,128)S(1)} %get-tuple-element.12.refs_1_), channel_id=1, source_target_pairs={{0,8},{2,10},{4,12},{6,14},{8,0},{10,2},{12,4},{14,6},{16,24},{18,... | collective-permute-start | bytes 393224 | tf_op jit(solution)/shard_map/ppermute | solution.py:541
  20.9 0.5 collective-permute-start.3
  21.4 0.0 collective-permute-start.2
  21.4 0.1 pad_add_fusion.refs_0_
  21.5 4.4 %collective-permute-done.5.refs_5_ = f32[256,128]{1,0:T(8,128)S(1)} collective-permute-done((f32[256,128]{1,0:T(8,128)S(1)}, f32[256,128]{1,0:T(8,128)S(1)}, u32[]{:S(2)}, u32[]{:S(2)}) %collective-permute-start.5) | collective-permute-done | bytes 131104 | tf_op jit(solution)/shard_map/ppermute | solution.py:541
  25.9 0.2 collective-permute-done.4.refs_4_
  26.1 0.0 collective-permute-done.3.refs_3_
  26.1 0.0 collective-permute-done.2.refs_2_
  26.1 0.9 %shard_map.116 = (f32[256,128]{1,0:T(8,128)S(1)}, f32[32,256]{1,0:T(8,128)S(1)}, f32[32,256]{1,0:T(8,128)S(1)}) custom-call(s32[4]{0:T(128)S(1)} %pad_add_fusion.refs_0_, f32[256,128]{1,0:T(8,128)S(1)} %get-tuple-element.12.refs_1_, f32[256,128]{1,0:T(8,128)S(1)} %collective-permute-done.2.refs_2_, f32[256,128]{1,0:T(8,128)S(1)} %collective-permute-done.3.refs_3_, ...), custom_call_target="tpu_custom_call" | custom-call | tf_op jit(solution)/shard_map/pallas_call | solution.py:210
  27.0 1.6 %collective-permute-start.6 = (f32[256,128]{1,0:T(8,128)S(1)}, f32[256,128]{1,0:T(8,128)S(1)}, u32[]{:S(2)}, u32[]{:S(2)}) collective-permute-start(f32[256,128]{1,0:T(8,128)S(1)} %get-tuple-element.13.refs_1_.refs_7_), channel_id=1, source_target_pairs={{0,1},{1,0},{2,3},{3,2},{4,5},{5,4},{6,7},{7,6},{8,9},{9,8},{10,11... | collective-permute-start | bytes 393224 | tf_op jit(solution)/shard_map/ppermute | solution.py:532
  28.6 0.0 collective-permute-start.8
  28.6 0.6 %collective-permute-start.7 = (f32[32,256]{1,0:T(8,128)S(1)}, f32[32,256]{1,0:T(8,128)S(1)}, u32[]{:S(2)}, u32[]{:S(2)}) collective-permute-start(f32[32,256]{1,0:T(8,128)S(1)} %get-tuple-element.14), channel_id=1, source_target_pairs={{0,2},{2,0},{4,6},{6,4},{8,10},{10,8},{12,14},{14,12},{16,18},{18,... | collective-permute-start | bytes 98312 | tf_op jit(solution)/shard_map/ppermute | solution.py:523
  29.2 1.5 %collective-permute-start.10 = (f32[32,256]{1,0:T(8,128)S(1)}, f32[32,256]{1,0:T(8,128)S(1)}, u32[]{:S(2)}, u32[]{:S(2)}) collective-permute-start(f32[32,256]{1,0:T(8,128)S(1)} %get-tuple-element.15), channel_id=1, source_target_pairs={{2,5},{3,4},{4,3},{5,2},{6,9},{7,8},{8,7},{9,6},{10,13},{11,12},{1... | collective-permute-start | bytes 98312 | tf_op jit(solution)/shard_map/ppermute | solution.py:525
  30.7 0.8 %collective-permute-start.9 = (f32[32,256]{1,0:T(8,128)S(1)}, f32[32,256]{1,0:T(8,128)S(1)}, u32[]{:S(2)}, u32[]{:S(2)}) collective-permute-start(f32[32,256]{1,0:T(8,128)S(1)} %get-tuple-element.15), channel_id=1, source_target_pairs={{2,4},{4,2},{6,8},{8,6},{10,12},{12,10},{14,16},{16,14},{18,20},{2... | collective-permute-start | bytes 98312 | tf_op jit(solution)/shard_map/ppermute | solution.py:523
  31.5 0.7 %collective-permute-done.8.refs_4_ = f32[32,256]{1,0:T(8,128)S(1)} collective-permute-done((f32[32,256]{1,0:T(8,128)S(1)}, f32[32,256]{1,0:T(8,128)S(1)}, u32[]{:S(2)}, u32[]{:S(2)}) %collective-permute-start.8) | collective-permute-done | bytes 32800 | tf_op jit(solution)/shard_map/ppermute | solution.py:525
  32.2 0.0 collective-permute-done.7.refs_3_
  32.2 0.9 %collective-permute-done.10.refs_6_ = f32[32,256]{1,0:T(8,128)S(1)} collective-permute-done((f32[32,256]{1,0:T(8,128)S(1)}, f32[32,256]{1,0:T(8,128)S(1)}, u32[]{:S(2)}, u32[]{:S(2)}) %collective-permute-start.10) | collective-permute-done | bytes 32800 | tf_op jit(solution)/shard_map/ppermute | solution.py:525
  33.1 0.0 collective-permute-done.9.refs_5_
  33.1 0.0 collective-permute-done.6.refs_2_.refs_8_
  33.1 6.8 %shard_map.117 = f32[256,128]{1,0:T(8,128)S(1)} custom-call(f32[1]{0:T(128)S(6)} %copy.12.refs_0_, f32[256,128]{1,0:T(8,128)S(1)} %get-tuple-element.13.refs_1_.refs_7_, f32[256,128]{1,0:T(8,128)S(1)} %collective-permute-done.6.refs_2_.refs_8_, f32[32,256]{1,0:T(8,128)S(1)} %collective-permute-done.7.refs_3_, f32[32,256]{1,0:T(8,128)S(1)} %collective-permute-done.8.refs_4_, ...), custom_call_target="tpu_custom_call" | custom-call | flops 10000000000 | tf_op jit(solution)/shard_map/pallas_call | solution.py:210
  39.9 1.6 %collective-permute-start.11 = (f32[256,128]{1,0:T(8,128)S(1)}, f32[256,128]{1,0:T(8,128)S(1)}, u32[]{:S(2)}, u32[]{:S(2)}) collective-permute-start(f32[256,128]{1,0:T(8,128)S(1)} %shard_map.117), channel_id=1, source_target_pairs={{0,1},{1,0},{2,3},{3,2},{4,5},{5,4},{6,7},{7,6},{8,9},{9,8},{10,11... | collective-permute-start | bytes 393224 | tf_op jit(solution)/shard_map/ppermute | solution.py:532
  41.4 3.5 %collective-permute-done.11 = f32[256,128]{1,0:T(8,128)S(1)} collective-permute-done((f32[256,128]{1,0:T(8,128)S(1)}, f32[256,128]{1,0:T(8,128)S(1)}, u32[]{:S(2)}, u32[]{:S(2)}) %collective-permute-start.11) | collective-permute-done | bytes 131104 | tf_op jit(solution)/shard_map/ppermute | solution.py:532
  44.9 6.3 %collective-permute-start.15 = (f32[256,128]{1,0:T(8,128)S(1)}, f32[256,128]{1,0:T(8,128)S(1)}, u32[]{:S(2)}, u32[]{:S(2)}) collective-permute-start(f32[256,128]{1,0:T(8,128)S(1)} %add.7.refs_1_), channel_id=1, source_target_pairs={{0,16},{2,18},{4,20},{6,22},{8,24},{10,26},{12,28},{14,30},{16,0},... | collective-permute-start | bytes 393224 | tf_op jit(solution)/shard_map/ppermute | solution.py:541
  51.3 0.7 %collective-permute-start.14 = (f32[256,128]{1,0:T(8,128)S(1)}, f32[256,128]{1,0:T(8,128)S(1)}, u32[]{:S(2)}, u32[]{:S(2)}) collective-permute-start(f32[256,128]{1,0:T(8,128)S(1)} %add.7.refs_1_), channel_id=1, source_target_pairs={{0,8},{2,10},{4,12},{6,14},{8,0},{10,2},{12,4},{14,6},{16,24},{18,... | collective-permute-start | bytes 393224 | tf_op jit(solution)/shard_map/ppermute | solution.py:541
  52.0 0.7 %collective-permute-start.13 = (f32[256,128]{1,0:T(8,128)S(1)}, f32[256,128]{1,0:T(8,128)S(1)}, u32[]{:S(2)}, u32[]{:S(2)}) collective-permute-start(f32[256,128]{1,0:T(8,128)S(1)} %add.7.refs_1_), channel_id=1, source_target_pairs={{0,4},{2,6},{4,0},{6,2},{8,12},{10,14},{12,8},{14,10},{16,20},{18,... | collective-permute-start | bytes 393224 | tf_op jit(solution)/shard_map/ppermute | solution.py:541
  52.7 0.0 collective-permute-start.12
  52.7 4.3 %collective-permute-done.15.refs_5_ = f32[256,128]{1,0:T(8,128)S(1)} collective-permute-done((f32[256,128]{1,0:T(8,128)S(1)}, f32[256,128]{1,0:T(8,128)S(1)}, u32[]{:S(2)}, u32[]{:S(2)}) %collective-permute-start.15) | collective-permute-done | bytes 131104 | tf_op jit(solution)/shard_map/ppermute | solution.py:541
  57.0 0.0 collective-permute-done.14.refs_4_
  57.0 0.0 collective-permute-done.13.refs_3_
  57.0 0.0 collective-permute-done.12.refs_2_
  57.0 1.4 %shard_map.118 = (f32[2,128,128]{2,1,0:T(8,128)}, f32[2,128,128]{2,1,0:T(8,128)}) custom-call(s32[4]{0:T(128)S(1)} %pad_add_fusion.refs_0_, f32[256,128]{1,0:T(8,128)S(1)} %add.7.refs_1_, f32[256,128]{1,0:T(8,128)S(1)} %collective-permute-done.12.refs_2_, f32[256,128]{1,0:T(8,128)S(1)} %collective-permute-done.13.refs_3_, ...), custom_call_target="tpu_custom_call" | custom-call | tf_op jit(solution)/shard_map/pallas_call | solution.py:210
  (9 shorter events, 0.0 us)
Async XLA Ops:
  1.6 1.5 %copy-start.2 = (f32[2,1,6,25,25]{4,1,3,2,0:T(1,128)S(1)}, f32[2,1,6,25,25]{4,1,3,2,0:T(1,128)}, u32[]{:S(2)}) copy-start(f32[2,1,6,25,25]{4,1,3,2,0:T(1,128)} %param.12) | copy-start | bytes 90004
  1.6 1.5 %copy-start.3 = (f32[1,6]{1,0:T(1,128)S(1)}, f32[1,6]{1,0:T(1,128)}, u32[]{:S(2)}) copy-start(f32[1,6]{1,0:T(1,128)} %refs_0_.3) | copy-start | bytes 76
  1.6 1.5 %copy-start.5 = (bf16[1408,256]{1,0:T(8,128)(2,1)S(1)}, bf16[1408,256]{1,0:T(8,128)(2,1)}, u32[]{:S(2)}) copy-start(bf16[1408,256]{1,0:T(8,128)(2,1)} %constant.6.clone.refs_2_) | copy-start | bytes 2162692
  1.9 3.9 %collective-permute-start = (f32[48,256]{1,0:T(8,128)S(1)}, f32[48,256]{1,0:T(8,128)S(1)}, u32[]{:S(2)}, u32[]{:S(2)}) collective-permute-start(f32[48,256]{1,0:T(8,128)S(1)} %get-tuple-element.10), channel_id=1, source_target_pairs={{0,2},{2,0},{4,6},{6,4},{8,10},{10,8},{12,14},{14,12},{16,18},{18,... | collective-permute-start | bytes 147464 | tf_op jit(solution)/shard_map/ppermute | solution.py:523
  2.4 3.4 %collective-permute-start.1 = (f32[48,256]{1,0:T(8,128)S(1)}, f32[48,256]{1,0:T(8,128)S(1)}, u32[]{:S(2)}, u32[]{:S(2)}) collective-permute-start(f32[48,256]{1,0:T(8,128)S(1)} %get-tuple-element.11), channel_id=1, source_target_pairs={{2,4},{4,2},{6,8},{8,6},{10,12},{12,10},{14,16},{16,14},{18,20},{2... | collective-permute-start | bytes 147464 | tf_op jit(solution)/shard_map/ppermute | solution.py:523
  3.1 2.7 %copy-start = (f32[2,128,128]{2,1,0:T(8,128)S(1)}, f32[2,128,128]{2,1,0:T(8,128)}, u32[]{:S(2)}) copy-start(f32[2,128,128]{2,1,0:T(8,128)} %refs_6_.2) | copy-start | bytes 393220
  3.1 2.7 %copy-start.1 = (s32[2,128,128]{2,1,0:T(8,128)S(1)}, s32[2,128,128]{2,1,0:T(8,128)}, u32[]{:S(2)}) copy-start(s32[2,128,128]{2,1,0:T(8,128)} %param.11) | copy-start | bytes 393220
  3.1 2.7 %copy-start.4 = (bf16[4000,256]{1,0:T(8,128)(2,1)S(1)}, bf16[4000,256]{1,0:T(8,128)(2,1)}, u32[]{:S(2)}) copy-start(bf16[4000,256]{1,0:T(8,128)(2,1)} %constant.7.clone.refs_6_.refs_10_) | copy-start | bytes 6144004
  5.8 15.6 %copy-start.6 = (s32[2]{0:T(128)S(1)}, s32[2]{0:T(128)}, u32[]{:S(2)}) copy-start(s32[2]{0:T(128)} %param.16) | copy-start | bytes 28
  5.8 15.6 %copy-start.7 = (s32[2]{0:T(128)S(1)}, s32[2]{0:T(128)}, u32[]{:S(2)}) copy-start(s32[2]{0:T(128)} %param.15) | copy-start | bytes 28
  12.7 13.3 %collective-permute-start.5 = (f32[256,128]{1,0:T(8,128)S(1)}, f32[256,128]{1,0:T(8,128)S(1)}, u32[]{:S(2)}, u32[]{:S(2)}) collective-permute-start(f32[256,128]{1,0:T(8,128)S(1)} %get-tuple-element.12.refs_1_), channel_id=1, source_target_pairs={{0,16},{2,18},{4,20},{6,22},{8,24},{10,26},{12,28},{14,30},{16,0},... | collective-permute-start | bytes 393224 | tf_op jit(solution)/shard_map/ppermute | solution.py:541
  19.3 6.8 %collective-permute-start.4 = (f32[256,128]{1,0:T(8,128)S(1)}, f32[256,128]{1,0:T(8,128)S(1)}, u32[]{:S(2)}, u32[]{:S(2)}) collective-permute-start(f32[256,128]{1,0:T(8,128)S(1)} %get-tuple-element.12.refs_1_), channel_id=1, source_target_pairs={{0,8},{2,10},{4,12},{6,14},{8,0},{10,2},{12,4},{14,6},{16,24},{18,... | collective-permute-start | bytes 393224 | tf_op jit(solution)/shard_map/ppermute | solution.py:541
  20.9 5.2 %collective-permute-start.3 = (f32[256,128]{1,0:T(8,128)S(1)}, f32[256,128]{1,0:T(8,128)S(1)}, u32[]{:S(2)}, u32[]{:S(2)}) collective-permute-start(f32[256,128]{1,0:T(8,128)S(1)} %get-tuple-element.12.refs_1_), channel_id=1, source_target_pairs={{0,4},{2,6},{4,0},{6,2},{8,12},{10,14},{12,8},{14,10},{16,20},{18,... | collective-permute-start | bytes 393224 | tf_op jit(solution)/shard_map/ppermute | solution.py:541
  21.4 4.7 %collective-permute-start.2 = (f32[256,128]{1,0:T(8,128)S(1)}, f32[256,128]{1,0:T(8,128)S(1)}, u32[]{:S(2)}, u32[]{:S(2)}) collective-permute-start(f32[256,128]{1,0:T(8,128)S(1)} %get-tuple-element.12.refs_1_), channel_id=1, source_target_pairs={{0,2},{2,0},{4,6},{6,4},{8,10},{10,8},{12,14},{14,12},{16,18},{18,... | collective-permute-start | bytes 393224 | tf_op jit(solution)/shard_map/ppermute | solution.py:541
  27.0 6.1 %collective-permute-start.6 = (f32[256,128]{1,0:T(8,128)S(1)}, f32[256,128]{1,0:T(8,128)S(1)}, u32[]{:S(2)}, u32[]{:S(2)}) collective-permute-start(f32[256,128]{1,0:T(8,128)S(1)} %get-tuple-element.13.refs_1_.refs_7_), channel_id=1, source_target_pairs={{0,1},{1,0},{2,3},{3,2},{4,5},{5,4},{6,7},{7,6},{8,9},{9,8},{10,11... | collective-permute-start | bytes 393224 | tf_op jit(solution)/shard_map/ppermute | solution.py:532
  28.6 3.7 %collective-permute-start.8 = (f32[32,256]{1,0:T(8,128)S(1)}, f32[32,256]{1,0:T(8,128)S(1)}, u32[]{:S(2)}, u32[]{:S(2)}) collective-permute-start(f32[32,256]{1,0:T(8,128)S(1)} %get-tuple-element.14), channel_id=1, source_target_pairs={{0,3},{1,2},{2,1},{3,0},{4,7},{5,6},{6,5},{7,4},{8,11},{9,10},{10,... | collective-permute-start | bytes 98312 | tf_op jit(solution)/shard_map/ppermute | solution.py:525
  28.6 3.7 %collective-permute-start.7 = (f32[32,256]{1,0:T(8,128)S(1)}, f32[32,256]{1,0:T(8,128)S(1)}, u32[]{:S(2)}, u32[]{:S(2)}) collective-permute-start(f32[32,256]{1,0:T(8,128)S(1)} %get-tuple-element.14), channel_id=1, source_target_pairs={{0,2},{2,0},{4,6},{6,4},{8,10},{10,8},{12,14},{14,12},{16,18},{18,... | collective-permute-start | bytes 98312 | tf_op jit(solution)/shard_map/ppermute | solution.py:523
  29.2 3.9 %collective-permute-start.10 = (f32[32,256]{1,0:T(8,128)S(1)}, f32[32,256]{1,0:T(8,128)S(1)}, u32[]{:S(2)}, u32[]{:S(2)}) collective-permute-start(f32[32,256]{1,0:T(8,128)S(1)} %get-tuple-element.15), channel_id=1, source_target_pairs={{2,5},{3,4},{4,3},{5,2},{6,9},{7,8},{8,7},{9,6},{10,13},{11,12},{1... | collective-permute-start | bytes 98312 | tf_op jit(solution)/shard_map/ppermute | solution.py:525
  30.7 2.4 %collective-permute-start.9 = (f32[32,256]{1,0:T(8,128)S(1)}, f32[32,256]{1,0:T(8,128)S(1)}, u32[]{:S(2)}, u32[]{:S(2)}) collective-permute-start(f32[32,256]{1,0:T(8,128)S(1)} %get-tuple-element.15), channel_id=1, source_target_pairs={{2,4},{4,2},{6,8},{8,6},{10,12},{12,10},{14,16},{16,14},{18,20},{2... | collective-permute-start | bytes 98312 | tf_op jit(solution)/shard_map/ppermute | solution.py:523
  39.9 5.0 %collective-permute-start.11 = (f32[256,128]{1,0:T(8,128)S(1)}, f32[256,128]{1,0:T(8,128)S(1)}, u32[]{:S(2)}, u32[]{:S(2)}) collective-permute-start(f32[256,128]{1,0:T(8,128)S(1)} %shard_map.117), channel_id=1, source_target_pairs={{0,1},{1,0},{2,3},{3,2},{4,5},{5,4},{6,7},{7,6},{8,9},{9,8},{10,11... | collective-permute-start | bytes 393224 | tf_op jit(solution)/shard_map/ppermute | solution.py:532
  44.9 12.1 %collective-permute-start.15 = (f32[256,128]{1,0:T(8,128)S(1)}, f32[256,128]{1,0:T(8,128)S(1)}, u32[]{:S(2)}, u32[]{:S(2)}) collective-permute-start(f32[256,128]{1,0:T(8,128)S(1)} %add.7.refs_1_), channel_id=1, source_target_pairs={{0,16},{2,18},{4,20},{6,22},{8,24},{10,26},{12,28},{14,30},{16,0},... | collective-permute-start | bytes 393224 | tf_op jit(solution)/shard_map/ppermute | solution.py:541
  51.3 5.7 %collective-permute-start.14 = (f32[256,128]{1,0:T(8,128)S(1)}, f32[256,128]{1,0:T(8,128)S(1)}, u32[]{:S(2)}, u32[]{:S(2)}) collective-permute-start(f32[256,128]{1,0:T(8,128)S(1)} %add.7.refs_1_), channel_id=1, source_target_pairs={{0,8},{2,10},{4,12},{6,14},{8,0},{10,2},{12,4},{14,6},{16,24},{18,... | collective-permute-start | bytes 393224 | tf_op jit(solution)/shard_map/ppermute | solution.py:541
  52.0 5.0 %collective-permute-start.13 = (f32[256,128]{1,0:T(8,128)S(1)}, f32[256,128]{1,0:T(8,128)S(1)}, u32[]{:S(2)}, u32[]{:S(2)}) collective-permute-start(f32[256,128]{1,0:T(8,128)S(1)} %add.7.refs_1_), channel_id=1, source_target_pairs={{0,4},{2,6},{4,0},{6,2},{8,12},{10,14},{12,8},{14,10},{16,20},{18,... | collective-permute-start | bytes 393224 | tf_op jit(solution)/shard_map/ppermute | solution.py:541
  52.7 4.3 %collective-permute-start.12 = (f32[256,128]{1,0:T(8,128)S(1)}, f32[256,128]{1,0:T(8,128)S(1)}, u32[]{:S(2)}, u32[]{:S(2)}) collective-permute-start(f32[256,128]{1,0:T(8,128)S(1)} %add.7.refs_1_), channel_id=1, source_target_pairs={{0,2},{2,0},{4,6},{6,4},{8,10},{10,8},{12,14},{14,12},{16,18},{18,... | collective-permute-start | bytes 393224 | tf_op jit(solution)/shard_map/ppermute | solution.py:541

commit v15 on v14

--- a/solution.py
+++ b/solution.py
@@ -19,10 +19,9 @@
 NY = 152
 NX = 176
 WIDE = 2 * HALO
-XB = 96
+XB = 88
 YB = 128
 NU = NY // 2 + 1
-NV = NX // 2 + 1
 ROWS = 160
 ROW0 = 8
 CHUNK = 16
@@ -41,12 +40,9 @@
 
 
 def x_rows(cols):
-    out = np.zeros((2 * XB, len(cols)))
-    ang = 2 * np.pi * np.outer(np.arange(NV), cols) / NX
-    out[:NV] = np.cos(ang)
-    out[XB : XB + NV] = np.sin(ang)
-    out[XB] = 0.0
-    out[XB + NV - 1] = 0.0
+    ang = 2 * np.pi * np.outer(np.arange(XB + 1), cols) / NX
+    out = np.concatenate([np.cos(ang[:XB]), np.sin(ang[:XB])])
+    out[XB] = np.cos(ang[XB])
     return out
 
 
@@ -67,10 +63,11 @@
 
 
 def x_back(cols):
-    kappa = np.zeros(2 * XB)
-    kappa[:NV] = half_weights(NV) / 2
-    kappa[XB : XB + NV] = half_weights(NV) / 2
-    return x_rows(cols).T * kappa
+    out = x_rows(cols).T
+    sign = 1 - 2.0 * (np.asarray(cols) % 2)
+    out[:, 0] = (1 + sign) / 2
+    out[:, XB] = (1 - sign) / 2
+    return out
 
 
 def y_back(rows):
@@ -166,16 +163,30 @@
     return mul(a_hi, b_hi) + (mul(a_lo, b_hi) + mul(a_hi, b_lo))
 
 
+def top_row(like):
+    return lax.broadcasted_iota(jnp.int32, like.shape, 0) == 0
+
+
+def signed_parts(cc, cs, sc, ss, special):
+    out = cc - ss, cs + sc, cc + ss, sc - cs
+    if special:
+        row0 = top_row(cc)
+        out = [jnp.where(row0, x, y) for x, y in zip((cc, cs, sc, -ss), out)]
+    return out
+
+
 def signed(spec):
-    cc, cs = spec[:XB, :YB], spec[:XB, YB:]
-    sc, ss = spec[XB:, :YB], spec[XB:, YB:]
-    return cc - ss, -(cs + sc), cc + ss, sc - cs
-
-
-def even_odd(pr, pi, mr, mi):
+    parts = (spec[:XB, :YB], spec[:XB, YB:], spec[XB:, :YB], spec[XB:, YB:])
+    pr, neg, mr, mi = signed_parts(*parts, True)
+    return pr, -neg, mr, mi
+
+
+def even_odd(pr, pi, mr, mi, special=True):
     top = jnp.concatenate([pr + mr, pi + mi], axis=1)
     low = jnp.concatenate([mi - pi, pr - mr], axis=1)
-    return jnp.concatenate([top, low], axis=0)
+    if special:
+        low = jnp.where(top_row(low), jnp.concatenate([pr - mr, pi - mi], axis=1), low)
+    return top, low
 
 
 def table_array(group):
@@ -323,16 +334,27 @@
 
     def products(t, c, slot):
         for part in range(2 * group):
-            for rows in chunks(XB):
+
+            def pieces(start, height):
+                rows = slice(start, start + height)
                 hpr, hpi, hmr, hmi = (h_ref[2 * group * c + part, j, rows] for j in range(4))
                 fpr, fpi, fmr, fmi = (f_ref[t, j, rows] for j in range(4))
                 pr, pi = hpr * fpr - hpi * fpi, hpr * fpi + hpi * fpr
                 mr, mi = hmr * fmr - hmi * fmi, hmr * fmi + hmi * fmr
-                starts = [2 * XB * part + rows.start, 2 * XB * part + XB + rows.start]
-                top = split(jnp.concatenate([pr + mr, pi + mi], axis=1))
-                low = split(jnp.concatenate([mi - pi, pr - mr], axis=1))
-                put(a_hi, slot, starts, (top[0], low[0]))
-                put(a_lo, slot, starts, (top[1], low[1]))
+                return even_odd(pr, pi, mr, mi, start == 0)
+
+            def store(start, value):
+                p_hi, p_lo = split(value)
+                put(a_hi, slot, [2 * XB * part + start], [p_hi])
+                put(a_lo, slot, [2 * XB * part + start], [p_lo])
+
+            carry, last_low = pieces(XB - 8, 8)
+            for start in range(0, XB - 8, CHUNK):
+                top, low = pieces(start, CHUNK)
+                store(start, top)
+                store(XB - 8 + start, jnp.concatenate([carry, low[:8]], axis=0))
+                carry = low[8:]
+            store(2 * XB - CHUNK, jnp.concatenate([carry, last_low], axis=0))
 
     def y_done(z_one, z_two, slot):
         for g in range(group):
@@ -384,14 +406,15 @@
 
     def add_back(t, c, slot):
         specs = dot(w_cat[slot], tb("y3"))
-        for rows in chunks(XB):
+        for start in range(0, XB, 8):
+            rows = slice(start, start + 8)
             acc = [0.0] * 4 if c == 0 else [tot[t, j, rows] for j in range(4)]
             for part in range(2 * group):
-                base = 2 * XB * part + rows.start
-                cos_rows, sin_rows = slice(base, base + CHUNK), slice(base + XB, base + XB + CHUNK)
-                cc, cs = specs[cos_rows, :YB], specs[cos_rows, YB:]
-                sc, ss = specs[sin_rows, :YB], specs[sin_rows, YB:]
-                bpr, neg, bmr, bmi = cc - ss, cs + sc, cc + ss, sc - cs
+                base = 2 * XB * part + start
+                cos, sin = specs[base : base + 8], specs[base + XB : base + XB + 8]
+                bpr, neg, bmr, bmi = signed_parts(
+                    cos[:, :YB], cos[:, YB:], sin[:, :YB], sin[:, YB:], start == 0
+                )
                 hpr, hpi, hmr, hmi = (h_ref[2 * group * c + part, j, rows] for j in range(4))
                 acc[0] = acc[0] + (hpr * bpr - hpi * neg)
                 acc[1] = acc[1] - (hpr * neg + hpi * bpr)
@@ -401,7 +424,8 @@
                 tot[t, j, rows] = acc[j]
 
     def finish(t):
-        r_hi, r_lo = split(even_odd(*(tot[t, j] for j in range(4))))
+        sums = even_odd(*(tot[t, j] for j in range(4)))
+        r_hi, r_lo = split(jnp.concatenate(sums, axis=0))
         u = dot(tb("x4"), jnp.concatenate([r_hi, r_hi, r_lo], axis=0))
         u_hi, u_lo = split(weight * u)
         term = dot3(tb(f"by{t}_hi"), tb(f"by{t}_lo"), u_hi, u_lo, dot_nt)

time: 58.6 us -> 57.7 us (0.985)
  Pallas kernels: 18.1 us -> 17.1 us
    pallas_call x6, Pallas kernels: 18.1 us -> 17.1 us  [call(): pl.pallas_call(wrapped, out_shape=out_shape, in_specs=[sm if i in smem el...]
where the time goes in v15:
time: 57.7 us; the launch traced here: 57.5 us
  starting transfers between devices  23.9 us (41%)
  Pallas kernels  17.1 us (30%)
  waiting for transfers between devices  13.9 us (24%)
  between operations  1.48 us (3%)
  other arithmetic  1.08 us (2%)
    pallas_call x6, Pallas kernels, call(): pl.pallas_call(wrapped, out_shape=out_shape, in_specs=[sm if i in smem el...  17.1 us
    ppermute x8, starting transfers between devices, from_partners(): lax.ppermute(grad, 'tile', [(i, i ^ bit) for i in range(n_tile)])  16.6 us
    ppermute x8, waiting for transfers between devices, from_partners(): lax.ppermute(grad, 'tile', [(i, i ^ bit) for i in range(n_tile)])  8.92 us
    ppermute x2, waiting for transfers between devices, depth_pair(): peer = lax.ppermute(x, 'depth', [(i, i ^ bit) for i in range(n_depth)])  3.45 us
    ppermute x2, starting transfers between devices, depth_pair(): peer = lax.ppermute(x, 'depth', [(i, i ^ bit) for i in range(n_depth)])  3.14 us
    ppermute x4, starting transfers between devices, move(): return lax.ppermute(x, 'tile', pairs)  2.62 us
    ppermute x2, waiting for transfers between devices, move(): return lax.ppermute(x, ('tile', 'depth'), both)  1.55 us
    ppermute x2, starting transfers between devices, move(): return lax.ppermute(x, ('tile', 'depth'), both)  1.52 us
  transfers between devices with their start and end apart: 16, of which 6 were waited for; matrix products, arithmetic and copies ran while one was open for 0% of the time, Pallas kernels for 3%

profile of v15, /device:TPU:0, one launch (start us, length us, event | category | flops | bytes accessed | tf_op | source)
XLA Modules:
  0.0 57.5 jit_solution(8251957585352973818)
XLA Ops:
  0.6 1.0 %multiply_add_fusion.refs_0_ = f32[256,128]{1,0:T(8,128)S(1)} fusion(s32[2,128,128]{2,1,0:T(8,128)} %param.11, f32[2,128,128]{2,1,0:T(8,128)} %refs_6_.2), kind=kLoop, calls=%fused_computation | loop fusion | flops 98304 | bytes 393216 | tf_op jit(solution)/shard_map/add | solution.py:593
  1.6 0.0 copy-start.2
  1.6 0.0 copy-start.3
  1.6 0.0 copy-start.5
  1.7 0.3 shard_map.113
  1.9 0.5 collective-permute-start
  2.4 0.7 %collective-permute-start.1 = (f32[48,256]{1,0:T(8,128)S(1)}, f32[48,256]{1,0:T(8,128)S(1)}, u32[]{:S(2)}, u32[]{:S(2)}) collective-permute-start(f32[48,256]{1,0:T(8,128)S(1)} %get-tuple-element.11), channel_id=1, source_target_pairs={{2,4},{4,2},{6,8},{8,6},{10,12},{12,10},{14,16},{16,14},{18,20},{2... | collective-permute-start | bytes 147464 | tf_op jit(solution)/shard_map/ppermute | solution.py:547
  3.1 0.0 copy-start
  3.1 0.0 copy-start.1
  3.1 0.0 copy-start.4
  3.2 1.9 %shard_map.114.refs_5_.refs_9_ = f32[12,4,88,128]{3,2,1,0:T(8,128)S(1)} custom-call(f32[1,6]{1,0:T(1,128)S(1)} %copy-done.3, f32[2,6,25,1,25]{4,3,2,1,0:T(1,128)S(1)} %bitcast.7, bf16[1376,256]{1,0:T(8,128)(2,1)S(1)} %copy-done.5), custom_call_target="tpu_custom_call" | custom-call | flops 3000000000 | bytes 4000000 | tf_op jit(solution)/shard_map/pallas_call | solution.py:221
  5.7 0.0 collective-permute-done.refs_3_
  5.7 0.0 collective-permute-done.1.refs_4_
  5.8 0.0 copy-start.6
  5.8 0.0 copy-start.7
  5.8 6.5 %shard_map.115 = (f32[256,128]{1,0:T(8,128)S(1)}, f32[2,4,88,128]{3,2,1,0:T(8,128)S(1)}, f32[160,256]{1,0:T(8,128)S(1)}) custom-call(f32[1]{0:T(128)S(6)} %copy.12.refs_0_, f32[256,128]{1,0:T(8,128)S(1)} %bitcast.5, s32[256,128]{1,0:T(8,128)S(1)} %bitcast.6, f32[48,256]{1,0:T(8,128)S(1)} %collective-permute-done.refs_3_, ...), custom_call_target="tpu_custom_call" | custom-call | flops 10000000000 | tf_op jit(solution)/shard_map/pallas_call | solution.py:221
  12.3 6.7 %collective-permute-start.5 = (f32[256,128]{1,0:T(8,128)S(1)}, f32[256,128]{1,0:T(8,128)S(1)}, u32[]{:S(2)}, u32[]{:S(2)}) collective-permute-start(f32[256,128]{1,0:T(8,128)S(1)} %get-tuple-element.12.refs_1_), channel_id=1, source_target_pairs={{0,16},{2,18},{4,20},{6,22},{8,24},{10,26},{12,28},{14,30},{16,0},... | collective-permute-start | bytes 393224 | tf_op jit(solution)/shard_map/ppermute | solution.py:565
  19.0 1.6 %collective-permute-start.4 = (f32[256,128]{1,0:T(8,128)S(1)}, f32[256,128]{1,0:T(8,128)S(1)}, u32[]{:S(2)}, u32[]{:S(2)}) collective-permute-start(f32[256,128]{1,0:T(8,128)S(1)} %get-tuple-element.12.refs_1_), channel_id=1, source_target_pairs={{0,8},{2,10},{4,12},{6,14},{8,0},{10,2},{12,4},{14,6},{16,24},{18,... | collective-permute-start | bytes 393224 | tf_op jit(solution)/shard_map/ppermute | solution.py:565
  20.6 0.5 collective-permute-start.3
  21.1 0.0 collective-permute-start.2
  21.1 0.1 pad_add_fusion.refs_0_
  21.2 4.4 %collective-permute-done.5.refs_5_ = f32[256,128]{1,0:T(8,128)S(1)} collective-permute-done((f32[256,128]{1,0:T(8,128)S(1)}, f32[256,128]{1,0:T(8,128)S(1)}, u32[]{:S(2)}, u32[]{:S(2)}) %collective-permute-start.5) | collective-permute-done | bytes 131104 | tf_op jit(solution)/shard_map/ppermute | solution.py:565
  25.6 0.2 collective-permute-done.4.refs_4_
  25.8 0.0 collective-permute-done.3.refs_3_
  25.8 0.0 collective-permute-done.2.refs_2_
  25.8 0.9 %shard_map.116 = (f32[256,128]{1,0:T(8,128)S(1)}, f32[32,256]{1,0:T(8,128)S(1)}, f32[32,256]{1,0:T(8,128)S(1)}) custom-call(s32[4]{0:T(128)S(1)} %pad_add_fusion.refs_0_, f32[256,128]{1,0:T(8,128)S(1)} %get-tuple-element.12.refs_1_, f32[256,128]{1,0:T(8,128)S(1)} %collective-permute-done.2.refs_2_, f32[256,128]{1,0:T(8,128)S(1)} %collective-permute-done.3.refs_3_, ...), custom_call_target="tpu_custom_call" | custom-call | tf_op jit(solution)/shard_map/pallas_call | solution.py:221
  26.7 1.6 %collective-permute-start.6 = (f32[256,128]{1,0:T(8,128)S(1)}, f32[256,128]{1,0:T(8,128)S(1)}, u32[]{:S(2)}, u32[]{:S(2)}) collective-permute-start(f32[256,128]{1,0:T(8,128)S(1)} %get-tuple-element.13.refs_1_.refs_7_), channel_id=1, source_target_pairs={{0,1},{1,0},{2,3},{3,2},{4,5},{5,4},{6,7},{7,6},{8,9},{9,8},{10,11... | collective-permute-start | bytes 393224 | tf_op jit(solution)/shard_map/ppermute | solution.py:556
  28.2 0.0 collective-permute-start.8
  28.2 0.6 %collective-permute-start.7 = (f32[32,256]{1,0:T(8,128)S(1)}, f32[32,256]{1,0:T(8,128)S(1)}, u32[]{:S(2)}, u32[]{:S(2)}) collective-permute-start(f32[32,256]{1,0:T(8,128)S(1)} %get-tuple-element.14), channel_id=1, source_target_pairs={{0,2},{2,0},{4,6},{6,4},{8,10},{10,8},{12,14},{14,12},{16,18},{18,... | collective-permute-start | bytes 98312 | tf_op jit(solution)/shard_map/ppermute | solution.py:547
  28.9 1.5 %collective-permute-start.10 = (f32[32,256]{1,0:T(8,128)S(1)}, f32[32,256]{1,0:T(8,128)S(1)}, u32[]{:S(2)}, u32[]{:S(2)}) collective-permute-start(f32[32,256]{1,0:T(8,128)S(1)} %get-tuple-element.15), channel_id=1, source_target_pairs={{2,5},{3,4},{4,3},{5,2},{6,9},{7,8},{8,7},{9,6},{10,13},{11,12},{1... | collective-permute-start | bytes 98312 | tf_op jit(solution)/shard_map/ppermute | solution.py:549
  30.4 0.8 %collective-permute-start.9 = (f32[32,256]{1,0:T(8,128)S(1)}, f32[32,256]{1,0:T(8,128)S(1)}, u32[]{:S(2)}, u32[]{:S(2)}) collective-permute-start(f32[32,256]{1,0:T(8,128)S(1)} %get-tuple-element.15), channel_id=1, source_target_pairs={{2,4},{4,2},{6,8},{8,6},{10,12},{12,10},{14,16},{16,14},{18,20},{2... | collective-permute-start | bytes 98312 | tf_op jit(solution)/shard_map/ppermute | solution.py:547
  31.2 0.7 %collective-permute-done.8.refs_4_ = f32[32,256]{1,0:T(8,128)S(1)} collective-permute-done((f32[32,256]{1,0:T(8,128)S(1)}, f32[32,256]{1,0:T(8,128)S(1)}, u32[]{:S(2)}, u32[]{:S(2)}) %collective-permute-start.8) | collective-permute-done | bytes 32800 | tf_op jit(solution)/shard_map/ppermute | solution.py:549
  31.9 0.0 collective-permute-done.7.refs_3_
  31.9 0.9 %collective-permute-done.10.refs_6_ = f32[32,256]{1,0:T(8,128)S(1)} collective-permute-done((f32[32,256]{1,0:T(8,128)S(1)}, f32[32,256]{1,0:T(8,128)S(1)}, u32[]{:S(2)}, u32[]{:S(2)}) %collective-permute-start.10) | collective-permute-done | bytes 32800 | tf_op jit(solution)/shard_map/ppermute | solution.py:549
  32.8 0.0 collective-permute-done.9.refs_5_
  32.8 0.0 collective-permute-done.6.refs_2_.refs_8_
  32.8 6.2 %shard_map.117 = f32[256,128]{1,0:T(8,128)S(1)} custom-call(f32[1]{0:T(128)S(6)} %copy.12.refs_0_, f32[256,128]{1,0:T(8,128)S(1)} %get-tuple-element.13.refs_1_.refs_7_, f32[256,128]{1,0:T(8,128)S(1)} %collective-permute-done.6.refs_2_.refs_8_, f32[32,256]{1,0:T(8,128)S(1)} %collective-permute-done.7.refs_3_, f32[32,256]{1,0:T(8,128)S(1)} %collective-permute-done.8.refs_4_, ...), custom_call_target="tpu_custom_call" | custom-call | flops 10000000000 | tf_op jit(solution)/shard_map/pallas_call | solution.py:221
  39.0 1.6 %collective-permute-start.11 = (f32[256,128]{1,0:T(8,128)S(1)}, f32[256,128]{1,0:T(8,128)S(1)}, u32[]{:S(2)}, u32[]{:S(2)}) collective-permute-start(f32[256,128]{1,0:T(8,128)S(1)} %shard_map.117), channel_id=1, source_target_pairs={{0,1},{1,0},{2,3},{3,2},{4,5},{5,4},{6,7},{7,6},{8,9},{9,8},{10,11... | collective-permute-start | bytes 393224 | tf_op jit(solution)/shard_map/ppermute | solution.py:556
  40.6 3.4 %collective-permute-done.11 = f32[256,128]{1,0:T(8,128)S(1)} collective-permute-done((f32[256,128]{1,0:T(8,128)S(1)}, f32[256,128]{1,0:T(8,128)S(1)}, u32[]{:S(2)}, u32[]{:S(2)}) %collective-permute-start.11) | collective-permute-done | bytes 131104 | tf_op jit(solution)/shard_map/ppermute | solution.py:556
  44.0 6.3 %collective-permute-start.15 = (f32[256,128]{1,0:T(8,128)S(1)}, f32[256,128]{1,0:T(8,128)S(1)}, u32[]{:S(2)}, u32[]{:S(2)}) collective-permute-start(f32[256,128]{1,0:T(8,128)S(1)} %add.7.refs_1_), channel_id=1, source_target_pairs={{0,16},{2,18},{4,20},{6,22},{8,24},{10,26},{12,28},{14,30},{16,0},... | collective-permute-start | bytes 393224 | tf_op jit(solution)/shard_map/ppermute | solution.py:565
  50.4 0.7 %collective-permute-start.14 = (f32[256,128]{1,0:T(8,128)S(1)}, f32[256,128]{1,0:T(8,128)S(1)}, u32[]{:S(2)}, u32[]{:S(2)}) collective-permute-start(f32[256,128]{1,0:T(8,128)S(1)} %add.7.refs_1_), channel_id=1, source_target_pairs={{0,8},{2,10},{4,12},{6,14},{8,0},{10,2},{12,4},{14,6},{16,24},{18,... | collective-permute-start | bytes 393224 | tf_op jit(solution)/shard_map/ppermute | solution.py:565
  51.1 0.7 %collective-permute-start.13 = (f32[256,128]{1,0:T(8,128)S(1)}, f32[256,128]{1,0:T(8,128)S(1)}, u32[]{:S(2)}, u32[]{:S(2)}) collective-permute-start(f32[256,128]{1,0:T(8,128)S(1)} %add.7.refs_1_), channel_id=1, source_target_pairs={{0,4},{2,6},{4,0},{6,2},{8,12},{10,14},{12,8},{14,10},{16,20},{18,... | collective-permute-start | bytes 393224 | tf_op jit(solution)/shard_map/ppermute | solution.py:565
  51.8 0.0 collective-permute-start.12
  51.8 4.3 %collective-permute-done.15.refs_5_ = f32[256,128]{1,0:T(8,128)S(1)} collective-permute-done((f32[256,128]{1,0:T(8,128)S(1)}, f32[256,128]{1,0:T(8,128)S(1)}, u32[]{:S(2)}, u32[]{:S(2)}) %collective-permute-start.15) | collective-permute-done | bytes 131104 | tf_op jit(solution)/shard_map/ppermute | solution.py:565
  56.1 0.0 collective-permute-done.14.refs_4_
  56.1 0.0 collective-permute-done.13.refs_3_
  56.1 0.0 collective-permute-done.12.refs_2_
  56.1 1.4 %shard_map.118 = (f32[2,128,128]{2,1,0:T(8,128)}, f32[2,128,128]{2,1,0:T(8,128)}) custom-call(s32[4]{0:T(128)S(1)} %pad_add_fusion.refs_0_, f32[256,128]{1,0:T(8,128)S(1)} %add.7.refs_1_, f32[256,128]{1,0:T(8,128)S(1)} %collective-permute-done.12.refs_2_, f32[256,128]{1,0:T(8,128)S(1)} %collective-permute-done.13.refs_3_, ...), custom_call_target="tpu_custom_call" | custom-call | tf_op jit(solution)/shard_map/pallas_call | solution.py:221
  (9 shorter events, 0.0 us)
Async XLA Ops:
  1.6 1.5 %copy-start.2 = (f32[2,1,6,25,25]{4,1,3,2,0:T(1,128)S(1)}, f32[2,1,6,25,25]{4,1,3,2,0:T(1,128)}, u32[]{:S(2)}) copy-start(f32[2,1,6,25,25]{4,1,3,2,0:T(1,128)} %param.12) | copy-start | bytes 90004
  1.6 1.5 %copy-start.3 = (f32[1,6]{1,0:T(1,128)S(1)}, f32[1,6]{1,0:T(1,128)}, u32[]{:S(2)}) copy-start(f32[1,6]{1,0:T(1,128)} %refs_0_.3) | copy-start | bytes 76
  1.6 1.5 %copy-start.5 = (bf16[1376,256]{1,0:T(8,128)(2,1)S(1)}, bf16[1376,256]{1,0:T(8,128)(2,1)}, u32[]{:S(2)}) copy-start(bf16[1376,256]{1,0:T(8,128)(2,1)} %constant.6.clone.refs_2_) | copy-start | bytes 2113540
  1.9 3.8 %collective-permute-start = (f32[48,256]{1,0:T(8,128)S(1)}, f32[48,256]{1,0:T(8,128)S(1)}, u32[]{:S(2)}, u32[]{:S(2)}) collective-permute-start(f32[48,256]{1,0:T(8,128)S(1)} %get-tuple-element.10), channel_id=1, source_target_pairs={{0,2},{2,0},{4,6},{6,4},{8,10},{10,8},{12,14},{14,12},{16,18},{18,... | collective-permute-start | bytes 147464 | tf_op jit(solution)/shard_map/ppermute | solution.py:547
  2.4 3.3 %collective-permute-start.1 = (f32[48,256]{1,0:T(8,128)S(1)}, f32[48,256]{1,0:T(8,128)S(1)}, u32[]{:S(2)}, u32[]{:S(2)}) collective-permute-start(f32[48,256]{1,0:T(8,128)S(1)} %get-tuple-element.11), channel_id=1, source_target_pairs={{2,4},{4,2},{6,8},{8,6},{10,12},{12,10},{14,16},{16,14},{18,20},{2... | collective-permute-start | bytes 147464 | tf_op jit(solution)/shard_map/ppermute | solution.py:547
  3.1 2.6 %copy-start = (f32[2,128,128]{2,1,0:T(8,128)S(1)}, f32[2,128,128]{2,1,0:T(8,128)}, u32[]{:S(2)}) copy-start(f32[2,128,128]{2,1,0:T(8,128)} %refs_6_.2) | copy-start | bytes 393220
  3.1 2.6 %copy-start.1 = (s32[2,128,128]{2,1,0:T(8,128)S(1)}, s32[2,128,128]{2,1,0:T(8,128)}, u32[]{:S(2)}) copy-start(s32[2,128,128]{2,1,0:T(8,128)} %param.11) | copy-start | bytes 393220
  3.1 2.6 %copy-start.4 = (bf16[3904,256]{1,0:T(8,128)(2,1)S(1)}, bf16[3904,256]{1,0:T(8,128)(2,1)}, u32[]{:S(2)}) copy-start(bf16[3904,256]{1,0:T(8,128)(2,1)} %constant.7.clone.refs_6_.refs_10_) | copy-start | bytes 5996548
  5.8 15.3 %copy-start.6 = (s32[2]{0:T(128)S(1)}, s32[2]{0:T(128)}, u32[]{:S(2)}) copy-start(s32[2]{0:T(128)} %param.16) | copy-start | bytes 28
  5.8 15.3 %copy-start.7 = (s32[2]{0:T(128)S(1)}, s32[2]{0:T(128)}, u32[]{:S(2)}) copy-start(s32[2]{0:T(128)} %param.15) | copy-start | bytes 28
  12.3 13.3 %collective-permute-start.5 = (f32[256,128]{1,0:T(8,128)S(1)}, f32[256,128]{1,0:T(8,128)S(1)}, u32[]{:S(2)}, u32[]{:S(2)}) collective-permute-start(f32[256,128]{1,0:T(8,128)S(1)} %get-tuple-element.12.refs_1_), channel_id=1, source_target_pairs={{0,16},{2,18},{4,20},{6,22},{8,24},{10,26},{12,28},{14,30},{16,0},... | collective-permute-start | bytes 393224 | tf_op jit(solution)/shard_map/ppermute | solution.py:565
  19.0 6.8 %collective-permute-start.4 = (f32[256,128]{1,0:T(8,128)S(1)}, f32[256,128]{1,0:T(8,128)S(1)}, u32[]{:S(2)}, u32[]{:S(2)}) collective-permute-start(f32[256,128]{1,0:T(8,128)S(1)} %get-tuple-element.12.refs_1_), channel_id=1, source_target_pairs={{0,8},{2,10},{4,12},{6,14},{8,0},{10,2},{12,4},{14,6},{16,24},{18,... | collective-permute-start | bytes 393224 | tf_op jit(solution)/shard_map/ppermute | solution.py:565
  20.6 5.2 %collective-permute-start.3 = (f32[256,128]{1,0:T(8,128)S(1)}, f32[256,128]{1,0:T(8,128)S(1)}, u32[]{:S(2)}, u32[]{:S(2)}) collective-permute-start(f32[256,128]{1,0:T(8,128)S(1)} %get-tuple-element.12.refs_1_), channel_id=1, source_target_pairs={{0,4},{2,6},{4,0},{6,2},{8,12},{10,14},{12,8},{14,10},{16,20},{18,... | collective-permute-start | bytes 393224 | tf_op jit(solution)/shard_map/ppermute | solution.py:565
  21.1 4.7 %collective-permute-start.2 = (f32[256,128]{1,0:T(8,128)S(1)}, f32[256,128]{1,0:T(8,128)S(1)}, u32[]{:S(2)}, u32[]{:S(2)}) collective-permute-start(f32[256,128]{1,0:T(8,128)S(1)} %get-tuple-element.12.refs_1_), channel_id=1, source_target_pairs={{0,2},{2,0},{4,6},{6,4},{8,10},{10,8},{12,14},{14,12},{16,18},{18,... | collective-permute-start | bytes 393224 | tf_op jit(solution)/shard_map/ppermute | solution.py:565
  26.7 6.1 %collective-permute-start.6 = (f32[256,128]{1,0:T(8,128)S(1)}, f32[256,128]{1,0:T(8,128)S(1)}, u32[]{:S(2)}, u32[]{:S(2)}) collective-permute-start(f32[256,128]{1,0:T(8,128)S(1)} %get-tuple-element.13.refs_1_.refs_7_), channel_id=1, source_target_pairs={{0,1},{1,0},{2,3},{3,2},{4,5},{5,4},{6,7},{7,6},{8,9},{9,8},{10,11... | collective-permute-start | bytes 393224 | tf_op jit(solution)/shard_map/ppermute | solution.py:556
  28.2 3.7 %collective-permute-start.8 = (f32[32,256]{1,0:T(8,128)S(1)}, f32[32,256]{1,0:T(8,128)S(1)}, u32[]{:S(2)}, u32[]{:S(2)}) collective-permute-start(f32[32,256]{1,0:T(8,128)S(1)} %get-tuple-element.14), channel_id=1, source_target_pairs={{0,3},{1,2},{2,1},{3,0},{4,7},{5,6},{6,5},{7,4},{8,11},{9,10},{10,... | collective-permute-start | bytes 98312 | tf_op jit(solution)/shard_map/ppermute | solution.py:549
  28.2 3.7 %collective-permute-start.7 = (f32[32,256]{1,0:T(8,128)S(1)}, f32[32,256]{1,0:T(8,128)S(1)}, u32[]{:S(2)}, u32[]{:S(2)}) collective-permute-start(f32[32,256]{1,0:T(8,128)S(1)} %get-tuple-element.14), channel_id=1, source_target_pairs={{0,2},{2,0},{4,6},{6,4},{8,10},{10,8},{12,14},{14,12},{16,18},{18,... | collective-permute-start | bytes 98312 | tf_op jit(solution)/shard_map/ppermute | solution.py:547
  28.9 3.9 %collective-permute-start.10 = (f32[32,256]{1,0:T(8,128)S(1)}, f32[32,256]{1,0:T(8,128)S(1)}, u32[]{:S(2)}, u32[]{:S(2)}) collective-permute-start(f32[32,256]{1,0:T(8,128)S(1)} %get-tuple-element.15), channel_id=1, source_target_pairs={{2,5},{3,4},{4,3},{5,2},{6,9},{7,8},{8,7},{9,6},{10,13},{11,12},{1... | collective-permute-start | bytes 98312 | tf_op jit(solution)/shard_map/ppermute | solution.py:549
  30.4 2.4 %collective-permute-start.9 = (f32[32,256]{1,0:T(8,128)S(1)}, f32[32,256]{1,0:T(8,128)S(1)}, u32[]{:S(2)}, u32[]{:S(2)}) collective-permute-start(f32[32,256]{1,0:T(8,128)S(1)} %get-tuple-element.15), channel_id=1, source_target_pairs={{2,4},{4,2},{6,8},{8,6},{10,12},{12,10},{14,16},{16,14},{18,20},{2... | collective-permute-start | bytes 98312 | tf_op jit(solution)/shard_map/ppermute | solution.py:547
  39.0 5.0 %collective-permute-start.11 = (f32[256,128]{1,0:T(8,128)S(1)}, f32[256,128]{1,0:T(8,128)S(1)}, u32[]{:S(2)}, u32[]{:S(2)}) collective-permute-start(f32[256,128]{1,0:T(8,128)S(1)} %shard_map.117), channel_id=1, source_target_pairs={{0,1},{1,0},{2,3},{3,2},{4,5},{5,4},{6,7},{7,6},{8,9},{9,8},{10,11... | collective-permute-start | bytes 393224 | tf_op jit(solution)/shard_map/ppermute | solution.py:556
  44.0 12.1 %collective-permute-start.15 = (f32[256,128]{1,0:T(8,128)S(1)}, f32[256,128]{1,0:T(8,128)S(1)}, u32[]{:S(2)}, u32[]{:S(2)}) collective-permute-start(f32[256,128]{1,0:T(8,128)S(1)} %add.7.refs_1_), channel_id=1, source_target_pairs={{0,16},{2,18},{4,20},{6,22},{8,24},{10,26},{12,28},{14,30},{16,0},... | collective-permute-start | bytes 393224 | tf_op jit(solution)/shard_map/ppermute | solution.py:565
  50.4 5.7 %collective-permute-start.14 = (f32[256,128]{1,0:T(8,128)S(1)}, f32[256,128]{1,0:T(8,128)S(1)}, u32[]{:S(2)}, u32[]{:S(2)}) collective-permute-start(f32[256,128]{1,0:T(8,128)S(1)} %add.7.refs_1_), channel_id=1, source_target_pairs={{0,8},{2,10},{4,12},{6,14},{8,0},{10,2},{12,4},{14,6},{16,24},{18,... | collective-permute-start | bytes 393224 | tf_op jit(solution)/shard_map/ppermute | solution.py:565
  51.1 5.0 %collective-permute-start.13 = (f32[256,128]{1,0:T(8,128)S(1)}, f32[256,128]{1,0:T(8,128)S(1)}, u32[]{:S(2)}, u32[]{:S(2)}) collective-permute-start(f32[256,128]{1,0:T(8,128)S(1)} %add.7.refs_1_), channel_id=1, source_target_pairs={{0,4},{2,6},{4,0},{6,2},{8,12},{10,14},{12,8},{14,10},{16,20},{18,... | collective-permute-start | bytes 393224 | tf_op jit(solution)/shard_map/ppermute | solution.py:565
  51.8 4.3 %collective-permute-start.12 = (f32[256,128]{1,0:T(8,128)S(1)}, f32[256,128]{1,0:T(8,128)S(1)}, u32[]{:S(2)}, u32[]{:S(2)}) collective-permute-start(f32[256,128]{1,0:T(8,128)S(1)} %add.7.refs_1_), channel_id=1, source_target_pairs={{0,2},{2,0},{4,6},{6,4},{8,10},{10,8},{12,14},{14,12},{16,18},{18,... | collective-permute-start | bytes 393224 | tf_op jit(solution)/shard_map/ppermute | solution.py:565

commit v16 on v15

--- a/solution.py
+++ b/solution.py
@@ -126,7 +126,9 @@
     y2_hi, y2_lo = (a.astype(np.float64) for a in np_split(y_back(core_rows)))
     y3_hi, y3_lo = (a.astype(np.float64) for a in np_split(y_lanes(core_rows)))
     grad = pack_split(parts)
-    grad += [("y2", np.concatenate([y2_hi, y2_lo], axis=1))]
+    upper = np.concatenate([y2_hi, y2_lo], axis=1)
+    lower = np.concatenate([y2_hi, np.zeros_like(y2_lo)], axis=1)
+    grad += [("y2", np.concatenate([upper, lower]))]
     grad += [("y3", np.concatenate([y3_hi, y3_hi, y3_lo]))]
     own = np.zeros((ROWS, CORE))
     own[np.arange(CORE) + WIDE - ROW0, np.arange(CORE)] = 1
@@ -306,7 +308,7 @@
 
 
 def gradient_body(kern, last, f_ref, tgt_ref, h_ref, thr_ref, tb, g_ref, work):
-    fld, inten, tot, a_hi, a_lo, b_cat, r_cat, w_cat = work
+    fld, inten, tot, a_cat, b_cat, r_cat, w_cat = work
     group = 2 if kern % 2 == 0 else 1
     count = kern // group
     chains = [(t, c) for t in range(2) for c in range(count)]
@@ -344,9 +346,8 @@
                 return even_odd(pr, pi, mr, mi, start == 0)
 
             def store(start, value):
-                p_hi, p_lo = split(value)
-                put(a_hi, slot, [2 * XB * part + start], [p_hi])
-                put(a_lo, slot, [2 * XB * part + start], [p_lo])
+                both = jnp.concatenate(split(value), axis=1)
+                put(a_cat, slot, [2 * XB * part + start], [both])
 
             carry, last_low = pieces(XB - 8, 8)
             for start in range(0, XB - 8, CHUNK):
@@ -356,13 +357,13 @@
                 carry = low[8:]
             store(2 * XB - CHUNK, jnp.concatenate([carry, last_low], axis=0))
 
-    def y_done(z_one, z_two, slot):
+    def y_done(z_now, slot):
         for g in range(group):
             for rows in chunks(2 * XB):
                 z = []
                 for part in range(2 * g, 2 * g + 2):
                     here = slice(2 * XB * part + rows.start, 2 * XB * part + rows.stop)
-                    z.append(z_one[here, :CORE] + (z_one[here, CORE:] + z_two[here]))
+                    z.append(z_now[here, :CORE] + z_now[here, CORE:])
                 z_hi, z_lo = split(jnp.concatenate(z, axis=1))
                 starts = [2 * XB * j + rows.start for j in range(3)]
                 put(b_cat, 2 * g + slot, starts, (z_hi, z_hi, z_lo))
@@ -436,8 +437,7 @@
         back, back_mid, back_old = at(i - lag), at(i - lag - 1), at(i - lag - 2)
         slot, other = i % 2, (i + 1) % 2
         if mid:
-            z_one = dot(a_hi[other], tb("y2"))
-            z_two = dot(a_lo[other], tb("y2", 0))
+            z_now = dot(a_cat[other], tb("y2"))
         if new:
             products(*new, slot)
         if back_mid:
@@ -449,7 +449,7 @@
         if back_old:
             add_back(*back_old, slot)
         if mid:
-            y_done(z_one, z_two, other)
+            y_done(z_now, other)
         if back_mid:
             for g in range(group):
                 x_back_done(w_now[g], g, other)
@@ -508,20 +508,40 @@
         rows = slice(CORE * t, CORE * t + CORE)
         value = jnp.where(table_ref[2 + t] == 1, turned[rows], other[t])
         tiles.append(0.5 * (own_ref[rows] + value))
-    return tiles
+    return tiles, hi, lo
+
+
+def matched_edges(table_ref, own_ref, hi, lo):
+    row = lax.broadcasted_iota(jnp.int32, (WIDE_PAD, CORE), 0)
+    lane = lax.broadcasted_iota(jnp.int32, (WIDE_PAD, CORE), 1)
+    picks = [picker(WIDE_PAD, 0, WIDE, CORE - WIDE), picker(WIDE_PAD, 0, WIDE, 0)]
+    for end in (WIDE - 1, CORE - 1):
+        hit = (row + lane == end) & (row < WIDE)
+        picks.append(jnp.where(hit, 1.0, 0.0).astype(bf16))
+    picks = jnp.concatenate(picks, axis=0)
+    own_hi, own_lo = split(own_ref[...])
+    own = dot_nt(picks[: 2 * WIDE_PAD], own_hi) + dot_nt(picks[: 2 * WIDE_PAD], own_lo)
+    other = dot_nt(picks, hi) + dot_nt(picks, lo)
+    chosen = []
+    for t in range(2):
+        lanes = slice(CORE * t, CORE * t + CORE)
+        plain, turned = other[: 2 * WIDE_PAD, lanes], other[2 * WIDE_PAD :, lanes]
+        chosen.append(jnp.where(table_ref[2 + t] == 1, turned, plain))
+    both = 0.5 * (own + jnp.concatenate(chosen, axis=1))
+    return both[:WIDE_PAD], both[WIDE_PAD:]
 
 
 def match_kernel(n_got, table_ref, own_ref, *refs):
     got_refs, (out_ref, *edge_refs) = refs[:n_got], refs[n_got:]
-    matched = jnp.concatenate(match(table_ref, own_ref, got_refs), axis=0)
-    out_ref[...] = matched
-    send_edges(*edges_of(WIDE_PAD, matched), *edge_refs)
+    tiles, hi, lo = match(table_ref, own_ref, got_refs)
+    send_edges(*matched_edges(table_ref, own_ref, hi, lo), *edge_refs)
+    out_ref[...] = jnp.concatenate(tiles, axis=0)
 
 
 def final_kernel(n_got, n_moves, table_ref, own_ref, *refs):
     got_refs, mask_ref, refs = refs[:n_got], refs[n_got], refs[n_got + 1 :]
     moves, (mask_out, grad_out) = refs[: 2 * n_moves], refs[2 * n_moves :]
-    for t, step in enumerate(match(table_ref, own_ref, got_refs)):
+    for t, step in enumerate(match(table_ref, own_ref, got_refs)[0]):
         rows = slice(CORE * t, CORE * t + CORE)
         now = mask_ref[t]
         for mine, peer in zip(moves[::2], moves[1::2]):
@@ -579,8 +599,7 @@
         pltpu.VMEM((2, kern, ROWS, 2 * CORE), f32),
         pltpu.VMEM((2, ROWS, CORE), f32),
         pltpu.VMEM((2, 4, XB, YB), f32),
-        pltpu.VMEM((2, group * 4 * XB, 2 * YB), bf16),
-        pltpu.VMEM((2, group * 4 * XB, 2 * YB), bf16),
+        pltpu.VMEM((2, group * 4 * XB, 4 * YB), bf16),
         pltpu.VMEM((2 * group, 6 * XB, 2 * CORE), bf16),
         pltpu.VMEM((2 * group, 3 * ROWS, 2 * CORE), bf16),
         pltpu.VMEM((2, group * 4 * XB, 3 * CORE), bf16),

time: 57.7 us -> 57.5 us (level)
  no operation moved by 1% of the time
where the time goes in v16:
time: 57.5 us; the launch traced here: 57.3 us
  starting transfers between devices  23.9 us (42%)
  Pallas kernels  16.9 us (29%)
  waiting for transfers between devices  13.9 us (24%)
  between operations  1.49 us (3%)
  other arithmetic  1.08 us (2%)
    pallas_call x6, Pallas kernels, call(): pl.pallas_call(wrapped, out_shape=out_shape, in_specs=[sm if i in smem el...  16.9 us
    ppermute x8, starting transfers between devices, from_partners(): lax.ppermute(grad, 'tile', [(i, i ^ bit) for i in range(n_tile)])  16.6 us
    ppermute x8, waiting for transfers between devices, from_partners(): lax.ppermute(grad, 'tile', [(i, i ^ bit) for i in range(n_tile)])  8.92 us
    ppermute x2, waiting for transfers between devices, depth_pair(): peer = lax.ppermute(x, 'depth', [(i, i ^ bit) for i in range(n_depth)])  3.45 us
    ppermute x2, starting transfers between devices, depth_pair(): peer = lax.ppermute(x, 'depth', [(i, i ^ bit) for i in range(n_depth)])  3.17 us
    ppermute x4, starting transfers between devices, move(): return lax.ppermute(x, 'tile', pairs)  2.62 us
    ppermute x2, waiting for transfers between devices, move(): return lax.ppermute(x, ('tile', 'depth'), both)  1.55 us
    ppermute x2, starting transfers between devices, move(): return lax.ppermute(x, ('tile', 'depth'), both)  1.52 us
  transfers between devices with their start and end apart: 16, of which 6 were waited for; matrix products, arithmetic and copies ran while one was open for 0% of the time, Pallas kernels for 3%

profile of v16, /device:TPU:0, one launch (start us, length us, event | category | flops | bytes accessed | tf_op | source)
XLA Modules:
  0.0 57.3 jit_solution(5165147310851601159)
XLA Ops:
  0.6 1.0 %multiply_add_fusion.refs_0_ = f32[256,128]{1,0:T(8,128)S(1)} fusion(s32[2,128,128]{2,1,0:T(8,128)} %param.11, f32[2,128,128]{2,1,0:T(8,128)} %refs_6_.2), kind=kLoop, calls=%fused_computation | loop fusion | flops 98304 | bytes 393216 | tf_op jit(solution)/shard_map/add | solution.py:612
  1.6 0.0 copy-start.2
  1.6 0.0 copy-start.3
  1.6 0.0 copy-start.5
  1.7 0.3 shard_map.113
  1.9 0.5 collective-permute-start
  2.4 0.7 %collective-permute-start.1 = (f32[48,256]{1,0:T(8,128)S(1)}, f32[48,256]{1,0:T(8,128)S(1)}, u32[]{:S(2)}, u32[]{:S(2)}) collective-permute-start(f32[48,256]{1,0:T(8,128)S(1)} %get-tuple-element.11), channel_id=1, source_target_pairs={{2,4},{4,2},{6,8},{8,6},{10,12},{12,10},{14,16},{16,14},{18,20},{2... | collective-permute-start | bytes 147464 | tf_op jit(solution)/shard_map/ppermute | solution.py:567
  3.1 0.0 copy-start
  3.1 0.0 copy-start.1
  3.1 0.0 copy-start.4
  3.2 1.9 %shard_map.114.refs_5_.refs_9_ = f32[12,4,88,128]{3,2,1,0:T(8,128)S(1)} custom-call(f32[1,6]{1,0:T(1,128)S(1)} %copy-done.3, f32[2,6,25,1,25]{4,3,2,1,0:T(1,128)S(1)} %bitcast.7, bf16[1376,256]{1,0:T(8,128)(2,1)S(1)} %copy-done.5), custom_call_target="tpu_custom_call" | custom-call | flops 3000000000 | bytes 4000000 | tf_op jit(solution)/shard_map/pallas_call | solution.py:223
  5.7 0.0 collective-permute-done.refs_3_
  5.7 0.0 collective-permute-done.1.refs_4_
  5.8 0.0 copy-start.6
  5.8 0.0 copy-start.7
  5.8 6.3 %shard_map.115 = (f32[256,128]{1,0:T(8,128)S(1)}, f32[2,4,88,128]{3,2,1,0:T(8,128)S(1)}, f32[160,256]{1,0:T(8,128)S(1)}) custom-call(f32[1]{0:T(128)S(6)} %copy.12.refs_0_, f32[256,128]{1,0:T(8,128)S(1)} %bitcast.5, s32[256,128]{1,0:T(8,128)S(1)} %bitcast.6, f32[48,256]{1,0:T(8,128)S(1)} %collective-permute-done.refs_3_, ...), custom_call_target="tpu_custom_call" | custom-call | flops 10000000000 | tf_op jit(solution)/shard_map/pallas_call | solution.py:223
  12.1 6.7 %collective-permute-start.5 = (f32[256,128]{1,0:T(8,128)S(1)}, f32[256,128]{1,0:T(8,128)S(1)}, u32[]{:S(2)}, u32[]{:S(2)}) collective-permute-start(f32[256,128]{1,0:T(8,128)S(1)} %get-tuple-element.12.refs_1_), channel_id=1, source_target_pairs={{0,16},{2,18},{4,20},{6,22},{8,24},{10,26},{12,28},{14,30},{16,0},... | collective-permute-start | bytes 393224 | tf_op jit(solution)/shard_map/ppermute | solution.py:585
  18.8 1.6 %collective-permute-start.4 = (f32[256,128]{1,0:T(8,128)S(1)}, f32[256,128]{1,0:T(8,128)S(1)}, u32[]{:S(2)}, u32[]{:S(2)}) collective-permute-start(f32[256,128]{1,0:T(8,128)S(1)} %get-tuple-element.12.refs_1_), channel_id=1, source_target_pairs={{0,8},{2,10},{4,12},{6,14},{8,0},{10,2},{12,4},{14,6},{16,24},{18,... | collective-permute-start | bytes 393224 | tf_op jit(solution)/shard_map/ppermute | solution.py:585
  20.4 0.5 collective-permute-start.3
  20.9 0.0 collective-permute-start.2
  20.9 0.1 pad_add_fusion.refs_0_
  21.0 4.4 %collective-permute-done.5.refs_5_ = f32[256,128]{1,0:T(8,128)S(1)} collective-permute-done((f32[256,128]{1,0:T(8,128)S(1)}, f32[256,128]{1,0:T(8,128)S(1)}, u32[]{:S(2)}, u32[]{:S(2)}) %collective-permute-start.5) | collective-permute-done | bytes 131104 | tf_op jit(solution)/shard_map/ppermute | solution.py:585
  25.4 0.2 collective-permute-done.4.refs_4_
  25.6 0.0 collective-permute-done.3.refs_3_
  25.6 0.0 collective-permute-done.2.refs_2_
  25.6 0.8 %shard_map.116 = (f32[256,128]{1,0:T(8,128)S(1)}, f32[32,256]{1,0:T(8,128)S(1)}, f32[32,256]{1,0:T(8,128)S(1)}) custom-call(s32[4]{0:T(128)S(1)} %pad_add_fusion.refs_0_, f32[256,128]{1,0:T(8,128)S(1)} %get-tuple-element.12.refs_1_, f32[256,128]{1,0:T(8,128)S(1)} %collective-permute-done.2.refs_2_, f32[256,128]{1,0:T(8,128)S(1)} %collective-permute-done.3.refs_3_, ...), custom_call_target="tpu_custom_call" | custom-call | tf_op jit(solution)/shard_map/pallas_call | solution.py:223
  26.4 1.6 %collective-permute-start.6 = (f32[256,128]{1,0:T(8,128)S(1)}, f32[256,128]{1,0:T(8,128)S(1)}, u32[]{:S(2)}, u32[]{:S(2)}) collective-permute-start(f32[256,128]{1,0:T(8,128)S(1)} %get-tuple-element.13.refs_1_.refs_7_), channel_id=1, source_target_pairs={{0,1},{1,0},{2,3},{3,2},{4,5},{5,4},{6,7},{7,6},{8,9},{9,8},{10,11... | collective-permute-start | bytes 393224 | tf_op jit(solution)/shard_map/ppermute | solution.py:576
  28.0 0.0 collective-permute-start.8
  28.0 0.6 %collective-permute-start.7 = (f32[32,256]{1,0:T(8,128)S(1)}, f32[32,256]{1,0:T(8,128)S(1)}, u32[]{:S(2)}, u32[]{:S(2)}) collective-permute-start(f32[32,256]{1,0:T(8,128)S(1)} %get-tuple-element.14), channel_id=1, source_target_pairs={{0,2},{2,0},{4,6},{6,4},{8,10},{10,8},{12,14},{14,12},{16,18},{18,... | collective-permute-start | bytes 98312 | tf_op jit(solution)/shard_map/ppermute | solution.py:567
  28.6 1.5 %collective-permute-start.10 = (f32[32,256]{1,0:T(8,128)S(1)}, f32[32,256]{1,0:T(8,128)S(1)}, u32[]{:S(2)}, u32[]{:S(2)}) collective-permute-start(f32[32,256]{1,0:T(8,128)S(1)} %get-tuple-element.15), channel_id=1, source_target_pairs={{2,5},{3,4},{4,3},{5,2},{6,9},{7,8},{8,7},{9,6},{10,13},{11,12},{1... | collective-permute-start | bytes 98312 | tf_op jit(solution)/shard_map/ppermute | solution.py:569
  30.1 0.8 %collective-permute-start.9 = (f32[32,256]{1,0:T(8,128)S(1)}, f32[32,256]{1,0:T(8,128)S(1)}, u32[]{:S(2)}, u32[]{:S(2)}) collective-permute-start(f32[32,256]{1,0:T(8,128)S(1)} %get-tuple-element.15), channel_id=1, source_target_pairs={{2,4},{4,2},{6,8},{8,6},{10,12},{12,10},{14,16},{16,14},{18,20},{2... | collective-permute-start | bytes 98312 | tf_op jit(solution)/shard_map/ppermute | solution.py:567
  31.0 0.7 %collective-permute-done.8.refs_4_ = f32[32,256]{1,0:T(8,128)S(1)} collective-permute-done((f32[32,256]{1,0:T(8,128)S(1)}, f32[32,256]{1,0:T(8,128)S(1)}, u32[]{:S(2)}, u32[]{:S(2)}) %collective-permute-start.8) | collective-permute-done | bytes 32800 | tf_op jit(solution)/shard_map/ppermute | solution.py:569
  31.7 0.0 collective-permute-done.7.refs_3_
  31.7 0.9 %collective-permute-done.10.refs_6_ = f32[32,256]{1,0:T(8,128)S(1)} collective-permute-done((f32[32,256]{1,0:T(8,128)S(1)}, f32[32,256]{1,0:T(8,128)S(1)}, u32[]{:S(2)}, u32[]{:S(2)}) %collective-permute-start.10) | collective-permute-done | bytes 32800 | tf_op jit(solution)/shard_map/ppermute | solution.py:569
  32.5 0.0 collective-permute-done.9.refs_5_
  32.5 0.0 collective-permute-done.6.refs_2_.refs_8_
  32.5 6.2 %shard_map.117 = f32[256,128]{1,0:T(8,128)S(1)} custom-call(f32[1]{0:T(128)S(6)} %copy.12.refs_0_, f32[256,128]{1,0:T(8,128)S(1)} %get-tuple-element.13.refs_1_.refs_7_, f32[256,128]{1,0:T(8,128)S(1)} %collective-permute-done.6.refs_2_.refs_8_, f32[32,256]{1,0:T(8,128)S(1)} %collective-permute-done.7.refs_3_, f32[32,256]{1,0:T(8,128)S(1)} %collective-permute-done.8.refs_4_, ...), custom_call_target="tpu_custom_call" | custom-call | flops 10000000000 | tf_op jit(solution)/shard_map/pallas_call | solution.py:223
  38.7 1.6 %collective-permute-start.11 = (f32[256,128]{1,0:T(8,128)S(1)}, f32[256,128]{1,0:T(8,128)S(1)}, u32[]{:S(2)}, u32[]{:S(2)}) collective-permute-start(f32[256,128]{1,0:T(8,128)S(1)} %shard_map.117), channel_id=1, source_target_pairs={{0,1},{1,0},{2,3},{3,2},{4,5},{5,4},{6,7},{7,6},{8,9},{9,8},{10,11... | collective-permute-start | bytes 393224 | tf_op jit(solution)/shard_map/ppermute | solution.py:576
  40.3 3.4 %collective-permute-done.11 = f32[256,128]{1,0:T(8,128)S(1)} collective-permute-done((f32[256,128]{1,0:T(8,128)S(1)}, f32[256,128]{1,0:T(8,128)S(1)}, u32[]{:S(2)}, u32[]{:S(2)}) %collective-permute-start.11) | collective-permute-done | bytes 131104 | tf_op jit(solution)/shard_map/ppermute | solution.py:576
  43.8 6.4 %collective-permute-start.15 = (f32[256,128]{1,0:T(8,128)S(1)}, f32[256,128]{1,0:T(8,128)S(1)}, u32[]{:S(2)}, u32[]{:S(2)}) collective-permute-start(f32[256,128]{1,0:T(8,128)S(1)} %add.7.refs_1_), channel_id=1, source_target_pairs={{0,16},{2,18},{4,20},{6,22},{8,24},{10,26},{12,28},{14,30},{16,0},... | collective-permute-start | bytes 393224 | tf_op jit(solution)/shard_map/ppermute | solution.py:585
  50.1 0.7 %collective-permute-start.14 = (f32[256,128]{1,0:T(8,128)S(1)}, f32[256,128]{1,0:T(8,128)S(1)}, u32[]{:S(2)}, u32[]{:S(2)}) collective-permute-start(f32[256,128]{1,0:T(8,128)S(1)} %add.7.refs_1_), channel_id=1, source_target_pairs={{0,8},{2,10},{4,12},{6,14},{8,0},{10,2},{12,4},{14,6},{16,24},{18,... | collective-permute-start | bytes 393224 | tf_op jit(solution)/shard_map/ppermute | solution.py:585
  50.8 0.7 %collective-permute-start.13 = (f32[256,128]{1,0:T(8,128)S(1)}, f32[256,128]{1,0:T(8,128)S(1)}, u32[]{:S(2)}, u32[]{:S(2)}) collective-permute-start(f32[256,128]{1,0:T(8,128)S(1)} %add.7.refs_1_), channel_id=1, source_target_pairs={{0,4},{2,6},{4,0},{6,2},{8,12},{10,14},{12,8},{14,10},{16,20},{18,... | collective-permute-start | bytes 393224 | tf_op jit(solution)/shard_map/ppermute | solution.py:585
  51.6 0.0 collective-permute-start.12
  51.6 4.3 %collective-permute-done.15.refs_5_ = f32[256,128]{1,0:T(8,128)S(1)} collective-permute-done((f32[256,128]{1,0:T(8,128)S(1)}, f32[256,128]{1,0:T(8,128)S(1)}, u32[]{:S(2)}, u32[]{:S(2)}) %collective-permute-start.15) | collective-permute-done | bytes 131104 | tf_op jit(solution)/shard_map/ppermute | solution.py:585
  55.8 0.0 collective-permute-done.14.refs_4_
  55.8 0.0 collective-permute-done.13.refs_3_
  55.8 0.0 collective-permute-done.12.refs_2_
  55.9 1.4 %shard_map.118 = (f32[2,128,128]{2,1,0:T(8,128)}, f32[2,128,128]{2,1,0:T(8,128)}) custom-call(s32[4]{0:T(128)S(1)} %pad_add_fusion.refs_0_, f32[256,128]{1,0:T(8,128)S(1)} %add.7.refs_1_, f32[256,128]{1,0:T(8,128)S(1)} %collective-permute-done.12.refs_2_, f32[256,128]{1,0:T(8,128)S(1)} %collective-permute-done.13.refs_3_, ...), custom_call_target="tpu_custom_call" | custom-call | tf_op jit(solution)/shard_map/pallas_call | solution.py:223
  (9 shorter events, 0.0 us)
Async XLA Ops:
  1.6 1.5 %copy-start.2 = (f32[2,1,6,25,25]{4,1,3,2,0:T(1,128)S(1)}, f32[2,1,6,25,25]{4,1,3,2,0:T(1,128)}, u32[]{:S(2)}) copy-start(f32[2,1,6,25,25]{4,1,3,2,0:T(1,128)} %param.12) | copy-start | bytes 90004
  1.6 1.5 %copy-start.3 = (f32[1,6]{1,0:T(1,128)S(1)}, f32[1,6]{1,0:T(1,128)}, u32[]{:S(2)}) copy-start(f32[1,6]{1,0:T(1,128)} %refs_0_.3) | copy-start | bytes 76
  1.6 1.5 %copy-start.5 = (bf16[1376,256]{1,0:T(8,128)(2,1)S(1)}, bf16[1376,256]{1,0:T(8,128)(2,1)}, u32[]{:S(2)}) copy-start(bf16[1376,256]{1,0:T(8,128)(2,1)} %constant.6.clone.refs_2_) | copy-start | bytes 2113540
  1.9 3.8 %collective-permute-start = (f32[48,256]{1,0:T(8,128)S(1)}, f32[48,256]{1,0:T(8,128)S(1)}, u32[]{:S(2)}, u32[]{:S(2)}) collective-permute-start(f32[48,256]{1,0:T(8,128)S(1)} %get-tuple-element.10), channel_id=1, source_target_pairs={{0,2},{2,0},{4,6},{6,4},{8,10},{10,8},{12,14},{14,12},{16,18},{18,... | collective-permute-start | bytes 147464 | tf_op jit(solution)/shard_map/ppermute | solution.py:567
  2.4 3.3 %collective-permute-start.1 = (f32[48,256]{1,0:T(8,128)S(1)}, f32[48,256]{1,0:T(8,128)S(1)}, u32[]{:S(2)}, u32[]{:S(2)}) collective-permute-start(f32[48,256]{1,0:T(8,128)S(1)} %get-tuple-element.11), channel_id=1, source_target_pairs={{2,4},{4,2},{6,8},{8,6},{10,12},{12,10},{14,16},{16,14},{18,20},{2... | collective-permute-start | bytes 147464 | tf_op jit(solution)/shard_map/ppermute | solution.py:567
  3.1 2.6 %copy-start = (f32[2,128,128]{2,1,0:T(8,128)S(1)}, f32[2,128,128]{2,1,0:T(8,128)}, u32[]{:S(2)}) copy-start(f32[2,128,128]{2,1,0:T(8,128)} %refs_6_.2) | copy-start | bytes 393220
  3.1 2.6 %copy-start.1 = (s32[2,128,128]{2,1,0:T(8,128)S(1)}, s32[2,128,128]{2,1,0:T(8,128)}, u32[]{:S(2)}) copy-start(s32[2,128,128]{2,1,0:T(8,128)} %param.11) | copy-start | bytes 393220
  3.1 2.6 %copy-start.4 = (bf16[4160,256]{1,0:T(8,128)(2,1)S(1)}, bf16[4160,256]{1,0:T(8,128)(2,1)}, u32[]{:S(2)}) copy-start(bf16[4160,256]{1,0:T(8,128)(2,1)} %constant.7.clone.refs_6_.refs_10_) | copy-start | bytes 6389764
  5.8 15.1 %copy-start.6 = (s32[2]{0:T(128)S(1)}, s32[2]{0:T(128)}, u32[]{:S(2)}) copy-start(s32[2]{0:T(128)} %param.16) | copy-start | bytes 28
  5.8 15.1 %copy-start.7 = (s32[2]{0:T(128)S(1)}, s32[2]{0:T(128)}, u32[]{:S(2)}) copy-start(s32[2]{0:T(128)} %param.15) | copy-start | bytes 28
  12.1 13.3 %collective-permute-start.5 = (f32[256,128]{1,0:T(8,128)S(1)}, f32[256,128]{1,0:T(8,128)S(1)}, u32[]{:S(2)}, u32[]{:S(2)}) collective-permute-start(f32[256,128]{1,0:T(8,128)S(1)} %get-tuple-element.12.refs_1_), channel_id=1, source_target_pairs={{0,16},{2,18},{4,20},{6,22},{8,24},{10,26},{12,28},{14,30},{16,0},... | collective-permute-start | bytes 393224 | tf_op jit(solution)/shard_map/ppermute | solution.py:585
  18.8 6.8 %collective-permute-start.4 = (f32[256,128]{1,0:T(8,128)S(1)}, f32[256,128]{1,0:T(8,128)S(1)}, u32[]{:S(2)}, u32[]{:S(2)}) collective-permute-start(f32[256,128]{1,0:T(8,128)S(1)} %get-tuple-element.12.refs_1_), channel_id=1, source_target_pairs={{0,8},{2,10},{4,12},{6,14},{8,0},{10,2},{12,4},{14,6},{16,24},{18,... | collective-permute-start | bytes 393224 | tf_op jit(solution)/shard_map/ppermute | solution.py:585
  20.4 5.2 %collective-permute-start.3 = (f32[256,128]{1,0:T(8,128)S(1)}, f32[256,128]{1,0:T(8,128)S(1)}, u32[]{:S(2)}, u32[]{:S(2)}) collective-permute-start(f32[256,128]{1,0:T(8,128)S(1)} %get-tuple-element.12.refs_1_), channel_id=1, source_target_pairs={{0,4},{2,6},{4,0},{6,2},{8,12},{10,14},{12,8},{14,10},{16,20},{18,... | collective-permute-start | bytes 393224 | tf_op jit(solution)/shard_map/ppermute | solution.py:585
  20.9 4.7 %collective-permute-start.2 = (f32[256,128]{1,0:T(8,128)S(1)}, f32[256,128]{1,0:T(8,128)S(1)}, u32[]{:S(2)}, u32[]{:S(2)}) collective-permute-start(f32[256,128]{1,0:T(8,128)S(1)} %get-tuple-element.12.refs_1_), channel_id=1, source_target_pairs={{0,2},{2,0},{4,6},{6,4},{8,10},{10,8},{12,14},{14,12},{16,18},{18,... | collective-permute-start | bytes 393224 | tf_op jit(solution)/shard_map/ppermute | solution.py:585
  26.4 6.1 %collective-permute-start.6 = (f32[256,128]{1,0:T(8,128)S(1)}, f32[256,128]{1,0:T(8,128)S(1)}, u32[]{:S(2)}, u32[]{:S(2)}) collective-permute-start(f32[256,128]{1,0:T(8,128)S(1)} %get-tuple-element.13.refs_1_.refs_7_), channel_id=1, source_target_pairs={{0,1},{1,0},{2,3},{3,2},{4,5},{5,4},{6,7},{7,6},{8,9},{9,8},{10,11... | collective-permute-start | bytes 393224 | tf_op jit(solution)/shard_map/ppermute | solution.py:576
  28.0 3.7 %collective-permute-start.8 = (f32[32,256]{1,0:T(8,128)S(1)}, f32[32,256]{1,0:T(8,128)S(1)}, u32[]{:S(2)}, u32[]{:S(2)}) collective-permute-start(f32[32,256]{1,0:T(8,128)S(1)} %get-tuple-element.14), channel_id=1, source_target_pairs={{0,3},{1,2},{2,1},{3,0},{4,7},{5,6},{6,5},{7,4},{8,11},{9,10},{10,... | collective-permute-start | bytes 98312 | tf_op jit(solution)/shard_map/ppermute | solution.py:569
  28.0 3.7 %collective-permute-start.7 = (f32[32,256]{1,0:T(8,128)S(1)}, f32[32,256]{1,0:T(8,128)S(1)}, u32[]{:S(2)}, u32[]{:S(2)}) collective-permute-start(f32[32,256]{1,0:T(8,128)S(1)} %get-tuple-element.14), channel_id=1, source_target_pairs={{0,2},{2,0},{4,6},{6,4},{8,10},{10,8},{12,14},{14,12},{16,18},{18,... | collective-permute-start | bytes 98312 | tf_op jit(solution)/shard_map/ppermute | solution.py:567
  28.6 3.9 %collective-permute-start.10 = (f32[32,256]{1,0:T(8,128)S(1)}, f32[32,256]{1,0:T(8,128)S(1)}, u32[]{:S(2)}, u32[]{:S(2)}) collective-permute-start(f32[32,256]{1,0:T(8,128)S(1)} %get-tuple-element.15), channel_id=1, source_target_pairs={{2,5},{3,4},{4,3},{5,2},{6,9},{7,8},{8,7},{9,6},{10,13},{11,12},{1... | collective-permute-start | bytes 98312 | tf_op jit(solution)/shard_map/ppermute | solution.py:569
  30.1 2.4 %collective-permute-start.9 = (f32[32,256]{1,0:T(8,128)S(1)}, f32[32,256]{1,0:T(8,128)S(1)}, u32[]{:S(2)}, u32[]{:S(2)}) collective-permute-start(f32[32,256]{1,0:T(8,128)S(1)} %get-tuple-element.15), channel_id=1, source_target_pairs={{2,4},{4,2},{6,8},{8,6},{10,12},{12,10},{14,16},{16,14},{18,20},{2... | collective-permute-start | bytes 98312 | tf_op jit(solution)/shard_map/ppermute | solution.py:567
  38.7 5.0 %collective-permute-start.11 = (f32[256,128]{1,0:T(8,128)S(1)}, f32[256,128]{1,0:T(8,128)S(1)}, u32[]{:S(2)}, u32[]{:S(2)}) collective-permute-start(f32[256,128]{1,0:T(8,128)S(1)} %shard_map.117), channel_id=1, source_target_pairs={{0,1},{1,0},{2,3},{3,2},{4,5},{5,4},{6,7},{7,6},{8,9},{9,8},{10,11... | collective-permute-start | bytes 393224 | tf_op jit(solution)/shard_map/ppermute | solution.py:576
  43.8 12.1 %collective-permute-start.15 = (f32[256,128]{1,0:T(8,128)S(1)}, f32[256,128]{1,0:T(8,128)S(1)}, u32[]{:S(2)}, u32[]{:S(2)}) collective-permute-start(f32[256,128]{1,0:T(8,128)S(1)} %add.7.refs_1_), channel_id=1, source_target_pairs={{0,16},{2,18},{4,20},{6,22},{8,24},{10,26},{12,28},{14,30},{16,0},... | collective-permute-start | bytes 393224 | tf_op jit(solution)/shard_map/ppermute | solution.py:585
  50.1 5.7 %collective-permute-start.14 = (f32[256,128]{1,0:T(8,128)S(1)}, f32[256,128]{1,0:T(8,128)S(1)}, u32[]{:S(2)}, u32[]{:S(2)}) collective-permute-start(f32[256,128]{1,0:T(8,128)S(1)} %add.7.refs_1_), channel_id=1, source_target_pairs={{0,8},{2,10},{4,12},{6,14},{8,0},{10,2},{12,4},{14,6},{16,24},{18,... | collective-permute-start | bytes 393224 | tf_op jit(solution)/shard_map/ppermute | solution.py:585
  50.8 5.0 %collective-permute-start.13 = (f32[256,128]{1,0:T(8,128)S(1)}, f32[256,128]{1,0:T(8,128)S(1)}, u32[]{:S(2)}, u32[]{:S(2)}) collective-permute-start(f32[256,128]{1,0:T(8,128)S(1)} %add.7.refs_1_), channel_id=1, source_target_pairs={{0,4},{2,6},{4,0},{6,2},{8,12},{10,14},{12,8},{14,10},{16,20},{18,... | collective-permute-start | bytes 393224 | tf_op jit(solution)/shard_map/ppermute | solution.py:585
  51.6 4.3 %collective-permute-start.12 = (f32[256,128]{1,0:T(8,128)S(1)}, f32[256,128]{1,0:T(8,128)S(1)}, u32[]{:S(2)}, u32[]{:S(2)}) collective-permute-start(f32[256,128]{1,0:T(8,128)S(1)} %add.7.refs_1_), channel_id=1, source_target_pairs={{0,2},{2,0},{4,6},{6,4},{8,10},{10,8},{12,14},{14,12},{16,18},{18,... | collective-permute-start | bytes 393224 | tf_op jit(solution)/shard_map/ppermute | solution.py:585

commit v17 on v16

--- a/solution.py
+++ b/solution.py
@@ -136,16 +136,16 @@
     for r in range(HALO):
         halo[HALO + r - ROW0, WIDE + r] = 1
         halo[WIDE + CORE + r - ROW0, CORE + WIDE + r] = 1
-    grad += [("sel_own", own), ("sel_halo", halo)]
+    grad += [("sel_halo", halo)]
     offs = np.arange(KSIZE) - HALO
     kx = np.zeros((2 * XB, 128))
     kx[:, :KSIZE] = x_rows(offs)
-    spec = [("kx", kx)]
+    spec = [("kx", kx), ("cx_own", x_rows(own_cols))]
     for m in range(4):
         ky = np.zeros((128, 2 * YB))
         ky[32 * m : 32 * m + KSIZE] = y_lanes(offs)
         spec.append((f"ky{m}", ky))
-    return {"grad": pack(grad), "spec": pack(pack_split(spec))}
+    return {"grad": pack(grad), "spec": pack(pack_split(spec) + [("sel_own", own)])}
 
 
 def split(x):
@@ -267,7 +267,12 @@
     send_edges(*edges_of(EDGE, mask, target.astype(bf16)), a_ref, b_ref)
 
 
-def spectra_kernel(kern, w_ref, ker_ref, tb, h_ref, hs_ref):
+def spectra_kernel(
+    kern, w_ref, ker_ref, mask_ref, target_ref, tb, h_ref, v_ref, tgt_ref, hs_ref
+):
+    m_hi, m_lo = split(mask_ref[...])
+    v_ref[...] = dot3(tb("cx_own_hi"), tb("cx_own_lo"), m_hi, m_lo, dot_nt)
+    tgt_ref[...] = dot_nt(tb("sel_own"), target_ref[...].astype(f32).astype(bf16))
     hs_ref[...] = jnp.zeros_like(hs_ref)
     for k in range(kern):
         for part in range(2):
@@ -380,7 +385,7 @@
                 inten[t, rows] = power if k == 0 else inten[t, rows] + power
 
     def slope_of(t):
-        resist = jax.nn.sigmoid(STEEPNESS * (inten[t] - thr_ref[0]))
+        resist = jax.nn.sigmoid(STEEPNESS * (inten[t] - thr_ref[...]))
         target = tgt_ref[:, CORE * t : CORE * t + CORE]
         slope = 2.0 * (resist - target) * STEEPNESS * resist * (1.0 - resist)
         inten[t] = jnp.where(inside, 2.0 * slope, 0.0)
@@ -460,15 +465,14 @@
 
 
 def first_kernel(
-    kern, last, thr_ref, mask_ref, target_ref, a_ref, b_ref, h_ref, tb,
+    kern, last, thr_ref, v_ref, t_ref, a_ref, b_ref, h_ref, tb,
     g_ref, f_ref, tgt_ref, *work,
 ):
-    m_hi, m_lo = split(mask_ref[...])
     v, left, right = sides(last, a_ref[...], b_ref[...], tb)
-    v = v + dot3(tb("cx_own_hi"), tb("cx_own_lo"), m_hi, m_lo, dot_nt)
+    v = v + v_ref[...]
     to_spectrum(v, tb, f_ref, None)
     tgt_ref[...] = (
-        dot_nt(tb("sel_own"), target_ref[...].astype(f32).astype(bf16))
+        t_ref[...]
         + dot(tb("sel_halo", 0)[:, :EDGE], left)
         + dot(tb("sel_halo", 1)[:, :EDGE], right)
     )
@@ -615,11 +619,16 @@
     )
     from_b, from_a = swap_edges(send_a, send_b)
     table = jnp.concatenate([partner_table, mirror_flags])
-    (spectra,) = call(
+    level = thresholds.reshape(1, 1)
+    spectra, own_v, own_goals = call(
         functools.partial(spectra_kernel, kern),
         "spec",
-        [socs_weights, kernels.transpose(0, 2, 3, 1, 4)],
-        [jax.ShapeDtypeStruct((2 * kern, 4, XB, YB), f32)],
+        [socs_weights, kernels.transpose(0, 2, 3, 1, 4), mask_rows, target_rows],
+        [
+            jax.ShapeDtypeStruct((2 * kern, 4, XB, YB), f32),
+            jax.ShapeDtypeStruct((2 * XB, tiles_dev * core), f32),
+            goal,
+        ],
         [pltpu.VMEM((32 * 2 * kern, 128), f32)],
         smem=(0,),
         flops=3 * 10**9,
@@ -628,10 +637,9 @@
     grad, freq_now, goals = call(
         functools.partial(first_kernel, kern, n_tile - 1),
         "grad",
-        [thresholds, mask_rows, target_rows, from_a, from_b, spectra],
+        [level, own_v, own_goals, from_a, from_b, spectra],
         [strip, freq, goal],
         scratch,
-        smem=(0,),
         flops=10**10,
     )
     moves = []
@@ -655,10 +663,9 @@
         grad, *rest = call(
             functools.partial(later_kernel, kern, n_tile - 1),
             "grad",
-            [thresholds, *moves[-2:], *rims, freq_now, goals, spectra],
+            [level, *moves[-2:], *rims, freq_now, goals, spectra],
             [strip, freq] if kept else [strip],
             scratch if kept else [pltpu.VMEM(freq.shape, f32)] + scratch,
-            smem=(0,),
             flops=10**10,
         )
         freq_now = rest[0] if kept else None

time: 57.5 us -> 58 us (level)
  transfers between devices with their start and end apart: 16 -> 16, of which waited for: 6 -> 6; matrix products, arithmetic and copies ran while one was open for 0% -> 0% of each run, Pallas kernels for 3% -> 4%
where the time goes in v17:
time: 58 us; the launch traced here: 57.8 us
  starting transfers between devices  23.7 us (41%)
  Pallas kernels  17.4 us (30%)
  waiting for transfers between devices  14.1 us (24%)
  between operations  1.49 us (3%)
  other arithmetic  1.08 us (2%)
    pallas_call x6, Pallas kernels, call(): pl.pallas_call(wrapped, out_shape=out_shape, in_specs=[sm if i in smem el...  17.4 us
    ppermute x8, starting transfers between devices, from_partners(): lax.ppermute(grad, 'tile', [(i, i ^ bit) for i in range(n_tile)])  16.4 us
    ppermute x8, waiting for transfers between devices, from_partners(): lax.ppermute(grad, 'tile', [(i, i ^ bit) for i in range(n_tile)])  9.09 us
    ppermute x2, waiting for transfers between devices, depth_pair(): peer = lax.ppermute(x, 'depth', [(i, i ^ bit) for i in range(n_depth)])  3.45 us
    ppermute x2, starting transfers between devices, depth_pair(): peer = lax.ppermute(x, 'depth', [(i, i ^ bit) for i in range(n_depth)])  3.17 us
    ppermute x4, starting transfers between devices, move(): return lax.ppermute(x, 'tile', pairs)  2.62 us
    ppermute x2, waiting for transfers between devices, move(): return lax.ppermute(x, ('tile', 'depth'), both)  1.55 us
    ppermute x2, starting transfers between devices, move(): return lax.ppermute(x, ('tile', 'depth'), both)  1.52 us
  transfers between devices with their start and end apart: 16, of which 6 were waited for; matrix products, arithmetic and copies ran while one was open for 0% of the time, Pallas kernels for 4%

profile of v17, /device:TPU:0, one launch (start us, length us, event | category | flops | bytes accessed | tf_op | source)
XLA Modules:
  0.0 57.8 jit_solution(10195816254520339633)
XLA Ops:
  0.6 1.0 %multiply_add_fusion.refs_0_ = f32[256,128]{1,0:T(8,128)S(1)} fusion(s32[2,128,128]{2,1,0:T(8,128)} %param.11, f32[2,128,128]{2,1,0:T(8,128)} %refs_6_.2), kind=kLoop, calls=%fused_computation | loop fusion | flops 98304 | bytes 393216 | tf_op jit(solution)/shard_map/add | solution.py:616
  1.6 0.0 copy-start
  1.6 0.0 copy-start.1
  1.6 0.0 copy-start.2
  1.7 0.0 copy-start.3
  1.7 0.0 copy-start.5
  1.7 0.3 shard_map.114
  1.9 0.5 collective-permute-start
  2.5 0.7 %collective-permute-start.1 = (f32[48,256]{1,0:T(8,128)S(1)}, f32[48,256]{1,0:T(8,128)S(1)}, u32[]{:S(2)}, u32[]{:S(2)}) collective-permute-start(f32[48,256]{1,0:T(8,128)S(1)} %get-tuple-element.16), channel_id=1, source_target_pairs={{2,4},{4,2},{6,8},{8,6},{10,12},{12,10},{14,16},{16,14},{18,20},{2... | collective-permute-start | bytes 147464 | tf_op jit(solution)/shard_map/ppermute | solution.py:571
  3.2 0.0 copy-start.4
  3.2 2.2 %shard_map.113 = (f32[12,4,88,128]{3,2,1,0:T(8,128)S(1)}, f32[176,256]{1,0:T(8,128)S(1)}, f32[160,256]{1,0:T(8,128)S(1)}) custom-call(f32[1,6]{1,0:T(1,128)S(1)} %copy-done.3, f32[2,6,25,1,25]{4,3,2,1,0:T(1,128)S(1)} %bitcast.10, f32[256,128]{1,0:T(8,128)S(1)} %bitcast.8, s32[256,128]{1,0:T(8,128)S(1)} %bitcast.9, bf16[1888,256]{1,0:T(8,128)(2,1)S(1)} %copy-done.5), custom_call_target="tpu_custom_call" | custom-call | flops 3000000000 | bytes 4000000 | tf_op jit(solution)/shard_map/pallas_call | solution.py:223
  6.0 0.0 collective-permute-done.refs_3_
  6.0 0.0 collective-permute-done.1.refs_4_
  6.0 0.0 copy-start.6
  6.1 0.0 copy-start.7
  6.1 6.5 %shard_map.115 = (f32[256,128]{1,0:T(8,128)S(1)}, f32[2,4,88,128]{3,2,1,0:T(8,128)S(1)}, f32[160,256]{1,0:T(8,128)S(1)}) custom-call(f32[1,1]{1,0:T(1,128)} %bitcast.6.refs_0_, f32[176,256]{1,0:T(8,128)S(1)} %get-tuple-element.13.refs_1_, f32[160,256]{1,0:T(8,128)S(1)} %get-tuple-element.14.refs_2_, f32[48,256]{1,0:T(8,128)S(1)} %collective-permute-done.refs_3_, ...), custom_call_target="tpu_custom_call" | custom-call | flops 10000000000 | tf_op jit(solution)/shard_map/pallas_call | solution.py:223
  12.6 6.6 %collective-permute-start.5 = (f32[256,128]{1,0:T(8,128)S(1)}, f32[256,128]{1,0:T(8,128)S(1)}, u32[]{:S(2)}, u32[]{:S(2)}) collective-permute-start(f32[256,128]{1,0:T(8,128)S(1)} %get-tuple-element.18.refs_1_), channel_id=1, source_target_pairs={{0,16},{2,18},{4,20},{6,22},{8,24},{10,26},{12,28},{14,30},{16,0},... | collective-permute-start | bytes 393224 | tf_op jit(solution)/shard_map/ppermute | solution.py:589
  19.1 1.6 %collective-permute-start.4 = (f32[256,128]{1,0:T(8,128)S(1)}, f32[256,128]{1,0:T(8,128)S(1)}, u32[]{:S(2)}, u32[]{:S(2)}) collective-permute-start(f32[256,128]{1,0:T(8,128)S(1)} %get-tuple-element.18.refs_1_), channel_id=1, source_target_pairs={{0,8},{2,10},{4,12},{6,14},{8,0},{10,2},{12,4},{14,6},{16,24},{18,... | collective-permute-start | bytes 393224 | tf_op jit(solution)/shard_map/ppermute | solution.py:589
  20.7 0.5 collective-permute-start.3
  21.2 0.0 collective-permute-start.2
  21.2 0.1 pad_add_fusion.refs_0_
  21.3 4.5 %collective-permute-done.5.refs_5_ = f32[256,128]{1,0:T(8,128)S(1)} collective-permute-done((f32[256,128]{1,0:T(8,128)S(1)}, f32[256,128]{1,0:T(8,128)S(1)}, u32[]{:S(2)}, u32[]{:S(2)}) %collective-permute-start.5) | collective-permute-done | bytes 131104 | tf_op jit(solution)/shard_map/ppermute | solution.py:589
  25.8 0.2 collective-permute-done.4.refs_4_
  26.0 0.0 collective-permute-done.3.refs_3_
  26.0 0.0 collective-permute-done.2.refs_2_
  26.0 0.8 %shard_map.116 = (f32[256,128]{1,0:T(8,128)S(1)}, f32[32,256]{1,0:T(8,128)S(1)}, f32[32,256]{1,0:T(8,128)S(1)}) custom-call(s32[4]{0:T(128)S(1)} %pad_add_fusion.refs_0_, f32[256,128]{1,0:T(8,128)S(1)} %get-tuple-element.18.refs_1_, f32[256,128]{1,0:T(8,128)S(1)} %collective-permute-done.2.refs_2_, f32[256,128]{1,0:T(8,128)S(1)} %collective-permute-done.3.refs_3_, ...), custom_call_target="tpu_custom_call" | custom-call | tf_op jit(solution)/shard_map/pallas_call | solution.py:223
  26.9 1.6 %collective-permute-start.6 = (f32[256,128]{1,0:T(8,128)S(1)}, f32[256,128]{1,0:T(8,128)S(1)}, u32[]{:S(2)}, u32[]{:S(2)}) collective-permute-start(f32[256,128]{1,0:T(8,128)S(1)} %get-tuple-element.19.refs_1_.refs_7_), channel_id=1, source_target_pairs={{0,1},{1,0},{2,3},{3,2},{4,5},{5,4},{6,7},{7,6},{8,9},{9,8},{10,11... | collective-permute-start | bytes 393224 | tf_op jit(solution)/shard_map/ppermute | solution.py:580
  28.4 0.0 collective-permute-start.8
  28.4 0.6 %collective-permute-start.7 = (f32[32,256]{1,0:T(8,128)S(1)}, f32[32,256]{1,0:T(8,128)S(1)}, u32[]{:S(2)}, u32[]{:S(2)}) collective-permute-start(f32[32,256]{1,0:T(8,128)S(1)} %get-tuple-element.20), channel_id=1, source_target_pairs={{0,2},{2,0},{4,6},{6,4},{8,10},{10,8},{12,14},{14,12},{16,18},{18,... | collective-permute-start | bytes 98312 | tf_op jit(solution)/shard_map/ppermute | solution.py:571
  29.1 1.5 %collective-permute-start.10 = (f32[32,256]{1,0:T(8,128)S(1)}, f32[32,256]{1,0:T(8,128)S(1)}, u32[]{:S(2)}, u32[]{:S(2)}) collective-permute-start(f32[32,256]{1,0:T(8,128)S(1)} %get-tuple-element.21), channel_id=1, source_target_pairs={{2,5},{3,4},{4,3},{5,2},{6,9},{7,8},{8,7},{9,6},{10,13},{11,12},{1... | collective-permute-start | bytes 98312 | tf_op jit(solution)/shard_map/ppermute | solution.py:573
  30.6 0.8 %collective-permute-start.9 = (f32[32,256]{1,0:T(8,128)S(1)}, f32[32,256]{1,0:T(8,128)S(1)}, u32[]{:S(2)}, u32[]{:S(2)}) collective-permute-start(f32[32,256]{1,0:T(8,128)S(1)} %get-tuple-element.21), channel_id=1, source_target_pairs={{2,4},{4,2},{6,8},{8,6},{10,12},{12,10},{14,16},{16,14},{18,20},{2... | collective-permute-start | bytes 98312 | tf_op jit(solution)/shard_map/ppermute | solution.py:571
  31.4 0.7 %collective-permute-done.8.refs_4_ = f32[32,256]{1,0:T(8,128)S(1)} collective-permute-done((f32[32,256]{1,0:T(8,128)S(1)}, f32[32,256]{1,0:T(8,128)S(1)}, u32[]{:S(2)}, u32[]{:S(2)}) %collective-permute-start.8) | collective-permute-done | bytes 32800 | tf_op jit(solution)/shard_map/ppermute | solution.py:573
  32.1 0.0 collective-permute-done.7.refs_3_
  32.1 0.9 %collective-permute-done.10.refs_6_ = f32[32,256]{1,0:T(8,128)S(1)} collective-permute-done((f32[32,256]{1,0:T(8,128)S(1)}, f32[32,256]{1,0:T(8,128)S(1)}, u32[]{:S(2)}, u32[]{:S(2)}) %collective-permute-start.10) | collective-permute-done | bytes 32800 | tf_op jit(solution)/shard_map/ppermute | solution.py:573
  33.0 0.0 collective-permute-done.9.refs_5_
  33.0 0.0 collective-permute-done.6.refs_2_.refs_8_
  33.0 6.2 %shard_map.117 = f32[256,128]{1,0:T(8,128)S(1)} custom-call(f32[1,1]{1,0:T(1,128)} %bitcast.7.refs_0_, f32[256,128]{1,0:T(8,128)S(1)} %get-tuple-element.19.refs_1_.refs_7_, f32[256,128]{1,0:T(8,128)S(1)} %collective-permute-done.6.refs_2_.refs_8_, f32[32,256]{1,0:T(8,128)S(1)} %collective-permute-done.7.refs_3_, ...), custom_call_target="tpu_custom_call" | custom-call | flops 10000000000 | tf_op jit(solution)/shard_map/pallas_call | solution.py:223
  39.2 1.6 %collective-permute-start.11 = (f32[256,128]{1,0:T(8,128)S(1)}, f32[256,128]{1,0:T(8,128)S(1)}, u32[]{:S(2)}, u32[]{:S(2)}) collective-permute-start(f32[256,128]{1,0:T(8,128)S(1)} %shard_map.117), channel_id=1, source_target_pairs={{0,1},{1,0},{2,3},{3,2},{4,5},{5,4},{6,7},{7,6},{8,9},{9,8},{10,11... | collective-permute-start | bytes 393224 | tf_op jit(solution)/shard_map/ppermute | solution.py:580
  40.8 3.4 %collective-permute-done.11 = f32[256,128]{1,0:T(8,128)S(1)} collective-permute-done((f32[256,128]{1,0:T(8,128)S(1)}, f32[256,128]{1,0:T(8,128)S(1)}, u32[]{:S(2)}, u32[]{:S(2)}) %collective-permute-start.11) | collective-permute-done | bytes 131104 | tf_op jit(solution)/shard_map/ppermute | solution.py:580
  44.3 6.3 %collective-permute-start.15 = (f32[256,128]{1,0:T(8,128)S(1)}, f32[256,128]{1,0:T(8,128)S(1)}, u32[]{:S(2)}, u32[]{:S(2)}) collective-permute-start(f32[256,128]{1,0:T(8,128)S(1)} %add.7.refs_1_), channel_id=1, source_target_pairs={{0,16},{2,18},{4,20},{6,22},{8,24},{10,26},{12,28},{14,30},{16,0},... | collective-permute-start | bytes 393224 | tf_op jit(solution)/shard_map/ppermute | solution.py:589
  50.5 0.7 %collective-permute-start.14 = (f32[256,128]{1,0:T(8,128)S(1)}, f32[256,128]{1,0:T(8,128)S(1)}, u32[]{:S(2)}, u32[]{:S(2)}) collective-permute-start(f32[256,128]{1,0:T(8,128)S(1)} %add.7.refs_1_), channel_id=1, source_target_pairs={{0,8},{2,10},{4,12},{6,14},{8,0},{10,2},{12,4},{14,6},{16,24},{18,... | collective-permute-start | bytes 393224 | tf_op jit(solution)/shard_map/ppermute | solution.py:589
  51.3 0.7 %collective-permute-start.13 = (f32[256,128]{1,0:T(8,128)S(1)}, f32[256,128]{1,0:T(8,128)S(1)}, u32[]{:S(2)}, u32[]{:S(2)}) collective-permute-start(f32[256,128]{1,0:T(8,128)S(1)} %add.7.refs_1_), channel_id=1, source_target_pairs={{0,4},{2,6},{4,0},{6,2},{8,12},{10,14},{12,8},{14,10},{16,20},{18,... | collective-permute-start | bytes 393224 | tf_op jit(solution)/shard_map/ppermute | solution.py:589
  52.0 0.0 collective-permute-start.12
  52.0 4.3 %collective-permute-done.15.refs_5_ = f32[256,128]{1,0:T(8,128)S(1)} collective-permute-done((f32[256,128]{1,0:T(8,128)S(1)}, f32[256,128]{1,0:T(8,128)S(1)}, u32[]{:S(2)}, u32[]{:S(2)}) %collective-permute-start.15) | collective-permute-done | bytes 131104 | tf_op jit(solution)/shard_map/ppermute | solution.py:589
  56.3 0.0 collective-permute-done.14.refs_4_
  56.3 0.0 collective-permute-done.13.refs_3_
  56.3 0.0 collective-permute-done.12.refs_2_
  56.3 1.4 %shard_map.118 = (f32[2,128,128]{2,1,0:T(8,128)}, f32[2,128,128]{2,1,0:T(8,128)}) custom-call(s32[4]{0:T(128)S(1)} %pad_add_fusion.refs_0_, f32[256,128]{1,0:T(8,128)S(1)} %add.7.refs_1_, f32[256,128]{1,0:T(8,128)S(1)} %collective-permute-done.12.refs_2_, f32[256,128]{1,0:T(8,128)S(1)} %collective-permute-done.13.refs_3_, ...), custom_call_target="tpu_custom_call" | custom-call | tf_op jit(solution)/shard_map/pallas_call | solution.py:223
  (9 shorter events, 0.0 us)
Async XLA Ops:
  1.6 1.5 %copy-start = (f32[2,128,128]{2,1,0:T(8,128)S(1)}, f32[2,128,128]{2,1,0:T(8,128)}, u32[]{:S(2)}) copy-start(f32[2,128,128]{2,1,0:T(8,128)} %refs_6_.2) | copy-start | bytes 393220
  1.6 1.5 %copy-start.1 = (s32[2,128,128]{2,1,0:T(8,128)S(1)}, s32[2,128,128]{2,1,0:T(8,128)}, u32[]{:S(2)}) copy-start(s32[2,128,128]{2,1,0:T(8,128)} %param.11) | copy-start | bytes 393220
  1.6 1.5 %copy-start.2 = (f32[2,1,6,25,25]{4,1,3,2,0:T(1,128)S(1)}, f32[2,1,6,25,25]{4,1,3,2,0:T(1,128)}, u32[]{:S(2)}) copy-start(f32[2,1,6,25,25]{4,1,3,2,0:T(1,128)} %param.12) | copy-start | bytes 90004
  1.7 1.5 %copy-start.3 = (f32[1,6]{1,0:T(1,128)S(1)}, f32[1,6]{1,0:T(1,128)}, u32[]{:S(2)}) copy-start(f32[1,6]{1,0:T(1,128)} %refs_0_.1) | copy-start | bytes 76
  1.7 1.5 %copy-start.5 = (bf16[1888,256]{1,0:T(8,128)(2,1)S(1)}, bf16[1888,256]{1,0:T(8,128)(2,1)}, u32[]{:S(2)}) copy-start(bf16[1888,256]{1,0:T(8,128)(2,1)} %constant.6.clone.refs_4_) | copy-start | bytes 2899972
  1.9 4.1 %collective-permute-start = (f32[48,256]{1,0:T(8,128)S(1)}, f32[48,256]{1,0:T(8,128)S(1)}, u32[]{:S(2)}, u32[]{:S(2)}) collective-permute-start(f32[48,256]{1,0:T(8,128)S(1)} %get-tuple-element.15), channel_id=1, source_target_pairs={{0,2},{2,0},{4,6},{6,4},{8,10},{10,8},{12,14},{14,12},{16,18},{18,... | collective-permute-start | bytes 147464 | tf_op jit(solution)/shard_map/ppermute | solution.py:571
  2.5 3.6 %collective-permute-start.1 = (f32[48,256]{1,0:T(8,128)S(1)}, f32[48,256]{1,0:T(8,128)S(1)}, u32[]{:S(2)}, u32[]{:S(2)}) collective-permute-start(f32[48,256]{1,0:T(8,128)S(1)} %get-tuple-element.16), channel_id=1, source_target_pairs={{2,4},{4,2},{6,8},{8,6},{10,12},{12,10},{14,16},{16,14},{18,20},{2... | collective-permute-start | bytes 147464 | tf_op jit(solution)/shard_map/ppermute | solution.py:571
  3.2 2.9 %copy-start.4 = (bf16[4000,256]{1,0:T(8,128)(2,1)S(1)}, bf16[4000,256]{1,0:T(8,128)(2,1)}, u32[]{:S(2)}) copy-start(bf16[4000,256]{1,0:T(8,128)(2,1)} %constant.7.clone.refs_6_.refs_10_) | copy-start | bytes 6144004
  6.0 15.2 %copy-start.6 = (s32[2]{0:T(128)S(1)}, s32[2]{0:T(128)}, u32[]{:S(2)}) copy-start(s32[2]{0:T(128)} %param.16) | copy-start | bytes 28
  6.1 15.2 %copy-start.7 = (s32[2]{0:T(128)S(1)}, s32[2]{0:T(128)}, u32[]{:S(2)}) copy-start(s32[2]{0:T(128)} %param.15) | copy-start | bytes 28
  12.6 13.3 %collective-permute-start.5 = (f32[256,128]{1,0:T(8,128)S(1)}, f32[256,128]{1,0:T(8,128)S(1)}, u32[]{:S(2)}, u32[]{:S(2)}) collective-permute-start(f32[256,128]{1,0:T(8,128)S(1)} %get-tuple-element.18.refs_1_), channel_id=1, source_target_pairs={{0,16},{2,18},{4,20},{6,22},{8,24},{10,26},{12,28},{14,30},{16,0},... | collective-permute-start | bytes 393224 | tf_op jit(solution)/shard_map/ppermute | solution.py:589
  19.1 6.9 %collective-permute-start.4 = (f32[256,128]{1,0:T(8,128)S(1)}, f32[256,128]{1,0:T(8,128)S(1)}, u32[]{:S(2)}, u32[]{:S(2)}) collective-permute-start(f32[256,128]{1,0:T(8,128)S(1)} %get-tuple-element.18.refs_1_), channel_id=1, source_target_pairs={{0,8},{2,10},{4,12},{6,14},{8,0},{10,2},{12,4},{14,6},{16,24},{18,... | collective-permute-start | bytes 393224 | tf_op jit(solution)/shard_map/ppermute | solution.py:589
  20.7 5.3 %collective-permute-start.3 = (f32[256,128]{1,0:T(8,128)S(1)}, f32[256,128]{1,0:T(8,128)S(1)}, u32[]{:S(2)}, u32[]{:S(2)}) collective-permute-start(f32[256,128]{1,0:T(8,128)S(1)} %get-tuple-element.18.refs_1_), channel_id=1, source_target_pairs={{0,4},{2,6},{4,0},{6,2},{8,12},{10,14},{12,8},{14,10},{16,20},{18,... | collective-permute-start | bytes 393224 | tf_op jit(solution)/shard_map/ppermute | solution.py:589
  21.2 4.8 %collective-permute-start.2 = (f32[256,128]{1,0:T(8,128)S(1)}, f32[256,128]{1,0:T(8,128)S(1)}, u32[]{:S(2)}, u32[]{:S(2)}) collective-permute-start(f32[256,128]{1,0:T(8,128)S(1)} %get-tuple-element.18.refs_1_), channel_id=1, source_target_pairs={{0,2},{2,0},{4,6},{6,4},{8,10},{10,8},{12,14},{14,12},{16,18},{18,... | collective-permute-start | bytes 393224 | tf_op jit(solution)/shard_map/ppermute | solution.py:589
  26.9 6.1 %collective-permute-start.6 = (f32[256,128]{1,0:T(8,128)S(1)}, f32[256,128]{1,0:T(8,128)S(1)}, u32[]{:S(2)}, u32[]{:S(2)}) collective-permute-start(f32[256,128]{1,0:T(8,128)S(1)} %get-tuple-element.19.refs_1_.refs_7_), channel_id=1, source_target_pairs={{0,1},{1,0},{2,3},{3,2},{4,5},{5,4},{6,7},{7,6},{8,9},{9,8},{10,11... | collective-permute-start | bytes 393224 | tf_op jit(solution)/shard_map/ppermute | solution.py:580
  28.4 3.7 %collective-permute-start.8 = (f32[32,256]{1,0:T(8,128)S(1)}, f32[32,256]{1,0:T(8,128)S(1)}, u32[]{:S(2)}, u32[]{:S(2)}) collective-permute-start(f32[32,256]{1,0:T(8,128)S(1)} %get-tuple-element.20), channel_id=1, source_target_pairs={{0,3},{1,2},{2,1},{3,0},{4,7},{5,6},{6,5},{7,4},{8,11},{9,10},{10,... | collective-permute-start | bytes 98312 | tf_op jit(solution)/shard_map/ppermute | solution.py:573
  28.4 3.7 %collective-permute-start.7 = (f32[32,256]{1,0:T(8,128)S(1)}, f32[32,256]{1,0:T(8,128)S(1)}, u32[]{:S(2)}, u32[]{:S(2)}) collective-permute-start(f32[32,256]{1,0:T(8,128)S(1)} %get-tuple-element.20), channel_id=1, source_target_pairs={{0,2},{2,0},{4,6},{6,4},{8,10},{10,8},{12,14},{14,12},{16,18},{18,... | collective-permute-start | bytes 98312 | tf_op jit(solution)/shard_map/ppermute | solution.py:571
  29.1 3.9 %collective-permute-start.10 = (f32[32,256]{1,0:T(8,128)S(1)}, f32[32,256]{1,0:T(8,128)S(1)}, u32[]{:S(2)}, u32[]{:S(2)}) collective-permute-start(f32[32,256]{1,0:T(8,128)S(1)} %get-tuple-element.21), channel_id=1, source_target_pairs={{2,5},{3,4},{4,3},{5,2},{6,9},{7,8},{8,7},{9,6},{10,13},{11,12},{1... | collective-permute-start | bytes 98312 | tf_op jit(solution)/shard_map/ppermute | solution.py:573
  30.6 2.4 %collective-permute-start.9 = (f32[32,256]{1,0:T(8,128)S(1)}, f32[32,256]{1,0:T(8,128)S(1)}, u32[]{:S(2)}, u32[]{:S(2)}) collective-permute-start(f32[32,256]{1,0:T(8,128)S(1)} %get-tuple-element.21), channel_id=1, source_target_pairs={{2,4},{4,2},{6,8},{8,6},{10,12},{12,10},{14,16},{16,14},{18,20},{2... | collective-permute-start | bytes 98312 | tf_op jit(solution)/shard_map/ppermute | solution.py:571
  39.2 5.0 %collective-permute-start.11 = (f32[256,128]{1,0:T(8,128)S(1)}, f32[256,128]{1,0:T(8,128)S(1)}, u32[]{:S(2)}, u32[]{:S(2)}) collective-permute-start(f32[256,128]{1,0:T(8,128)S(1)} %shard_map.117), channel_id=1, source_target_pairs={{0,1},{1,0},{2,3},{3,2},{4,5},{5,4},{6,7},{7,6},{8,9},{9,8},{10,11... | collective-permute-start | bytes 393224 | tf_op jit(solution)/shard_map/ppermute | solution.py:580
  44.3 12.1 %collective-permute-start.15 = (f32[256,128]{1,0:T(8,128)S(1)}, f32[256,128]{1,0:T(8,128)S(1)}, u32[]{:S(2)}, u32[]{:S(2)}) collective-permute-start(f32[256,128]{1,0:T(8,128)S(1)} %add.7.refs_1_), channel_id=1, source_target_pairs={{0,16},{2,18},{4,20},{6,22},{8,24},{10,26},{12,28},{14,30},{16,0},... | collective-permute-start | bytes 393224 | tf_op jit(solution)/shard_map/ppermute | solution.py:589
  50.5 5.8 %collective-permute-start.14 = (f32[256,128]{1,0:T(8,128)S(1)}, f32[256,128]{1,0:T(8,128)S(1)}, u32[]{:S(2)}, u32[]{:S(2)}) collective-permute-start(f32[256,128]{1,0:T(8,128)S(1)} %add.7.refs_1_), channel_id=1, source_target_pairs={{0,8},{2,10},{4,12},{6,14},{8,0},{10,2},{12,4},{14,6},{16,24},{18,... | collective-permute-start | bytes 393224 | tf_op jit(solution)/shard_map/ppermute | solution.py:589
  51.3 5.1 %collective-permute-start.13 = (f32[256,128]{1,0:T(8,128)S(1)}, f32[256,128]{1,0:T(8,128)S(1)}, u32[]{:S(2)}, u32[]{:S(2)}) collective-permute-start(f32[256,128]{1,0:T(8,128)S(1)} %add.7.refs_1_), channel_id=1, source_target_pairs={{0,4},{2,6},{4,0},{6,2},{8,12},{10,14},{12,8},{14,10},{16,20},{18,... | collective-permute-start | bytes 393224 | tf_op jit(solution)/shard_map/ppermute | solution.py:589
  52.0 4.4 %collective-permute-start.12 = (f32[256,128]{1,0:T(8,128)S(1)}, f32[256,128]{1,0:T(8,128)S(1)}, u32[]{:S(2)}, u32[]{:S(2)}) collective-permute-start(f32[256,128]{1,0:T(8,128)S(1)} %add.7.refs_1_), channel_id=1, source_target_pairs={{0,2},{2,0},{4,6},{6,4},{8,10},{10,8},{12,14},{14,12},{16,18},{18,... | collective-permute-start | bytes 393224 | tf_op jit(solution)/shard_map/ppermute | solution.py:589

commit v18 on v16

--- a/solution.py
+++ b/solution.py
@@ -309,7 +309,7 @@
 
 def gradient_body(kern, last, f_ref, tgt_ref, h_ref, thr_ref, tb, g_ref, work):
     fld, inten, tot, a_cat, b_cat, r_cat, w_cat = work
-    group = 2 if kern % 2 == 0 else 1
+    group = 1
     count = kern // group
     chains = [(t, c) for t in range(2) for c in range(count)]
     lag = count + 2
@@ -594,7 +594,7 @@
     freq = jax.ShapeDtypeStruct((2, 4, XB, YB), f32)
     goal = jax.ShapeDtypeStruct((ROWS, 2 * CORE), f32)
     tiles = jax.ShapeDtypeStruct((tiles_dev, core, core), f32)
-    group = 2 if kern % 2 == 0 else 1
+    group = 1
     scratch = [
         pltpu.VMEM((2, kern, ROWS, 2 * CORE), f32),
         pltpu.VMEM((2, ROWS, CORE), f32),

time: 57.5 us -> 58.2 us (1.012)
  Pallas kernels: 16.9 us -> 17.6 us
    pallas_call x6, Pallas kernels: 16.9 us -> 17.6 us  [call(): pl.pallas_call(wrapped, out_shape=out_shape, in_specs=[sm if i in smem el...]
where the time goes in v18:
time: 58.2 us; the launch traced here: 58.1 us
  starting transfers between devices  23.9 us (41%)
  Pallas kernels  17.6 us (30%)
  waiting for transfers between devices  13.9 us (24%)
  between operations  1.49 us (3%)
  other arithmetic  1.08 us (2%)
    pallas_call x6, Pallas kernels, call(): pl.pallas_call(wrapped, out_shape=out_shape, in_specs=[sm if i in smem el...  17.6 us
    ppermute x8, starting transfers between devices, from_partners(): lax.ppermute(grad, 'tile', [(i, i ^ bit) for i in range(n_tile)])  16.6 us
    ppermute x8, waiting for transfers between devices, from_partners(): lax.ppermute(grad, 'tile', [(i, i ^ bit) for i in range(n_tile)])  8.9 us
    ppermute x2, waiting for transfers between devices, depth_pair(): peer = lax.ppermute(x, 'depth', [(i, i ^ bit) for i in range(n_depth)])  3.43 us
    ppermute x2, starting transfers between devices, depth_pair(): peer = lax.ppermute(x, 'depth', [(i, i ^ bit) for i in range(n_depth)])  3.2 us
    ppermute x4, starting transfers between devices, move(): return lax.ppermute(x, 'tile', pairs)  2.6 us
    ppermute x2, starting transfers between devices, move(): return lax.ppermute(x, ('tile', 'depth'), both)  1.54 us
    ppermute x2, waiting for transfers between devices, move(): return lax.ppermute(x, ('tile', 'depth'), both)  1.54 us
  transfers between devices with their start and end apart: 16, of which 6 were waited for; matrix products, arithmetic and copies ran while one was open for 0% of the time, Pallas kernels for 3%

profile of v18, /device:TPU:0, one launch (start us, length us, event | category | flops | bytes accessed | tf_op | source)
XLA Modules:
  0.0 58.1 jit_solution(1194178226203241715)
XLA Ops:
  0.6 1.0 %multiply_add_fusion.refs_0_ = f32[256,128]{1,0:T(8,128)S(1)} fusion(s32[2,128,128]{2,1,0:T(8,128)} %param.11, f32[2,128,128]{2,1,0:T(8,128)} %refs_6_.2), kind=kLoop, calls=%fused_computation | loop fusion | flops 98304 | bytes 393216 | tf_op jit(solution)/shard_map/add | solution.py:612
  1.6 0.0 copy-start.2
  1.6 0.0 copy-start.3
  1.6 0.0 copy-start.5
  1.7 0.3 shard_map.113
  1.9 0.5 collective-permute-start
  2.4 0.7 %collective-permute-start.1 = (f32[48,256]{1,0:T(8,128)S(1)}, f32[48,256]{1,0:T(8,128)S(1)}, u32[]{:S(2)}, u32[]{:S(2)}) collective-permute-start(f32[48,256]{1,0:T(8,128)S(1)} %get-tuple-element.11), channel_id=1, source_target_pairs={{2,4},{4,2},{6,8},{8,6},{10,12},{12,10},{14,16},{16,14},{18,20},{2... | collective-permute-start | bytes 147464 | tf_op jit(solution)/shard_map/ppermute | solution.py:567
  3.1 0.0 copy-start
  3.1 0.0 copy-start.1
  3.1 0.0 copy-start.4
  3.2 1.9 %shard_map.114.refs_5_.refs_9_ = f32[12,4,88,128]{3,2,1,0:T(8,128)S(1)} custom-call(f32[1,6]{1,0:T(1,128)S(1)} %copy-done.3, f32[2,6,25,1,25]{4,3,2,1,0:T(1,128)S(1)} %bitcast.7, bf16[1376,256]{1,0:T(8,128)(2,1)S(1)} %copy-done.5), custom_call_target="tpu_custom_call" | custom-call | flops 3000000000 | bytes 4000000 | tf_op jit(solution)/shard_map/pallas_call | solution.py:223
  5.7 0.0 collective-permute-done.refs_3_
  5.7 0.0 collective-permute-done.1.refs_4_
  5.8 0.0 copy-start.6
  5.8 0.0 copy-start.7
  5.8 6.6 %shard_map.115 = (f32[256,128]{1,0:T(8,128)S(1)}, f32[2,4,88,128]{3,2,1,0:T(8,128)S(1)}, f32[160,256]{1,0:T(8,128)S(1)}) custom-call(f32[1]{0:T(128)S(6)} %copy.12.refs_0_, f32[256,128]{1,0:T(8,128)S(1)} %bitcast.5, s32[256,128]{1,0:T(8,128)S(1)} %bitcast.6, f32[48,256]{1,0:T(8,128)S(1)} %collective-permute-done.refs_3_, ...), custom_call_target="tpu_custom_call" | custom-call | flops 10000000000 | tf_op jit(solution)/shard_map/pallas_call | solution.py:223
  12.4 6.7 %collective-permute-start.5 = (f32[256,128]{1,0:T(8,128)S(1)}, f32[256,128]{1,0:T(8,128)S(1)}, u32[]{:S(2)}, u32[]{:S(2)}) collective-permute-start(f32[256,128]{1,0:T(8,128)S(1)} %get-tuple-element.12.refs_1_), channel_id=1, source_target_pairs={{0,16},{2,18},{4,20},{6,22},{8,24},{10,26},{12,28},{14,30},{16,0},... | collective-permute-start | bytes 393224 | tf_op jit(solution)/shard_map/ppermute | solution.py:585
  19.2 1.6 %collective-permute-start.4 = (f32[256,128]{1,0:T(8,128)S(1)}, f32[256,128]{1,0:T(8,128)S(1)}, u32[]{:S(2)}, u32[]{:S(2)}) collective-permute-start(f32[256,128]{1,0:T(8,128)S(1)} %get-tuple-element.12.refs_1_), channel_id=1, source_target_pairs={{0,8},{2,10},{4,12},{6,14},{8,0},{10,2},{12,4},{14,6},{16,24},{18,... | collective-permute-start | bytes 393224 | tf_op jit(solution)/shard_map/ppermute | solution.py:585
  20.7 0.5 collective-permute-start.3
  21.2 0.0 collective-permute-start.2
  21.2 0.1 pad_add_fusion.refs_0_
  21.3 4.4 %collective-permute-done.5.refs_5_ = f32[256,128]{1,0:T(8,128)S(1)} collective-permute-done((f32[256,128]{1,0:T(8,128)S(1)}, f32[256,128]{1,0:T(8,128)S(1)}, u32[]{:S(2)}, u32[]{:S(2)}) %collective-permute-start.5) | collective-permute-done | bytes 131104 | tf_op jit(solution)/shard_map/ppermute | solution.py:585
  25.8 0.2 collective-permute-done.4.refs_4_
  25.9 0.0 collective-permute-done.3.refs_3_
  25.9 0.0 collective-permute-done.2.refs_2_
  25.9 0.8 %shard_map.116 = (f32[256,128]{1,0:T(8,128)S(1)}, f32[32,256]{1,0:T(8,128)S(1)}, f32[32,256]{1,0:T(8,128)S(1)}) custom-call(s32[4]{0:T(128)S(1)} %pad_add_fusion.refs_0_, f32[256,128]{1,0:T(8,128)S(1)} %get-tuple-element.12.refs_1_, f32[256,128]{1,0:T(8,128)S(1)} %collective-permute-done.2.refs_2_, f32[256,128]{1,0:T(8,128)S(1)} %collective-permute-done.3.refs_3_, ...), custom_call_target="tpu_custom_call" | custom-call | tf_op jit(solution)/shard_map/pallas_call | solution.py:223
  26.8 1.6 %collective-permute-start.6 = (f32[256,128]{1,0:T(8,128)S(1)}, f32[256,128]{1,0:T(8,128)S(1)}, u32[]{:S(2)}, u32[]{:S(2)}) collective-permute-start(f32[256,128]{1,0:T(8,128)S(1)} %get-tuple-element.13.refs_1_.refs_7_), channel_id=1, source_target_pairs={{0,1},{1,0},{2,3},{3,2},{4,5},{5,4},{6,7},{7,6},{8,9},{9,8},{10,11... | collective-permute-start | bytes 393224 | tf_op jit(solution)/shard_map/ppermute | solution.py:576
  28.4 0.0 collective-permute-start.8
  28.4 0.6 %collective-permute-start.7 = (f32[32,256]{1,0:T(8,128)S(1)}, f32[32,256]{1,0:T(8,128)S(1)}, u32[]{:S(2)}, u32[]{:S(2)}) collective-permute-start(f32[32,256]{1,0:T(8,128)S(1)} %get-tuple-element.14), channel_id=1, source_target_pairs={{0,2},{2,0},{4,6},{6,4},{8,10},{10,8},{12,14},{14,12},{16,18},{18,... | collective-permute-start | bytes 98312 | tf_op jit(solution)/shard_map/ppermute | solution.py:567
  29.0 1.5 %collective-permute-start.10 = (f32[32,256]{1,0:T(8,128)S(1)}, f32[32,256]{1,0:T(8,128)S(1)}, u32[]{:S(2)}, u32[]{:S(2)}) collective-permute-start(f32[32,256]{1,0:T(8,128)S(1)} %get-tuple-element.15), channel_id=1, source_target_pairs={{2,5},{3,4},{4,3},{5,2},{6,9},{7,8},{8,7},{9,6},{10,13},{11,12},{1... | collective-permute-start | bytes 98312 | tf_op jit(solution)/shard_map/ppermute | solution.py:569
  30.5 0.8 %collective-permute-start.9 = (f32[32,256]{1,0:T(8,128)S(1)}, f32[32,256]{1,0:T(8,128)S(1)}, u32[]{:S(2)}, u32[]{:S(2)}) collective-permute-start(f32[32,256]{1,0:T(8,128)S(1)} %get-tuple-element.15), channel_id=1, source_target_pairs={{2,4},{4,2},{6,8},{8,6},{10,12},{12,10},{14,16},{16,14},{18,20},{2... | collective-permute-start | bytes 98312 | tf_op jit(solution)/shard_map/ppermute | solution.py:567
  31.3 0.7 %collective-permute-done.8.refs_4_ = f32[32,256]{1,0:T(8,128)S(1)} collective-permute-done((f32[32,256]{1,0:T(8,128)S(1)}, f32[32,256]{1,0:T(8,128)S(1)}, u32[]{:S(2)}, u32[]{:S(2)}) %collective-permute-start.8) | collective-permute-done | bytes 32800 | tf_op jit(solution)/shard_map/ppermute | solution.py:569
  32.0 0.0 collective-permute-done.7.refs_3_
  32.0 0.8 %collective-permute-done.10.refs_6_ = f32[32,256]{1,0:T(8,128)S(1)} collective-permute-done((f32[32,256]{1,0:T(8,128)S(1)}, f32[32,256]{1,0:T(8,128)S(1)}, u32[]{:S(2)}, u32[]{:S(2)}) %collective-permute-start.10) | collective-permute-done | bytes 32800 | tf_op jit(solution)/shard_map/ppermute | solution.py:569
  32.9 0.0 collective-permute-done.9.refs_5_
  32.9 0.0 collective-permute-done.6.refs_2_.refs_8_
  32.9 6.6 %shard_map.117 = f32[256,128]{1,0:T(8,128)S(1)} custom-call(f32[1]{0:T(128)S(6)} %copy.12.refs_0_, f32[256,128]{1,0:T(8,128)S(1)} %get-tuple-element.13.refs_1_.refs_7_, f32[256,128]{1,0:T(8,128)S(1)} %collective-permute-done.6.refs_2_.refs_8_, f32[32,256]{1,0:T(8,128)S(1)} %collective-permute-done.7.refs_3_, f32[32,256]{1,0:T(8,128)S(1)} %collective-permute-done.8.refs_4_, ...), custom_call_target="tpu_custom_call" | custom-call | flops 10000000000 | tf_op jit(solution)/shard_map/pallas_call | solution.py:223
  39.5 1.6 %collective-permute-start.11 = (f32[256,128]{1,0:T(8,128)S(1)}, f32[256,128]{1,0:T(8,128)S(1)}, u32[]{:S(2)}, u32[]{:S(2)}) collective-permute-start(f32[256,128]{1,0:T(8,128)S(1)} %shard_map.117), channel_id=1, source_target_pairs={{0,1},{1,0},{2,3},{3,2},{4,5},{5,4},{6,7},{7,6},{8,9},{9,8},{10,11... | collective-permute-start | bytes 393224 | tf_op jit(solution)/shard_map/ppermute | solution.py:576
  41.1 3.4 %collective-permute-done.11 = f32[256,128]{1,0:T(8,128)S(1)} collective-permute-done((f32[256,128]{1,0:T(8,128)S(1)}, f32[256,128]{1,0:T(8,128)S(1)}, u32[]{:S(2)}, u32[]{:S(2)}) %collective-permute-start.11) | collective-permute-done | bytes 131104 | tf_op jit(solution)/shard_map/ppermute | solution.py:576
  44.5 6.4 %collective-permute-start.15 = (f32[256,128]{1,0:T(8,128)S(1)}, f32[256,128]{1,0:T(8,128)S(1)}, u32[]{:S(2)}, u32[]{:S(2)}) collective-permute-start(f32[256,128]{1,0:T(8,128)S(1)} %add.7.refs_1_), channel_id=1, source_target_pairs={{0,16},{2,18},{4,20},{6,22},{8,24},{10,26},{12,28},{14,30},{16,0},... | collective-permute-start | bytes 393224 | tf_op jit(solution)/shard_map/ppermute | solution.py:585
  50.9 0.7 %collective-permute-start.14 = (f32[256,128]{1,0:T(8,128)S(1)}, f32[256,128]{1,0:T(8,128)S(1)}, u32[]{:S(2)}, u32[]{:S(2)}) collective-permute-start(f32[256,128]{1,0:T(8,128)S(1)} %add.7.refs_1_), channel_id=1, source_target_pairs={{0,8},{2,10},{4,12},{6,14},{8,0},{10,2},{12,4},{14,6},{16,24},{18,... | collective-permute-start | bytes 393224 | tf_op jit(solution)/shard_map/ppermute | solution.py:585
  51.6 0.7 %collective-permute-start.13 = (f32[256,128]{1,0:T(8,128)S(1)}, f32[256,128]{1,0:T(8,128)S(1)}, u32[]{:S(2)}, u32[]{:S(2)}) collective-permute-start(f32[256,128]{1,0:T(8,128)S(1)} %add.7.refs_1_), channel_id=1, source_target_pairs={{0,4},{2,6},{4,0},{6,2},{8,12},{10,14},{12,8},{14,10},{16,20},{18,... | collective-permute-start | bytes 393224 | tf_op jit(solution)/shard_map/ppermute | solution.py:585
  52.3 0.0 collective-permute-start.12
  52.3 4.3 %collective-permute-done.15.refs_5_ = f32[256,128]{1,0:T(8,128)S(1)} collective-permute-done((f32[256,128]{1,0:T(8,128)S(1)}, f32[256,128]{1,0:T(8,128)S(1)}, u32[]{:S(2)}, u32[]{:S(2)}) %collective-permute-start.15) | collective-permute-done | bytes 131104 | tf_op jit(solution)/shard_map/ppermute | solution.py:585
  56.6 0.0 collective-permute-done.14.refs_4_
  56.6 0.0 collective-permute-done.13.refs_3_
  56.6 0.0 collective-permute-done.12.refs_2_
  56.6 1.4 %shard_map.118 = (f32[2,128,128]{2,1,0:T(8,128)}, f32[2,128,128]{2,1,0:T(8,128)}) custom-call(s32[4]{0:T(128)S(1)} %pad_add_fusion.refs_0_, f32[256,128]{1,0:T(8,128)S(1)} %add.7.refs_1_, f32[256,128]{1,0:T(8,128)S(1)} %collective-permute-done.12.refs_2_, f32[256,128]{1,0:T(8,128)S(1)} %collective-permute-done.13.refs_3_, ...), custom_call_target="tpu_custom_call" | custom-call | tf_op jit(solution)/shard_map/pallas_call | solution.py:223
  (9 shorter events, 0.0 us)
Async XLA Ops:
  1.6 1.5 %copy-start.2 = (f32[2,1,6,25,25]{4,1,3,2,0:T(1,128)S(1)}, f32[2,1,6,25,25]{4,1,3,2,0:T(1,128)}, u32[]{:S(2)}) copy-start(f32[2,1,6,25,25]{4,1,3,2,0:T(1,128)} %param.12) | copy-start | bytes 90004
  1.6 1.5 %copy-start.3 = (f32[1,6]{1,0:T(1,128)S(1)}, f32[1,6]{1,0:T(1,128)}, u32[]{:S(2)}) copy-start(f32[1,6]{1,0:T(1,128)} %refs_0_.3) | copy-start | bytes 76
  1.6 1.5 %copy-start.5 = (bf16[1376,256]{1,0:T(8,128)(2,1)S(1)}, bf16[1376,256]{1,0:T(8,128)(2,1)}, u32[]{:S(2)}) copy-start(bf16[1376,256]{1,0:T(8,128)(2,1)} %constant.6.clone.refs_2_) | copy-start | bytes 2113540
  1.9 3.8 %collective-permute-start = (f32[48,256]{1,0:T(8,128)S(1)}, f32[48,256]{1,0:T(8,128)S(1)}, u32[]{:S(2)}, u32[]{:S(2)}) collective-permute-start(f32[48,256]{1,0:T(8,128)S(1)} %get-tuple-element.10), channel_id=1, source_target_pairs={{0,2},{2,0},{4,6},{6,4},{8,10},{10,8},{12,14},{14,12},{16,18},{18,... | collective-permute-start | bytes 147464 | tf_op jit(solution)/shard_map/ppermute | solution.py:567
  2.4 3.3 %collective-permute-start.1 = (f32[48,256]{1,0:T(8,128)S(1)}, f32[48,256]{1,0:T(8,128)S(1)}, u32[]{:S(2)}, u32[]{:S(2)}) collective-permute-start(f32[48,256]{1,0:T(8,128)S(1)} %get-tuple-element.11), channel_id=1, source_target_pairs={{2,4},{4,2},{6,8},{8,6},{10,12},{12,10},{14,16},{16,14},{18,20},{2... | collective-permute-start | bytes 147464 | tf_op jit(solution)/shard_map/ppermute | solution.py:567
  3.1 2.6 %copy-start = (f32[2,128,128]{2,1,0:T(8,128)S(1)}, f32[2,128,128]{2,1,0:T(8,128)}, u32[]{:S(2)}) copy-start(f32[2,128,128]{2,1,0:T(8,128)} %refs_6_.2) | copy-start | bytes 393220
  3.1 2.6 %copy-start.1 = (s32[2,128,128]{2,1,0:T(8,128)S(1)}, s32[2,128,128]{2,1,0:T(8,128)}, u32[]{:S(2)}) copy-start(s32[2,128,128]{2,1,0:T(8,128)} %param.11) | copy-start | bytes 393220
  3.1 2.6 %copy-start.4 = (bf16[4160,256]{1,0:T(8,128)(2,1)S(1)}, bf16[4160,256]{1,0:T(8,128)(2,1)}, u32[]{:S(2)}) copy-start(bf16[4160,256]{1,0:T(8,128)(2,1)} %constant.7.clone.refs_6_.refs_10_) | copy-start | bytes 6389764
  5.8 15.5 %copy-start.6 = (s32[2]{0:T(128)S(1)}, s32[2]{0:T(128)}, u32[]{:S(2)}) copy-start(s32[2]{0:T(128)} %param.16) | copy-start | bytes 28
  5.8 15.5 %copy-start.7 = (s32[2]{0:T(128)S(1)}, s32[2]{0:T(128)}, u32[]{:S(2)}) copy-start(s32[2]{0:T(128)} %param.15) | copy-start | bytes 28
  12.4 13.3 %collective-permute-start.5 = (f32[256,128]{1,0:T(8,128)S(1)}, f32[256,128]{1,0:T(8,128)S(1)}, u32[]{:S(2)}, u32[]{:S(2)}) collective-permute-start(f32[256,128]{1,0:T(8,128)S(1)} %get-tuple-element.12.refs_1_), channel_id=1, source_target_pairs={{0,16},{2,18},{4,20},{6,22},{8,24},{10,26},{12,28},{14,30},{16,0},... | collective-permute-start | bytes 393224 | tf_op jit(solution)/shard_map/ppermute | solution.py:585
  19.2 6.8 %collective-permute-start.4 = (f32[256,128]{1,0:T(8,128)S(1)}, f32[256,128]{1,0:T(8,128)S(1)}, u32[]{:S(2)}, u32[]{:S(2)}) collective-permute-start(f32[256,128]{1,0:T(8,128)S(1)} %get-tuple-element.12.refs_1_), channel_id=1, source_target_pairs={{0,8},{2,10},{4,12},{6,14},{8,0},{10,2},{12,4},{14,6},{16,24},{18,... | collective-permute-start | bytes 393224 | tf_op jit(solution)/shard_map/ppermute | solution.py:585
  20.7 5.2 %collective-permute-start.3 = (f32[256,128]{1,0:T(8,128)S(1)}, f32[256,128]{1,0:T(8,128)S(1)}, u32[]{:S(2)}, u32[]{:S(2)}) collective-permute-start(f32[256,128]{1,0:T(8,128)S(1)} %get-tuple-element.12.refs_1_), channel_id=1, source_target_pairs={{0,4},{2,6},{4,0},{6,2},{8,12},{10,14},{12,8},{14,10},{16,20},{18,... | collective-permute-start | bytes 393224 | tf_op jit(solution)/shard_map/ppermute | solution.py:585
  21.2 4.7 %collective-permute-start.2 = (f32[256,128]{1,0:T(8,128)S(1)}, f32[256,128]{1,0:T(8,128)S(1)}, u32[]{:S(2)}, u32[]{:S(2)}) collective-permute-start(f32[256,128]{1,0:T(8,128)S(1)} %get-tuple-element.12.refs_1_), channel_id=1, source_target_pairs={{0,2},{2,0},{4,6},{6,4},{8,10},{10,8},{12,14},{14,12},{16,18},{18,... | collective-permute-start | bytes 393224 | tf_op jit(solution)/shard_map/ppermute | solution.py:585
  26.8 6.1 %collective-permute-start.6 = (f32[256,128]{1,0:T(8,128)S(1)}, f32[256,128]{1,0:T(8,128)S(1)}, u32[]{:S(2)}, u32[]{:S(2)}) collective-permute-start(f32[256,128]{1,0:T(8,128)S(1)} %get-tuple-element.13.refs_1_.refs_7_), channel_id=1, source_target_pairs={{0,1},{1,0},{2,3},{3,2},{4,5},{5,4},{6,7},{7,6},{8,9},{9,8},{10,11... | collective-permute-start | bytes 393224 | tf_op jit(solution)/shard_map/ppermute | solution.py:576
  28.4 3.7 %collective-permute-start.8 = (f32[32,256]{1,0:T(8,128)S(1)}, f32[32,256]{1,0:T(8,128)S(1)}, u32[]{:S(2)}, u32[]{:S(2)}) collective-permute-start(f32[32,256]{1,0:T(8,128)S(1)} %get-tuple-element.14), channel_id=1, source_target_pairs={{0,3},{1,2},{2,1},{3,0},{4,7},{5,6},{6,5},{7,4},{8,11},{9,10},{10,... | collective-permute-start | bytes 98312 | tf_op jit(solution)/shard_map/ppermute | solution.py:569
  28.4 3.7 %collective-permute-start.7 = (f32[32,256]{1,0:T(8,128)S(1)}, f32[32,256]{1,0:T(8,128)S(1)}, u32[]{:S(2)}, u32[]{:S(2)}) collective-permute-start(f32[32,256]{1,0:T(8,128)S(1)} %get-tuple-element.14), channel_id=1, source_target_pairs={{0,2},{2,0},{4,6},{6,4},{8,10},{10,8},{12,14},{14,12},{16,18},{18,... | collective-permute-start | bytes 98312 | tf_op jit(solution)/shard_map/ppermute | solution.py:567
  29.0 3.9 %collective-permute-start.10 = (f32[32,256]{1,0:T(8,128)S(1)}, f32[32,256]{1,0:T(8,128)S(1)}, u32[]{:S(2)}, u32[]{:S(2)}) collective-permute-start(f32[32,256]{1,0:T(8,128)S(1)} %get-tuple-element.15), channel_id=1, source_target_pairs={{2,5},{3,4},{4,3},{5,2},{6,9},{7,8},{8,7},{9,6},{10,13},{11,12},{1... | collective-permute-start | bytes 98312 | tf_op jit(solution)/shard_map/ppermute | solution.py:569
  30.5 2.4 %collective-permute-start.9 = (f32[32,256]{1,0:T(8,128)S(1)}, f32[32,256]{1,0:T(8,128)S(1)}, u32[]{:S(2)}, u32[]{:S(2)}) collective-permute-start(f32[32,256]{1,0:T(8,128)S(1)} %get-tuple-element.15), channel_id=1, source_target_pairs={{2,4},{4,2},{6,8},{8,6},{10,12},{12,10},{14,16},{16,14},{18,20},{2... | collective-permute-start | bytes 98312 | tf_op jit(solution)/shard_map/ppermute | solution.py:567
  39.5 5.0 %collective-permute-start.11 = (f32[256,128]{1,0:T(8,128)S(1)}, f32[256,128]{1,0:T(8,128)S(1)}, u32[]{:S(2)}, u32[]{:S(2)}) collective-permute-start(f32[256,128]{1,0:T(8,128)S(1)} %shard_map.117), channel_id=1, source_target_pairs={{0,1},{1,0},{2,3},{3,2},{4,5},{5,4},{6,7},{7,6},{8,9},{9,8},{10,11... | collective-permute-start | bytes 393224 | tf_op jit(solution)/shard_map/ppermute | solution.py:576
  44.5 12.1 %collective-permute-start.15 = (f32[256,128]{1,0:T(8,128)S(1)}, f32[256,128]{1,0:T(8,128)S(1)}, u32[]{:S(2)}, u32[]{:S(2)}) collective-permute-start(f32[256,128]{1,0:T(8,128)S(1)} %add.7.refs_1_), channel_id=1, source_target_pairs={{0,16},{2,18},{4,20},{6,22},{8,24},{10,26},{12,28},{14,30},{16,0},... | collective-permute-start | bytes 393224 | tf_op jit(solution)/shard_map/ppermute | solution.py:585
  50.9 5.7 %collective-permute-start.14 = (f32[256,128]{1,0:T(8,128)S(1)}, f32[256,128]{1,0:T(8,128)S(1)}, u32[]{:S(2)}, u32[]{:S(2)}) collective-permute-start(f32[256,128]{1,0:T(8,128)S(1)} %add.7.refs_1_), channel_id=1, source_target_pairs={{0,8},{2,10},{4,12},{6,14},{8,0},{10,2},{12,4},{14,6},{16,24},{18,... | collective-permute-start | bytes 393224 | tf_op jit(solution)/shard_map/ppermute | solution.py:585
  51.6 5.0 %collective-permute-start.13 = (f32[256,128]{1,0:T(8,128)S(1)}, f32[256,128]{1,0:T(8,128)S(1)}, u32[]{:S(2)}, u32[]{:S(2)}) collective-permute-start(f32[256,128]{1,0:T(8,128)S(1)} %add.7.refs_1_), channel_id=1, source_target_pairs={{0,4},{2,6},{4,0},{6,2},{8,12},{10,14},{12,8},{14,10},{16,20},{18,... | collective-permute-start | bytes 393224 | tf_op jit(solution)/shard_map/ppermute | solution.py:585
  52.3 4.3 %collective-permute-start.12 = (f32[256,128]{1,0:T(8,128)S(1)}, f32[256,128]{1,0:T(8,128)S(1)}, u32[]{:S(2)}, u32[]{:S(2)}) collective-permute-start(f32[256,128]{1,0:T(8,128)S(1)} %add.7.refs_1_), channel_id=1, source_target_pairs={{0,2},{2,0},{4,6},{6,4},{8,10},{10,8},{12,14},{14,12},{16,18},{18,... | collective-permute-start | bytes 393224 | tf_op jit(solution)/shard_map/ppermute | solution.py:585
